TPU v7x, 32 devices: a whole 2x2x4 slice. The times are simulated.
32 devices in a mesh: dp: 4 (over z), ctx: 8 (over y, x, core).
Axes of the slice: x: 2, y: 2, z: 4, core: 2. Of those that a mesh axis runs over, the one named last changes fastest.
Arguments:
- tokens: bfloat16 [1536, 4096], P('ctx'), may hold values from -6 to 6
- w_in: bfloat16 [4096, 3, 4096], P('ctx', None, 'dp'), may hold values from -0.09375 to 0.09375
- short_filter: float32 [3, 3, 4096], P(None, None, 'dp'), may hold values from -3.5 to 3.5
- mode_decay: float32 [8, 4096], P(None, 'dp'), may hold values from 0 to 1
- residue: float32 [8, 4096], P(None, 'dp'), may hold values from -2 to 2
- w_out: bfloat16 [4096, 4096], P('dp'), may hold values from -0.125 to 0.125
Outputs:
- block_out: bfloat16 [1536, 4096], P('ctx', 'dp')
All inputs are finite; a program needn't handle non-finite values.
Results may differ from a plain program's by a relative error of at most 0.018.
Values may be sent and summed in bfloat16 or wider, within the bound.
No kernel may reach another device: no remote copies, remote signals or barrier semaphores. Data moves between devices by JAX's collectives and lax.ppermute only.
A program may use at most 128 MiB of HBM per device.

v0:
```python
import jax
import jax.numpy as jnp
from jax import lax
from jax.sharding import PartitionSpec as P

BLK = 64


def from_behind(block, axis, distance):
    devices = range(lax.axis_size(axis))
    route = [(i - distance, i) for i in devices if i - distance in devices]
    return lax.ppermute(block, axis, route)


def prefix(value, axis, join, neutral):
    count, mine = (lax.axis_size(axis), lax.axis_index(axis))
    pieces = jax.tree.map(lambda part: lax.all_gather(part, axis), value)
    subtotal = jax.tree.map(
        lambda part, zero: jnp.full_like(part, 0) + jnp.asarray(zero, part.dtype), value, neutral
    )

    def lap(position, subtotal):
        longer = join(subtotal, jax.tree.map(lambda part: part[position], pieces))
        return jax.tree.map(lambda new, old: jnp.where(position < mine, new, old), longer, subtotal)

    return lax.fori_loop(0, count - 1, lap, subtotal)


def on_device(tokens, w_in, short_filter, mode_decay, residue, w_out):
    row_count = tokens.shape[0]
    chan_count = w_in.shape[2]
    short_count = short_filter.shape[0]
    mode_count = mode_decay.shape[0]
    earlier_rows = from_behind(tokens[row_count - (short_count - 1) :], "ctx", 1)
    source = jnp.concatenate([earlier_rows, tokens], 0)
    projected = jnp.einsum(
        "td,dgc->tgc",
        source,
        lax.all_gather(w_in, "ctx", axis=0, tiled=True),
        preferred_element_type=jnp.float32,
    )
    featured = jnp.zeros((row_count, 3, chan_count), jnp.float32)
    for j in range(short_count):
        featured = (
            featured
            + short_filter[j] * projected[short_count - 1 - j : short_count - 1 - j + row_count]
        )
    mixed = (featured[:, 1] * featured[:, 2]).astype(jnp.bfloat16)
    medium = mixed.astype(jnp.float32)
    highest = lax.Precision.HIGHEST
    mode_gain = residue * jnp.sqrt(1.0 - mode_decay * mode_decay)
    block_len = BLK
    block_times = jnp.arange(block_len).astype(jnp.float32)
    power_in = jnp.power(mode_decay[None], block_times[:, None, None])
    kernel_head = jnp.sum(mode_gain[None] * power_in, 1)
    lag_index = jnp.arange(block_len)[:, None] - jnp.arange(block_len)[None, :]
    toeplitz = jnp.where(
        (lag_index >= 0)[:, :, None], kernel_head[jnp.clip(lag_index, 0, block_len - 1)], 0.0
    )
    carry_weights = mode_gain[None] * power_in * mode_decay[None]
    state_weights = power_in[::-1]
    decay_block = jnp.power(mode_decay, float(block_len))
    blocks = medium.reshape(row_count // block_len, block_len, chan_count)

    def block_step(carried, block_rows):
        inner = jnp.einsum("tsc,sc->tc", toeplitz, block_rows, precision=highest)
        inner = inner + jnp.einsum("tnc,nc->tc", carry_weights, carried, precision=highest)
        carried = decay_block * carried + jnp.einsum(
            "snc,sc->nc", state_weights, block_rows, precision=highest
        )
        return (carried, inner)

    zero_state = jnp.zeros((mode_count, chan_count), jnp.float32)
    local_end, local_part = lax.scan(block_step, zero_state, blocks)
    local_part = local_part.reshape(row_count, chan_count)
    decay_device = jnp.power(mode_decay, float(row_count))

    def combine_states(earlier, later):
        return (earlier[0] * later[0], later[0] * earlier[1] + later[1])

    identity = (jnp.ones((mode_count, chan_count), jnp.float32), zero_state)
    scanned = prefix((decay_device, local_end), "ctx", combine_states, identity)
    entering = scanned[1]
    row_times = jnp.arange(1, row_count + 1).astype(jnp.float32)
    entry_weights = mode_gain[None] * jnp.power(mode_decay[None], row_times[:, None, None])
    long_part = local_part + jnp.einsum("tnc,nc->tc", entry_weights, entering, precision=highest)
    gated = (featured[:, 0] * long_part).astype(jnp.bfloat16)
    out_term = jnp.dot(gated, w_out, preferred_element_type=jnp.float32)
    return lax.psum_scatter(out_term.astype(jnp.bfloat16), "dp", scatter_dimension=1, tiled=True)


def solution(mesh):
    return jax.shard_map(
        on_device,
        mesh=mesh,
        in_specs=(
            P("ctx", None),
            P("ctx", None, "dp"),
            P(None, None, "dp"),
            P(None, "dp"),
            P(None, "dp"),
            P("dp", None),
        ),
        out_specs=P("ctx", "dp"),
        check_vma=False,
    )
```

profile of v0, /device:TPU:0, one launch (start us, length us, event | category | flops | bytes accessed | tf_op | source)
XLA Modules:
  0.0 266.2 jit_solution(15091010876531769246)
XLA Ops:
  6.5 0.0 copy-start.2
  6.5 0.0 copy-start.4
  6.5 0.0 all-gather.4.cloned.1.call-start
  6.5 0.7 all-gather.4.cloned.1.call-update
  7.3 0.0 reduce-scatter.2.cloned.1.call-start
  7.3 0.9 slice.31
  8.2 2.4 collective-permute-start
  10.6 0.1 reshape.63
  10.6 0.0 copy-done.2
  10.6 0.0 copy-done.4
  10.7 5.1 %multiply_reduce_fusion.4 = (f32[64,1024]{1,0:T(8,128)S(1)}, f32[64,8,1024]{2,1,0:T(8,128)}) fusion(f32[8,1024]{1,0:T(8,128)S(1)} %get-tuple-element.345, f32[64]{0:T(128)S(1)} %iota_convert_fusion, f32[8,1024]{1,0:T(8,128)S(1)} %copy-done.2), kind=kLoop, calls=%fused_computation.20 | loop fusion | flops 983040 | bytes 2425088 | tf_op jit(solution)/shard_map/reduce_sum | solution.py:55
  15.8 0.0 copy-start.3
  15.8 18.5 %gather_fusion = f32[4096,1024]{1,0:T(8,128)} fusion(f32[64,1024]{1,0:T(8,128)S(1)} %get-tuple-element.236, s32[4096]{0:T(1024)S(1)} %broadcast_clamp_fusion), kind=kCustom, calls=%fused_computation | custom fusion | bytes 33570816 | tf_op jit(solution)/shard_map/gather | solution.py:58
  34.3 0.0 copy-done.3
  34.3 11.4 %broadcast_select_fusion = f32[64,64,1024]{2,1,0:T(8,128)} fusion(f32[64,64,1024]{2,1,0:T(8,128)} %bitcast.78, pred[64,64]{1,0:T(8,128)(4,1)S(1)} %subtract_compare_fusion), kind=kLoop, calls=%fused_computation.12 | loop fusion | flops 4194304 | bytes 33558528 | tf_op jit(solution)/shard_map/jit(_where)/select_n | solution.py:57
  45.7 12.0 %all-gather = f32[64,1024]{1,0:T(8,128)S(1)} all-gather(f32[8,1024]{1,0:T(8,128)S(1)} %get-tuple-element.240), channel_id=2, replica_groups=mesh['dp'=4,'ctx'=8] {'ctx'}, dimensions={0}, use_global_device_ids=true | all-gather | bytes 294912 | tf_op jit(solution)/shard_map/all_gather | solution.py:17
  57.7 1.7 rev.3
  59.4 0.0 collective-permute-done
  59.4 78.9 %all-gather.4.cloned.1.call-done = bf16[4096,3,1024]{2,0,1:T(8,128)(2,1)} async-done(((bf16[512,3,1024]{2,0,1:T(8,128)(2,1)}), bf16[4096,3,1024]{2,0,1:T(8,128)(2,1)}) %all-gather.4.cloned.1.call-update) | async-done | bytes 25165840 | tf_op jit(solution)/shard_map/all_gather | solution.py:39
  138.4 11.3 %fusion.5 = f32[194,3,1024]{2,0,1:T(8,128)S(1)} fusion(bf16[4096,3,1024]{2,0,1:T(8,128)(2,1)} %all-gather.4.cloned.1.call-done, bf16[192,4096]{1,0:T(8,128)(2,1)} %param.10, bf16[2,4096]{1,0:T(2,128)(2,1)S(1)} %collective-permute-done), kind=kOutput, calls=%fused_computation.22 | convolution fusion | flops 4885348352 | bytes 29138944 | tf_op jit(solution)/shard_map/td,dgc->tgc/dot_general | solution.py:36
  149.7 0.7 fusion.3
  150.4 0.0 copy-start
  150.4 1.4 copy-done
  151.8 0.1 fusion.8
  151.9 1.0 convert.1
  152.9 42.4 %while.27 = (s32[]{:T(128)}, f32[8,1024]{1,0:T(8,128)S(1)}, f32[3,64,1024]{2,1,0:T(8,128)}, f32[8,1024]{1,0:T(8,128)S(1)}, f32[3,64,1024]{2,1,0:T(8,128)}, /*ind...) while((s32[]{:T(128)}, f32[8,1024]{1,0:T(8,128)S(1)}, ...), condition=%wide.region_2.3_spmd.clone, body=%wide.region_1.2_spmd.clone.sunk | while | flops 11485187 | bytes 21529476 | solution.py:74
  152.9 1.0 dynamic-slice_bitcast_fusion.2
  153.9 0.4 multiply_reduce_fusion.8
  154.3 3.6 %multiply_reduce_fusion.10 = f32[1024,64]{0,1:T(8,128)S(1)} fusion(f32[1024,8]{0,1:T(8,128)S(1)} %get-tuple-element.331, f32[64]{0:T(128)S(1)} %get-tuple-element.368, f32[8,1024]{1,0:T(8,128)S(1)} %get-tuple-element.370, f32[8,1024]{1,0:T(8,128)S(1)} %get-tuple-element.369), kind=kLoop, calls=%fused_computation.6.clone.1 | loop fusion | flops 2031616 | bytes 360704 | tf_op jit(solution)/shard_map/while/body/eval_jaxpr/tnc,nc->tc/dot_general | solution.py:67
  157.9 8.4 %multiply_reduce_fusion.9 = f32[1024,64]{0,1:T(8,128)S(1)} fusion(f32[64,64,1024]{2,1,0:T(8,128)} %get-tuple-element.367, f32[1024,64]{0,1:T(8,128)S(1)} %dynamic-slice_bitcast_fusion.2), kind=kLoop, calls=%fused_computation.5.clone.1 | loop fusion | flops 8323072 | bytes 17301504 | tf_op jit(solution)/shard_map/while/body/eval_jaxpr/tsc,sc->tc/dot_general | solution.py:66
  166.3 0.8 bitcast_dynamic-update-slice_fusion.2
  167.1 1.0 dynamic-slice_bitcast_fusion.2
  168.0 0.4 multiply_reduce_fusion.8
  168.5 3.6 %multiply_reduce_fusion.10 = f32[1024,64]{0,1:T(8,128)S(1)} fusion(f32[1024,8]{0,1:T(8,128)S(1)} %get-tuple-element.331, f32[64]{0:T(128)S(1)} %get-tuple-element.368, f32[8,1024]{1,0:T(8,128)S(1)} %get-tuple-element.370, f32[8,1024]{1,0:T(8,128)S(1)} %get-tuple-element.369), kind=kLoop, calls=%fused_computation.6.clone.1 | loop fusion | flops 2031616 | bytes 360704 | tf_op jit(solution)/shard_map/while/body/eval_jaxpr/tnc,nc->tc/dot_general | solution.py:67
  172.0 8.4 %multiply_reduce_fusion.9 = f32[1024,64]{0,1:T(8,128)S(1)} fusion(f32[64,64,1024]{2,1,0:T(8,128)} %get-tuple-element.367, f32[1024,64]{0,1:T(8,128)S(1)} %dynamic-slice_bitcast_fusion.2), kind=kLoop, calls=%fused_computation.5.clone.1 | loop fusion | flops 8323072 | bytes 17301504 | tf_op jit(solution)/shard_map/while/body/eval_jaxpr/tsc,sc->tc/dot_general | solution.py:66
  180.5 0.7 bitcast_dynamic-update-slice_fusion.2
  181.2 1.0 dynamic-slice_bitcast_fusion.2
  182.2 0.4 multiply_reduce_fusion.8
  182.6 3.6 %multiply_reduce_fusion.10 = f32[1024,64]{0,1:T(8,128)S(1)} fusion(f32[1024,8]{0,1:T(8,128)S(1)} %get-tuple-element.331, f32[64]{0:T(128)S(1)} %get-tuple-element.368, f32[8,1024]{1,0:T(8,128)S(1)} %get-tuple-element.370, f32[8,1024]{1,0:T(8,128)S(1)} %get-tuple-element.369), kind=kLoop, calls=%fused_computation.6.clone.1 | loop fusion | flops 2031616 | bytes 360704 | tf_op jit(solution)/shard_map/while/body/eval_jaxpr/tnc,nc->tc/dot_general | solution.py:67
  186.2 8.4 %multiply_reduce_fusion.9 = f32[1024,64]{0,1:T(8,128)S(1)} fusion(f32[64,64,1024]{2,1,0:T(8,128)} %get-tuple-element.367, f32[1024,64]{0,1:T(8,128)S(1)} %dynamic-slice_bitcast_fusion.2), kind=kLoop, calls=%fused_computation.5.clone.1 | loop fusion | flops 8323072 | bytes 17301504 | tf_op jit(solution)/shard_map/while/body/eval_jaxpr/tsc,sc->tc/dot_general | solution.py:66
  194.6 0.7 bitcast_dynamic-update-slice_fusion.2
  195.3 0.0 copy-start.1
  195.3 9.4 %all-gather.1 = f32[64,1024]{1,0:T(8,128)S(1)} all-gather(f32[8,1024]{1,0:T(8,128)S(1)} %get-tuple-element.143), channel_id=3, replica_groups=mesh['dp'=4,'ctx'=8] {'ctx'}, dimensions={0}, use_global_device_ids=true | all-gather | bytes 294912 | tf_op jit(solution)/shard_map/all_gather | solution.py:17
  204.7 0.5 while.28
  205.2 10.9 %multiply_reduce_fusion.3 = f32[1024,192]{0,1:T(8,128)S(1)} fusion(f32[1024,8]{0,1:T(8,128)S(1)} %bitcast.80, f32[192]{0:T(256)S(1)} %add_convert_fusion, f32[8,1024]{1,0:T(8,128)S(1)} %get-tuple-element.400, f32[8,1024]{1,0:T(8,128)S(1)} %get-tuple-element.401), kind=kLoop, calls=%fused_computation.13 | loop fusion | flops 4521984 | bytes 885504 | tf_op jit(solution)/shard_map/tnc,nc->tc/dot_general | solution.py:86
  216.2 0.0 copy-done.1
  216.2 1.3 fusion.10
  217.5 6.4 %convolution_convert_fusion = bf16[192,4096]{1,0:T(8,128)(2,1)} fusion(bf16[192,1024]{1,0:T(8,128)(2,1)S(1)} %fusion.10, bf16[1024,4096]{1,0:T(8,128)(2,1)} %param.15), kind=kOutput, calls=%fused_computation.14 | convolution fusion | flops 1611399168 | bytes 10354688 | tf_op jit(solution)/shard_map/dot_general | solution.py:88
  223.9 0.0 reduce-scatter.2.cloned.1.call-update
  223.9 35.4 %reduce-scatter.2.cloned.1.call-done = bf16[192,1024]{1,0:T(8,128)(2,1)} async-done(((bf16[192,4096]{1,0:T(8,128)(2,1)}), bf16[192,1024]{1,0:T(8,128)(2,1)}) %reduce-scatter.2.cloned.1.call-update) | async-done | bytes 393232 | tf_op jit(solution)/shard_map/reduce_scatter | solution.py:89
  (20 shorter events, 0.2 us)
Async XLA Ops:
  6.5 4.1 %copy-start.2 = (f32[8,1024]{1,0:T(8,128)S(1)}, f32[8,1024]{1,0:T(8,128)}, u32[]{:S(2)}) copy-start(f32[8,1024]{1,0:T(8,128)} %param.13) | copy-start | bytes 98308
  6.5 4.1 %copy-start.4 = (f32[8,1024]{1,0:T(8,128)S(1)}, f32[8,1024]{1,0:T(8,128)}, u32[]{:S(2)}) copy-start(f32[8,1024]{1,0:T(8,128)} %param.14) | copy-start | bytes 98308
  6.5 131.8 %all-gather.4.cloned.1.call-start = ((), (), s32[]{:S(2)}) async-start(), calls=%async_computation.1 | async-start | bytes 28311552 | tf_op jit(solution)/shard_map/all_gather | solution.py:39
  7.3 252.1 %reduce-scatter.2.cloned.1.call-start = ((), (), s32[]{:S(2)}) async-start(), calls=%async_computation.2 | async-start | bytes 1966080 | tf_op jit(solution)/shard_map/reduce_scatter | solution.py:89
  8.2 51.3 %collective-permute-start = (bf16[2,4096]{1,0:T(2,128)(2,1)S(1)}, bf16[2,4096]{1,0:T(2,128)(2,1)S(1)}, u32[]{:S(2)}, u32[]{:S(2)}) collective-permute-start(bf16[2,4096]{1,0:T(2,128)(2,1)S(1)} %slice.31), channel_id=1, source_target_pairs={{0,1},{1,2},{2,3},{3,4},{4,5},{5,6},{6,7},{8,9},{9,10},{10,11},{11... | collective-permute-start | bytes 49160 | tf_op jit(solution)/shard_map/ppermute | solution.py:12
  15.8 18.5 %copy-start.3 = (f32[3,3,1024]{2,1,0:T(4,128)S(1)}, f32[3,3,1024]{2,1,0:T(4,128)}, u32[]{:S(2)}) copy-start(f32[3,3,1024]{2,1,0:T(4,128)} %param.12) | copy-start | bytes 110596
  150.4 1.4 copy-start
  195.3 20.8 %copy-start.1 = (f32[3,64,1024]{2,1,0:T(8,128)S(1)}, f32[3,64,1024]{2,1,0:T(8,128)}, u32[]{:S(2)}) copy-start(f32[3,64,1024]{2,1,0:T(8,128)} %get-tuple-element.142) | copy-start | bytes 2359300
Sparse Core Ops, SparseCore 0:
  9.3 129.0 all-gather.3
  224.0 35.2 reduce-scatter.1
where the time goes:
time: 267 us; the launch traced here: 266 us
  waiting for transfers between devices  115 us (43%)
  other arithmetic  70.1 us (26%)
  local copies, waits for them, and re-layouts  25.5 us (10%)
  blocking collectives  21.4 us (8%)
  matrix products  17.7 us (7%)
  between operations  13.5 us (5%)
    all_gather x1, waiting for transfers between devices, on_device(): lax.all_gather(w_in, 'ctx', axis=0, tiled=True)  78.9 us
    reduce_scatter x1, waiting for transfers between devices, on_device(): lax.psum_scatter(out_term.astype(jnp.bfloat16), 'dp', scatter_dimension=1...  35.4 us
    dot_general x3, other arithmetic, block_step(): inner = jnp.einsum('tsc,sc->tc', toeplitz, block_rows, precision=highest)  25.2 us
    all_gather x2, blocking collectives, prefix(): pieces = jax.tree.map(lambda part: lax.all_gather(part, axis), value)  21.4 us
    gather x1, local copies, waits for them, and re-layouts, on_device(): kernel_head[jnp.clip(lag_index, 0, block_len - 1)]  18.5 us
    select_n x1, other arithmetic, on_device(): jnp.where((lag_index >= 0)[:, :, None], kernel_head[jnp.clip(lag_index, 0...  11.4 us
    dot_general x1, matrix products, on_device(): jnp.einsum('td,dgc->tgc', source, lax.all_gather(w_in, 'ctx', axis=0, til...  11.3 us
    dot_general x1, other arithmetic, on_device(): jnp.einsum('tnc,nc->tc', entry_weights, entering, precision=highest)  10.9 us
  transfers between devices with their start and end apart: 3, of which 2 were waited for; matrix products, arithmetic and copies ran while one was open for 14% of the time, Pallas kernels for 0%

commit v1 on v0

--- a/solution.py
+++ b/solution.py
@@ -1,9 +1,15 @@
+import functools
+
 import jax
 import jax.numpy as jnp
 from jax import lax
+from jax.experimental import pallas as pl
+from jax.experimental.pallas import tpu as pltpu
 from jax.sharding import PartitionSpec as P
 
 BLK = 64
+F32, BF16 = jnp.float32, jnp.bfloat16
+VMEM_LIMIT = 48 * 1024 * 1024
 
 
 def from_behind(block, axis, distance):
@@ -26,7 +32,7 @@
     return lax.fori_loop(0, count - 1, lap, subtotal)
 
 
-def on_device(tokens, w_in, short_filter, mode_decay, residue, w_out):
+def on_device_any(tokens, w_in, short_filter, mode_decay, residue, w_out):
     row_count = tokens.shape[0]
     chan_count = w_in.shape[2]
     short_count = short_filter.shape[0]
@@ -89,7 +95,295 @@
     return lax.psum_scatter(out_term.astype(jnp.bfloat16), "dp", scatter_dimension=1, tiled=True)
 
 
+def project_kernel(order, *refs, pieces):
+    x_refs, (own_ref, other_ref, out_ref, rows) = refs[:pieces], refs[pieces:]
+    high = x_refs[0].shape[0]
+    depth = own_ref.shape[1]
+    half = out_ref.shape[-1]
+
+    @pl.when((pl.program_id(0) == 0) & (pl.program_id(1) == 0))
+    def _():
+        for i, x_ref in enumerate(x_refs):
+            rows[pl.ds(pl.multiple_of(order[i] * high, high), high), :] = x_ref[...]
+
+    total = jnp.dot(rows[:, :depth], own_ref[0], preferred_element_type=F32)
+    total += jnp.dot(rows[:, depth:], other_ref[0], preferred_element_type=F32)
+    core = order[2 * pieces]
+    for h in range(2):
+        out_ref[0, core ^ h] = total[:, h * half : (h + 1) * half].astype(out_ref.dtype)
+
+
+def project(order, xs, own, other, slots, kind):
+    pieces = len(xs)
+    streams, depth, chans = own.shape
+    high = xs[0].shape[0]
+    wide = chans // pieces
+    half = wide // 2
+    first = slots[0]
+    step = slots[1] - slots[0] if len(slots) > 1 else 0
+    weight = pl.BlockSpec(
+        (1, depth, wide), lambda s, g, order: (g, 0, order[pieces + first + step * s])
+    )
+    return pl.pallas_call(
+        functools.partial(project_kernel, pieces=pieces),
+        out_shape=jax.ShapeDtypeStruct((len(slots), 2, pieces * high, streams * half), kind),
+        grid_spec=pltpu.PrefetchScalarGridSpec(
+            num_scalar_prefetch=1,
+            grid=(len(slots), streams),
+            in_specs=[pl.BlockSpec(x.shape, lambda s, g, order: (0, 0)) for x in xs]
+            + [weight, weight],
+            out_specs=pl.BlockSpec(
+                (1, 2, pieces * high, half), lambda s, g, order: (s, 0, 0, g)
+            ),
+            scratch_shapes=[pltpu.VMEM((pieces * high, 2 * depth), BF16)],
+        ),
+        compiler_params=pltpu.CompilerParams(vmem_limit_bytes=VMEM_LIMIT),
+        cost_estimate=pl.CostEstimate(
+            flops=2 * len(slots) * pieces * high * 2 * depth * streams * wide,
+            bytes_accessed=len(slots) * 2 * depth * streams * wide * 2,
+            transcendentals=0,
+        ),
+        name="project",
+    )(order, *xs, own, other)
+
+
+def hyena_kernel(
+    core, own_ref, near_ref, far_ref, swap_ref, filt_ref, decay_ref, residue_ref,
+    out_ref, rows, mixed_s, gate_s, state, enter, edge, *, blocks,
+):
+    high = rows.shape[1] // blocks
+    chans = rows.shape[2]
+    modes = decay_ref.shape[0]
+    taps = filt_ref.shape[0]
+    mine = core[0]
+
+    def place(p, _):
+        here = pl.ds(pl.multiple_of(p * high, high), high)
+        own_at = pl.ds(pl.multiple_of((2 * p + mine) * high, high), high)
+        swap_at = pl.ds(pl.multiple_of((2 * p + 1 - mine) * high, high), high)
+        for g in range(3):
+            lanes = slice(g * chans, (g + 1) * chans)
+            rows[g, own_at, :] = (
+                own_ref[here, lanes]
+                + near_ref[here, lanes].astype(F32)
+                + far_ref[here, lanes].astype(F32)
+            )
+            rows[g, swap_at, :] = swap_ref[here, lanes].astype(F32)
+        return 0
+
+    lax.fori_loop(0, blocks // 2, place, 0)
+
+    for k in range(1, taps):
+        for g in range(3):
+            edge[k - 1, g, 0:1, :] = jnp.zeros((1, chans), F32)
+            for b in range(1, blocks):
+                edge[k - 1, g, b : b + 1, :] = rows[g, b * high - k : b * high - k + 1, :]
+
+    decay = [jnp.broadcast_to(decay_ref[n : n + 1, :], (blocks, chans)) for n in range(modes)]
+    filt = [
+        [jnp.broadcast_to(filt_ref[j, g : g + 1, :], (blocks, chans)) for g in range(3)]
+        for j in range(taps)
+    ]
+
+    def first_pass(t, carry):
+        states, earlier = carry
+        now = [rows[g, pl.ds(t, blocks, stride=high), :] for g in range(3)]
+        featured = []
+        for g in range(3):
+            value = filt[0][g] * now[g]
+            for k in range(1, taps):
+                value = value + filt[k][g] * earlier[k - 1][g]
+            featured.append(value)
+        mixed = (featured[1] * featured[2]).astype(BF16).astype(F32)
+        mixed_s[t] = mixed
+        gate_s[t] = featured[0]
+        states = tuple(decay[n] * states[n] + mixed for n in range(modes))
+        return states, (tuple(now),) + tuple(earlier[:-1])
+
+    zeros = tuple(jnp.zeros((blocks, chans), F32) for _ in range(modes))
+    before = tuple(tuple(edge[k, g] for g in range(3)) for k in range(taps - 1))
+    states, _ = lax.fori_loop(0, high, first_pass, (zeros, before), unroll=4)
+    for n in range(modes):
+        state[n * blocks : (n + 1) * blocks, :] = states[n]
+
+    rate = decay_ref[...]
+    across = jnp.ones_like(rate)
+    power, left = rate, high
+    while left:
+        if left & 1:
+            across = across * power
+        left >>= 1
+        if left:
+            power = power * power
+    entering = jnp.zeros((modes, chans), F32)
+    for b in range(blocks):
+        enter[pl.ds(b, modes, stride=blocks), :] = entering
+        entering = across * entering + state[pl.ds(b, modes, stride=blocks), :]
+
+    gain = residue_ref[...] * jnp.sqrt(1.0 - rate * rate)
+    gains = [jnp.broadcast_to(gain[n : n + 1, :], (blocks, chans)) for n in range(modes)]
+
+    def second_pass(t, states):
+        mixed = mixed_s[t]
+        states = tuple(decay[n] * states[n] + mixed for n in range(modes))
+        terms = [gains[n] * states[n] for n in range(modes)]
+        while len(terms) > 1:
+            terms = [sum(terms[i : i + 2][1:], terms[i]) for i in range(0, len(terms), 2)]
+        rows[0, pl.ds(t, blocks, stride=high), :] = gate_s[t] * terms[0]
+        return states
+
+    begin = tuple(enter[n * blocks : (n + 1) * blocks, :] for n in range(modes))
+    lax.fori_loop(0, high, second_pass, begin, unroll=4)
+    out_ref[...] = rows[0].astype(BF16)
+
+
+def hyena(core, own, near, far, swap, short_filter, mode_decay, residue, blocks):
+    rows_count, lanes = own.shape
+    chans = lanes // 3
+    total = 2 * rows_count
+    high = total // blocks
+    modes = mode_decay.shape[0]
+    taps = short_filter.shape[0]
+    whole = pl.BlockSpec(memory_space=pltpu.VMEM)
+    return pl.pallas_call(
+        functools.partial(hyena_kernel, blocks=blocks),
+        out_shape=jax.ShapeDtypeStruct((total, chans), BF16),
+        in_specs=[pl.BlockSpec(memory_space=pltpu.SMEM)] + [whole] * 7,
+        out_specs=whole,
+        scratch_shapes=[
+            pltpu.VMEM((3, total, chans), F32),
+            pltpu.VMEM((high, blocks, chans), F32),
+            pltpu.VMEM((high, blocks, chans), F32),
+            pltpu.VMEM((modes * blocks, chans), F32),
+            pltpu.VMEM((modes * blocks, chans), F32),
+            pltpu.VMEM((taps - 1, 3, blocks, chans), F32),
+        ],
+        compiler_params=pltpu.CompilerParams(vmem_limit_bytes=VMEM_LIMIT),
+        cost_estimate=pl.CostEstimate(
+            flops=total * chans * 60, bytes_accessed=total * chans * 20, transcendentals=0
+        ),
+        name="hyena",
+    )(core, own, near, far, swap, short_filter, mode_decay, residue)
+
+
+def out_kernel(pick, x_ref, w_ref, out_ref):
+    out_ref[...] = jnp.dot(x_ref[...], w_ref[...], preferred_element_type=F32).astype(out_ref.dtype)
+
+
+def out_columns(pick, x, w, groups, kind):
+    rows, depth = x.shape
+    wide = w.shape[1] // groups
+    tile = min(wide, 512)
+    tiles = wide // tile
+    return pl.pallas_call(
+        out_kernel,
+        out_shape=jax.ShapeDtypeStruct((rows, wide), kind),
+        grid_spec=pltpu.PrefetchScalarGridSpec(
+            num_scalar_prefetch=1,
+            grid=(tiles,),
+            in_specs=[
+                pl.BlockSpec((rows, depth), lambda i, pick: (0, 0)),
+                pl.BlockSpec((depth, tile), lambda i, pick: (0, pick[0] * tiles + i)),
+            ],
+            out_specs=pl.BlockSpec((rows, tile), lambda i, pick: (0, i)),
+        ),
+        compiler_params=pltpu.CompilerParams(vmem_limit_bytes=VMEM_LIMIT),
+        cost_estimate=pl.CostEstimate(
+            flops=2 * rows * depth * wide, bytes_accessed=depth * wide * 2, transcendentals=0
+        ),
+        name="out_columns",
+    )(pick, x, w)
+
+
+def output_over_line(gated, w_out):
+    z = lax.axis_index("dp")
+    table = jnp.array([[3, 0, 3, 0], [1, 2, 1, 2], [2, 3, 0, 1], [0, 1, 2, 3]], jnp.int32)
+    picks = lax.dynamic_slice_in_dim(table, z, 1, 1)
+    pair = out_columns(picks[0], gated, w_out, 4, BF16)
+    pair_in = lax.ppermute(pair, "dp", [(0, 1), (1, 0), (2, 3), (3, 2)])
+    side = out_columns(picks[1], gated, w_out, 4, BF16)
+    middle_in = lax.ppermute(side, "dp", [(1, 2), (2, 1)])
+    far = out_columns(picks[2], gated, w_out, 4, F32)
+    own = out_columns(picks[3], gated, w_out, 4, F32)
+    inner = (z == 1) | (z == 2)
+    pair_in = pair_in.astype(F32)
+    far = jnp.where(inner, far + pair_in, far).astype(BF16)
+    far_in = lax.ppermute(far, "dp", [(0, 2), (1, 3), (2, 0), (3, 1)])
+    side_in = lax.ppermute(side, "dp", [(0, 1), (3, 2)])
+    own = own + middle_in.astype(F32) + jnp.where(inner, 0.0, pair_in)
+    return (own + far_in.astype(F32) + side_in.astype(F32)).astype(BF16)
+
+
+def on_device_chips(tokens, w_in, short_filter, mode_decay, residue, w_out):
+    count = lax.axis_size("ctx")
+    chips = count // 2
+    me = lax.axis_index("ctx")
+    core, chip = me % 2, me // 2
+    depth, streams, chans = w_in.shape
+    part = chans // count
+
+    def across(i, slot):
+        high_bit, low_bit = slot >> 1, slot & 1
+        step = (high_bit + 2 * low_bit) if i % 2 == 0 else (2 * high_bit + low_bit)
+        return i ^ (2 * step)
+
+    def route(slot):
+        return [(i, across(i, slot)) for i in range(count)]
+
+    def relative(slot):
+        high_bit, low_bit = slot >> 1, slot & 1
+        return jnp.where(core == 0, high_bit + 2 * low_bit, 2 * high_bit + low_bit)
+
+    slot_chip = [chip ^ relative(s) for s in range(chips)]
+    order = jnp.stack(slot_chip + slot_chip + [core]).astype(jnp.int32)
+
+    own_w = jnp.transpose(w_in, (1, 0, 2))
+    swap = [(i, i ^ 1) for i in range(count)]
+    other_w = lax.ppermute(own_w, "ctx", swap)
+
+    xs = []
+    for s in range(chips):
+        block = jnp.concatenate(
+            [
+                lax.dynamic_slice_in_dim(tokens, (2 * slot_chip[s] + (core ^ h)) * depth, depth, 1)
+                for h in range(2)
+            ],
+            1,
+        )
+        xs.append(block if s == 0 else lax.ppermute(block, "ctx", route(s)))
+
+    both = project(order, xs, own_w, other_w, [3], BF16)
+    both_in = lax.ppermute(both, "ctx", route(2))
+    first = project(order, xs, own_w, other_w, [2], BF16)
+    first_in = lax.ppermute(first, "ctx", route(2))
+    second = project(order, xs, own_w, other_w, [1], F32)
+    own = project(order, xs, own_w, other_w, [0], F32)[0]
+    second = (second + both_in.astype(F32)).astype(BF16)[0]
+    second_in = [lax.ppermute(second[h], "ctx", route(1)) for h in (1, 0)][::-1]
+    first_in = first_in[0]
+    other_half = (own[1] + first_in[1].astype(F32) + second_in[1].astype(F32)).astype(BF16)
+    other_half = lax.ppermute(other_half, "ctx", swap)
+
+    here = me * part
+    taps = lax.dynamic_slice_in_dim(short_filter, here, part, 2)
+    decay = lax.dynamic_slice_in_dim(mode_decay, here, part, 1)
+    weight = lax.dynamic_slice_in_dim(residue, here, part, 1)
+    gated = hyena(
+        core.astype(jnp.int32)[None], own[0], first_in[0], second_in[0], other_half,
+        taps, decay, weight, count,
+    )
+    gated = lax.all_to_all(gated, "ctx", 0, 1, tiled=True)
+    return output_over_line(gated, w_out)
+
+
 def solution(mesh):
+    count, groups = mesh.shape["ctx"], mesh.shape["dp"]
+
+    def on_device(tokens, w_in, *rest):
+        lanes = w_in.shape[2] // count
+        chips = count == 8 and groups == 4 and w_in.shape[2] % count == 0 and lanes % 128 == 0
+        return (on_device_chips if chips else on_device_any)(tokens, w_in, *rest)
+
     return jax.shard_map(
         on_device,
         mesh=mesh,

time: 267 us -> 127 us (0.48)
  other arithmetic: 70.1 us -> 5.96 us
  waiting for transfers between devices: 115 us -> 60.9 us
  Pallas kernels: 0 us -> 33.5 us
  blocking collectives: 21.4 us -> 0 us
  local copies, waits for them, and re-layouts: 25.5 us -> 5.08 us
  starting transfers between devices: 2.4 us -> 20.2 us
  matrix products: 17.7 us -> 0 us
  between operations: 13.5 us -> 0.21 us
    all_gather x1 -> x0, waiting for transfers between devices: 78.9 us -> none  [on_device(): lax.all_gather(w_in, 'ctx', axis=0, tiled=True)]
    ppermute x1 -> x13, waiting for transfers between devices: 0.01 us -> 53.3 us  [the longest x3 15.5 us: on_device_chips(): xs.append(block if s == 0 else lax.ppermute(block, 'ctx', route(s)))]
    dot_general x10 -> x0, other arithmetic: 48.1 us -> none  [the longest x3 25.2 us: block_step(): inner = jnp.einsum('tsc,sc->tc', toeplitz, block_rows, precision=highest)]
    reduce_scatter x1 -> x0, waiting for transfers between devices: 35.4 us -> none  [on_device(): lax.psum_scatter(out_term.astype(jnp.bfloat16), 'dp', scatter_dimension=1...]
    pallas_call x0 -> x9, Pallas kernels: none -> 33.5 us  [the longest x4 18.4 us: project(): pl.pallas_call(functools.partial(project_kernel, pieces=pieces), out_shap...]
    all_gather x2 -> x0, blocking collectives: 21.4 us -> none  [prefix(): pieces = jax.tree.map(lambda part: lax.all_gather(part, axis), value)]
    gather x1 -> x0, local copies, waits for them, and re-layouts: 18.5 us -> none  [on_device(): kernel_head[jnp.clip(lag_index, 0, block_len - 1)]]
    dot_general x2 -> x0, matrix products: 17.7 us -> none  [the longest x1 11.3 us: on_device(): jnp.einsum('td,dgc->tgc', source, lax.all_gather(w_in, 'ctx', axis=0, til...]
  transfers between devices with their start and end apart: 3 -> 14, of which waited for: 2 -> 10; matrix products, arithmetic and copies ran while one was open for 14% -> 8% of each run, Pallas kernels for 0% -> 18%
where the time goes in v1:
time: 127 us; the launch traced here: 126 us
  waiting for transfers between devices  60.9 us (48%)
  Pallas kernels  33.5 us (26%)
  starting transfers between devices  20.2 us (16%)
  other arithmetic  5.96 us (5%)
  local copies, waits for them, and re-layouts  5.08 us (4%)
    pallas_call x4, Pallas kernels, project(): pl.pallas_call(functools.partial(project_kernel, pieces=pieces), out_shap...  18.4 us
    ppermute x3, waiting for transfers between devices, on_device_chips(): xs.append(block if s == 0 else lax.ppermute(block, 'ctx', route(s)))  15.5 us
    ppermute x1, waiting for transfers between devices, output_over_line(): far_in = lax.ppermute(far, 'dp', [(0, 2), (1, 3), (2, 0), (3, 1)])  14.6 us
    ppermute x1, waiting for transfers between devices, on_device_chips(): first_in = lax.ppermute(first, 'ctx', route(2))  13.5 us
    pallas_call x4, Pallas kernels, out_columns(): pl.pallas_call(out_kernel, out_shape=jax.ShapeDtypeStruct((rows, wide), k...  10.8 us
    all_to_all x1, waiting for transfers between devices, on_device_chips(): gated = lax.all_to_all(gated, 'ctx', 0, 1, tiled=True)  7.58 us
    ppermute x1, waiting for transfers between devices, on_device_chips(): both_in = lax.ppermute(both, 'ctx', route(2))  4.58 us
    pallas_call x1, Pallas kernels, hyena(): pl.pallas_call(functools.partial(hyena_kernel, blocks=blocks), out_shape=...  4.31 us
  transfers between devices with their start and end apart: 14, of which 10 were waited for; matrix products, arithmetic and copies ran while one was open for 8% of the time, Pallas kernels for 18%

profile of v1, /device:TPU:0, one launch (start us, length us, event | category | flops | bytes accessed | tf_op | source)
XLA Modules:
  0.0 125.8 jit_solution(15340304061370551758)
XLA Ops:
  0.0 0.0 copy-start
  0.0 0.5 collective-permute-start.3
  0.5 2.2 %constant_dynamic-slice_fusion.4 = (bf16[192,512]{1,0:T(8,128)(2,1)S(1)}, bf16[192,512]{1,0:T(8,128)(2,1)S(1)}, bf16[192,512]{1,0:T(8,128)(2,1)S(1)}, bf16[192,5...) fusion(bf16[192,4096]{1,0:T(8,128)(2,1)} %param.7, ...), kind=kLoop, calls=%fused_computation.25 | loop fusion | bytes 3145760 | tf_op jit(solution)/shard_map/dynamic_slice | solution.py:348
  2.7 0.0 copy-start.1
  2.7 0.8 pad_maximum_fusion.3
  3.5 3.6 %collective-permute-start.2 = (bf16[192,1024]{1,0:T(8,128)(2,1)}, bf16[192,1024]{1,0:T(8,128)(2,1)}, u32[]{:S(2)}, u32[]{:S(2)}) collective-permute-start(bf16[192,1024]{1,0:T(8,128)(2,1)} %pad_maximum_fusion.3), channel_id=1, source_target_pairs={{0,6},{1,7},{2,4},{3,5},{4,2},{5,3},{6,0},{7,1},{8,14},{9,15},{10,... | collective-permute-start | bytes 1179656 | tf_op jit(solution)/shard_map/ppermute | solution.py:353
  7.0 0.8 pad_maximum_fusion.2
  7.8 0.5 collective-permute-start.1
  8.4 0.8 pad_maximum_fusion.1
  9.1 0.0 collective-permute-start
  9.2 0.1 stack.24.order
  9.3 1.0 pad_maximum_fusion.refs_0_
  10.2 0.0 copy-start.2
  10.2 7.1 %collective-permute-done.2.refs_3_ = bf16[192,1024]{1,0:T(8,128)(2,1)} collective-permute-done((bf16[192,1024]{1,0:T(8,128)(2,1)}, bf16[192,1024]{1,0:T(8,128)(2,1)}, u32[]{:S(2)}, u32[]{:S(2)}) %collective-permute-start.2) | collective-permute-done | bytes 393248 | tf_op jit(solution)/shard_map/ppermute | solution.py:353
  17.4 8.4 %collective-permute-done.1.refs_2_ = bf16[192,1024]{1,0:T(8,128)(2,1)} collective-permute-done((bf16[192,1024]{1,0:T(8,128)(2,1)}, bf16[192,1024]{1,0:T(8,128)(2,1)}, u32[]{:S(2)}, u32[]{:S(2)}) %collective-permute-start.1) | collective-permute-done | bytes 393248 | tf_op jit(solution)/shard_map/ppermute | solution.py:353
  25.8 0.0 collective-permute-done.refs_1_
  25.8 0.0 collective-permute-done.3.refs_5_
  25.8 0.0 copy-done.1
  25.8 4.4 %project.7 = bf16[1,2,768,384]{3,2,1,0:T(8,128)(2,1)S(1)} custom-call(s32[9]{0:T(128)S(1)} %stack.24.order, bf16[192,1024]{1,0:T(8,128)(2,1)S(1)} %pad_maximum_fusion.refs_0_, bf16[192,1024]{1,0:T(8,128)(2,1)} %collective-permute-done.refs_1_, bf16[192,1024]{1,0:T(8,128)(2,1)} %collective-permute-done.1.refs_2_, ...), custom_call_target="tpu_custom_call" | custom-call | flops 1207959552 | bytes 1572864 | tf_op jit(solution)/shard_map/project/pallas_call | solution.py:127
  30.2 1.6 %collective-permute-start.5 = (bf16[1,2,768,384]{3,2,1,0:T(8,128)(2,1)S(1)}, bf16[1,2,768,384]{3,2,1,0:T(8,128)(2,1)S(1)}, u32[]{:S(2)}, u32[]{:S(2)}) collective-permute-start(bf16[1,2,768,384]{3,2,1,0:T(8,128)(2,1)S(1)} %project.7), channel_id=1, source_target_pairs={{0,2},{1,5},{2,0},{3,7},{4,6},{5,1},{6,4},{7,3},{8,10},{9,13},{10,... | collective-permute-start | bytes 3538952 | tf_op jit(solution)/shard_map/ppermute | solution.py:356
  31.7 5.1 %project.5 = bf16[1,2,768,384]{3,2,1,0:T(8,128)(2,1)} custom-call(s32[9]{0:T(128)S(1)} %stack.24.order, bf16[192,1024]{1,0:T(8,128)(2,1)S(1)} %pad_maximum_fusion.refs_0_, bf16[192,1024]{1,0:T(8,128)(2,1)} %collective-permute-done.refs_1_, bf16[192,1024]{1,0:T(8,128)(2,1)} %collective-permute-done.1.refs_2_, ...), custom_call_target="tpu_custom_call" | custom-call | flops 1207959552 | bytes 1572864 | tf_op jit(solution)/shard_map/project/pallas_call | solution.py:127
  36.9 0.5 collective-permute-start.4
  37.4 0.0 copy-done.2
  37.4 4.5 %project.6 = f32[1,2,768,384]{3,2,1,0:T(8,128)S(1)} custom-call(s32[9]{0:T(128)S(1)} %stack.24.order, bf16[192,1024]{1,0:T(8,128)(2,1)S(1)} %pad_maximum_fusion.refs_0_, bf16[192,1024]{1,0:T(8,128)(2,1)} %collective-permute-done.refs_1_, bf16[192,1024]{1,0:T(8,128)(2,1)} %collective-permute-done.1.refs_2_, bf16[192,1024]{1,0:T(8,128)(2,1)} %collective-permute-done.2.refs_3_, ...), custom_call_target="tpu_custom_call" | custom-call | flops 1207959552 | bytes 1572864 | tf_op jit(solution)/shard_map/project/pallas_call | solution.py:127
  41.9 4.6 %collective-permute-done.5 = bf16[1,2,768,384]{3,2,1,0:T(8,128)(2,1)S(1)} collective-permute-done((bf16[1,2,768,384]{3,2,1,0:T(8,128)(2,1)S(1)}, bf16[1,2,768,384]{3,2,1,0:T(8,128)(2,1)S(1)}, u32[]{:S(2)}, u32[]{:S(2)}) %collective-permute-start.5) | collective-permute-done | bytes 1179680 | tf_op jit(solution)/shard_map/ppermute | solution.py:356
  46.5 0.2 add_convert_fusion
  46.7 0.0 copy-start.3
  46.7 1.1 slice_bitcast_fusion.1
  47.8 1.4 %collective-permute-start.7 = (bf16[768,384]{1,0:T(8,128)(2,1)}, bf16[768,384]{1,0:T(8,128)(2,1)}, u32[]{:S(2)}, u32[]{:S(2)}) collective-permute-start(bf16[768,384]{1,0:T(8,128)(2,1)} %get-tuple-element.13), channel_id=1, source_target_pairs={{0,4},{1,3},{2,6},{3,1},{4,0},{5,7},{6,2},{7,5},{8,12},{9,11},{10,... | collective-permute-start | bytes 1769480 | tf_op jit(solution)/shard_map/ppermute | solution.py:362
  49.3 0.7 constant_dynamic-slice_fusion
  50.0 0.0 copy-done.3
  50.0 4.5 %project.4 = f32[1,2,768,384]{3,2,1,0:T(8,128)S(1)} custom-call(s32[9]{0:T(128)S(1)} %stack.24.order, bf16[192,1024]{1,0:T(8,128)(2,1)S(1)} %copy-done.3, bf16[192,1024]{1,0:T(8,128)(2,1)} %collective-permute-done.refs_1_, bf16[192,1024]{1,0:T(8,128)(2,1)} %collective-permute-done.1.refs_2_, bf16[192,1024]{1,0:T(8,128)(2,1)} %collective-permute-done.2.refs_3_, ...), custom_call_target="tpu_custom_call" | custom-call | flops 1207959552 | bytes 1572864 | tf_op jit(solution)/shard_map/project/pallas_call | solution.py:127
  54.4 0.0 copy-done.4
  54.4 0.7 collective-permute-start.6
  55.1 13.5 %collective-permute-done.4 = bf16[1,2,768,384]{3,2,1,0:T(8,128)(2,1)S(1)} collective-permute-done((bf16[1,2,768,384]{3,2,1,0:T(8,128)(2,1)}, bf16[1,2,768,384]{3,2,1,0:T(8,128)(2,1)S(1)}, u32[]{:S(2)}, u32[]{:S(2)}) %collective-permute-start.4) | collective-permute-done | bytes 1179680 | tf_op jit(solution)/shard_map/ppermute | solution.py:358
  68.6 0.0 collective-permute-done.7
  68.6 1.2 fusion.2
  69.9 0.1 collective-permute-start.8
  70.0 0.0 copy-done
  70.0 0.1 slice_bitcast_fusion.own_ref
  70.1 0.1 slice_bitcast_fusion.3.near_ref
  70.2 0.3 collective-permute-done.6.far_ref
  70.5 1.5 %collective-permute-done.8.swap_ref = bf16[768,384]{1,0:T(8,128)(2,1)S(1)} collective-permute-done((bf16[768,384]{1,0:T(8,128)(2,1)S(1)}, bf16[768,384]{1,0:T(8,128)(2,1)S(1)}, u32[]{:S(2)}, u32[]{:S(2)}) %collective-permute-start.8) | collective-permute-done | bytes 589856 | tf_op jit(solution)/shard_map/ppermute | solution.py:365
  72.0 4.3 %hyena.1 = bf16[1536,128]{1,0:T(8,128)(2,1)} custom-call(s32[1]{0:T(128)} %bitcast.1.core, f32[768,384]{1,0:T(8,128)S(1)} %slice_bitcast_fusion.own_ref, bf16[768,384]{1,0:T(8,128)(2,1)S(1)} %slice_bitcast_fusion.3.near_ref, bf16[768,384]{1,0:T(8,128)(2,1)S(1)} %collective-permute-done.6.far_ref, bf16[768,384]{1,0:T(8,128)(2,1)S(1)} %collective-permute-done.8.swap_ref, ...), custom_call_target="tpu_custom_call" | custom-call | flops 11796480 | bytes 3932160 | tf_op jit(solution)/shard_map/hyena/pallas_call | solution.py:248
  76.3 3.5 %all-to-all-start = ((bf16[8,192,128]{2,1,0:T(8,128)(2,1)}), bf16[8,192,128]{2,1,0:T(8,128)(2,1)S(1)}, u32[]{:S(2)}, u32[]{:S(2)}) async-start(bf16[8,192,128]{2,1,0:T(8,128)(2,1)} %bitcast.12), calls=%async_computation | async-start | bytes 786432 | tf_op jit(solution)/shard_map/all_to_all | solution.py:375
  79.7 0.0 copy-done.5
  79.8 0.1 constant_dynamic-slice_fusion.11
  79.8 0.6 fusion.8
  80.4 7.6 %all-to-all-done = bf16[8,192,128]{2,1,0:T(8,128)(2,1)S(1)} async-done(((bf16[8,192,128]{2,1,0:T(8,128)(2,1)}), bf16[8,192,128]{2,1,0:T(8,128)(2,1)S(1)}, u32[]{:S(2)}, u32[]{:S(2)}) %all-to-all-start) | async-done | bytes 393248 | tf_op jit(solution)/shard_map/all_to_all | solution.py:375
  88.0 0.1 copy_bitcast_fusion.x_ref
  88.1 2.6 %out_columns.6 = bf16[192,1024]{1,0:T(8,128)(2,1)S(1)} custom-call(s32[1]{0:T(128)} %bitcast.15.pick, bf16[192,1024]{1,0:T(8,128)(2,1)S(1)} %copy_bitcast_fusion.x_ref, bf16[1024,4096]{1,0:T(8,128)(2,1)} %w_ref.7), custom_call_target="tpu_custom_call" | custom-call | flops 402653184 | bytes 2097152 | tf_op jit(solution)/shard_map/out_columns/pallas_call | solution.py:278
  90.7 1.5 %collective-permute-start.10 = (bf16[192,1024]{1,0:T(8,128)(2,1)S(1)}, bf16[192,1024]{1,0:T(8,128)(2,1)S(1)}, u32[]{:S(2)}, u32[]{:S(2)}) collective-permute-start(bf16[192,1024]{1,0:T(8,128)(2,1)S(1)} %out_columns.6), channel_id=1, source_target_pairs={{0,8},{8,0},{16,24},{24,16},{1,9},{9,1},{17,25},{25,17},{2,10},{10... | collective-permute-start | bytes 1179656 | tf_op jit(solution)/shard_map/ppermute | solution.py:303
  92.2 2.7 %out_columns.5 = bf16[192,1024]{1,0:T(8,128)(2,1)S(1)} custom-call(s32[1]{0:T(128)} %bitcast.14.pick, bf16[192,1024]{1,0:T(8,128)(2,1)S(1)} %copy_bitcast_fusion.x_ref, bf16[1024,4096]{1,0:T(8,128)(2,1)} %w_ref.7), custom_call_target="tpu_custom_call" | custom-call | flops 402653184 | bytes 2097152 | tf_op jit(solution)/shard_map/out_columns/pallas_call | solution.py:278
  95.0 2.5 %collective-permute-start.12 = (bf16[192,1024]{1,0:T(8,128)(2,1)S(1)}, bf16[192,1024]{1,0:T(8,128)(2,1)S(1)}, u32[]{:S(2)}, u32[]{:S(2)}) collective-permute-start(bf16[192,1024]{1,0:T(8,128)(2,1)S(1)} %out_columns.5), channel_id=1, source_target_pairs={{0,8},{24,16},{1,9},{25,17},{2,10},{26,18},{3,11},{27,19},{4,12},{... | collective-permute-start | bytes 1179656 | tf_op jit(solution)/shard_map/ppermute | solution.py:312
  97.5 0.7 collective-permute-start.9
  98.2 2.8 %out_columns.7 = f32[192,1024]{1,0:T(8,128)S(1)} custom-call(s32[1]{0:T(128)} %bitcast.16.pick, bf16[192,1024]{1,0:T(8,128)(2,1)S(1)} %copy_bitcast_fusion.x_ref, bf16[1024,4096]{1,0:T(8,128)(2,1)} %w_ref.7), custom_call_target="tpu_custom_call" | custom-call | flops 402653184 | bytes 2097152 | tf_op jit(solution)/shard_map/out_columns/pallas_call | solution.py:278
  100.9 0.9 collective-permute-done.10
  101.8 0.1 fusion.7
  101.9 3.2 %collective-permute-start.11 = (bf16[192,1024]{1,0:T(8,128)(2,1)S(1)}, bf16[192,1024]{1,0:T(8,128)(2,1)S(1)}, u32[]{:S(2)}, u32[]{:S(2)}) collective-permute-start(bf16[192,1024]{1,0:T(8,128)(2,1)S(1)} %fusion.7), channel_id=1, source_target_pairs={{0,16},{8,24},{16,0},{24,8},{1,17},{9,25},{17,1},{25,9},{2,18},{10... | collective-permute-start | bytes 1179656 | tf_op jit(solution)/shard_map/ppermute | solution.py:311
  105.1 2.7 %out_columns.4 = f32[192,1024]{1,0:T(8,128)S(1)} custom-call(s32[1]{0:T(128)} %bitcast.pick, bf16[192,1024]{1,0:T(8,128)(2,1)S(1)} %copy_bitcast_fusion.x_ref, bf16[1024,4096]{1,0:T(8,128)(2,1)} %w_ref.7), custom_call_target="tpu_custom_call" | custom-call | flops 402653184 | bytes 2097152 | tf_op jit(solution)/shard_map/out_columns/pallas_call | solution.py:278
  107.8 2.4 %collective-permute-done.12 = bf16[192,1024]{1,0:T(8,128)(2,1)S(1)} collective-permute-done((bf16[192,1024]{1,0:T(8,128)(2,1)S(1)}, bf16[192,1024]{1,0:T(8,128)(2,1)S(1)}, u32[]{:S(2)}, u32[]{:S(2)}) %collective-permute-start.12) | collective-permute-done | bytes 393248 | tf_op jit(solution)/shard_map/ppermute | solution.py:312
  110.2 0.0 collective-permute-done.9
  110.2 14.6 %collective-permute-done.11 = bf16[192,1024]{1,0:T(8,128)(2,1)S(1)} collective-permute-done((bf16[192,1024]{1,0:T(8,128)(2,1)S(1)}, bf16[192,1024]{1,0:T(8,128)(2,1)S(1)}, u32[]{:S(2)}, u32[]{:S(2)}) %collective-permute-start.11) | collective-permute-done | bytes 393248 | tf_op jit(solution)/shard_map/ppermute | solution.py:311
  124.8 1.1 fusion.6
  (3 shorter events, 0.0 us)
Async XLA Ops:
  0.0 70.0 %copy-start = (f32[3,3,1024]{2,1,0:T(4,128)S(1)}, f32[3,3,1024]{2,1,0:T(4,128)}, u32[]{:S(2)}) copy-start(f32[3,3,1024]{2,1,0:T(4,128)} %param.9) | copy-start | bytes 110596
  0.0 25.8 %collective-permute-start.3 = (bf16[3,512,1024]{2,1,0:T(8,128)(2,1)}, bf16[3,512,1024]{2,1,0:T(8,128)(2,1)}, u32[]{:S(2)}, u32[]{:S(2)}) collective-permute-start(bf16[3,512,1024]{2,1,0:T(8,128)(2,1)} %bitcast.31), channel_id=1, source_target_pairs={{0,1},{1,0},{2,3},{3,2},{4,5},{5,4},{6,7},{7,6},{8,9},{9,8},{10,11... | collective-permute-start | bytes 9437192 | tf_op jit(solution)/shard_map/ppermute | solution.py:342
  2.7 23.1 %copy-start.1 = (bf16[512,3,1024]{2,0,1:T(8,128)(2,1)S(1)}, bf16[512,3,1024]{2,0,1:T(8,128)(2,1)}, u32[]{:S(2)}) copy-start(bf16[512,3,1024]{2,0,1:T(8,128)(2,1)} %param.8) | copy-start | bytes 9437188
  3.5 13.9 %collective-permute-start.2 = (bf16[192,1024]{1,0:T(8,128)(2,1)}, bf16[192,1024]{1,0:T(8,128)(2,1)}, u32[]{:S(2)}, u32[]{:S(2)}) collective-permute-start(bf16[192,1024]{1,0:T(8,128)(2,1)} %pad_maximum_fusion.3), channel_id=1, source_target_pairs={{0,6},{1,7},{2,4},{3,5},{4,2},{5,3},{6,0},{7,1},{8,14},{9,15},{10,... | collective-permute-start | bytes 1179656 | tf_op jit(solution)/shard_map/ppermute | solution.py:353
  7.8 18.0 %collective-permute-start.1 = (bf16[192,1024]{1,0:T(8,128)(2,1)}, bf16[192,1024]{1,0:T(8,128)(2,1)}, u32[]{:S(2)}, u32[]{:S(2)}) collective-permute-start(bf16[192,1024]{1,0:T(8,128)(2,1)} %pad_maximum_fusion.2), channel_id=1, source_target_pairs={{0,2},{1,5},{2,0},{3,7},{4,6},{5,1},{6,4},{7,3},{8,10},{9,13},{10,... | collective-permute-start | bytes 1179656 | tf_op jit(solution)/shard_map/ppermute | solution.py:353
  9.1 16.6 %collective-permute-start = (bf16[192,1024]{1,0:T(8,128)(2,1)}, bf16[192,1024]{1,0:T(8,128)(2,1)}, u32[]{:S(2)}, u32[]{:S(2)}) collective-permute-start(bf16[192,1024]{1,0:T(8,128)(2,1)} %pad_maximum_fusion.1), channel_id=1, source_target_pairs={{0,4},{1,3},{2,6},{3,1},{4,0},{5,7},{6,2},{7,5},{8,12},{9,11},{10,... | collective-permute-start | bytes 1179656 | tf_op jit(solution)/shard_map/ppermute | solution.py:353
  10.2 27.2 %copy-start.2 = (bf16[192,1024]{1,0:T(8,128)(2,1)}, bf16[192,1024]{1,0:T(8,128)(2,1)S(1)}, u32[]{:S(2)}) copy-start(bf16[192,1024]{1,0:T(8,128)(2,1)S(1)} %pad_maximum_fusion.refs_0_) | copy-start | bytes 1179652
  30.2 16.3 %collective-permute-start.5 = (bf16[1,2,768,384]{3,2,1,0:T(8,128)(2,1)S(1)}, bf16[1,2,768,384]{3,2,1,0:T(8,128)(2,1)S(1)}, u32[]{:S(2)}, u32[]{:S(2)}) collective-permute-start(bf16[1,2,768,384]{3,2,1,0:T(8,128)(2,1)S(1)} %project.7), channel_id=1, source_target_pairs={{0,2},{1,5},{2,0},{3,7},{4,6},{5,1},{6,4},{7,3},{8,10},{9,13},{10,... | collective-permute-start | bytes 3538952 | tf_op jit(solution)/shard_map/ppermute | solution.py:356
  36.9 31.8 %collective-permute-start.4 = (bf16[1,2,768,384]{3,2,1,0:T(8,128)(2,1)}, bf16[1,2,768,384]{3,2,1,0:T(8,128)(2,1)S(1)}, u32[]{:S(2)}, u32[]{:S(2)}) collective-permute-start(bf16[1,2,768,384]{3,2,1,0:T(8,128)(2,1)} %project.5), channel_id=1, source_target_pairs={{0,2},{1,5},{2,0},{3,7},{4,6},{5,1},{6,4},{7,3},{8,10},{9,13},{10,... | collective-permute-start | bytes 3538952 | tf_op jit(solution)/shard_map/ppermute | solution.py:358
  46.7 3.3 %copy-start.3 = (bf16[192,1024]{1,0:T(8,128)(2,1)S(1)}, bf16[192,1024]{1,0:T(8,128)(2,1)}, u32[]{:S(2)}) copy-start(bf16[192,1024]{1,0:T(8,128)(2,1)} %copy-done.2) | copy-start | bytes 1179652
  47.8 20.8 %collective-permute-start.7 = (bf16[768,384]{1,0:T(8,128)(2,1)}, bf16[768,384]{1,0:T(8,128)(2,1)}, u32[]{:S(2)}, u32[]{:S(2)}) collective-permute-start(bf16[768,384]{1,0:T(8,128)(2,1)} %get-tuple-element.13), channel_id=1, source_target_pairs={{0,4},{1,3},{2,6},{3,1},{4,0},{5,7},{6,2},{7,5},{8,12},{9,11},{10,... | collective-permute-start | bytes 1769480 | tf_op jit(solution)/shard_map/ppermute | solution.py:362
  50.0 4.5 %copy-start.4 = (bf16[768,384]{1,0:T(8,128)(2,1)S(1)}, bf16[768,384]{1,0:T(8,128)(2,1)}, u32[]{:S(2)}) copy-start(bf16[768,384]{1,0:T(8,128)(2,1)} %get-tuple-element.14) | copy-start | bytes 1769476
  54.4 16.0 %collective-permute-start.6 = (bf16[768,384]{1,0:T(8,128)(2,1)S(1)}, bf16[768,384]{1,0:T(8,128)(2,1)S(1)}, u32[]{:S(2)}, u32[]{:S(2)}) collective-permute-start(bf16[768,384]{1,0:T(8,128)(2,1)S(1)} %copy-done.4), channel_id=1, source_target_pairs={{0,4},{1,3},{2,6},{3,1},{4,0},{5,7},{6,2},{7,5},{8,12},{9,11},{10,... | collective-permute-start | bytes 1769480 | tf_op jit(solution)/shard_map/ppermute | solution.py:362
  69.9 2.1 %collective-permute-start.8 = (bf16[768,384]{1,0:T(8,128)(2,1)S(1)}, bf16[768,384]{1,0:T(8,128)(2,1)S(1)}, u32[]{:S(2)}, u32[]{:S(2)}) collective-permute-start(bf16[768,384]{1,0:T(8,128)(2,1)S(1)} %fusion.2), channel_id=1, source_target_pairs={{0,1},{1,0},{2,3},{3,2},{4,5},{5,4},{6,7},{7,6},{8,9},{9,8},{10,11... | collective-permute-start | bytes 1769480 | tf_op jit(solution)/shard_map/ppermute | solution.py:365
  72.0 7.8 %copy-start.5 = (s32[4,4]{1,0:T(4,128)S(1)}, s32[4,4]{1,0:T(4,128)}, u32[]{:S(2)}) copy-start(s32[4,4]{1,0:T(4,128)} %constant.50.clone) | copy-start | bytes 196
  76.3 11.7 %all-to-all-start = ((bf16[8,192,128]{2,1,0:T(8,128)(2,1)}), bf16[8,192,128]{2,1,0:T(8,128)(2,1)S(1)}, u32[]{:S(2)}, u32[]{:S(2)}) async-start(bf16[8,192,128]{2,1,0:T(8,128)(2,1)} %bitcast.12), calls=%async_computation | async-start | bytes 786432 | tf_op jit(solution)/shard_map/all_to_all | solution.py:375
  90.7 11.1 %collective-permute-start.10 = (bf16[192,1024]{1,0:T(8,128)(2,1)S(1)}, bf16[192,1024]{1,0:T(8,128)(2,1)S(1)}, u32[]{:S(2)}, u32[]{:S(2)}) collective-permute-start(bf16[192,1024]{1,0:T(8,128)(2,1)S(1)} %out_columns.6), channel_id=1, source_target_pairs={{0,8},{8,0},{16,24},{24,16},{1,9},{9,1},{17,25},{25,17},{2,10},{10... | collective-permute-start | bytes 1179656 | tf_op jit(solution)/shard_map/ppermute | solution.py:303
  95.0 15.3 %collective-permute-start.12 = (bf16[192,1024]{1,0:T(8,128)(2,1)S(1)}, bf16[192,1024]{1,0:T(8,128)(2,1)S(1)}, u32[]{:S(2)}, u32[]{:S(2)}) collective-permute-start(bf16[192,1024]{1,0:T(8,128)(2,1)S(1)} %out_columns.5), channel_id=1, source_target_pairs={{0,8},{24,16},{1,9},{25,17},{2,10},{26,18},{3,11},{27,19},{4,12},{... | collective-permute-start | bytes 1179656 | tf_op jit(solution)/shard_map/ppermute | solution.py:312
  97.5 12.8 %collective-permute-start.9 = (bf16[192,1024]{1,0:T(8,128)(2,1)S(1)}, bf16[192,1024]{1,0:T(8,128)(2,1)S(1)}, u32[]{:S(2)}, u32[]{:S(2)}) collective-permute-start(bf16[192,1024]{1,0:T(8,128)(2,1)S(1)} %out_columns.5), channel_id=1, source_target_pairs={{8,16},{16,8},{9,17},{17,9},{10,18},{18,10},{11,19},{19,11},{12,20... | collective-permute-start | bytes 1179656 | tf_op jit(solution)/shard_map/ppermute | solution.py:305
  101.9 22.9 %collective-permute-start.11 = (bf16[192,1024]{1,0:T(8,128)(2,1)S(1)}, bf16[192,1024]{1,0:T(8,128)(2,1)S(1)}, u32[]{:S(2)}, u32[]{:S(2)}) collective-permute-start(bf16[192,1024]{1,0:T(8,128)(2,1)S(1)} %fusion.7), channel_id=1, source_target_pairs={{0,16},{8,24},{16,0},{24,8},{1,17},{9,25},{17,1},{25,9},{2,18},{10... | collective-permute-start | bytes 1179656 | tf_op jit(solution)/shard_map/ppermute | solution.py:311

commit v2 on v0

--- a/solution.py
+++ b/solution.py
@@ -1,9 +1,15 @@
+import functools
+
 import jax
 import jax.numpy as jnp
 from jax import lax
+from jax.experimental import pallas as pl
+from jax.experimental.pallas import tpu as pltpu
 from jax.sharding import PartitionSpec as P
 
 BLK = 64
+F32, BF16 = jnp.float32, jnp.bfloat16
+VMEM_LIMIT = 12 * 1024 * 1024
 
 
 def from_behind(block, axis, distance):
@@ -26,7 +32,7 @@
     return lax.fori_loop(0, count - 1, lap, subtotal)
 
 
-def on_device(tokens, w_in, short_filter, mode_decay, residue, w_out):
+def on_device_any(tokens, w_in, short_filter, mode_decay, residue, w_out):
     row_count = tokens.shape[0]
     chan_count = w_in.shape[2]
     short_count = short_filter.shape[0]
@@ -89,7 +95,455 @@
     return lax.psum_scatter(out_term.astype(jnp.bfloat16), "dp", scatter_dimension=1, tiled=True)
 
 
+def local(kernel, name, shapes, scalars, arrays, scratch=()):
+    whole = pl.BlockSpec(memory_space=pltpu.VMEM)
+    out = [jax.ShapeDtypeStruct(*shape) for shape in shapes]
+    return pl.pallas_call(
+        kernel,
+        out_shape=out if len(out) > 1 else out[0],
+        in_specs=[pl.BlockSpec(memory_space=pltpu.SMEM)] + [whole] * len(arrays),
+        out_specs=[whole] * len(out) if len(out) > 1 else whole,
+        scratch_shapes=list(scratch),
+        compiler_params=pltpu.CompilerParams(vmem_limit_bytes=VMEM_LIMIT),
+        name=name,
+    )(scalars, *arrays)
+
+
+def columns(index, wide):
+    return pl.ds(pl.multiple_of(index * wide, wide), wide)
+
+
+def cut(order, tokens, pieces):
+    high, wide = tokens.shape[0], tokens.shape[1] // pieces
+
+    def kernel(order, tokens_ref, *out_refs):
+        for s, out_ref in enumerate(out_refs):
+            out_ref[...] = tokens_ref[:, columns(order[s], wide)]
+
+    return local(kernel, "cut", [((high, wide), tokens.dtype)] * pieces, order, [tokens])
+
+
+def stage(*arrays):
+    count = len(arrays)
+
+    def kernel(*refs):
+        sems = refs[2 * count]
+        copies = [
+            pltpu.make_async_copy(refs[i], refs[count + i], sems.at[i]) for i in range(count)
+        ]
+        for copy in copies:
+            copy.start()
+        for copy in copies:
+            copy.wait()
+
+    return pl.pallas_call(
+        kernel,
+        out_shape=[jax.ShapeDtypeStruct(x.shape, x.dtype) for x in arrays],
+        in_specs=[pl.BlockSpec(memory_space=pl.ANY)] * count,
+        out_specs=[pl.BlockSpec(memory_space=pltpu.VMEM)] * count,
+        scratch_shapes=[pltpu.SemaphoreType.DMA((count,))],
+        compiler_params=pltpu.CompilerParams(vmem_limit_bytes=VMEM_LIMIT),
+        name="stage",
+    )(*arrays)
+
+
+def gather_rows(core, x_refs, rows):
+    high, depth = x_refs[0].shape[0], rows.shape[2]
+    for i, x_ref in enumerate(x_refs):
+        for h in range(2):
+            rows[core ^ h, i * high : (i + 1) * high, :] = x_ref[:, h * depth : (h + 1) * depth]
+
+
+def project_mix(order, xs, own, other, slots, kind):
+    chips = len(xs)
+    streams, depth, chans = own.shape
+    high = xs[0].shape[0]
+    wide = chans // chips
+    half = wide // 2
+
+    def kernel(order, *refs):
+        x_refs, (own_ref, other_ref, out_ref, rows) = refs[:chips], refs[chips:]
+        core = order[2 * chips]
+        gather_rows(core, x_refs, rows)
+        for i, slot in enumerate(slots):
+            at = columns(order[slot], wide)
+            for g in range(1, streams):
+                total = jnp.dot(rows[0], own_ref[g, :, at], preferred_element_type=F32)
+                total += jnp.dot(rows[1], other_ref[g, :, at], preferred_element_type=F32)
+                total = total.astype(kind)
+                lanes = slice((g - 1) * half, g * half)
+                for h in range(2):
+                    out_ref[i, core ^ h, :, lanes] = total[:, h * half : (h + 1) * half]
+
+    shape = (len(slots), 2, chips * high, (streams - 1) * half)
+    scratch = [pltpu.VMEM((2, chips * high, depth), BF16)]
+    return local(kernel, "project_mix", [(shape, kind)], order, [*xs, own, other], scratch)
+
+
+def last_rows(order, xs, count):
+    high, wide = xs[0].shape
+
+    def kernel(order, *refs):
+        for s in range(len(xs)):
+            refs[-1][s] = refs[s][high - count :, :]
+
+    return local(kernel, "last_rows", [((len(xs), count, wide), BF16)], order, xs)
+
+
+def project_query(order, xs, before, own, other, short_filter):
+    chips = len(xs)
+    _, depth, chans = own.shape
+    high = xs[0].shape[0]
+    some = before.shape[1]
+    step = some + high
+    taps = short_filter.shape[0]
+    tile = min(chans, 256)
+
+    def kernel(order, *refs):
+        x_refs = refs[:chips]
+        before_ref, own_ref, other_ref, filt_ref, sent_ref, rest_ref, rows, ends, total = refs[chips:]
+        core = order[2 * chips]
+        ends[0] = jnp.zeros_like(ends[0])
+        for s in range(chips):
+            ends[order[chips + s] + 1] = before_ref[s]
+        for i, x_ref in enumerate(x_refs):
+            end = ends[order[i] + core]
+            for h in range(2):
+                lanes = slice(h * depth, (h + 1) * depth)
+                rows[core ^ h, i * step : i * step + some, :] = end[:, lanes]
+                rows[core ^ h, i * step + some : (i + 1) * step, :] = x_ref[:, lanes]
+        for at in (slice(i, i + tile) for i in range(0, chans, tile)):
+            total[...] = jnp.dot(
+                rows[0], own_ref[0, :, at], preferred_element_type=F32
+            ) + jnp.dot(rows[1], other_ref[0, :, at], preferred_element_type=F32)
+            for i in range(chips):
+                first = i * step + some
+                value = filt_ref[0, 0:1, at] * total[first : first + high, :]
+                for j in range(1, taps):
+                    value = value + filt_ref[j, 0:1, at] * total[first - j : first - j + high, :]
+                if i < 2:
+                    rest_ref[i, :, at] = value
+                else:
+                    sent_ref[3 - i, :, at] = value.astype(BF16)
+
+    shapes = [((2, high, chans), BF16), ((2, high, chans), F32)]
+    scratch = [
+        pltpu.VMEM((2, chips * step, depth), BF16),
+        pltpu.VMEM((chips + 1, some, 2 * depth), BF16),
+        pltpu.VMEM((chips * step, tile), F32),
+    ]
+    arrays = [*xs, before, own, other, short_filter]
+    return local(kernel, "project_query", shapes, order, arrays, scratch)
+
+
+def second_share(order, rest, both_in, chips):
+    shape = (1,) + rest.shape[1:]
+    high = rest.shape[2] // chips
+
+    def kernel(order, rest_ref, both_ref, out_ref):
+        for h in range(2):
+            for s in range(chips):
+                here, there = (slice(i * high, (i + 1) * high) for i in (s, s ^ 2))
+                term = both_ref[0, h, there, :].astype(F32)
+                out_ref[0, h, here, :] = (rest_ref[0, h, here, :] + term).astype(BF16)
+
+    return local(kernel, "second_share", [(shape, BF16)], order, [rest, both_in])
+
+
+def own_share(order, rest, first_in, second_in, chips):
+    _, _, rows, lanes = rest.shape
+    high = rows // chips
+
+    def kernel(order, rest_ref, first_ref, second_ref, own_ref, other_ref):
+        for h, out_ref in ((1, other_ref), (0, own_ref)):
+            for s in range(chips):
+                here, first, second = (slice(i * high, (i + 1) * high) for i in (s, s ^ 2, s ^ 1))
+                total = rest_ref[1, h, here, :] + first_ref[0, h, first, :].astype(F32)
+                total = total + second_ref[0, h, second, :].astype(F32)
+                out_ref[here, :] = total.astype(out_ref.dtype)
+
+    shapes = [((rows, lanes), F32), ((rows, lanes), BF16)]
+    return local(kernel, "own_share", shapes, order, [rest, first_in, second_in])
+
+
+def hyena_kernel(
+    order, own_ref, swap_ref, filt_ref, decay_ref, residue_ref,
+    keep_ref, send_ref, rows, mixed_s, state, enter, edge, *, blocks,
+):
+    high = rows.shape[1] // blocks
+    chans = rows.shape[2]
+    modes = decay_ref.shape[0]
+    taps = filt_ref.shape[0]
+    chips = blocks // 2
+    core = order[2 * chips]
+    channels = columns(order[2 * chips + 1], chans)
+
+    for s in range(chips):
+        here = slice(s * high, (s + 1) * high)
+        own_at = columns(2 * order[s] + core, high)
+        swap_at = columns(2 * order[chips + s] + 1 - core, high)
+        for g in range(2):
+            lanes = slice(g * chans, (g + 1) * chans)
+            rows[g, own_at, :] = own_ref[here, lanes]
+            rows[g, swap_at, :] = swap_ref[here, lanes].astype(F32)
+
+    for k in range(1, taps):
+        for g in range(2):
+            edge[k - 1, g, 0:1, :] = jnp.zeros((1, chans), F32)
+            for b in range(1, blocks):
+                edge[k - 1, g, b : b + 1, :] = rows[g, b * high - k : b * high - k + 1, :]
+
+    rate = decay_ref[:, channels]
+    taps_of = [filt_ref[j, :, channels] for j in range(taps)]
+    decay = [jnp.broadcast_to(rate[n : n + 1, :], (blocks, chans)) for n in range(modes)]
+    filt = [
+        [jnp.broadcast_to(taps_of[j][g + 1 : g + 2, :], (blocks, chans)) for g in range(2)]
+        for j in range(taps)
+    ]
+
+    def first_pass(t, carry):
+        states, earlier = carry
+        now = [rows[g, pl.ds(t, blocks, stride=high), :] for g in range(2)]
+        featured = []
+        for g in range(2):
+            value = filt[0][g] * now[g]
+            for k in range(1, taps):
+                value = value + filt[k][g] * earlier[k - 1][g]
+            featured.append(value)
+        mixed = (featured[0] * featured[1]).astype(BF16).astype(F32)
+        mixed_s[t] = mixed
+        states = tuple(decay[n] * states[n] + mixed for n in range(modes))
+        return states, (tuple(now),) + tuple(earlier[:-1])
+
+    zeros = tuple(jnp.zeros((blocks, chans), F32) for _ in range(modes))
+    before = tuple(tuple(edge[k, g] for g in range(2)) for k in range(taps - 1))
+    states, _ = lax.fori_loop(0, high, first_pass, (zeros, before), unroll=4)
+    for n in range(modes):
+        state[n * blocks : (n + 1) * blocks, :] = states[n]
+
+    across = jnp.ones_like(rate)
+    power, left = rate, high
+    while left:
+        if left & 1:
+            across = across * power
+        left >>= 1
+        if left:
+            power = power * power
+    entering = jnp.zeros((modes, chans), F32)
+    for b in range(blocks):
+        enter[pl.ds(b, modes, stride=blocks), :] = entering
+        entering = across * entering + state[pl.ds(b, modes, stride=blocks), :]
+
+    gain = residue_ref[:, channels] * jnp.sqrt(1.0 - rate * rate)
+    gains = [jnp.broadcast_to(gain[n : n + 1, :], (blocks, chans)) for n in range(modes)]
+
+    def second_pass(t, states):
+        mixed = mixed_s[t]
+        states = tuple(decay[n] * states[n] + mixed for n in range(modes))
+        terms = [gains[n] * states[n] for n in range(modes)]
+        while len(terms) > 1:
+            terms = [sum(terms[i : i + 2][1:], terms[i]) for i in range(0, len(terms), 2)]
+        rows[0, pl.ds(t, blocks, stride=high), :] = terms[0]
+        return states
+
+    begin = tuple(enter[n * blocks : (n + 1) * blocks, :] for n in range(modes))
+    lax.fori_loop(0, high, second_pass, begin, unroll=4)
+    for s in range(chips):
+        keep_ref[s] = rows[0, columns(2 * order[s] + core, high), :].astype(BF16)
+        send_ref[s] = rows[0, columns(2 * order[chips + s] + 1 - core, high), :].astype(BF16)
+
+
+def hyena(order, own, swap, short_filter, mode_decay, residue, blocks):
+    rows_count, lanes = own.shape
+    chans = lanes // 2
+    total = 2 * rows_count
+    high = total // blocks
+    modes, taps = mode_decay.shape[0], short_filter.shape[0]
+    scratch = [
+        pltpu.VMEM((2, total, chans), F32),
+        pltpu.VMEM((high, blocks, chans), F32),
+        pltpu.VMEM((modes * blocks, chans), F32),
+        pltpu.VMEM((modes * blocks, chans), F32),
+        pltpu.VMEM((taps - 1, 2, blocks, chans), F32),
+    ]
+    arrays = [own, swap, short_filter, mode_decay, residue]
+    kernel = functools.partial(hyena_kernel, blocks=blocks)
+    shapes = [((blocks // 2, high, chans), BF16)] * 2
+    return local(kernel, "hyena", shapes, order, arrays, scratch)
+
+
+def pair_up(order, keep, other):
+    chips, high, chans = keep.shape
+
+    def kernel(order, keep_ref, other_ref, *out_refs):
+        for s, out_ref in enumerate(out_refs):
+            out_ref[0] = keep_ref[s]
+            out_ref[1] = other_ref[s]
+
+    return local(kernel, "pair_up", [((2, high, chans), BF16)] * chips, order, [keep, other])
+
+
+def query_second(order, rest, q_in, pieces):
+    _, rows, chans = rest.shape
+    share = chans // pieces
+
+    def kernel(order, rest_ref, in_ref, *out_refs):
+        for i, out_ref in enumerate(out_refs):
+            at = slice(i * share, (i + 1) * share)
+            out_ref[...] = (rest_ref[1, :, at] + in_ref[0, :, at].astype(F32)).astype(BF16)
+
+    shapes = [((rows, share), BF16)] * pieces
+    return local(kernel, "query_second", shapes, order, [rest, q_in])
+
+
+def gate(scalars, rest, q_in, second_in, long_parts, w_out, groups):
+    rows, chans = second_in[0].shape[0], rest.shape[2]
+    chips = len(long_parts)
+    part = long_parts[0].shape[2]
+    wide = w_out.shape[1] // groups
+    first_pick = 2 * chips + 2
+
+    def kernel(scalars, rest_ref, in_ref, *refs):
+        second_refs = refs[: len(second_in)]
+        long_refs = refs[len(second_in) : len(second_in) + chips]
+        w_ref, gated_ref, pair_ref, side_ref, query = refs[len(second_in) + chips :]
+        core = scalars[2 * chips]
+        query[...] = rest_ref[0] + in_ref[1].astype(F32)
+        share = second_refs[0].shape[1]
+        for i, ref in enumerate(second_refs):
+            query[:, i * share : (i + 1) * share] += ref[...].astype(F32)
+        for s, ref in enumerate(long_refs):
+            for h in range(2):
+                at = columns(2 * scalars[s] + (core ^ h), part)
+                gated_ref[:, at] = (query[:, at] * ref[h].astype(F32)).astype(BF16)
+        for pick, out_ref in enumerate((pair_ref, side_ref)):
+            total = jnp.dot(
+                gated_ref[...],
+                w_ref[:, columns(scalars[first_pick + pick], wide)],
+                preferred_element_type=F32,
+            )
+            out_ref[...] = total.astype(BF16)
+
+    shapes = [((rows, chans), BF16), ((rows, wide), BF16), ((rows, wide), BF16)]
+    arrays = [rest, q_in, *second_in, *long_parts, w_out]
+    scratch = [pltpu.VMEM((rows, chans), F32)]
+    return local(kernel, "gate", shapes, scalars, arrays, scratch)
+
+
+def out_columns(picks, pick, x, w_out, groups, kind):
+    wide = w_out.shape[1] // groups
+
+    def kernel(picks, x_ref, w_ref, out_ref):
+        total = jnp.dot(
+            x_ref[...], w_ref[:, columns(picks[pick], wide)], preferred_element_type=F32
+        )
+        out_ref[...] = total.astype(kind)
+
+    return local(kernel, "out_columns", [((x.shape[0], wide), kind)], picks, [x, w_out])
+
+
+def line_picks():
+    z = lax.axis_index("dp")
+    table = [[3, 0, 3, 0], [1, 2, 1, 2], [2, 3, 0, 1], [0, 1, 2, 3], [0, 1, 1, 0]]
+    return jnp.stack([sum(jnp.where(z == i, v, 0) for i, v in enumerate(row)) for row in table])
+
+
+def output_over_line(picks, gated, pair, side, w_out, groups):
+    pair_in = lax.ppermute(pair, "dp", [(0, 1), (1, 0), (2, 3), (3, 2)])
+    far = out_columns(picks, 2, gated, w_out, groups, BF16)
+    end_in = lax.ppermute(far, "dp", [(0, 2), (3, 1)])
+    middle_in = lax.ppermute(side, "dp", [(1, 2), (2, 1)])
+    side_in = lax.ppermute(side, "dp", [(0, 1), (3, 2)])
+    own = out_columns(picks, 3, gated, w_out, groups, F32)
+
+    def add(picks, far_ref, pair_ref, out_ref):
+        out_ref[...] = (far_ref[...].astype(F32) + pair_ref[...].astype(F32)).astype(BF16)
+
+    both = local(add, "both", [(far.shape, BF16)], picks, [far, pair_in])
+    far_in = lax.ppermute(both, "dp", [(1, 3), (2, 0)])
+
+    def total(picks, own_ref, pair_ref, *refs):
+        out_ref = refs[-1]
+        inner = picks[4] == 1
+        value = own_ref[...] + jnp.where(inner, 0.0, pair_ref[...].astype(F32))
+        for ref in refs[:-1]:
+            value = value + ref[...].astype(F32)
+        out_ref[...] = value.astype(BF16)
+
+    arrays = [own, pair_in, middle_in, end_in, side_in, far_in]
+    return local(total, "total", [(own.shape, BF16)], picks, arrays)
+
+
+def on_device_chips(tokens, w_in, short_filter, mode_decay, residue, w_out):
+    count, groups = lax.axis_size("ctx"), lax.axis_size("dp")
+    chips = count // 2
+    me = lax.axis_index("ctx")
+    core, chip = me % 2, me // 2
+
+    def across(i, slot):
+        high_bit, low_bit = slot >> 1, slot & 1
+        step = (high_bit + 2 * low_bit) if i % 2 == 0 else (2 * high_bit + low_bit)
+        return i ^ (2 * step)
+
+    def route(slot):
+        return [(i, across(i, slot)) for i in range(count)]
+
+    def relative(slot, core):
+        high_bit, low_bit = slot >> 1, slot & 1
+        return jnp.where(core == 0, high_bit + 2 * low_bit, 2 * high_bit + low_bit)
+
+    slot_chip = [chip ^ relative(s, core) for s in range(chips)]
+    slot_other = [chip ^ relative(s, 1 - core) for s in range(chips)]
+    order = jnp.stack(slot_chip + slot_other + [core, me]).astype(jnp.int32)
+    picks = line_picks().astype(jnp.int32)
+    both_scalars = jnp.concatenate([order, picks])
+    order, picks, both_scalars = lax.optimization_barrier((order, picks, both_scalars))
+
+    own_w = jnp.transpose(w_in, (1, 0, 2))
+    swap = [(i, i ^ 1) for i in range(count)]
+
+    other_w = lax.ppermute(own_w, "ctx", swap)
+    xs = cut(order, tokens, chips)
+    own_w, w_out, xs = lax.optimization_barrier((own_w, w_out, xs))
+    own_w, w_out = stage(own_w, w_out)
+    xs = [xs[0]] + [lax.ppermute(xs[s], "ctx", route(s)) for s in (1, 2, 3)]
+
+    both = project_mix(order, xs, own_w, other_w, [3], BF16)
+    both_in = lax.ppermute(both, "ctx", route(2))
+    xs, both = lax.optimization_barrier((xs, both))
+    first = project_mix(order, xs, own_w, other_w, [2], BF16)
+    first_in = lax.ppermute(first, "ctx", route(2))
+    xs, first = lax.optimization_barrier((xs, first))
+    rest = project_mix(order, xs, own_w, other_w, [1, 0], F32)
+    second = second_share(order, rest, both_in, chips)
+    second_in = lax.ppermute(second, "ctx", route(1))
+
+    xs, second = lax.optimization_barrier((xs, second))
+    before = lax.ppermute(last_rows(order, xs, 16), "ctx", swap)
+    q_sent, q_rest = project_query(order, xs, before, own_w, other_w, short_filter)
+    q_rest, rest = lax.optimization_barrier((q_rest, rest))
+
+    own, other_half = own_share(order, rest, first_in, second_in, chips)
+    other_half = lax.ppermute(other_half, "ctx", swap)
+    q_sent, own = lax.optimization_barrier((q_sent, own))
+    q_in = lax.ppermute(q_sent, "ctx", route(2))
+    keep, send = hyena(order, own, other_half, short_filter, mode_decay, residue, count)
+    long_parts = pair_up(order, keep, lax.ppermute(send, "ctx", swap))
+    q_rest, long_parts = lax.optimization_barrier((q_rest, long_parts))
+    q_second = [lax.ppermute(q, "ctx", route(1)) for q in query_second(order, q_rest, q_in, 2)]
+    long_parts = [long_parts[0]] + [lax.ppermute(long_parts[s], "ctx", route(s)) for s in (1, 2, 3)]
+    gated, pair, side = gate(both_scalars, q_rest, q_in, q_second, long_parts, w_out, groups)
+    return output_over_line(picks, gated, pair, side, w_out, groups)
+
+
 def solution(mesh):
+    count, groups = mesh.shape["ctx"], mesh.shape["dp"]
+
+    def on_device(tokens, w_in, *rest):
+        lanes = w_in.shape[2] // count
+        chips = count == 8 and groups == 4 and w_in.shape[2] % count == 0 and lanes % 128 == 0
+        return (on_device_chips if chips else on_device_any)(tokens, w_in, *rest)
+
     return jax.shard_map(
         on_device,
         mesh=mesh,

time: 267 us -> 116 us (0.43)
  other arithmetic: 70.1 us -> 0 us
  waiting for transfers between devices: 115 us -> 60.6 us
  Pallas kernels: 0 us -> 23.4 us
  starting transfers between devices: 2.4 us -> 24.5 us
  blocking collectives: 21.4 us -> 0 us
  local copies, waits for them, and re-layouts: 25.5 us -> 6.96 us
  matrix products: 17.7 us -> 0 us
  between operations: 13.5 us -> 0.22 us
    all_gather x1 -> x0, waiting for transfers between devices: 78.9 us -> none  [on_device(): lax.all_gather(w_in, 'ctx', axis=0, tiled=True)]
    ppermute x1 -> x21, waiting for transfers between devices: 0.01 us -> 60.6 us  [the longest x1 12.5 us: output_over_line(): end_in = lax.ppermute(far, 'dp', [(0, 2), (3, 1)])]
    dot_general x10 -> x0, other arithmetic: 48.1 us -> none  [the longest x3 25.2 us: block_step(): inner = jnp.einsum('tsc,sc->tc', toeplitz, block_rows, precision=highest)]
    reduce_scatter x1 -> x0, waiting for transfers between devices: 35.4 us -> none  [on_device(): lax.psum_scatter(out_term.astype(jnp.bfloat16), 'dp', scatter_dimension=1...]
    pallas_call x0 -> x17, Pallas kernels: none -> 23.4 us  [the longest x16 22.6 us: local(): pl.pallas_call(kernel, out_shape=out if len(out) > 1 else out[0], in_spec...]
    ppermute x1 -> x21, starting transfers between devices: 2.36 us -> 24.5 us  [the longest x1 4.25 us: output_over_line(): end_in = lax.ppermute(far, 'dp', [(0, 2), (3, 1)])]
    all_gather x2 -> x0, blocking collectives: 21.4 us -> none  [prefix(): pieces = jax.tree.map(lambda part: lax.all_gather(part, axis), value)]
    gather x1 -> x0, local copies, waits for them, and re-layouts: 18.5 us -> none  [on_device(): kernel_head[jnp.clip(lag_index, 0, block_len - 1)]]
  transfers between devices with their start and end apart: 3 -> 21, of which waited for: 2 -> 14; matrix products, arithmetic and copies ran while one was open for 14% -> 0% of each run, Pallas kernels for 0% -> 15%
where the time goes in v2:
time: 116 us
  waiting for transfers between devices  60.6 us (52%)
  starting transfers between devices  24.5 us (21%)
  Pallas kernels  23.4 us (20%)
  local copies, waits for them, and re-layouts  6.96 us (6%)
    pallas_call x16, Pallas kernels, local(): pl.pallas_call(kernel, out_shape=out if len(out) > 1 else out[0], in_spec...  22.6 us
    ppermute x1, waiting for transfers between devices, output_over_line(): end_in = lax.ppermute(far, 'dp', [(0, 2), (3, 1)])  12.5 us
    ppermute x3, waiting for transfers between devices, on_device_chips(): xs = [xs[0]] + [lax.ppermute(xs[s], 'ctx', route(s)) for s in (1, 2, 3)]  11.8 us
    ppermute x1, waiting for transfers between devices, on_device_chips(): first_in = lax.ppermute(first, 'ctx', route(2))  8.54 us
    unnamed x12, local copies, waits for them, and re-layouts  6.7 us
    ppermute x3, waiting for transfers between devices, on_device_chips(): lax.ppermute(long_parts[s], 'ctx', route(s))  6.48 us
    ppermute x1, waiting for transfers between devices, output_over_line(): far_in = lax.ppermute(both, 'dp', [(1, 3), (2, 0)])  6.17 us
    ppermute x1, waiting for transfers between devices, on_device_chips(): both_in = lax.ppermute(both, 'ctx', route(2))  5.59 us
  transfers between devices with their start and end apart: 21, of which 14 were waited for; matrix products, arithmetic and copies ran while one was open for 0% of the time, Pallas kernels for 15%

profile of v2, /device:TPU:0, one launch (start us, length us, event | category | flops | bytes accessed | tf_op | source)
XLA Modules:
  0.0 115.6 jit_solution(7075927681110968854)
XLA Ops:
  0.0 0.5 collective-permute-start.3
  0.5 0.1 stack.55.order
  0.5 0.1 concatenate.4.scalars
  0.6 0.1 stack.61.picks
  0.7 1.4 %copy-done.2 = bf16[192,4096]{1,0:T(8,128)(2,1)S(1)} copy-done((bf16[192,4096]{1,0:T(8,128)(2,1)S(1)}, bf16[192,4096]{1,0:T(8,128)(2,1)}, u32[]{:S(2)}) %copy-start.2) | copy-done | bytes 1572888
  2.1 0.6 cut.1
  2.8 2.6 %collective-permute-start = (bf16[192,1024]{1,0:T(8,128)(2,1)S(1)}, bf16[192,1024]{1,0:T(8,128)(2,1)S(1)}, u32[]{:S(2)}, u32[]{:S(2)}) collective-permute-start(bf16[192,1024]{1,0:T(8,128)(2,1)S(1)} %get-tuple-element.64), channel_id=1, source_target_pairs={{0,4},{1,3},{2,6},{3,1},{4,0},{5,7},{6,2},{7,5},{8,12},{9,11},{10,... | collective-permute-start | bytes 1179656 | tf_op jit(solution)/shard_map/ppermute | solution.py:509
  5.4 1.5 %collective-permute-start.1 = (bf16[192,1024]{1,0:T(8,128)(2,1)S(1)}, bf16[192,1024]{1,0:T(8,128)(2,1)S(1)}, u32[]{:S(2)}, u32[]{:S(2)}) collective-permute-start(bf16[192,1024]{1,0:T(8,128)(2,1)S(1)} %get-tuple-element.65), channel_id=1, source_target_pairs={{0,2},{1,5},{2,0},{3,7},{4,6},{5,1},{6,4},{7,3},{8,10},{9,13},{10,... | collective-permute-start | bytes 1179656 | tf_op jit(solution)/shard_map/ppermute | solution.py:509
  6.9 0.0 collective-permute-start.2
  6.9 3.4 %copy-done = bf16[1024,4096]{1,0:T(8,128)(2,1)S(1)} copy-done((bf16[1024,4096]{1,0:T(8,128)(2,1)S(1)}, bf16[1024,4096]{1,0:T(8,128)(2,1)}, u32[]{:S(2)}) %copy-start) | copy-done | bytes 8388632
  10.3 1.9 %copy-done.1 = bf16[512,3,1024]{2,0,1:T(8,128)(2,1)S(1)} copy-done((bf16[512,3,1024]{2,0,1:T(8,128)(2,1)S(1)}, bf16[512,3,1024]{2,0,1:T(8,128)(2,1)}, u32[]{:S(2)}) %copy-start.1) | copy-done | bytes 3145752
  12.2 0.8 stage.1
  13.0 3.0 %collective-permute-done.refs_1_ = bf16[192,1024]{1,0:T(8,128)(2,1)S(1)} collective-permute-done((bf16[192,1024]{1,0:T(8,128)(2,1)S(1)}, bf16[192,1024]{1,0:T(8,128)(2,1)S(1)}, u32[]{:S(2)}, u32[]{:S(2)}) %collective-permute-start) | collective-permute-done | bytes 393248 | tf_op jit(solution)/shard_map/ppermute | solution.py:509
  16.0 1.4 %collective-permute-done.1.refs_2_ = bf16[192,1024]{1,0:T(8,128)(2,1)S(1)} collective-permute-done((bf16[192,1024]{1,0:T(8,128)(2,1)S(1)}, bf16[192,1024]{1,0:T(8,128)(2,1)S(1)}, u32[]{:S(2)}, u32[]{:S(2)}) %collective-permute-start.1) | collective-permute-done | bytes 393248 | tf_op jit(solution)/shard_map/ppermute | solution.py:509
  17.4 7.4 %collective-permute-done.2.refs_3_ = bf16[192,1024]{1,0:T(8,128)(2,1)S(1)} collective-permute-done((bf16[192,1024]{1,0:T(8,128)(2,1)S(1)}, bf16[192,1024]{1,0:T(8,128)(2,1)S(1)}, u32[]{:S(2)}, u32[]{:S(2)}) %collective-permute-start.2) | collective-permute-done | bytes 393248 | tf_op jit(solution)/shard_map/ppermute | solution.py:509
  24.8 1.7 %project_mix.3 = bf16[1,2,768,256]{3,2,1,0:T(8,128)(2,1)S(1)} custom-call(s32[10]{0:T(128)S(1)} %stack.55.order, bf16[192,1024]{1,0:T(8,128)(2,1)S(1)} %get-tuple-element.78.refs_0_, bf16[192,1024]{1,0:T(8,128)(2,1)S(1)} %collective-permute-done.refs_1_, bf16[192,1024]{1,0:T(8,128)(2,1)S(1)} %collective-permute-done.1.refs_2_, ...), custom_call_target="tpu_custom_call" | custom-call | tf_op jit(solution)/shard_map/project_mix/pallas_call | solution.py:101
  26.5 1.5 %collective-permute-start.4 = (bf16[1,2,768,256]{3,2,1,0:T(8,128)(2,1)S(1)}, bf16[1,2,768,256]{3,2,1,0:T(8,128)(2,1)S(1)}, u32[]{:S(2)}, u32[]{:S(2)}) collective-permute-start(bf16[1,2,768,256]{3,2,1,0:T(8,128)(2,1)S(1)} %project_mix.3), channel_id=1, source_target_pairs={{0,2},{1,5},{2,0},{3,7},{4,6},{5,1},{6,4},{7,3},{8,10},{9,13},{10,... | collective-permute-start | bytes 2359304 | tf_op jit(solution)/shard_map/ppermute | solution.py:512
  28.0 1.7 %project_mix.4 = bf16[1,2,768,256]{3,2,1,0:T(8,128)(2,1)S(1)} custom-call(s32[10]{0:T(128)S(1)} %stack.55.order, bf16[192,1024]{1,0:T(8,128)(2,1)S(1)} %get-tuple-element.78.refs_0_, bf16[192,1024]{1,0:T(8,128)(2,1)S(1)} %collective-permute-done.refs_1_, bf16[192,1024]{1,0:T(8,128)(2,1)S(1)} %collective-permute-done.1.refs_2_, ...), custom_call_target="tpu_custom_call" | custom-call | tf_op jit(solution)/shard_map/project_mix/pallas_call | solution.py:101
  29.7 0.6 collective-permute-start.6
  30.3 2.6 %project_mix.5.rest_ref = f32[2,2,768,256]{3,2,1,0:T(8,128)S(1)} custom-call(s32[10]{0:T(128)S(1)} %stack.55.order, bf16[192,1024]{1,0:T(8,128)(2,1)S(1)} %get-tuple-element.78.refs_0_, bf16[192,1024]{1,0:T(8,128)(2,1)S(1)} %collective-permute-done.refs_1_, bf16[192,1024]{1,0:T(8,128)(2,1)S(1)} %collective-permute-done.1.refs_2_, ...), custom_call_target="tpu_custom_call" | custom-call | tf_op jit(solution)/shard_map/project_mix/pallas_call | solution.py:101
  32.9 0.0 copy-start.3
  33.0 5.6 %collective-permute-done.4.both_ref = bf16[1,2,768,256]{3,2,1,0:T(8,128)(2,1)S(1)} collective-permute-done((bf16[1,2,768,256]{3,2,1,0:T(8,128)(2,1)S(1)}, bf16[1,2,768,256]{3,2,1,0:T(8,128)(2,1)S(1)}, u32[]{:S(2)}, u32[]{:S(2)}) %collective-permute-start.4) | collective-permute-done | bytes 786464 | tf_op jit(solution)/shard_map/ppermute | solution.py:512
  38.5 0.7 second_share.1
  39.2 0.4 collective-permute-start.7
  39.7 0.5 last_rows.1
  40.2 0.1 collective-permute-start.5
  40.3 1.3 %collective-permute-done.5.refs_4_ = bf16[4,16,1024]{2,1,0:T(8,128)(2,1)S(1)} collective-permute-done((bf16[4,16,1024]{2,1,0:T(8,128)(2,1)S(1)}, bf16[4,16,1024]{2,1,0:T(8,128)(2,1)S(1)}, u32[]{:S(2)}, u32[]{:S(2)}) %collective-permute-start.5) | collective-permute-done | bytes 131104 | tf_op jit(solution)/shard_map/ppermute | solution.py:522
  41.6 3.0 %project_query.1 = (bf16[2,192,1024]{2,1,0:T(8,128)(2,1)S(1)}, f32[2,192,1024]{2,1,0:T(8,128)S(1)}) custom-call(s32[10]{0:T(128)S(1)} %stack.55.order, bf16[192,1024]{1,0:T(8,128)(2,1)S(1)} %get-tuple-element.78.refs_0_, bf16[192,1024]{1,0:T(8,128)(2,1)S(1)} %collective-permute-done.refs_1_, bf16[192,1024]{1,0:T(8,128)(2,1)S(1)} %collective-permute-done.1.refs_2_, ...), custom_call_target="tpu_custom_call" | custom-call | tf_op jit(solution)/shard_map/project_query/pallas_call | solution.py:101
  44.6 0.0 copy-start.4
  44.6 0.0 copy-start.5
  44.6 8.5 %collective-permute-done.6.first_ref = bf16[1,2,768,256]{3,2,1,0:T(8,128)(2,1)S(1)} collective-permute-done((bf16[1,2,768,256]{3,2,1,0:T(8,128)(2,1)S(1)}, bf16[1,2,768,256]{3,2,1,0:T(8,128)(2,1)S(1)}, u32[]{:S(2)}, u32[]{:S(2)}) %collective-permute-start.6) | collective-permute-done | bytes 786464 | tf_op jit(solution)/shard_map/ppermute | solution.py:515
  53.2 0.9 collective-permute-done.7.second_ref
  54.1 0.8 own_share.1
  54.9 1.1 collective-permute-start.10
  56.0 0.1 collective-permute-start.8
  56.2 1.6 %collective-permute-done.8.swap_ref = bf16[768,256]{1,0:T(8,128)(2,1)S(1)} collective-permute-done((bf16[768,256]{1,0:T(8,128)(2,1)S(1)}, bf16[768,256]{1,0:T(8,128)(2,1)S(1)}, u32[]{:S(2)}, u32[]{:S(2)}) %collective-permute-start.8) | collective-permute-done | bytes 393248 | tf_op jit(solution)/shard_map/ppermute | solution.py:527
  57.8 3.4 %hyena.1 = (bf16[4,192,128]{2,1,0:T(8,128)(2,1)S(1)}, bf16[4,192,128]{2,1,0:T(8,128)(2,1)S(1)}) custom-call(s32[10]{0:T(128)S(1)} %stack.55.order, f32[768,256]{1,0:T(8,128)S(1)} %get-tuple-element.87.own_ref, bf16[768,256]{1,0:T(8,128)(2,1)S(1)} %collective-permute-done.8.swap_ref, f32[3,3,1024]{2,1,0:T(4,128)S(1)} %copy-done.3, f32[8,1024]{1,0:T(8,128)S(1)} %copy-done.4, ...), custom_call_target="tpu_custom_call" | custom-call | tf_op jit(solution)/shard_map/hyena/pallas_call | solution.py:101
  61.2 0.2 collective-permute-start.9
  61.4 1.3 %collective-permute-done.9.other_ref = bf16[4,192,128]{2,1,0:T(8,128)(2,1)S(1)} collective-permute-done((bf16[4,192,128]{2,1,0:T(8,128)(2,1)S(1)}, bf16[4,192,128]{2,1,0:T(8,128)(2,1)S(1)}, u32[]{:S(2)}, u32[]{:S(2)}) %collective-permute-start.9) | collective-permute-done | bytes 196640 | tf_op jit(solution)/shard_map/ppermute | solution.py:531
  62.7 0.6 pair_up.1
  63.2 3.7 %collective-permute-done.10.in_ref = bf16[2,192,1024]{2,1,0:T(8,128)(2,1)S(1)} collective-permute-done((bf16[2,192,1024]{2,1,0:T(8,128)(2,1)S(1)}, bf16[2,192,1024]{2,1,0:T(8,128)(2,1)S(1)}, u32[]{:S(2)}, u32[]{:S(2)}) %collective-permute-start.10) | collective-permute-done | bytes 786464 | tf_op jit(solution)/shard_map/ppermute | solution.py:529
  66.9 0.6 query_second.1
  67.5 1.3 %collective-permute-start.11 = (bf16[192,512]{1,0:T(8,128)(2,1)S(1)}, bf16[192,512]{1,0:T(8,128)(2,1)S(1)}, u32[]{:S(2)}, u32[]{:S(2)}) collective-permute-start(bf16[192,512]{1,0:T(8,128)(2,1)S(1)} %get-tuple-element.97), channel_id=1, source_target_pairs={{0,4},{1,3},{2,6},{3,1},{4,0},{5,7},{6,2},{7,5},{8,12},{9,11},{10,... | collective-permute-start | bytes 589832 | tf_op jit(solution)/shard_map/ppermute | solution.py:533
  68.8 0.8 collective-permute-start.12
  69.6 1.2 %collective-permute-start.13 = (bf16[2,192,128]{2,1,0:T(8,128)(2,1)S(1)}, bf16[2,192,128]{2,1,0:T(8,128)(2,1)S(1)}, u32[]{:S(2)}, u32[]{:S(2)}) collective-permute-start(bf16[2,192,128]{2,1,0:T(8,128)(2,1)S(1)} %get-tuple-element.100), channel_id=1, source_target_pairs={{0,4},{1,3},{2,6},{3,1},{4,0},{5,7},{6,2},{7,5},{8,12},{9,11},{10,... | collective-permute-start | bytes 294920 | tf_op jit(solution)/shard_map/ppermute | solution.py:534
  70.8 1.4 %collective-permute-start.14 = (bf16[2,192,128]{2,1,0:T(8,128)(2,1)S(1)}, bf16[2,192,128]{2,1,0:T(8,128)(2,1)S(1)}, u32[]{:S(2)}, u32[]{:S(2)}) collective-permute-start(bf16[2,192,128]{2,1,0:T(8,128)(2,1)S(1)} %get-tuple-element.101), channel_id=1, source_target_pairs={{0,2},{1,5},{2,0},{3,7},{4,6},{5,1},{6,4},{7,3},{8,10},{9,13},{10,... | collective-permute-start | bytes 294920 | tf_op jit(solution)/shard_map/ppermute | solution.py:534
  72.2 0.9 collective-permute-start.15
  73.1 6.5 %collective-permute-done.13.refs_3_ = bf16[2,192,128]{2,1,0:T(8,128)(2,1)S(1)} collective-permute-done((bf16[2,192,128]{2,1,0:T(8,128)(2,1)S(1)}, bf16[2,192,128]{2,1,0:T(8,128)(2,1)S(1)}, u32[]{:S(2)}, u32[]{:S(2)}) %collective-permute-start.13) | collective-permute-done | bytes 98336 | tf_op jit(solution)/shard_map/ppermute | solution.py:534
  79.6 0.0 collective-permute-done.14.refs_4_
  79.6 0.0 collective-permute-done.15.refs_5_
  79.6 0.0 collective-permute-done.11.refs_0_
  79.6 1.9 %gate.1 = (bf16[192,1024]{1,0:T(8,128)(2,1)S(1)}, bf16[192,1024]{1,0:T(8,128)(2,1)S(1)}, bf16[192,1024]{1,0:T(8,128)(2,1)S(1)}) custom-call(s32[15]{0:T(128)S(1)} %concatenate.4.scalars, f32[2,192,1024]{2,1,0:T(8,128)S(1)} %get-tuple-element.95.rest_ref, bf16[2,192,1024]{2,1,0:T(8,128)(2,1)S(1)} %collective-permute-done.10.in_ref, ...), custom_call_target="tpu_custom_call" | custom-call | tf_op jit(solution)/shard_map/gate/pallas_call | solution.py:101
  81.5 1.2 %collective-permute-start.16 = (bf16[192,1024]{1,0:T(8,128)(2,1)S(1)}, bf16[192,1024]{1,0:T(8,128)(2,1)S(1)}, u32[]{:S(2)}, u32[]{:S(2)}) collective-permute-start(bf16[192,1024]{1,0:T(8,128)(2,1)S(1)} %get-tuple-element.105), channel_id=1, source_target_pairs={{0,8},{8,0},{16,24},{24,16},{1,9},{9,1},{17,25},{25,17},{2,10},{10... | collective-permute-start | bytes 1179656 | tf_op jit(solution)/shard_map/ppermute | solution.py:452
  82.7 2.8 %collective-permute-start.19 = (bf16[192,1024]{1,0:T(8,128)(2,1)S(1)}, bf16[192,1024]{1,0:T(8,128)(2,1)S(1)}, u32[]{:S(2)}, u32[]{:S(2)}) collective-permute-start(bf16[192,1024]{1,0:T(8,128)(2,1)S(1)} %get-tuple-element.106), channel_id=1, source_target_pairs={{0,8},{24,16},{1,9},{25,17},{2,10},{26,18},{3,11},{27,19},{4,12},{... | collective-permute-start | bytes 1179656 | tf_op jit(solution)/shard_map/ppermute | solution.py:456
  85.5 0.7 collective-permute-start.17
  86.2 1.1 out_columns.3.far_ref
  87.3 4.2 %collective-permute-start.18 = (bf16[192,1024]{1,0:T(8,128)(2,1)S(1)}, bf16[192,1024]{1,0:T(8,128)(2,1)S(1)}, u32[]{:S(2)}, u32[]{:S(2)}) collective-permute-start(bf16[192,1024]{1,0:T(8,128)(2,1)S(1)} %out_columns.3.far_ref), channel_id=1, source_target_pairs={{0,16},{24,8},{1,17},{25,9},{2,18},{26,10},{3,19},{27,11},{4,20},{... | collective-permute-start | bytes 1179656 | tf_op jit(solution)/shard_map/ppermute | solution.py:454
  91.6 0.6 collective-permute-done.16.pair_ref
  92.3 0.6 both.1
  92.9 1.3 %collective-permute-start.20 = (bf16[192,1024]{1,0:T(8,128)(2,1)S(1)}, bf16[192,1024]{1,0:T(8,128)(2,1)S(1)}, u32[]{:S(2)}, u32[]{:S(2)}) collective-permute-start(bf16[192,1024]{1,0:T(8,128)(2,1)S(1)} %both.1), channel_id=1, source_target_pairs={{8,24},{16,0},{9,25},{17,1},{10,26},{18,2},{11,27},{19,3},{12,28},... | collective-permute-start | bytes 1179656 | tf_op jit(solution)/shard_map/ppermute | solution.py:463
  94.2 1.1 out_columns.2.own_ref
  95.3 12.5 %collective-permute-done.18.refs_1_ = bf16[192,1024]{1,0:T(8,128)(2,1)S(1)} collective-permute-done((bf16[192,1024]{1,0:T(8,128)(2,1)S(1)}, bf16[192,1024]{1,0:T(8,128)(2,1)S(1)}, u32[]{:S(2)}, u32[]{:S(2)}) %collective-permute-start.18) | collective-permute-done | bytes 393248 | tf_op jit(solution)/shard_map/ppermute | solution.py:454
  107.8 6.2 %collective-permute-done.20.refs_3_ = bf16[192,1024]{1,0:T(8,128)(2,1)S(1)} collective-permute-done((bf16[192,1024]{1,0:T(8,128)(2,1)S(1)}, bf16[192,1024]{1,0:T(8,128)(2,1)S(1)}, u32[]{:S(2)}, u32[]{:S(2)}) %collective-permute-start.20) | collective-permute-done | bytes 393248 | tf_op jit(solution)/shard_map/ppermute | solution.py:463
  114.0 1.6 %total.1 = bf16[192,1024]{1,0:T(8,128)(2,1)} custom-call(s32[5]{0:T(128)S(1)} %stack.61.picks, f32[192,1024]{1,0:T(8,128)S(1)} %out_columns.2.own_ref, bf16[192,1024]{1,0:T(8,128)(2,1)S(1)} %collective-permute-done.16.pair_ref, bf16[192,1024]{1,0:T(8,128)(2,1)S(1)} %collective-permute-done.17.refs_0_, bf16[192,1024]{1,0:T(8,128)(2,1)S(1)} %collective-permute-done.18.refs_1_, ...), custom_call_target="tpu_custom_call" | custom-call | tf_op jit(solution)/shard_map/total/pallas_call | solution.py:101
  (10 shorter events, 0.0 us)
Async XLA Ops:
  0.0 24.8 %collective-permute-start.3 = (bf16[3,512,1024]{2,1,0:T(8,128)(2,1)}, bf16[3,512,1024]{2,1,0:T(8,128)(2,1)S(1)}, u32[]{:S(2)}, u32[]{:S(2)}) collective-permute-start(bf16[3,512,1024]{2,1,0:T(8,128)(2,1)} %bitcast.14), channel_id=1, source_target_pairs={{0,1},{1,0},{2,3},{3,2},{4,5},{5,4},{6,7},{7,6},{8,9},{9,8},{10,11... | collective-permute-start | bytes 9437192 | tf_op jit(solution)/shard_map/ppermute | solution.py:505
  0.7 1.4 %copy-start.2 = (bf16[192,4096]{1,0:T(8,128)(2,1)S(1)}, bf16[192,4096]{1,0:T(8,128)(2,1)}, u32[]{:S(2)}) copy-start(bf16[192,4096]{1,0:T(8,128)(2,1)} %tokens_ref.1) | copy-start | bytes 4718596
  2.8 13.2 %collective-permute-start = (bf16[192,1024]{1,0:T(8,128)(2,1)S(1)}, bf16[192,1024]{1,0:T(8,128)(2,1)S(1)}, u32[]{:S(2)}, u32[]{:S(2)}) collective-permute-start(bf16[192,1024]{1,0:T(8,128)(2,1)S(1)} %get-tuple-element.64), channel_id=1, source_target_pairs={{0,4},{1,3},{2,6},{3,1},{4,0},{5,7},{6,2},{7,5},{8,12},{9,11},{10,... | collective-permute-start | bytes 1179656 | tf_op jit(solution)/shard_map/ppermute | solution.py:509
  5.4 12.1 %collective-permute-start.1 = (bf16[192,1024]{1,0:T(8,128)(2,1)S(1)}, bf16[192,1024]{1,0:T(8,128)(2,1)S(1)}, u32[]{:S(2)}, u32[]{:S(2)}) collective-permute-start(bf16[192,1024]{1,0:T(8,128)(2,1)S(1)} %get-tuple-element.65), channel_id=1, source_target_pairs={{0,2},{1,5},{2,0},{3,7},{4,6},{5,1},{6,4},{7,3},{8,10},{9,13},{10,... | collective-permute-start | bytes 1179656 | tf_op jit(solution)/shard_map/ppermute | solution.py:509
  6.9 17.9 %collective-permute-start.2 = (bf16[192,1024]{1,0:T(8,128)(2,1)S(1)}, bf16[192,1024]{1,0:T(8,128)(2,1)S(1)}, u32[]{:S(2)}, u32[]{:S(2)}) collective-permute-start(bf16[192,1024]{1,0:T(8,128)(2,1)S(1)} %get-tuple-element.66), channel_id=1, source_target_pairs={{0,6},{1,7},{2,4},{3,5},{4,2},{5,3},{6,0},{7,1},{8,14},{9,15},{10,... | collective-permute-start | bytes 1179656 | tf_op jit(solution)/shard_map/ppermute | solution.py:509
  6.9 3.4 %copy-start = (bf16[1024,4096]{1,0:T(8,128)(2,1)S(1)}, bf16[1024,4096]{1,0:T(8,128)(2,1)}, u32[]{:S(2)}) copy-start(bf16[1024,4096]{1,0:T(8,128)(2,1)} %refs_1_) | copy-start | bytes 25165828
  10.3 1.9 %copy-start.1 = (bf16[512,3,1024]{2,0,1:T(8,128)(2,1)S(1)}, bf16[512,3,1024]{2,0,1:T(8,128)(2,1)}, u32[]{:S(2)}) copy-start(bf16[512,3,1024]{2,0,1:T(8,128)(2,1)} %param.7) | copy-start | bytes 9437188
  26.5 12.1 %collective-permute-start.4 = (bf16[1,2,768,256]{3,2,1,0:T(8,128)(2,1)S(1)}, bf16[1,2,768,256]{3,2,1,0:T(8,128)(2,1)S(1)}, u32[]{:S(2)}, u32[]{:S(2)}) collective-permute-start(bf16[1,2,768,256]{3,2,1,0:T(8,128)(2,1)S(1)} %project_mix.3), channel_id=1, source_target_pairs={{0,2},{1,5},{2,0},{3,7},{4,6},{5,1},{6,4},{7,3},{8,10},{9,13},{10,... | collective-permute-start | bytes 2359304 | tf_op jit(solution)/shard_map/ppermute | solution.py:512
  29.7 23.4 %collective-permute-start.6 = (bf16[1,2,768,256]{3,2,1,0:T(8,128)(2,1)S(1)}, bf16[1,2,768,256]{3,2,1,0:T(8,128)(2,1)S(1)}, u32[]{:S(2)}, u32[]{:S(2)}) collective-permute-start(bf16[1,2,768,256]{3,2,1,0:T(8,128)(2,1)S(1)} %project_mix.4), channel_id=1, source_target_pairs={{0,2},{1,5},{2,0},{3,7},{4,6},{5,1},{6,4},{7,3},{8,10},{9,13},{10,... | collective-permute-start | bytes 2359304 | tf_op jit(solution)/shard_map/ppermute | solution.py:515
  32.9 8.7 %copy-start.3 = (f32[3,3,1024]{2,1,0:T(4,128)S(1)}, f32[3,3,1024]{2,1,0:T(4,128)}, u32[]{:S(2)}) copy-start(f32[3,3,1024]{2,1,0:T(4,128)} %filt_ref.1) | copy-start | bytes 110596
  39.2 14.8 %collective-permute-start.7 = (bf16[1,2,768,256]{3,2,1,0:T(8,128)(2,1)S(1)}, bf16[1,2,768,256]{3,2,1,0:T(8,128)(2,1)S(1)}, u32[]{:S(2)}, u32[]{:S(2)}) collective-permute-start(bf16[1,2,768,256]{3,2,1,0:T(8,128)(2,1)S(1)} %second_share.1), channel_id=1, source_target_pairs={{0,4},{1,3},{2,6},{3,1},{4,0},{5,7},{6,2},{7,5},{8,12},{9,11},{10,... | collective-permute-start | bytes 2359304 | tf_op jit(solution)/shard_map/ppermute | solution.py:519
  40.2 1.4 %collective-permute-start.5 = (bf16[4,16,1024]{2,1,0:T(8,128)(2,1)S(1)}, bf16[4,16,1024]{2,1,0:T(8,128)(2,1)S(1)}, u32[]{:S(2)}, u32[]{:S(2)}) collective-permute-start(bf16[4,16,1024]{2,1,0:T(8,128)(2,1)S(1)} %last_rows.1), channel_id=1, source_target_pairs={{0,1},{1,0},{2,3},{3,2},{4,5},{5,4},{6,7},{7,6},{8,9},{9,8},{10,11... | collective-permute-start | bytes 393224 | tf_op jit(solution)/shard_map/ppermute | solution.py:522
  44.6 13.1 %copy-start.4 = (f32[8,1024]{1,0:T(8,128)S(1)}, f32[8,1024]{1,0:T(8,128)}, u32[]{:S(2)}) copy-start(f32[8,1024]{1,0:T(8,128)} %decay_ref.1) | copy-start | bytes 98308
  44.6 13.1 %copy-start.5 = (f32[8,1024]{1,0:T(8,128)S(1)}, f32[8,1024]{1,0:T(8,128)}, u32[]{:S(2)}) copy-start(f32[8,1024]{1,0:T(8,128)} %residue_ref.1) | copy-start | bytes 98308
  54.9 12.1 %collective-permute-start.10 = (bf16[2,192,1024]{2,1,0:T(8,128)(2,1)S(1)}, bf16[2,192,1024]{2,1,0:T(8,128)(2,1)S(1)}, u32[]{:S(2)}, u32[]{:S(2)}) collective-permute-start(bf16[2,192,1024]{2,1,0:T(8,128)(2,1)S(1)} %get-tuple-element.96), channel_id=1, source_target_pairs={{0,2},{1,5},{2,0},{3,7},{4,6},{5,1},{6,4},{7,3},{8,10},{9,13},{10,... | collective-permute-start | bytes 2359304 | tf_op jit(solution)/shard_map/ppermute | solution.py:529
  56.0 1.7 %collective-permute-start.8 = (bf16[768,256]{1,0:T(8,128)(2,1)S(1)}, bf16[768,256]{1,0:T(8,128)(2,1)S(1)}, u32[]{:S(2)}, u32[]{:S(2)}) collective-permute-start(bf16[768,256]{1,0:T(8,128)(2,1)S(1)} %get-tuple-element.88), channel_id=1, source_target_pairs={{0,1},{1,0},{2,3},{3,2},{4,5},{5,4},{6,7},{7,6},{8,9},{9,8},{10,11... | collective-permute-start | bytes 1179656 | tf_op jit(solution)/shard_map/ppermute | solution.py:527
  61.2 1.5 %collective-permute-start.9 = (bf16[4,192,128]{2,1,0:T(8,128)(2,1)S(1)}, bf16[4,192,128]{2,1,0:T(8,128)(2,1)S(1)}, u32[]{:S(2)}, u32[]{:S(2)}) collective-permute-start(bf16[4,192,128]{2,1,0:T(8,128)(2,1)S(1)} %get-tuple-element.90), channel_id=1, source_target_pairs={{0,1},{1,0},{2,3},{3,2},{4,5},{5,4},{6,7},{7,6},{8,9},{9,8},{10,11... | collective-permute-start | bytes 589832 | tf_op jit(solution)/shard_map/ppermute | solution.py:531
  67.5 12.1 %collective-permute-start.11 = (bf16[192,512]{1,0:T(8,128)(2,1)S(1)}, bf16[192,512]{1,0:T(8,128)(2,1)S(1)}, u32[]{:S(2)}, u32[]{:S(2)}) collective-permute-start(bf16[192,512]{1,0:T(8,128)(2,1)S(1)} %get-tuple-element.97), channel_id=1, source_target_pairs={{0,4},{1,3},{2,6},{3,1},{4,0},{5,7},{6,2},{7,5},{8,12},{9,11},{10,... | collective-permute-start | bytes 589832 | tf_op jit(solution)/shard_map/ppermute | solution.py:533
  68.8 10.8 %collective-permute-start.12 = (bf16[192,512]{1,0:T(8,128)(2,1)S(1)}, bf16[192,512]{1,0:T(8,128)(2,1)S(1)}, u32[]{:S(2)}, u32[]{:S(2)}) collective-permute-start(bf16[192,512]{1,0:T(8,128)(2,1)S(1)} %get-tuple-element.98), channel_id=1, source_target_pairs={{0,4},{1,3},{2,6},{3,1},{4,0},{5,7},{6,2},{7,5},{8,12},{9,11},{10,... | collective-permute-start | bytes 589832 | tf_op jit(solution)/shard_map/ppermute | solution.py:533
  69.6 10.0 %collective-permute-start.13 = (bf16[2,192,128]{2,1,0:T(8,128)(2,1)S(1)}, bf16[2,192,128]{2,1,0:T(8,128)(2,1)S(1)}, u32[]{:S(2)}, u32[]{:S(2)}) collective-permute-start(bf16[2,192,128]{2,1,0:T(8,128)(2,1)S(1)} %get-tuple-element.100), channel_id=1, source_target_pairs={{0,4},{1,3},{2,6},{3,1},{4,0},{5,7},{6,2},{7,5},{8,12},{9,11},{10,... | collective-permute-start | bytes 294920 | tf_op jit(solution)/shard_map/ppermute | solution.py:534
  70.8 8.8 %collective-permute-start.14 = (bf16[2,192,128]{2,1,0:T(8,128)(2,1)S(1)}, bf16[2,192,128]{2,1,0:T(8,128)(2,1)S(1)}, u32[]{:S(2)}, u32[]{:S(2)}) collective-permute-start(bf16[2,192,128]{2,1,0:T(8,128)(2,1)S(1)} %get-tuple-element.101), channel_id=1, source_target_pairs={{0,2},{1,5},{2,0},{3,7},{4,6},{5,1},{6,4},{7,3},{8,10},{9,13},{10,... | collective-permute-start | bytes 294920 | tf_op jit(solution)/shard_map/ppermute | solution.py:534
  72.2 7.4 %collective-permute-start.15 = (bf16[2,192,128]{2,1,0:T(8,128)(2,1)S(1)}, bf16[2,192,128]{2,1,0:T(8,128)(2,1)S(1)}, u32[]{:S(2)}, u32[]{:S(2)}) collective-permute-start(bf16[2,192,128]{2,1,0:T(8,128)(2,1)S(1)} %get-tuple-element.102), channel_id=1, source_target_pairs={{0,6},{1,7},{2,4},{3,5},{4,2},{5,3},{6,0},{7,1},{8,14},{9,15},{10,... | collective-permute-start | bytes 294920 | tf_op jit(solution)/shard_map/ppermute | solution.py:534
  81.5 10.8 %collective-permute-start.16 = (bf16[192,1024]{1,0:T(8,128)(2,1)S(1)}, bf16[192,1024]{1,0:T(8,128)(2,1)S(1)}, u32[]{:S(2)}, u32[]{:S(2)}) collective-permute-start(bf16[192,1024]{1,0:T(8,128)(2,1)S(1)} %get-tuple-element.105), channel_id=1, source_target_pairs={{0,8},{8,0},{16,24},{24,16},{1,9},{9,1},{17,25},{25,17},{2,10},{10... | collective-permute-start | bytes 1179656 | tf_op jit(solution)/shard_map/ppermute | solution.py:452
  82.7 25.1 %collective-permute-start.19 = (bf16[192,1024]{1,0:T(8,128)(2,1)S(1)}, bf16[192,1024]{1,0:T(8,128)(2,1)S(1)}, u32[]{:S(2)}, u32[]{:S(2)}) collective-permute-start(bf16[192,1024]{1,0:T(8,128)(2,1)S(1)} %get-tuple-element.106), channel_id=1, source_target_pairs={{0,8},{24,16},{1,9},{25,17},{2,10},{26,18},{3,11},{27,19},{4,12},{... | collective-permute-start | bytes 1179656 | tf_op jit(solution)/shard_map/ppermute | solution.py:456
  85.5 22.3 %collective-permute-start.17 = (bf16[192,1024]{1,0:T(8,128)(2,1)S(1)}, bf16[192,1024]{1,0:T(8,128)(2,1)S(1)}, u32[]{:S(2)}, u32[]{:S(2)}) collective-permute-start(bf16[192,1024]{1,0:T(8,128)(2,1)S(1)} %get-tuple-element.106), channel_id=1, source_target_pairs={{8,16},{16,8},{9,17},{17,9},{10,18},{18,10},{11,19},{19,11},{12,20... | collective-permute-start | bytes 1179656 | tf_op jit(solution)/shard_map/ppermute | solution.py:455
  87.3 20.5 %collective-permute-start.18 = (bf16[192,1024]{1,0:T(8,128)(2,1)S(1)}, bf16[192,1024]{1,0:T(8,128)(2,1)S(1)}, u32[]{:S(2)}, u32[]{:S(2)}) collective-permute-start(bf16[192,1024]{1,0:T(8,128)(2,1)S(1)} %out_columns.3.far_ref), channel_id=1, source_target_pairs={{0,16},{24,8},{1,17},{25,9},{2,18},{26,10},{3,19},{27,11},{4,20},{... | collective-permute-start | bytes 1179656 | tf_op jit(solution)/shard_map/ppermute | solution.py:454
  92.9 21.1 %collective-permute-start.20 = (bf16[192,1024]{1,0:T(8,128)(2,1)S(1)}, bf16[192,1024]{1,0:T(8,128)(2,1)S(1)}, u32[]{:S(2)}, u32[]{:S(2)}) collective-permute-start(bf16[192,1024]{1,0:T(8,128)(2,1)S(1)} %both.1), channel_id=1, source_target_pairs={{8,24},{16,0},{9,25},{17,1},{10,26},{18,2},{11,27},{19,3},{12,28},... | collective-permute-start | bytes 1179656 | tf_op jit(solution)/shard_map/ppermute | solution.py:463

commit v3 on v2

--- a/solution.py
+++ b/solution.py
@@ -116,11 +116,29 @@
 def cut(order, tokens, pieces):
     high, wide = tokens.shape[0], tokens.shape[1] // pieces
 
-    def kernel(order, tokens_ref, *out_refs):
+    def part(order, tokens_ref, out_ref):
+        here = columns(order[2 * pieces + 2], high // 2)
+        out_ref[...] = tokens_ref[here, columns(order[pieces - 1], wide)]
+
+    def rest(order, tokens_ref, *out_refs):
         for s, out_ref in enumerate(out_refs):
             out_ref[...] = tokens_ref[:, columns(order[s], wide)]
 
-    return local(kernel, "cut", [((high, wide), tokens.dtype)] * pieces, order, [tokens])
+    last = local(part, "cut_part", [((high // 2, wide), tokens.dtype)], order, [tokens])
+    last, tokens = lax.optimization_barrier((last, tokens))
+    shapes = [((high, wide), tokens.dtype)] * (pieces - 1)
+    return [*local(rest, "cut", shapes, order, [tokens]), last]
+
+
+def join_rows(order, mine, other):
+    half, wide = mine.shape
+    at = order.shape[0] - 1
+
+    def kernel(order, mine_ref, other_ref, out_ref):
+        out_ref[columns(order[at], half), :] = mine_ref[...]
+        out_ref[columns(1 - order[at], half), :] = other_ref[...]
+
+    return local(kernel, "join_rows", [((2 * half, wide), mine.dtype)], order, [mine, other])
 
 
 def stage(*arrays):
@@ -201,7 +219,7 @@
 
     def kernel(order, *refs):
         x_refs = refs[:chips]
-        before_ref, own_ref, other_ref, filt_ref, sent_ref, rest_ref, rows, ends, total = refs[chips:]
+        before_ref, own_ref, other_ref, filt_ref, *out_refs, rows, ends, total = refs[chips:]
         core = order[2 * chips]
         ends[0] = jnp.zeros_like(ends[0])
         for s in range(chips):
@@ -221,12 +239,9 @@
                 value = filt_ref[0, 0:1, at] * total[first : first + high, :]
                 for j in range(1, taps):
                     value = value + filt_ref[j, 0:1, at] * total[first - j : first - j + high, :]
-                if i < 2:
-                    rest_ref[i, :, at] = value
-                else:
-                    sent_ref[3 - i, :, at] = value.astype(BF16)
-
-    shapes = [((2, high, chans), BF16), ((2, high, chans), F32)]
+                out_refs[i][:, at] = value.astype(out_refs[i].dtype)
+
+    shapes = [((high, chans), F32 if i < 2 else BF16) for i in range(chips)]
     scratch = [
         pltpu.VMEM((2, chips * step, depth), BF16),
         pltpu.VMEM((chips + 1, some, 2 * depth), BF16),
@@ -383,35 +398,25 @@
     return local(kernel, "pair_up", [((2, high, chans), BF16)] * chips, order, [keep, other])
 
 
-def query_second(order, rest, q_in, pieces):
-    _, rows, chans = rest.shape
-    share = chans // pieces
-
-    def kernel(order, rest_ref, in_ref, *out_refs):
-        for i, out_ref in enumerate(out_refs):
-            at = slice(i * share, (i + 1) * share)
-            out_ref[...] = (rest_ref[1, :, at] + in_ref[0, :, at].astype(F32)).astype(BF16)
-
-    shapes = [((rows, share), BF16)] * pieces
-    return local(kernel, "query_second", shapes, order, [rest, q_in])
-
-
-def gate(scalars, rest, q_in, second_in, long_parts, w_out, groups):
-    rows, chans = second_in[0].shape[0], rest.shape[2]
+def query_second(order, rest, q_in):
+    def kernel(order, rest_ref, in_ref, out_ref):
+        out_ref[...] = (rest_ref[...] + in_ref[...].astype(F32)).astype(BF16)
+
+    return local(kernel, "query_second", [(rest.shape, BF16)], order, [rest, q_in])
+
+
+def gate(scalars, queries, long_parts, w_out, groups):
+    rows, chans = queries[0].shape
     chips = len(long_parts)
     part = long_parts[0].shape[2]
     wide = w_out.shape[1] // groups
-    first_pick = 2 * chips + 2
-
-    def kernel(scalars, rest_ref, in_ref, *refs):
-        second_refs = refs[: len(second_in)]
-        long_refs = refs[len(second_in) : len(second_in) + chips]
-        w_ref, gated_ref, pair_ref, side_ref, query = refs[len(second_in) + chips :]
+    first_pick = 2 * chips + 3
+
+    def kernel(scalars, *refs):
+        query_refs, long_refs = refs[: len(queries)], refs[len(queries) : len(queries) + chips]
+        w_ref, gated_ref, pair_ref, side_ref, query = refs[len(queries) + chips :]
         core = scalars[2 * chips]
-        query[...] = rest_ref[0] + in_ref[1].astype(F32)
-        share = second_refs[0].shape[1]
-        for i, ref in enumerate(second_refs):
-            query[:, i * share : (i + 1) * share] += ref[...].astype(F32)
+        query[...] = sum(ref[...].astype(F32) for ref in query_refs)
         for s, ref in enumerate(long_refs):
             for h in range(2):
                 at = columns(2 * scalars[s] + (core ^ h), part)
@@ -425,7 +430,7 @@
             out_ref[...] = total.astype(BF16)
 
     shapes = [((rows, chans), BF16), ((rows, wide), BF16), ((rows, wide), BF16)]
-    arrays = [rest, q_in, *second_in, *long_parts, w_out]
+    arrays = [*queries, *long_parts, w_out]
     scratch = [pltpu.VMEM((rows, chans), F32)]
     return local(kernel, "gate", shapes, scalars, arrays, scratch)
 
@@ -451,8 +456,9 @@
 def output_over_line(picks, gated, pair, side, w_out, groups):
     pair_in = lax.ppermute(pair, "dp", [(0, 1), (1, 0), (2, 3), (3, 2)])
     far = out_columns(picks, 2, gated, w_out, groups, BF16)
+    middle_in = lax.ppermute(side, "dp", [(1, 2), (2, 1)])
+    side, far = lax.optimization_barrier((side, far))
     end_in = lax.ppermute(far, "dp", [(0, 2), (3, 1)])
-    middle_in = lax.ppermute(side, "dp", [(1, 2), (2, 1)])
     side_in = lax.ppermute(side, "dp", [(0, 1), (3, 2)])
     own = out_columns(picks, 3, gated, w_out, groups, F32)
 
@@ -494,7 +500,7 @@
 
     slot_chip = [chip ^ relative(s, core) for s in range(chips)]
     slot_other = [chip ^ relative(s, 1 - core) for s in range(chips)]
-    order = jnp.stack(slot_chip + slot_other + [core, me]).astype(jnp.int32)
+    order = jnp.stack(slot_chip + slot_other + [core, me, lax.axis_index("dp") % 2]).astype(jnp.int32)
     picks = line_picks().astype(jnp.int32)
     both_scalars = jnp.concatenate([order, picks])
     order, picks, both_scalars = lax.optimization_barrier((order, picks, both_scalars))
@@ -506,7 +512,10 @@
     xs = cut(order, tokens, chips)
     own_w, w_out, xs = lax.optimization_barrier((own_w, w_out, xs))
     own_w, w_out = stage(own_w, w_out)
-    xs = [xs[0]] + [lax.ppermute(xs[s], "ctx", route(s)) for s in (1, 2, 3)]
+    half = lax.ppermute(xs[3], "ctx", route(3))
+    other = lax.ppermute(half, "dp", [(i, i ^ 1) for i in range(groups)])
+    xs = [xs[0]] + [lax.ppermute(xs[s], "ctx", route(s)) for s in (1, 2)]
+    xs.append(join_rows(order, half, other))
 
     both = project_mix(order, xs, own_w, other_w, [3], BF16)
     both_in = lax.ppermute(both, "ctx", route(2))
@@ -520,19 +529,22 @@
 
     xs, second = lax.optimization_barrier((xs, second))
     before = lax.ppermute(last_rows(order, xs, 16), "ctx", swap)
-    q_sent, q_rest = project_query(order, xs, before, own_w, other_w, short_filter)
-    q_rest, rest = lax.optimization_barrier((q_rest, rest))
+    q_own, q_next, q_first, q_both = project_query(order, xs, before, own_w, other_w, short_filter)
+    q_own, rest = lax.optimization_barrier((q_own, rest))
 
     own, other_half = own_share(order, rest, first_in, second_in, chips)
     other_half = lax.ppermute(other_half, "ctx", swap)
-    q_sent, own = lax.optimization_barrier((q_sent, own))
-    q_in = lax.ppermute(q_sent, "ctx", route(2))
+    q_both, q_first, own = lax.optimization_barrier((q_both, q_first, own))
+    q_both = lax.ppermute(q_both, "ctx", route(2))
+    q_first = lax.ppermute(q_first, "ctx", route(2))
     keep, send = hyena(order, own, other_half, short_filter, mode_decay, residue, count)
+    q_next, keep, send = lax.optimization_barrier((q_next, keep, send))
+    q_second = query_second(order, q_next, q_both)
     long_parts = pair_up(order, keep, lax.ppermute(send, "ctx", swap))
-    q_rest, long_parts = lax.optimization_barrier((q_rest, long_parts))
-    q_second = [lax.ppermute(q, "ctx", route(1)) for q in query_second(order, q_rest, q_in, 2)]
+    q_second = lax.ppermute(q_second, "ctx", route(1))
     long_parts = [long_parts[0]] + [lax.ppermute(long_parts[s], "ctx", route(s)) for s in (1, 2, 3)]
-    gated, pair, side = gate(both_scalars, q_rest, q_in, q_second, long_parts, w_out, groups)
+    queries = [q_own, q_first, q_second]
+    gated, pair, side = gate(both_scalars, queries, long_parts, w_out, groups)
     return output_over_line(picks, gated, pair, side, w_out, groups)
 
 

time: 116 us -> 111 us (0.957)
  waiting for transfers between devices: 60.6 us -> 51.1 us
  starting transfers between devices: 24.5 us -> 29.7 us
  local copies, waits for them, and re-layouts: 6.96 us -> 5.08 us
    ppermute x6 -> x7, waiting for transfers between devices: 15.5 us -> 9.24 us  [the longest x1 5.15 us: on_device_chips(): half = lax.ppermute(xs[3], 'ctx', route(3))]
    ppermute x1, waiting for transfers between devices: 0.01 us -> 5.26 us  [output_over_line(): side_in = lax.ppermute(side, 'dp', [(0, 1), (3, 2)])]
    ppermute x1, waiting for transfers between devices: 12.5 us -> 7.63 us  [output_over_line(): end_in = lax.ppermute(far, 'dp', [(0, 2), (3, 1)])]
    ppermute x1, starting transfers between devices: 2.79 us -> 6.31 us  [output_over_line(): side_in = lax.ppermute(side, 'dp', [(0, 1), (3, 2)])]
    ppermute x1, starting transfers between devices: 4.25 us -> 1.31 us  [output_over_line(): end_in = lax.ppermute(far, 'dp', [(0, 2), (3, 1)])]
    ppermute x6 -> x7, starting transfers between devices: 7.36 us -> 9.65 us  [the longest x1 3.51 us: on_device_chips(): half = lax.ppermute(xs[3], 'ctx', route(3))]
    unnamed x12, local copies, waits for them, and re-layouts: 6.7 us -> 4.81 us
    ppermute x1, waiting for transfers between devices: 1.59 us -> 0.01 us  [on_device_chips(): other_half = lax.ppermute(other_half, 'ctx', swap)]
  transfers between devices with their start and end apart: 21 -> 22, of which waited for: 14 -> 16; matrix products, arithmetic and copies ran while one was open for 0% -> 0% of each run, Pallas kernels for 15% -> 17%
where the time goes in v3:
time: 111 us
  waiting for transfers between devices  51.1 us (46%)
  starting transfers between devices  29.7 us (27%)
  Pallas kernels  24.5 us (22%)
  local copies, waits for them, and re-layouts  5.08 us (5%)
    pallas_call x18, Pallas kernels, local(): pl.pallas_call(kernel, out_shape=out if len(out) > 1 else out[0], in_spec...  23.7 us
    ppermute x1, waiting for transfers between devices, output_over_line(): end_in = lax.ppermute(far, 'dp', [(0, 2), (3, 1)])  7.63 us
    ppermute x1, waiting for transfers between devices, on_device_chips(): first_in = lax.ppermute(first, 'ctx', route(2))  7.34 us
    ppermute x1, starting transfers between devices, output_over_line(): side_in = lax.ppermute(side, 'dp', [(0, 1), (3, 2)])  6.31 us
    ppermute x1, waiting for transfers between devices, output_over_line(): far_in = lax.ppermute(both, 'dp', [(1, 3), (2, 0)])  6.18 us
    ppermute x3, waiting for transfers between devices, on_device_chips(): lax.ppermute(long_parts[s], 'ctx', route(s))  5.81 us
    ppermute x1, waiting for transfers between devices, on_device_chips(): both_in = lax.ppermute(both, 'ctx', route(2))  5.58 us
    ppermute x1, waiting for transfers between devices, output_over_line(): side_in = lax.ppermute(side, 'dp', [(0, 1), (3, 2)])  5.26 us
  transfers between devices with their start and end apart: 22, of which 16 were waited for; matrix products, arithmetic and copies ran while one was open for 0% of the time, Pallas kernels for 17%

profile of v3, /device:TPU:0, one launch (start us, length us, event | category | flops | bytes accessed | tf_op | source)
XLA Modules:
  0.0 110.5 jit_solution(18256672719315933583)
XLA Ops:
  0.0 0.5 collective-permute-start.4
  0.5 0.1 stack.59.order
  0.5 0.1 concatenate.4.scalars
  0.6 0.1 stack.65.picks
  0.7 1.4 %copy-done.1 = bf16[192,4096]{1,0:T(8,128)(2,1)S(1)} copy-done((bf16[192,4096]{1,0:T(8,128)(2,1)S(1)}, bf16[192,4096]{1,0:T(8,128)(2,1)}, u32[]{:S(2)}) %copy-start.1) | copy-done | bytes 1572888
  2.1 0.6 cut_part.1
  2.7 0.6 cut.1
  3.3 3.5 %collective-permute-start.2 = (bf16[96,1024]{1,0:T(8,128)(2,1)S(1)}, bf16[96,1024]{1,0:T(8,128)(2,1)S(1)}, u32[]{:S(2)}, u32[]{:S(2)}) collective-permute-start(bf16[96,1024]{1,0:T(8,128)(2,1)S(1)} %cut_part.1), channel_id=1, source_target_pairs={{0,6},{1,7},{2,4},{3,5},{4,2},{5,3},{6,0},{7,1},{8,14},{9,15},{10,... | collective-permute-start | bytes 589832 | tf_op jit(solution)/shard_map/ppermute | solution.py:515
  6.8 0.5 collective-permute-start
  7.4 0.1 collective-permute-start.1
  7.5 5.2 %collective-permute-done.2.mine_ref = bf16[96,1024]{1,0:T(8,128)(2,1)S(1)} collective-permute-done((bf16[96,1024]{1,0:T(8,128)(2,1)S(1)}, bf16[96,1024]{1,0:T(8,128)(2,1)S(1)}, u32[]{:S(2)}, u32[]{:S(2)}) %collective-permute-start.2) | collective-permute-done | bytes 196640 | tf_op jit(solution)/shard_map/ppermute | solution.py:515
  12.6 2.0 %collective-permute-start.3 = (bf16[96,1024]{1,0:T(8,128)(2,1)S(1)}, bf16[96,1024]{1,0:T(8,128)(2,1)S(1)}, u32[]{:S(2)}, u32[]{:S(2)}) collective-permute-start(bf16[96,1024]{1,0:T(8,128)(2,1)S(1)} %collective-permute-done.2.mine_ref), channel_id=1, source_target_pairs={{0,8},{8,0},{16,24},{24,16},{1,9},{9,1},{17,25},{25,17},{2,10},{10... | collective-permute-start | bytes 589832 | tf_op jit(solution)/shard_map/ppermute | solution.py:516
  14.6 3.4 %copy-done = bf16[1024,4096]{1,0:T(8,128)(2,1)S(1)} copy-done((bf16[1024,4096]{1,0:T(8,128)(2,1)S(1)}, bf16[1024,4096]{1,0:T(8,128)(2,1)}, u32[]{:S(2)}) %copy-start) | copy-done | bytes 8388632
  18.0 0.8 stage.1
  18.8 0.4 collective-permute-done.3.other_ref
  19.2 0.6 join_rows.1.refs_3_
  19.8 1.1 collective-permute-done.refs_1_
  20.8 0.3 collective-permute-done.1.refs_2_
  21.1 1.7 %project_mix.3 = bf16[1,2,768,256]{3,2,1,0:T(8,128)(2,1)S(1)} custom-call(s32[11]{0:T(128)S(1)} %stack.59.order, bf16[192,1024]{1,0:T(8,128)(2,1)S(1)} %get-tuple-element.81.refs_0_, bf16[192,1024]{1,0:T(8,128)(2,1)S(1)} %collective-permute-done.refs_1_, bf16[192,1024]{1,0:T(8,128)(2,1)S(1)} %collective-permute-done.1.refs_2_, ...), custom_call_target="tpu_custom_call" | custom-call | tf_op jit(solution)/shard_map/project_mix/pallas_call | solution.py:101
  22.9 1.6 %collective-permute-start.5 = (bf16[1,2,768,256]{3,2,1,0:T(8,128)(2,1)S(1)}, bf16[1,2,768,256]{3,2,1,0:T(8,128)(2,1)S(1)}, u32[]{:S(2)}, u32[]{:S(2)}) collective-permute-start(bf16[1,2,768,256]{3,2,1,0:T(8,128)(2,1)S(1)} %project_mix.3), channel_id=1, source_target_pairs={{0,2},{1,5},{2,0},{3,7},{4,6},{5,1},{6,4},{7,3},{8,10},{9,13},{10,... | collective-permute-start | bytes 2359304 | tf_op jit(solution)/shard_map/ppermute | solution.py:521
  24.4 1.7 %project_mix.4 = bf16[1,2,768,256]{3,2,1,0:T(8,128)(2,1)S(1)} custom-call(s32[11]{0:T(128)S(1)} %stack.59.order, bf16[192,1024]{1,0:T(8,128)(2,1)S(1)} %get-tuple-element.81.refs_0_, bf16[192,1024]{1,0:T(8,128)(2,1)S(1)} %collective-permute-done.refs_1_, bf16[192,1024]{1,0:T(8,128)(2,1)S(1)} %collective-permute-done.1.refs_2_, ...), custom_call_target="tpu_custom_call" | custom-call | tf_op jit(solution)/shard_map/project_mix/pallas_call | solution.py:101
  26.1 0.6 collective-permute-start.7
  26.7 2.6 %project_mix.5.rest_ref = f32[2,2,768,256]{3,2,1,0:T(8,128)S(1)} custom-call(s32[11]{0:T(128)S(1)} %stack.59.order, bf16[192,1024]{1,0:T(8,128)(2,1)S(1)} %get-tuple-element.81.refs_0_, bf16[192,1024]{1,0:T(8,128)(2,1)S(1)} %collective-permute-done.refs_1_, bf16[192,1024]{1,0:T(8,128)(2,1)S(1)} %collective-permute-done.1.refs_2_, ...), custom_call_target="tpu_custom_call" | custom-call | tf_op jit(solution)/shard_map/project_mix/pallas_call | solution.py:101
  29.3 0.0 copy-start.3
  29.3 5.6 %collective-permute-done.5.both_ref = bf16[1,2,768,256]{3,2,1,0:T(8,128)(2,1)S(1)} collective-permute-done((bf16[1,2,768,256]{3,2,1,0:T(8,128)(2,1)S(1)}, bf16[1,2,768,256]{3,2,1,0:T(8,128)(2,1)S(1)}, u32[]{:S(2)}, u32[]{:S(2)}) %collective-permute-start.5) | collective-permute-done | bytes 786464 | tf_op jit(solution)/shard_map/ppermute | solution.py:521
  34.9 0.7 second_share.1
  35.6 1.5 %collective-permute-start.8 = (bf16[1,2,768,256]{3,2,1,0:T(8,128)(2,1)S(1)}, bf16[1,2,768,256]{3,2,1,0:T(8,128)(2,1)S(1)}, u32[]{:S(2)}, u32[]{:S(2)}) collective-permute-start(bf16[1,2,768,256]{3,2,1,0:T(8,128)(2,1)S(1)} %second_share.1), channel_id=1, source_target_pairs={{0,4},{1,3},{2,6},{3,1},{4,0},{5,7},{6,2},{7,5},{8,12},{9,11},{10,... | collective-permute-start | bytes 2359304 | tf_op jit(solution)/shard_map/ppermute | solution.py:528
  37.1 0.5 last_rows.1
  37.7 0.1 collective-permute-start.6
  37.7 1.3 %collective-permute-done.6.refs_4_ = bf16[4,16,1024]{2,1,0:T(8,128)(2,1)S(1)} collective-permute-done((bf16[4,16,1024]{2,1,0:T(8,128)(2,1)S(1)}, bf16[4,16,1024]{2,1,0:T(8,128)(2,1)S(1)}, u32[]{:S(2)}, u32[]{:S(2)}) %collective-permute-start.6) | collective-permute-done | bytes 131104 | tf_op jit(solution)/shard_map/ppermute | solution.py:531
  39.1 3.0 %project_query.1 = (f32[192,1024]{1,0:T(8,128)S(1)}, f32[192,1024]{1,0:T(8,128)S(1)}, bf16[192,1024]{1,0:T(8,128)(2,1)S(1)}, bf16[192,1024]{1,0:T(8,128)(2,1)S(1)}) custom-call(s32[11]{0:T(128)S(1)} %stack.59.order, bf16[192,1024]{1,0:T(8,128)(2,1)S(1)} %get-tuple-element.81.refs_0_, bf16[192,1024]{1,0:T(8,128)(2,1)S(1)} %collective-permute-done.refs_1_, ...), custom_call_target="tpu_custom_call" | custom-call | tf_op jit(solution)/shard_map/project_query/pallas_call | solution.py:101
  42.0 0.0 copy-start.4
  42.1 0.0 copy-start.5
  42.1 7.3 %collective-permute-done.7.first_ref = bf16[1,2,768,256]{3,2,1,0:T(8,128)(2,1)S(1)} collective-permute-done((bf16[1,2,768,256]{3,2,1,0:T(8,128)(2,1)S(1)}, bf16[1,2,768,256]{3,2,1,0:T(8,128)(2,1)S(1)}, u32[]{:S(2)}, u32[]{:S(2)}) %collective-permute-start.7) | collective-permute-done | bytes 786464 | tf_op jit(solution)/shard_map/ppermute | solution.py:524
  49.4 1.2 %collective-permute-done.8.second_ref = bf16[1,2,768,256]{3,2,1,0:T(8,128)(2,1)S(1)} collective-permute-done((bf16[1,2,768,256]{3,2,1,0:T(8,128)(2,1)S(1)}, bf16[1,2,768,256]{3,2,1,0:T(8,128)(2,1)S(1)}, u32[]{:S(2)}, u32[]{:S(2)}) %collective-permute-start.8) | collective-permute-done | bytes 786464 | tf_op jit(solution)/shard_map/ppermute | solution.py:528
  50.6 0.8 own_share.1
  51.4 1.1 collective-permute-start.10
  52.4 1.5 %collective-permute-start.11 = (bf16[192,1024]{1,0:T(8,128)(2,1)S(1)}, bf16[192,1024]{1,0:T(8,128)(2,1)S(1)}, u32[]{:S(2)}, u32[]{:S(2)}) collective-permute-start(bf16[192,1024]{1,0:T(8,128)(2,1)S(1)} %get-tuple-element.98), channel_id=1, source_target_pairs={{0,2},{1,5},{2,0},{3,7},{4,6},{5,1},{6,4},{7,3},{8,10},{9,13},{10,... | collective-permute-start | bytes 1179656 | tf_op jit(solution)/shard_map/ppermute | solution.py:538
  53.9 0.5 collective-permute-start.9
  54.5 3.4 %hyena.1 = (bf16[4,192,128]{2,1,0:T(8,128)(2,1)S(1)}, bf16[4,192,128]{2,1,0:T(8,128)(2,1)S(1)}) custom-call(s32[11]{0:T(128)S(1)} %stack.59.order, f32[768,256]{1,0:T(8,128)S(1)} %get-tuple-element.93.own_ref, bf16[768,256]{1,0:T(8,128)(2,1)S(1)} %collective-permute-done.10.swap_ref, f32[3,3,1024]{2,1,0:T(4,128)S(1)} %copy-done.3, f32[8,1024]{1,0:T(8,128)S(1)} %copy-done.4, ...), custom_call_target="tpu_custom_call" | custom-call | tf_op jit(solution)/shard_map/hyena/pallas_call | solution.py:101
  57.9 2.3 %collective-permute-done.11.in_ref = bf16[192,1024]{1,0:T(8,128)(2,1)S(1)} collective-permute-done((bf16[192,1024]{1,0:T(8,128)(2,1)S(1)}, bf16[192,1024]{1,0:T(8,128)(2,1)S(1)}, u32[]{:S(2)}, u32[]{:S(2)}) %collective-permute-start.11) | collective-permute-done | bytes 393248 | tf_op jit(solution)/shard_map/ppermute | solution.py:538
  60.2 0.6 query_second.1
  60.8 1.5 %collective-permute-start.12 = (bf16[192,1024]{1,0:T(8,128)(2,1)S(1)}, bf16[192,1024]{1,0:T(8,128)(2,1)S(1)}, u32[]{:S(2)}, u32[]{:S(2)}) collective-permute-start(bf16[192,1024]{1,0:T(8,128)(2,1)S(1)} %query_second.1), channel_id=1, source_target_pairs={{0,4},{1,3},{2,6},{3,1},{4,0},{5,7},{6,2},{7,5},{8,12},{9,11},{10,... | collective-permute-start | bytes 1179656 | tf_op jit(solution)/shard_map/ppermute | solution.py:544
  62.3 1.4 %collective-permute-done.13.other_ref = bf16[4,192,128]{2,1,0:T(8,128)(2,1)S(1)} collective-permute-done((bf16[4,192,128]{2,1,0:T(8,128)(2,1)S(1)}, bf16[4,192,128]{2,1,0:T(8,128)(2,1)S(1)}, u32[]{:S(2)}, u32[]{:S(2)}) %collective-permute-start.13) | collective-permute-done | bytes 196640 | tf_op jit(solution)/shard_map/ppermute | solution.py:543
  63.8 0.6 pair_up.1
  64.4 0.7 collective-permute-start.14
  65.0 1.5 %collective-permute-start.15 = (bf16[2,192,128]{2,1,0:T(8,128)(2,1)S(1)}, bf16[2,192,128]{2,1,0:T(8,128)(2,1)S(1)}, u32[]{:S(2)}, u32[]{:S(2)}) collective-permute-start(bf16[2,192,128]{2,1,0:T(8,128)(2,1)S(1)} %get-tuple-element.103), channel_id=1, source_target_pairs={{0,2},{1,5},{2,0},{3,7},{4,6},{5,1},{6,4},{7,3},{8,10},{9,13},{10,... | collective-permute-start | bytes 294920 | tf_op jit(solution)/shard_map/ppermute | solution.py:545
  66.5 1.4 %collective-permute-start.16 = (bf16[2,192,128]{2,1,0:T(8,128)(2,1)S(1)}, bf16[2,192,128]{2,1,0:T(8,128)(2,1)S(1)}, u32[]{:S(2)}, u32[]{:S(2)}) collective-permute-start(bf16[2,192,128]{2,1,0:T(8,128)(2,1)S(1)} %get-tuple-element.104), channel_id=1, source_target_pairs={{0,6},{1,7},{2,4},{3,5},{4,2},{5,3},{6,0},{7,1},{8,14},{9,15},{10,... | collective-permute-start | bytes 294920 | tf_op jit(solution)/shard_map/ppermute | solution.py:545
  67.9 2.9 %collective-permute-done.14.refs_4_ = bf16[2,192,128]{2,1,0:T(8,128)(2,1)S(1)} collective-permute-done((bf16[2,192,128]{2,1,0:T(8,128)(2,1)S(1)}, bf16[2,192,128]{2,1,0:T(8,128)(2,1)S(1)}, u32[]{:S(2)}, u32[]{:S(2)}) %collective-permute-start.14) | collective-permute-done | bytes 98336 | tf_op jit(solution)/shard_map/ppermute | solution.py:545
  70.8 2.9 %collective-permute-done.16.refs_6_ = bf16[2,192,128]{2,1,0:T(8,128)(2,1)S(1)} collective-permute-done((bf16[2,192,128]{2,1,0:T(8,128)(2,1)S(1)}, bf16[2,192,128]{2,1,0:T(8,128)(2,1)S(1)}, u32[]{:S(2)}, u32[]{:S(2)}) %collective-permute-start.16) | collective-permute-done | bytes 98336 | tf_op jit(solution)/shard_map/ppermute | solution.py:545
  73.7 1.8 %gate.1 = (bf16[192,1024]{1,0:T(8,128)(2,1)S(1)}, bf16[192,1024]{1,0:T(8,128)(2,1)S(1)}, bf16[192,1024]{1,0:T(8,128)(2,1)S(1)}) custom-call(s32[16]{0:T(128)S(1)} %concatenate.4.scalars, f32[192,1024]{1,0:T(8,128)S(1)} %get-tuple-element.86.refs_0_, bf16[192,1024]{1,0:T(8,128)(2,1)S(1)} %collective-permute-done.9.refs_1_, ...), custom_call_target="tpu_custom_call" | custom-call | tf_op jit(solution)/shard_map/gate/pallas_call | solution.py:101
  75.6 1.6 %collective-permute-start.17 = (bf16[192,1024]{1,0:T(8,128)(2,1)S(1)}, bf16[192,1024]{1,0:T(8,128)(2,1)S(1)}, u32[]{:S(2)}, u32[]{:S(2)}) collective-permute-start(bf16[192,1024]{1,0:T(8,128)(2,1)S(1)} %get-tuple-element.107), channel_id=1, source_target_pairs={{0,8},{8,0},{16,24},{24,16},{1,9},{9,1},{17,25},{25,17},{2,10},{10... | collective-permute-start | bytes 1179656 | tf_op jit(solution)/shard_map/ppermute | solution.py:457
  77.2 0.7 collective-permute-start.18
  77.9 1.1 %out_columns.3.far_ref = bf16[192,1024]{1,0:T(8,128)(2,1)S(1)} custom-call(s32[5]{0:T(128)S(1)} %stack.65.picks, bf16[192,1024]{1,0:T(8,128)(2,1)S(1)} %get-tuple-element.106.x_ref, bf16[1024,4096]{1,0:T(8,128)(2,1)S(1)} %get-tuple-element.105.refs_7_.w_ref), custom_call_target="tpu_custom_call" | custom-call | tf_op jit(solution)/shard_map/out_columns/pallas_call | solution.py:101
  79.0 6.3 %collective-permute-start.20 = (bf16[192,1024]{1,0:T(8,128)(2,1)S(1)}, bf16[192,1024]{1,0:T(8,128)(2,1)S(1)}, u32[]{:S(2)}, u32[]{:S(2)}) collective-permute-start(bf16[192,1024]{1,0:T(8,128)(2,1)S(1)} %get-tuple-element.110), channel_id=1, source_target_pairs={{0,8},{24,16},{1,9},{25,17},{2,10},{26,18},{3,11},{27,19},{4,12},{... | collective-permute-start | bytes 1179656 | tf_op jit(solution)/shard_map/ppermute | solution.py:462
  85.4 1.3 %collective-permute-start.19 = (bf16[192,1024]{1,0:T(8,128)(2,1)S(1)}, bf16[192,1024]{1,0:T(8,128)(2,1)S(1)}, u32[]{:S(2)}, u32[]{:S(2)}) collective-permute-start(bf16[192,1024]{1,0:T(8,128)(2,1)S(1)} %out_columns.3.far_ref), channel_id=1, source_target_pairs={{0,16},{24,8},{1,17},{25,9},{2,18},{26,10},{3,19},{27,11},{4,20},{... | collective-permute-start | bytes 1179656 | tf_op jit(solution)/shard_map/ppermute | solution.py:461
  86.7 0.1 collective-permute-done.17.pair_ref
  86.8 0.6 both.1
  87.4 1.3 %collective-permute-start.21 = (bf16[192,1024]{1,0:T(8,128)(2,1)S(1)}, bf16[192,1024]{1,0:T(8,128)(2,1)S(1)}, u32[]{:S(2)}, u32[]{:S(2)}) collective-permute-start(bf16[192,1024]{1,0:T(8,128)(2,1)S(1)} %both.1), channel_id=1, source_target_pairs={{8,24},{16,0},{9,25},{17,1},{10,26},{18,2},{11,27},{19,3},{12,28},... | collective-permute-start | bytes 1179656 | tf_op jit(solution)/shard_map/ppermute | solution.py:469
  88.7 1.1 %out_columns.2.own_ref = f32[192,1024]{1,0:T(8,128)S(1)} custom-call(s32[5]{0:T(128)S(1)} %stack.65.picks, bf16[192,1024]{1,0:T(8,128)(2,1)S(1)} %get-tuple-element.106.x_ref, bf16[1024,4096]{1,0:T(8,128)(2,1)S(1)} %get-tuple-element.105.refs_7_.w_ref), custom_call_target="tpu_custom_call" | custom-call | tf_op jit(solution)/shard_map/out_columns/pallas_call | solution.py:101
  89.9 5.3 %collective-permute-done.20.refs_2_ = bf16[192,1024]{1,0:T(8,128)(2,1)S(1)} collective-permute-done((bf16[192,1024]{1,0:T(8,128)(2,1)S(1)}, bf16[192,1024]{1,0:T(8,128)(2,1)S(1)}, u32[]{:S(2)}, u32[]{:S(2)}) %collective-permute-start.20) | collective-permute-done | bytes 393248 | tf_op jit(solution)/shard_map/ppermute | solution.py:462
  95.1 7.6 %collective-permute-done.19.refs_1_ = bf16[192,1024]{1,0:T(8,128)(2,1)S(1)} collective-permute-done((bf16[192,1024]{1,0:T(8,128)(2,1)S(1)}, bf16[192,1024]{1,0:T(8,128)(2,1)S(1)}, u32[]{:S(2)}, u32[]{:S(2)}) %collective-permute-start.19) | collective-permute-done | bytes 393248 | tf_op jit(solution)/shard_map/ppermute | solution.py:461
  102.8 6.2 %collective-permute-done.21.refs_3_ = bf16[192,1024]{1,0:T(8,128)(2,1)S(1)} collective-permute-done((bf16[192,1024]{1,0:T(8,128)(2,1)S(1)}, bf16[192,1024]{1,0:T(8,128)(2,1)S(1)}, u32[]{:S(2)}, u32[]{:S(2)}) %collective-permute-start.21) | collective-permute-done | bytes 393248 | tf_op jit(solution)/shard_map/ppermute | solution.py:469
  108.9 1.6 %total.1 = bf16[192,1024]{1,0:T(8,128)(2,1)} custom-call(s32[5]{0:T(128)S(1)} %stack.65.picks, f32[192,1024]{1,0:T(8,128)S(1)} %out_columns.2.own_ref, bf16[192,1024]{1,0:T(8,128)(2,1)S(1)} %collective-permute-done.17.pair_ref, bf16[192,1024]{1,0:T(8,128)(2,1)S(1)} %collective-permute-done.18.refs_0_, bf16[192,1024]{1,0:T(8,128)(2,1)S(1)} %collective-permute-done.19.refs_1_, ...), custom_call_target="tpu_custom_call" | custom-call | tf_op jit(solution)/shard_map/total/pallas_call | solution.py:101
  (14 shorter events, 0.0 us)
Async XLA Ops:
  0.0 21.1 %collective-permute-start.4 = (bf16[3,512,1024]{2,1,0:T(8,128)(2,1)}, bf16[3,512,1024]{2,1,0:T(8,128)(2,1)S(1)}, u32[]{:S(2)}, u32[]{:S(2)}) collective-permute-start(bf16[3,512,1024]{2,1,0:T(8,128)(2,1)} %bitcast.15), channel_id=1, source_target_pairs={{0,1},{1,0},{2,3},{3,2},{4,5},{5,4},{6,7},{7,6},{8,9},{9,8},{10,11... | collective-permute-start | bytes 9437192 | tf_op jit(solution)/shard_map/ppermute | solution.py:511
  0.7 1.4 %copy-start.1 = (bf16[192,4096]{1,0:T(8,128)(2,1)S(1)}, bf16[192,4096]{1,0:T(8,128)(2,1)}, u32[]{:S(2)}) copy-start(bf16[192,4096]{1,0:T(8,128)(2,1)} %tokens_ref.2) | copy-start | bytes 4718596
  2.1 12.5 %copy-start.2 = (bf16[512,3,1024]{2,0,1:T(8,128)(2,1)S(1)}, bf16[512,3,1024]{2,0,1:T(8,128)(2,1)}, u32[]{:S(2)}) copy-start(bf16[512,3,1024]{2,0,1:T(8,128)(2,1)} %param.7) | copy-start | bytes 9437188
  3.3 9.3 %collective-permute-start.2 = (bf16[96,1024]{1,0:T(8,128)(2,1)S(1)}, bf16[96,1024]{1,0:T(8,128)(2,1)S(1)}, u32[]{:S(2)}, u32[]{:S(2)}) collective-permute-start(bf16[96,1024]{1,0:T(8,128)(2,1)S(1)} %cut_part.1), channel_id=1, source_target_pairs={{0,6},{1,7},{2,4},{3,5},{4,2},{5,3},{6,0},{7,1},{8,14},{9,15},{10,... | collective-permute-start | bytes 589832 | tf_op jit(solution)/shard_map/ppermute | solution.py:515
  6.8 14.0 %collective-permute-start = (bf16[192,1024]{1,0:T(8,128)(2,1)S(1)}, bf16[192,1024]{1,0:T(8,128)(2,1)S(1)}, u32[]{:S(2)}, u32[]{:S(2)}) collective-permute-start(bf16[192,1024]{1,0:T(8,128)(2,1)S(1)} %get-tuple-element.67), channel_id=1, source_target_pairs={{0,4},{1,3},{2,6},{3,1},{4,0},{5,7},{6,2},{7,5},{8,12},{9,11},{10,... | collective-permute-start | bytes 1179656 | tf_op jit(solution)/shard_map/ppermute | solution.py:517
  7.4 13.8 %collective-permute-start.1 = (bf16[192,1024]{1,0:T(8,128)(2,1)S(1)}, bf16[192,1024]{1,0:T(8,128)(2,1)S(1)}, u32[]{:S(2)}, u32[]{:S(2)}) collective-permute-start(bf16[192,1024]{1,0:T(8,128)(2,1)S(1)} %get-tuple-element.68), channel_id=1, source_target_pairs={{0,2},{1,5},{2,0},{3,7},{4,6},{5,1},{6,4},{7,3},{8,10},{9,13},{10,... | collective-permute-start | bytes 1179656 | tf_op jit(solution)/shard_map/ppermute | solution.py:517
  12.6 6.6 %collective-permute-start.3 = (bf16[96,1024]{1,0:T(8,128)(2,1)S(1)}, bf16[96,1024]{1,0:T(8,128)(2,1)S(1)}, u32[]{:S(2)}, u32[]{:S(2)}) collective-permute-start(bf16[96,1024]{1,0:T(8,128)(2,1)S(1)} %collective-permute-done.2.mine_ref), channel_id=1, source_target_pairs={{0,8},{8,0},{16,24},{24,16},{1,9},{9,1},{17,25},{25,17},{2,10},{10... | collective-permute-start | bytes 589832 | tf_op jit(solution)/shard_map/ppermute | solution.py:516
  14.6 3.4 %copy-start = (bf16[1024,4096]{1,0:T(8,128)(2,1)S(1)}, bf16[1024,4096]{1,0:T(8,128)(2,1)}, u32[]{:S(2)}) copy-start(bf16[1024,4096]{1,0:T(8,128)(2,1)} %refs_1_) | copy-start | bytes 25165828
  22.9 12.1 %collective-permute-start.5 = (bf16[1,2,768,256]{3,2,1,0:T(8,128)(2,1)S(1)}, bf16[1,2,768,256]{3,2,1,0:T(8,128)(2,1)S(1)}, u32[]{:S(2)}, u32[]{:S(2)}) collective-permute-start(bf16[1,2,768,256]{3,2,1,0:T(8,128)(2,1)S(1)} %project_mix.3), channel_id=1, source_target_pairs={{0,2},{1,5},{2,0},{3,7},{4,6},{5,1},{6,4},{7,3},{8,10},{9,13},{10,... | collective-permute-start | bytes 2359304 | tf_op jit(solution)/shard_map/ppermute | solution.py:521
  26.1 23.3 %collective-permute-start.7 = (bf16[1,2,768,256]{3,2,1,0:T(8,128)(2,1)S(1)}, bf16[1,2,768,256]{3,2,1,0:T(8,128)(2,1)S(1)}, u32[]{:S(2)}, u32[]{:S(2)}) collective-permute-start(bf16[1,2,768,256]{3,2,1,0:T(8,128)(2,1)S(1)} %project_mix.4), channel_id=1, source_target_pairs={{0,2},{1,5},{2,0},{3,7},{4,6},{5,1},{6,4},{7,3},{8,10},{9,13},{10,... | collective-permute-start | bytes 2359304 | tf_op jit(solution)/shard_map/ppermute | solution.py:524
  29.3 9.8 %copy-start.3 = (f32[3,3,1024]{2,1,0:T(4,128)S(1)}, f32[3,3,1024]{2,1,0:T(4,128)}, u32[]{:S(2)}) copy-start(f32[3,3,1024]{2,1,0:T(4,128)} %filt_ref.1) | copy-start | bytes 110596
  35.6 15.0 %collective-permute-start.8 = (bf16[1,2,768,256]{3,2,1,0:T(8,128)(2,1)S(1)}, bf16[1,2,768,256]{3,2,1,0:T(8,128)(2,1)S(1)}, u32[]{:S(2)}, u32[]{:S(2)}) collective-permute-start(bf16[1,2,768,256]{3,2,1,0:T(8,128)(2,1)S(1)} %second_share.1), channel_id=1, source_target_pairs={{0,4},{1,3},{2,6},{3,1},{4,0},{5,7},{6,2},{7,5},{8,12},{9,11},{10,... | collective-permute-start | bytes 2359304 | tf_op jit(solution)/shard_map/ppermute | solution.py:528
  37.7 1.4 %collective-permute-start.6 = (bf16[4,16,1024]{2,1,0:T(8,128)(2,1)S(1)}, bf16[4,16,1024]{2,1,0:T(8,128)(2,1)S(1)}, u32[]{:S(2)}, u32[]{:S(2)}) collective-permute-start(bf16[4,16,1024]{2,1,0:T(8,128)(2,1)S(1)} %last_rows.1), channel_id=1, source_target_pairs={{0,1},{1,0},{2,3},{3,2},{4,5},{5,4},{6,7},{7,6},{8,9},{9,8},{10,11... | collective-permute-start | bytes 393224 | tf_op jit(solution)/shard_map/ppermute | solution.py:531
  42.0 12.4 %copy-start.4 = (f32[8,1024]{1,0:T(8,128)S(1)}, f32[8,1024]{1,0:T(8,128)}, u32[]{:S(2)}) copy-start(f32[8,1024]{1,0:T(8,128)} %decay_ref.1) | copy-start | bytes 98308
  42.1 12.4 %copy-start.5 = (f32[8,1024]{1,0:T(8,128)S(1)}, f32[8,1024]{1,0:T(8,128)}, u32[]{:S(2)}) copy-start(f32[8,1024]{1,0:T(8,128)} %residue_ref.1) | copy-start | bytes 98308
  51.4 3.1 %collective-permute-start.10 = (bf16[768,256]{1,0:T(8,128)(2,1)S(1)}, bf16[768,256]{1,0:T(8,128)(2,1)S(1)}, u32[]{:S(2)}, u32[]{:S(2)}) collective-permute-start(bf16[768,256]{1,0:T(8,128)(2,1)S(1)} %get-tuple-element.94), channel_id=1, source_target_pairs={{0,1},{1,0},{2,3},{3,2},{4,5},{5,4},{6,7},{7,6},{8,9},{9,8},{10,11... | collective-permute-start | bytes 1179656 | tf_op jit(solution)/shard_map/ppermute | solution.py:536
  52.4 7.8 %collective-permute-start.11 = (bf16[192,1024]{1,0:T(8,128)(2,1)S(1)}, bf16[192,1024]{1,0:T(8,128)(2,1)S(1)}, u32[]{:S(2)}, u32[]{:S(2)}) collective-permute-start(bf16[192,1024]{1,0:T(8,128)(2,1)S(1)} %get-tuple-element.98), channel_id=1, source_target_pairs={{0,2},{1,5},{2,0},{3,7},{4,6},{5,1},{6,4},{7,3},{8,10},{9,13},{10,... | collective-permute-start | bytes 1179656 | tf_op jit(solution)/shard_map/ppermute | solution.py:538
  53.9 14.0 %collective-permute-start.9 = (bf16[192,1024]{1,0:T(8,128)(2,1)S(1)}, bf16[192,1024]{1,0:T(8,128)(2,1)S(1)}, u32[]{:S(2)}, u32[]{:S(2)}) collective-permute-start(bf16[192,1024]{1,0:T(8,128)(2,1)S(1)} %get-tuple-element.91), channel_id=1, source_target_pairs={{0,2},{1,5},{2,0},{3,7},{4,6},{5,1},{6,4},{7,3},{8,10},{9,13},{10,... | collective-permute-start | bytes 1179656 | tf_op jit(solution)/shard_map/ppermute | solution.py:539
  60.8 12.9 %collective-permute-start.12 = (bf16[192,1024]{1,0:T(8,128)(2,1)S(1)}, bf16[192,1024]{1,0:T(8,128)(2,1)S(1)}, u32[]{:S(2)}, u32[]{:S(2)}) collective-permute-start(bf16[192,1024]{1,0:T(8,128)(2,1)S(1)} %query_second.1), channel_id=1, source_target_pairs={{0,4},{1,3},{2,6},{3,1},{4,0},{5,7},{6,2},{7,5},{8,12},{9,11},{10,... | collective-permute-start | bytes 1179656 | tf_op jit(solution)/shard_map/ppermute | solution.py:544
  62.3 1.4 %collective-permute-start.13 = (bf16[4,192,128]{2,1,0:T(8,128)(2,1)S(1)}, bf16[4,192,128]{2,1,0:T(8,128)(2,1)S(1)}, u32[]{:S(2)}, u32[]{:S(2)}) collective-permute-start(bf16[4,192,128]{2,1,0:T(8,128)(2,1)S(1)} %get-tuple-element.100), channel_id=1, source_target_pairs={{0,1},{1,0},{2,3},{3,2},{4,5},{5,4},{6,7},{7,6},{8,9},{9,8},{10,11... | collective-permute-start | bytes 589832 | tf_op jit(solution)/shard_map/ppermute | solution.py:543
  64.4 6.4 %collective-permute-start.14 = (bf16[2,192,128]{2,1,0:T(8,128)(2,1)S(1)}, bf16[2,192,128]{2,1,0:T(8,128)(2,1)S(1)}, u32[]{:S(2)}, u32[]{:S(2)}) collective-permute-start(bf16[2,192,128]{2,1,0:T(8,128)(2,1)S(1)} %get-tuple-element.102), channel_id=1, source_target_pairs={{0,4},{1,3},{2,6},{3,1},{4,0},{5,7},{6,2},{7,5},{8,12},{9,11},{10,... | collective-permute-start | bytes 294920 | tf_op jit(solution)/shard_map/ppermute | solution.py:545
  65.0 5.8 %collective-permute-start.15 = (bf16[2,192,128]{2,1,0:T(8,128)(2,1)S(1)}, bf16[2,192,128]{2,1,0:T(8,128)(2,1)S(1)}, u32[]{:S(2)}, u32[]{:S(2)}) collective-permute-start(bf16[2,192,128]{2,1,0:T(8,128)(2,1)S(1)} %get-tuple-element.103), channel_id=1, source_target_pairs={{0,2},{1,5},{2,0},{3,7},{4,6},{5,1},{6,4},{7,3},{8,10},{9,13},{10,... | collective-permute-start | bytes 294920 | tf_op jit(solution)/shard_map/ppermute | solution.py:545
  66.5 7.2 %collective-permute-start.16 = (bf16[2,192,128]{2,1,0:T(8,128)(2,1)S(1)}, bf16[2,192,128]{2,1,0:T(8,128)(2,1)S(1)}, u32[]{:S(2)}, u32[]{:S(2)}) collective-permute-start(bf16[2,192,128]{2,1,0:T(8,128)(2,1)S(1)} %get-tuple-element.104), channel_id=1, source_target_pairs={{0,6},{1,7},{2,4},{3,5},{4,2},{5,3},{6,0},{7,1},{8,14},{9,15},{10,... | collective-permute-start | bytes 294920 | tf_op jit(solution)/shard_map/ppermute | solution.py:545
  75.6 11.2 %collective-permute-start.17 = (bf16[192,1024]{1,0:T(8,128)(2,1)S(1)}, bf16[192,1024]{1,0:T(8,128)(2,1)S(1)}, u32[]{:S(2)}, u32[]{:S(2)}) collective-permute-start(bf16[192,1024]{1,0:T(8,128)(2,1)S(1)} %get-tuple-element.107), channel_id=1, source_target_pairs={{0,8},{8,0},{16,24},{24,16},{1,9},{9,1},{17,25},{25,17},{2,10},{10... | collective-permute-start | bytes 1179656 | tf_op jit(solution)/shard_map/ppermute | solution.py:457
  77.2 25.5 %collective-permute-start.18 = (bf16[192,1024]{1,0:T(8,128)(2,1)S(1)}, bf16[192,1024]{1,0:T(8,128)(2,1)S(1)}, u32[]{:S(2)}, u32[]{:S(2)}) collective-permute-start(bf16[192,1024]{1,0:T(8,128)(2,1)S(1)} %get-tuple-element.110), channel_id=1, source_target_pairs={{8,16},{16,8},{9,17},{17,9},{10,18},{18,10},{11,19},{19,11},{12,20... | collective-permute-start | bytes 1179656 | tf_op jit(solution)/shard_map/ppermute | solution.py:459
  79.0 16.1 %collective-permute-start.20 = (bf16[192,1024]{1,0:T(8,128)(2,1)S(1)}, bf16[192,1024]{1,0:T(8,128)(2,1)S(1)}, u32[]{:S(2)}, u32[]{:S(2)}) collective-permute-start(bf16[192,1024]{1,0:T(8,128)(2,1)S(1)} %get-tuple-element.110), channel_id=1, source_target_pairs={{0,8},{24,16},{1,9},{25,17},{2,10},{26,18},{3,11},{27,19},{4,12},{... | collective-permute-start | bytes 1179656 | tf_op jit(solution)/shard_map/ppermute | solution.py:462
  85.4 17.4 %collective-permute-start.19 = (bf16[192,1024]{1,0:T(8,128)(2,1)S(1)}, bf16[192,1024]{1,0:T(8,128)(2,1)S(1)}, u32[]{:S(2)}, u32[]{:S(2)}) collective-permute-start(bf16[192,1024]{1,0:T(8,128)(2,1)S(1)} %out_columns.3.far_ref), channel_id=1, source_target_pairs={{0,16},{24,8},{1,17},{25,9},{2,18},{26,10},{3,19},{27,11},{4,20},{... | collective-permute-start | bytes 1179656 | tf_op jit(solution)/shard_map/ppermute | solution.py:461
  87.4 21.5 %collective-permute-start.21 = (bf16[192,1024]{1,0:T(8,128)(2,1)S(1)}, bf16[192,1024]{1,0:T(8,128)(2,1)S(1)}, u32[]{:S(2)}, u32[]{:S(2)}) collective-permute-start(bf16[192,1024]{1,0:T(8,128)(2,1)S(1)} %both.1), channel_id=1, source_target_pairs={{8,24},{16,0},{9,25},{17,1},{10,26},{18,2},{11,27},{19,3},{12,28},... | collective-permute-start | bytes 1179656 | tf_op jit(solution)/shard_map/ppermute | solution.py:469

commit v4 on v3

--- a/solution.py
+++ b/solution.py
@@ -116,18 +116,14 @@
 def cut(order, tokens, pieces):
     high, wide = tokens.shape[0], tokens.shape[1] // pieces
 
-    def part(order, tokens_ref, out_ref):
+    def kernel(order, tokens_ref, *out_refs):
         here = columns(order[2 * pieces + 2], high // 2)
-        out_ref[...] = tokens_ref[here, columns(order[pieces - 1], wide)]
-
-    def rest(order, tokens_ref, *out_refs):
-        for s, out_ref in enumerate(out_refs):
+        out_refs[pieces - 1][...] = tokens_ref[here, columns(order[pieces - 1], wide)]
+        for s, out_ref in enumerate(out_refs[: pieces - 1]):
             out_ref[...] = tokens_ref[:, columns(order[s], wide)]
 
-    last = local(part, "cut_part", [((high // 2, wide), tokens.dtype)], order, [tokens])
-    last, tokens = lax.optimization_barrier((last, tokens))
-    shapes = [((high, wide), tokens.dtype)] * (pieces - 1)
-    return [*local(rest, "cut", shapes, order, [tokens]), last]
+    shapes = [((high, wide), tokens.dtype)] * (pieces - 1) + [((high // 2, wide), tokens.dtype)]
+    return local(kernel, "cut", shapes, order, [tokens])
 
 
 def join_rows(order, mine, other):
@@ -216,6 +212,7 @@
     step = some + high
     taps = short_filter.shape[0]
     tile = min(chans, 256)
+    extra = tile if chans > tile else 0
 
     def kernel(order, *refs):
         x_refs = refs[:chips]
@@ -239,9 +236,17 @@
                 value = filt_ref[0, 0:1, at] * total[first : first + high, :]
                 for j in range(1, taps):
                     value = value + filt_ref[j, 0:1, at] * total[first - j : first - j + high, :]
-                out_refs[i][:, at] = value.astype(out_refs[i].dtype)
-
-    shapes = [((high, chans), F32 if i < 2 else BF16) for i in range(chips)]
+                if i < 2:
+                    out_refs[i][:, at] = value
+                elif i == 3:
+                    out_refs[3][:, at] = value.astype(BF16)
+                elif at.start < extra:
+                    out_refs[3][:, chans + at.start : chans + at.stop] = value.astype(BF16)
+                else:
+                    out_refs[2][:, at.start - extra : at.stop - extra] = value.astype(BF16)
+
+    shapes = [((high, chans), F32)] * 2
+    shapes += [((high, chans - extra), BF16), ((high, chans + extra), BF16)]
     scratch = [
         pltpu.VMEM((2, chips * step, depth), BF16),
         pltpu.VMEM((chips + 1, some, 2 * depth), BF16),
@@ -252,37 +257,37 @@
 
 
 def second_share(order, rest, both_in, chips):
-    shape = (1,) + rest.shape[1:]
-    high = rest.shape[2] // chips
-
-    def kernel(order, rest_ref, both_ref, out_ref):
-        for h in range(2):
+    _, _, rows, lanes = rest.shape
+    high = rows // chips
+
+    def kernel(order, rest_ref, both_ref, *out_refs):
+        for h, out_ref in enumerate(out_refs):
             for s in range(chips):
                 here, there = (slice(i * high, (i + 1) * high) for i in (s, s ^ 2))
                 term = both_ref[0, h, there, :].astype(F32)
-                out_ref[0, h, here, :] = (rest_ref[0, h, here, :] + term).astype(BF16)
-
-    return local(kernel, "second_share", [(shape, BF16)], order, [rest, both_in])
-
-
-def own_share(order, rest, first_in, second_in, chips):
+                out_ref[here, :] = (rest_ref[0, h, here, :] + term).astype(BF16)
+
+    shapes = [((rows, lanes), BF16)] * 2
+    return local(kernel, "second_share", shapes, order, [rest, both_in])
+
+
+def first_share(order, rest, first_in, chips):
     _, _, rows, lanes = rest.shape
     high = rows // chips
 
-    def kernel(order, rest_ref, first_ref, second_ref, own_ref, other_ref):
+    def kernel(order, rest_ref, first_ref, own_ref, other_ref):
         for h, out_ref in ((1, other_ref), (0, own_ref)):
             for s in range(chips):
-                here, first, second = (slice(i * high, (i + 1) * high) for i in (s, s ^ 2, s ^ 1))
+                here, first = (slice(i * high, (i + 1) * high) for i in (s, s ^ 2))
                 total = rest_ref[1, h, here, :] + first_ref[0, h, first, :].astype(F32)
-                total = total + second_ref[0, h, second, :].astype(F32)
                 out_ref[here, :] = total.astype(out_ref.dtype)
 
     shapes = [((rows, lanes), F32), ((rows, lanes), BF16)]
-    return local(kernel, "own_share", shapes, order, [rest, first_in, second_in])
+    return local(kernel, "first_share", shapes, order, [rest, first_in])
 
 
 def hyena_kernel(
-    order, own_ref, swap_ref, filt_ref, decay_ref, residue_ref,
+    order, own_ref, swap_ref, second_ref, swap_second_ref, filt_ref, decay_ref, residue_ref,
     keep_ref, send_ref, rows, mixed_s, state, enter, edge, *, blocks,
 ):
     high = rows.shape[1] // blocks
@@ -294,13 +299,15 @@
     channels = columns(order[2 * chips + 1], chans)
 
     for s in range(chips):
-        here = slice(s * high, (s + 1) * high)
+        here, second = (slice(i * high, (i + 1) * high) for i in (s, s ^ 1))
         own_at = columns(2 * order[s] + core, high)
         swap_at = columns(2 * order[chips + s] + 1 - core, high)
         for g in range(2):
             lanes = slice(g * chans, (g + 1) * chans)
-            rows[g, own_at, :] = own_ref[here, lanes]
-            rows[g, swap_at, :] = swap_ref[here, lanes].astype(F32)
+            rows[g, own_at, :] = own_ref[here, lanes] + second_ref[second, lanes].astype(F32)
+            rows[g, swap_at, :] = swap_ref[here, lanes].astype(F32) + swap_second_ref[
+                second, lanes
+            ].astype(F32)
 
     for k in range(1, taps):
         for g in range(2):
@@ -332,7 +339,7 @@
 
     zeros = tuple(jnp.zeros((blocks, chans), F32) for _ in range(modes))
     before = tuple(tuple(edge[k, g] for g in range(2)) for k in range(taps - 1))
-    states, _ = lax.fori_loop(0, high, first_pass, (zeros, before), unroll=4)
+    states, _ = lax.fori_loop(0, high, first_pass, (zeros, before), unroll=16)
     for n in range(modes):
         state[n * blocks : (n + 1) * blocks, :] = states[n]
 
@@ -362,14 +369,14 @@
         return states
 
     begin = tuple(enter[n * blocks : (n + 1) * blocks, :] for n in range(modes))
-    lax.fori_loop(0, high, second_pass, begin, unroll=4)
+    lax.fori_loop(0, high, second_pass, begin, unroll=16)
     for s in range(chips):
         keep_ref[s] = rows[0, columns(2 * order[s] + core, high), :].astype(BF16)
         send_ref[s] = rows[0, columns(2 * order[chips + s] + 1 - core, high), :].astype(BF16)
 
 
-def hyena(order, own, swap, short_filter, mode_decay, residue, blocks):
-    rows_count, lanes = own.shape
+def hyena(order, parts, short_filter, mode_decay, residue, blocks):
+    rows_count, lanes = parts[0].shape
     chans = lanes // 2
     total = 2 * rows_count
     high = total // blocks
@@ -381,28 +388,24 @@
         pltpu.VMEM((modes * blocks, chans), F32),
         pltpu.VMEM((taps - 1, 2, blocks, chans), F32),
     ]
-    arrays = [own, swap, short_filter, mode_decay, residue]
+    arrays = [*parts, short_filter, mode_decay, residue]
     kernel = functools.partial(hyena_kernel, blocks=blocks)
     shapes = [((blocks // 2, high, chans), BF16)] * 2
     return local(kernel, "hyena", shapes, order, arrays, scratch)
 
 
-def pair_up(order, keep, other):
-    chips, high, chans = keep.shape
-
-    def kernel(order, keep_ref, other_ref, *out_refs):
+def payloads(order, q_next, q_in, keep, other):
+    chips, high, _ = keep.shape
+    chans = q_next.shape[1]
+
+    def kernel(order, next_ref, in_ref, keep_ref, other_ref, second_ref, *out_refs):
+        second_ref[...] = (next_ref[...] + in_ref[:, :chans].astype(F32)).astype(BF16)
         for s, out_ref in enumerate(out_refs):
             out_ref[0] = keep_ref[s]
             out_ref[1] = other_ref[s]
 
-    return local(kernel, "pair_up", [((2, high, chans), BF16)] * chips, order, [keep, other])
-
-
-def query_second(order, rest, q_in):
-    def kernel(order, rest_ref, in_ref, out_ref):
-        out_ref[...] = (rest_ref[...] + in_ref[...].astype(F32)).astype(BF16)
-
-    return local(kernel, "query_second", [(rest.shape, BF16)], order, [rest, q_in])
+    shapes = [(q_next.shape, BF16)] + [((2, high, keep.shape[2]), BF16)] * chips
+    return local(kernel, "payloads", shapes, order, [q_next, q_in, keep, other])
 
 
 def gate(scalars, queries, long_parts, w_out, groups):
@@ -416,7 +419,11 @@
         query_refs, long_refs = refs[: len(queries)], refs[len(queries) : len(queries) + chips]
         w_ref, gated_ref, pair_ref, side_ref, query = refs[len(queries) + chips :]
         core = scalars[2 * chips]
-        query[...] = sum(ref[...].astype(F32) for ref in query_refs)
+        own_ref, second_ref, both_ref, first_ref = query_refs
+        extra = both_ref.shape[1] - chans
+        query[...] = own_ref[...] + second_ref[...].astype(F32)
+        query[:, :extra] += both_ref[:, chans:].astype(F32)
+        query[:, extra:] += first_ref[...].astype(F32)
         for s, ref in enumerate(long_refs):
             for h in range(2):
                 at = columns(2 * scalars[s] + (core ^ h), part)
@@ -468,16 +475,19 @@
     both = local(add, "both", [(far.shape, BF16)], picks, [far, pair_in])
     far_in = lax.ppermute(both, "dp", [(1, 3), (2, 0)])
 
-    def total(picks, own_ref, pair_ref, *refs):
-        out_ref = refs[-1]
+    def early(picks, own_ref, pair_ref, *refs):
         inner = picks[4] == 1
         value = own_ref[...] + jnp.where(inner, 0.0, pair_ref[...].astype(F32))
         for ref in refs[:-1]:
             value = value + ref[...].astype(F32)
-        out_ref[...] = value.astype(BF16)
-
-    arrays = [own, pair_in, middle_in, end_in, side_in, far_in]
-    return local(total, "total", [(own.shape, BF16)], picks, arrays)
+        refs[-1][...] = value
+
+    def total(picks, early_ref, far_ref, out_ref):
+        out_ref[...] = (early_ref[...] + far_ref[...].astype(F32)).astype(BF16)
+
+    arrays = [own, pair_in, middle_in, end_in, side_in]
+    own = local(early, "early", [(own.shape, F32)], picks, arrays)
+    return local(total, "total", [(own.shape, BF16)], picks, [own, far_in])
 
 
 def on_device_chips(tokens, w_in, short_filter, mode_decay, residue, w_out):
@@ -524,26 +534,27 @@
     first_in = lax.ppermute(first, "ctx", route(2))
     xs, first = lax.optimization_barrier((xs, first))
     rest = project_mix(order, xs, own_w, other_w, [1, 0], F32)
-    second = second_share(order, rest, both_in, chips)
+    second, swap_second = second_share(order, rest, both_in, chips)
     second_in = lax.ppermute(second, "ctx", route(1))
+    swap_second = lax.ppermute(swap_second, "ctx", [(i, j ^ 1) for i, j in route(1)])
 
     xs, second = lax.optimization_barrier((xs, second))
     before = lax.ppermute(last_rows(order, xs, 16), "ctx", swap)
     q_own, q_next, q_first, q_both = project_query(order, xs, before, own_w, other_w, short_filter)
     q_own, rest = lax.optimization_barrier((q_own, rest))
 
-    own, other_half = own_share(order, rest, first_in, second_in, chips)
+    own, other_half = first_share(order, rest, first_in, chips)
     other_half = lax.ppermute(other_half, "ctx", swap)
     q_both, q_first, own = lax.optimization_barrier((q_both, q_first, own))
     q_both = lax.ppermute(q_both, "ctx", route(2))
     q_first = lax.ppermute(q_first, "ctx", route(2))
-    keep, send = hyena(order, own, other_half, short_filter, mode_decay, residue, count)
-    q_next, keep, send = lax.optimization_barrier((q_next, keep, send))
-    q_second = query_second(order, q_next, q_both)
-    long_parts = pair_up(order, keep, lax.ppermute(send, "ctx", swap))
+    parts = [own, other_half, second_in, swap_second]
+    keep, send = hyena(order, parts, short_filter, mode_decay, residue, count)
+    other_long = lax.ppermute(send, "ctx", swap)
+    q_second, *long_parts = payloads(order, q_next, q_both, keep, other_long)
     q_second = lax.ppermute(q_second, "ctx", route(1))
     long_parts = [long_parts[0]] + [lax.ppermute(long_parts[s], "ctx", route(s)) for s in (1, 2, 3)]
-    queries = [q_own, q_first, q_second]
+    queries = [q_own, q_second, q_both, q_first]
     gated, pair, side = gate(both_scalars, queries, long_parts, w_out, groups)
     return output_over_line(picks, gated, pair, side, w_out, groups)
 

time: 111 us -> 107 us (0.964)
  waiting for transfers between devices: 51.1 us -> 45.3 us
  local copies, waits for them, and re-layouts: 5.08 us -> 6.97 us
  starting transfers between devices: 29.7 us -> 30.9 us
    ppermute x1, waiting for transfers between devices: 0.01 us -> 4.99 us  [on_device_chips(): q_first = lax.ppermute(q_first, 'ctx', route(2))]
    ppermute x3, waiting for transfers between devices: 5.81 us -> 3.44 us  [on_device_chips(): lax.ppermute(long_parts[s], 'ctx', route(s))]
    ppermute x1, waiting for transfers between devices: 7.34 us -> 5.19 us  [on_device_chips(): first_in = lax.ppermute(first, 'ctx', route(2))]
    unnamed x12, local copies, waits for them, and re-layouts: 4.81 us -> 6.7 us
    ppermute x1, waiting for transfers between devices: 7.63 us -> 6.16 us  [output_over_line(): end_in = lax.ppermute(far, 'dp', [(0, 2), (3, 1)])]
    ppermute x2, waiting for transfers between devices: 1.36 us -> 0.01 us  [on_device_chips(): xs = [xs[0]] + [lax.ppermute(xs[s], 'ctx', route(s)) for s in (1, 2)]]
    ppermute x1, waiting for transfers between devices: 1.33 us -> 0.01 us  [on_device_chips(): before = lax.ppermute(last_rows(order, xs, 16), 'ctx', swap)]
    ppermute x1 -> x2, starting transfers between devices: 0.01 us -> 1.3 us  [the longest x1 1.23 us: on_device_chips(): lax.ppermute(swap_second, 'ctx', [(i, j ^ 1) for i, j in route(1)])]
  transfers between devices with their start and end apart: 22 -> 23, of which waited for: 16 -> 10; matrix products, arithmetic and copies ran while one was open for 0% -> 0% of each run, Pallas kernels for 17% -> 17%
where the time goes in v4:
time: 107 us
  waiting for transfers between devices  45.3 us (42%)
  starting transfers between devices  30.9 us (29%)
  Pallas kernels  23.4 us (22%)
  local copies, waits for them, and re-layouts  6.97 us (7%)
    pallas_call x17, Pallas kernels, local(): pl.pallas_call(kernel, out_shape=out if len(out) > 1 else out[0], in_spec...  22.6 us
    unnamed x12, local copies, waits for them, and re-layouts  6.7 us
    ppermute x1, starting transfers between devices, output_over_line(): side_in = lax.ppermute(side, 'dp', [(0, 1), (3, 2)])  6.3 us
    ppermute x1, waiting for transfers between devices, output_over_line(): end_in = lax.ppermute(far, 'dp', [(0, 2), (3, 1)])  6.16 us
    ppermute x1, waiting for transfers between devices, on_device_chips(): both_in = lax.ppermute(both, 'ctx', route(2))  5.58 us
    ppermute x1, waiting for transfers between devices, output_over_line(): far_in = lax.ppermute(both, 'dp', [(1, 3), (2, 0)])  5.3 us
    ppermute x1, waiting for transfers between devices, on_device_chips(): first_in = lax.ppermute(first, 'ctx', route(2))  5.19 us
    ppermute x1, waiting for transfers between devices, on_device_chips(): half = lax.ppermute(xs[3], 'ctx', route(3))  5.15 us
  transfers between devices with their start and end apart: 23, of which 10 were waited for; matrix products, arithmetic and copies ran while one was open for 0% of the time, Pallas kernels for 17%

profile of v4, /device:TPU:0, one launch (start us, length us, event | category | flops | bytes accessed | tf_op | source)
XLA Modules:
  0.0 106.9 jit_solution(12749843980652710710)
XLA Ops:
  0.0 0.5 collective-permute-start.4
  0.5 0.1 stack.59.order
  0.5 0.1 concatenate.4.scalars
  0.6 0.1 stack.65.picks
  0.7 1.4 %copy-done.2 = bf16[192,4096]{1,0:T(8,128)(2,1)S(1)} copy-done((bf16[192,4096]{1,0:T(8,128)(2,1)S(1)}, bf16[192,4096]{1,0:T(8,128)(2,1)}, u32[]{:S(2)}) %copy-start.2) | copy-done | bytes 1572888
  2.1 0.6 cut.1
  2.8 3.5 %collective-permute-start.2 = (bf16[96,1024]{1,0:T(8,128)(2,1)S(1)}, bf16[96,1024]{1,0:T(8,128)(2,1)S(1)}, u32[]{:S(2)}, u32[]{:S(2)}) collective-permute-start(bf16[96,1024]{1,0:T(8,128)(2,1)S(1)} %get-tuple-element.67), channel_id=1, source_target_pairs={{0,6},{1,7},{2,4},{3,5},{4,2},{5,3},{6,0},{7,1},{8,14},{9,15},{10,... | collective-permute-start | bytes 589832 | tf_op jit(solution)/shard_map/ppermute | solution.py:525
  6.3 0.5 collective-permute-start
  6.8 0.1 collective-permute-start.1
  6.9 5.2 %collective-permute-done.2.mine_ref = bf16[96,1024]{1,0:T(8,128)(2,1)S(1)} collective-permute-done((bf16[96,1024]{1,0:T(8,128)(2,1)S(1)}, bf16[96,1024]{1,0:T(8,128)(2,1)S(1)}, u32[]{:S(2)}, u32[]{:S(2)}) %collective-permute-start.2) | collective-permute-done | bytes 196640 | tf_op jit(solution)/shard_map/ppermute | solution.py:525
  12.1 2.0 %collective-permute-start.3 = (bf16[96,1024]{1,0:T(8,128)(2,1)S(1)}, bf16[96,1024]{1,0:T(8,128)(2,1)S(1)}, u32[]{:S(2)}, u32[]{:S(2)}) collective-permute-start(bf16[96,1024]{1,0:T(8,128)(2,1)S(1)} %collective-permute-done.2.mine_ref), channel_id=1, source_target_pairs={{0,8},{8,0},{16,24},{24,16},{1,9},{9,1},{17,25},{25,17},{2,10},{10... | collective-permute-start | bytes 589832 | tf_op jit(solution)/shard_map/ppermute | solution.py:526
  14.1 3.4 %copy-done = bf16[1024,4096]{1,0:T(8,128)(2,1)S(1)} copy-done((bf16[1024,4096]{1,0:T(8,128)(2,1)S(1)}, bf16[1024,4096]{1,0:T(8,128)(2,1)}, u32[]{:S(2)}) %copy-start) | copy-done | bytes 8388632
  17.4 1.9 %copy-done.1 = bf16[512,3,1024]{2,0,1:T(8,128)(2,1)S(1)} copy-done((bf16[512,3,1024]{2,0,1:T(8,128)(2,1)S(1)}, bf16[512,3,1024]{2,0,1:T(8,128)(2,1)}, u32[]{:S(2)}) %copy-start.1) | copy-done | bytes 3145752
  19.3 0.8 stage.1
  20.1 0.6 join_rows.1.refs_3_
  20.7 0.0 collective-permute-done.refs_1_
  20.7 0.0 collective-permute-done.4.refs_5_.refs_6_
  20.7 1.7 %project_mix.3 = bf16[1,2,768,256]{3,2,1,0:T(8,128)(2,1)S(1)} custom-call(s32[11]{0:T(128)S(1)} %stack.59.order, bf16[192,1024]{1,0:T(8,128)(2,1)S(1)} %get-tuple-element.80.refs_0_, bf16[192,1024]{1,0:T(8,128)(2,1)S(1)} %collective-permute-done.refs_1_, bf16[192,1024]{1,0:T(8,128)(2,1)S(1)} %collective-permute-done.1.refs_2_, ...), custom_call_target="tpu_custom_call" | custom-call | tf_op jit(solution)/shard_map/project_mix/pallas_call | solution.py:101
  22.5 1.6 %collective-permute-start.5 = (bf16[1,2,768,256]{3,2,1,0:T(8,128)(2,1)S(1)}, bf16[1,2,768,256]{3,2,1,0:T(8,128)(2,1)S(1)}, u32[]{:S(2)}, u32[]{:S(2)}) collective-permute-start(bf16[1,2,768,256]{3,2,1,0:T(8,128)(2,1)S(1)} %project_mix.3), channel_id=1, source_target_pairs={{0,2},{1,5},{2,0},{3,7},{4,6},{5,1},{6,4},{7,3},{8,10},{9,13},{10,... | collective-permute-start | bytes 2359304 | tf_op jit(solution)/shard_map/ppermute | solution.py:531
  24.0 1.7 %project_mix.4 = bf16[1,2,768,256]{3,2,1,0:T(8,128)(2,1)S(1)} custom-call(s32[11]{0:T(128)S(1)} %stack.59.order, bf16[192,1024]{1,0:T(8,128)(2,1)S(1)} %get-tuple-element.80.refs_0_, bf16[192,1024]{1,0:T(8,128)(2,1)S(1)} %collective-permute-done.refs_1_, bf16[192,1024]{1,0:T(8,128)(2,1)S(1)} %collective-permute-done.1.refs_2_, ...), custom_call_target="tpu_custom_call" | custom-call | tf_op jit(solution)/shard_map/project_mix/pallas_call | solution.py:101
  25.7 0.6 collective-permute-start.7
  26.3 2.6 %project_mix.5.rest_ref = f32[2,2,768,256]{3,2,1,0:T(8,128)S(1)} custom-call(s32[11]{0:T(128)S(1)} %stack.59.order, bf16[192,1024]{1,0:T(8,128)(2,1)S(1)} %get-tuple-element.80.refs_0_, bf16[192,1024]{1,0:T(8,128)(2,1)S(1)} %collective-permute-done.refs_1_, bf16[192,1024]{1,0:T(8,128)(2,1)S(1)} %collective-permute-done.1.refs_2_, ...), custom_call_target="tpu_custom_call" | custom-call | tf_op jit(solution)/shard_map/project_mix/pallas_call | solution.py:101
  28.9 0.0 copy-start.3
  28.9 5.6 %collective-permute-done.5.both_ref = bf16[1,2,768,256]{3,2,1,0:T(8,128)(2,1)S(1)} collective-permute-done((bf16[1,2,768,256]{3,2,1,0:T(8,128)(2,1)S(1)}, bf16[1,2,768,256]{3,2,1,0:T(8,128)(2,1)S(1)}, u32[]{:S(2)}, u32[]{:S(2)}) %collective-permute-start.5) | collective-permute-done | bytes 786464 | tf_op jit(solution)/shard_map/ppermute | solution.py:531
  34.5 0.7 second_share.1
  35.2 0.6 last_rows.1
  35.8 0.1 collective-permute-start.6
  35.9 1.6 %collective-permute-start.10 = (bf16[768,256]{1,0:T(8,128)(2,1)S(1)}, bf16[768,256]{1,0:T(8,128)(2,1)S(1)}, u32[]{:S(2)}, u32[]{:S(2)}) collective-permute-start(bf16[768,256]{1,0:T(8,128)(2,1)S(1)} %get-tuple-element.79), channel_id=1, source_target_pairs={{0,4},{1,3},{2,6},{3,1},{4,0},{5,7},{6,2},{7,5},{8,12},{9,11},{10,... | collective-permute-start | bytes 1179656 | tf_op jit(solution)/shard_map/ppermute | solution.py:538
  37.4 1.2 %collective-permute-start.11 = (bf16[768,256]{1,0:T(8,128)(2,1)S(1)}, bf16[768,256]{1,0:T(8,128)(2,1)S(1)}, u32[]{:S(2)}, u32[]{:S(2)}) collective-permute-start(bf16[768,256]{1,0:T(8,128)(2,1)S(1)} %get-tuple-element.94), channel_id=1, source_target_pairs={{0,5},{1,2},{2,7},{3,0},{4,1},{5,6},{6,3},{7,4},{8,13},{9,10},{10,... | collective-permute-start | bytes 1179656 | tf_op jit(solution)/shard_map/ppermute | solution.py:539
  38.7 0.0 collective-permute-done.6.refs_4_
  38.7 3.0 %project_query.1 = (f32[192,1024]{1,0:T(8,128)S(1)}, f32[192,1024]{1,0:T(8,128)S(1)}, bf16[192,768]{1,0:T(8,128)(2,1)S(1)}, bf16[192,1280]{1,0:T(8,128)(2,1)S(1)}) custom-call(s32[11]{0:T(128)S(1)} %stack.59.order, bf16[192,1024]{1,0:T(8,128)(2,1)S(1)} %get-tuple-element.80.refs_0_, bf16[192,1024]{1,0:T(8,128)(2,1)S(1)} %collective-permute-done.refs_1_, ...), custom_call_target="tpu_custom_call" | custom-call | tf_op jit(solution)/shard_map/project_query/pallas_call | solution.py:101
  41.6 0.0 copy-start.4
  41.7 0.0 copy-start.5
  41.7 5.2 %collective-permute-done.7.first_ref = bf16[1,2,768,256]{3,2,1,0:T(8,128)(2,1)S(1)} collective-permute-done((bf16[1,2,768,256]{3,2,1,0:T(8,128)(2,1)S(1)}, bf16[1,2,768,256]{3,2,1,0:T(8,128)(2,1)S(1)}, u32[]{:S(2)}, u32[]{:S(2)}) %collective-permute-start.7) | collective-permute-done | bytes 786464 | tf_op jit(solution)/shard_map/ppermute | solution.py:534
  46.9 0.7 first_share.1
  47.6 0.1 collective-permute-start.9
  47.7 1.6 %collective-permute-start.8 = (bf16[192,1280]{1,0:T(8,128)(2,1)S(1)}, bf16[192,1280]{1,0:T(8,128)(2,1)S(1)}, u32[]{:S(2)}, u32[]{:S(2)}) collective-permute-start(bf16[192,1280]{1,0:T(8,128)(2,1)S(1)} %get-tuple-element.91), channel_id=1, source_target_pairs={{0,2},{1,5},{2,0},{3,7},{4,6},{5,1},{6,4},{7,3},{8,10},{9,13},{10,... | collective-permute-start | bytes 1474568 | tf_op jit(solution)/shard_map/ppermute | solution.py:549
  49.2 2.1 %collective-permute-done.11.swap_second_ref = bf16[768,256]{1,0:T(8,128)(2,1)S(1)} collective-permute-done((bf16[768,256]{1,0:T(8,128)(2,1)S(1)}, bf16[768,256]{1,0:T(8,128)(2,1)S(1)}, u32[]{:S(2)}, u32[]{:S(2)}) %collective-permute-start.11) | collective-permute-done | bytes 393248 | tf_op jit(solution)/shard_map/ppermute | solution.py:539
  51.4 2.9 %hyena.1 = (bf16[4,192,128]{2,1,0:T(8,128)(2,1)S(1)}, bf16[4,192,128]{2,1,0:T(8,128)(2,1)S(1)}) custom-call(s32[11]{0:T(128)S(1)} %stack.59.order, f32[768,256]{1,0:T(8,128)S(1)} %get-tuple-element.92.own_ref, bf16[768,256]{1,0:T(8,128)(2,1)S(1)} %collective-permute-done.9.swap_ref, bf16[768,256]{1,0:T(8,128)(2,1)S(1)} %collective-permute-done.10.second_ref, ...), custom_call_target="tpu_custom_call" | custom-call | tf_op jit(solution)/shard_map/hyena/pallas_call | solution.py:101
  54.3 0.1 collective-permute-start.12
  54.4 2.2 %collective-permute-done.8.in_ref.refs_2_ = bf16[192,1280]{1,0:T(8,128)(2,1)S(1)} collective-permute-done((bf16[192,1280]{1,0:T(8,128)(2,1)S(1)}, bf16[192,1280]{1,0:T(8,128)(2,1)S(1)}, u32[]{:S(2)}, u32[]{:S(2)}) %collective-permute-start.8) | collective-permute-done | bytes 491552 | tf_op jit(solution)/shard_map/ppermute | solution.py:549
  56.6 0.6 payloads.1
  57.3 1.6 %collective-permute-start.13 = (bf16[192,1024]{1,0:T(8,128)(2,1)S(1)}, bf16[192,1024]{1,0:T(8,128)(2,1)S(1)}, u32[]{:S(2)}, u32[]{:S(2)}) collective-permute-start(bf16[192,1024]{1,0:T(8,128)(2,1)S(1)} %get-tuple-element.97), channel_id=1, source_target_pairs={{0,4},{1,3},{2,6},{3,1},{4,0},{5,7},{6,2},{7,5},{8,12},{9,11},{10,... | collective-permute-start | bytes 1179656 | tf_op jit(solution)/shard_map/ppermute | solution.py:555
  58.9 1.5 %collective-permute-start.14 = (bf16[192,768]{1,0:T(8,128)(2,1)S(1)}, bf16[192,768]{1,0:T(8,128)(2,1)S(1)}, u32[]{:S(2)}, u32[]{:S(2)}) collective-permute-start(bf16[192,768]{1,0:T(8,128)(2,1)S(1)} %get-tuple-element.98), channel_id=1, source_target_pairs={{0,2},{1,5},{2,0},{3,7},{4,6},{5,1},{6,4},{7,3},{8,10},{9,13},{10,... | collective-permute-start | bytes 884744 | tf_op jit(solution)/shard_map/ppermute | solution.py:550
  60.3 0.5 collective-permute-start.15
  60.9 0.5 collective-permute-start.16
  61.4 2.4 %collective-permute-start.17 = (bf16[2,192,128]{2,1,0:T(8,128)(2,1)S(1)}, bf16[2,192,128]{2,1,0:T(8,128)(2,1)S(1)}, u32[]{:S(2)}, u32[]{:S(2)}) collective-permute-start(bf16[2,192,128]{2,1,0:T(8,128)(2,1)S(1)} %get-tuple-element.102), channel_id=1, source_target_pairs={{0,6},{1,7},{2,4},{3,5},{4,2},{5,3},{6,0},{7,1},{8,14},{9,15},{10,... | collective-permute-start | bytes 294920 | tf_op jit(solution)/shard_map/ppermute | solution.py:556
  63.8 5.0 %collective-permute-done.14.refs_3_ = bf16[192,768]{1,0:T(8,128)(2,1)S(1)} collective-permute-done((bf16[192,768]{1,0:T(8,128)(2,1)S(1)}, bf16[192,768]{1,0:T(8,128)(2,1)S(1)}, u32[]{:S(2)}, u32[]{:S(2)}) %collective-permute-start.14) | collective-permute-done | bytes 294944 | tf_op jit(solution)/shard_map/ppermute | solution.py:550
  68.8 3.4 %collective-permute-done.15.refs_5_ = bf16[2,192,128]{2,1,0:T(8,128)(2,1)S(1)} collective-permute-done((bf16[2,192,128]{2,1,0:T(8,128)(2,1)S(1)}, bf16[2,192,128]{2,1,0:T(8,128)(2,1)S(1)}, u32[]{:S(2)}, u32[]{:S(2)}) %collective-permute-start.15) | collective-permute-done | bytes 98336 | tf_op jit(solution)/shard_map/ppermute | solution.py:556
  72.2 0.0 collective-permute-done.16.refs_6_
  72.3 1.9 %gate.1 = (bf16[192,1024]{1,0:T(8,128)(2,1)S(1)}, bf16[192,1024]{1,0:T(8,128)(2,1)S(1)}, bf16[192,1024]{1,0:T(8,128)(2,1)S(1)}) custom-call(s32[16]{0:T(128)S(1)} %concatenate.4.scalars, f32[192,1024]{1,0:T(8,128)S(1)} %get-tuple-element.85.refs_0_, bf16[192,1024]{1,0:T(8,128)(2,1)S(1)} %collective-permute-done.13.refs_1_, ...), custom_call_target="tpu_custom_call" | custom-call | tf_op jit(solution)/shard_map/gate/pallas_call | solution.py:101
  74.1 1.5 %collective-permute-start.18 = (bf16[192,1024]{1,0:T(8,128)(2,1)S(1)}, bf16[192,1024]{1,0:T(8,128)(2,1)S(1)}, u32[]{:S(2)}, u32[]{:S(2)}) collective-permute-start(bf16[192,1024]{1,0:T(8,128)(2,1)S(1)} %get-tuple-element.105), channel_id=1, source_target_pairs={{0,8},{8,0},{16,24},{24,16},{1,9},{9,1},{17,25},{25,17},{2,10},{10... | collective-permute-start | bytes 1179656 | tf_op jit(solution)/shard_map/ppermute | solution.py:464
  75.6 0.7 collective-permute-start.19
  76.3 1.1 %out_columns.3.far_ref = bf16[192,1024]{1,0:T(8,128)(2,1)S(1)} custom-call(s32[5]{0:T(128)S(1)} %stack.65.picks, bf16[192,1024]{1,0:T(8,128)(2,1)S(1)} %get-tuple-element.104.x_ref, bf16[1024,4096]{1,0:T(8,128)(2,1)S(1)} %get-tuple-element.103.refs_8_.w_ref), custom_call_target="tpu_custom_call" | custom-call | tf_op jit(solution)/shard_map/out_columns/pallas_call | solution.py:101
  77.4 6.3 %collective-permute-start.21 = (bf16[192,1024]{1,0:T(8,128)(2,1)S(1)}, bf16[192,1024]{1,0:T(8,128)(2,1)S(1)}, u32[]{:S(2)}, u32[]{:S(2)}) collective-permute-start(bf16[192,1024]{1,0:T(8,128)(2,1)S(1)} %get-tuple-element.108), channel_id=1, source_target_pairs={{0,8},{24,16},{1,9},{25,17},{2,10},{26,18},{3,11},{27,19},{4,12},{... | collective-permute-start | bytes 1179656 | tf_op jit(solution)/shard_map/ppermute | solution.py:469
  83.7 1.3 %collective-permute-start.20 = (bf16[192,1024]{1,0:T(8,128)(2,1)S(1)}, bf16[192,1024]{1,0:T(8,128)(2,1)S(1)}, u32[]{:S(2)}, u32[]{:S(2)}) collective-permute-start(bf16[192,1024]{1,0:T(8,128)(2,1)S(1)} %out_columns.3.far_ref), channel_id=1, source_target_pairs={{0,16},{24,8},{1,17},{25,9},{2,18},{26,10},{3,19},{27,11},{4,20},{... | collective-permute-start | bytes 1179656 | tf_op jit(solution)/shard_map/ppermute | solution.py:468
  85.1 0.6 both.1
  85.7 1.3 %collective-permute-start.22 = (bf16[192,1024]{1,0:T(8,128)(2,1)S(1)}, bf16[192,1024]{1,0:T(8,128)(2,1)S(1)}, u32[]{:S(2)}, u32[]{:S(2)}) collective-permute-start(bf16[192,1024]{1,0:T(8,128)(2,1)S(1)} %both.1), channel_id=1, source_target_pairs={{8,24},{16,0},{9,25},{17,1},{10,26},{18,2},{11,27},{19,3},{12,28},... | collective-permute-start | bytes 1179656 | tf_op jit(solution)/shard_map/ppermute | solution.py:476
  87.0 1.1 %out_columns.2.own_ref = f32[192,1024]{1,0:T(8,128)S(1)} custom-call(s32[5]{0:T(128)S(1)} %stack.65.picks, bf16[192,1024]{1,0:T(8,128)(2,1)S(1)} %get-tuple-element.104.x_ref, bf16[1024,4096]{1,0:T(8,128)(2,1)S(1)} %get-tuple-element.103.refs_8_.w_ref), custom_call_target="tpu_custom_call" | custom-call | tf_op jit(solution)/shard_map/out_columns/pallas_call | solution.py:101
  88.1 5.1 %collective-permute-done.21.refs_2_ = bf16[192,1024]{1,0:T(8,128)(2,1)S(1)} collective-permute-done((bf16[192,1024]{1,0:T(8,128)(2,1)S(1)}, bf16[192,1024]{1,0:T(8,128)(2,1)S(1)}, u32[]{:S(2)}, u32[]{:S(2)}) %collective-permute-start.21) | collective-permute-done | bytes 393248 | tf_op jit(solution)/shard_map/ppermute | solution.py:469
  93.3 6.2 %collective-permute-done.20.refs_1_ = bf16[192,1024]{1,0:T(8,128)(2,1)S(1)} collective-permute-done((bf16[192,1024]{1,0:T(8,128)(2,1)S(1)}, bf16[192,1024]{1,0:T(8,128)(2,1)S(1)}, u32[]{:S(2)}, u32[]{:S(2)}) %collective-permute-start.20) | collective-permute-done | bytes 393248 | tf_op jit(solution)/shard_map/ppermute | solution.py:468
  99.4 0.8 early.1.early_ref
  100.2 5.3 %collective-permute-done.22.far_ref = bf16[192,1024]{1,0:T(8,128)(2,1)S(1)} collective-permute-done((bf16[192,1024]{1,0:T(8,128)(2,1)S(1)}, bf16[192,1024]{1,0:T(8,128)(2,1)S(1)}, u32[]{:S(2)}, u32[]{:S(2)}) %collective-permute-start.22) | collective-permute-done | bytes 393248 | tf_op jit(solution)/shard_map/ppermute | solution.py:476
  105.5 1.4 %total.1 = bf16[192,1024]{1,0:T(8,128)(2,1)} custom-call(s32[5]{0:T(128)S(1)} %stack.65.picks, f32[192,1024]{1,0:T(8,128)S(1)} %early.1.early_ref, bf16[192,1024]{1,0:T(8,128)(2,1)S(1)} %collective-permute-done.22.far_ref), custom_call_target="tpu_custom_call" | custom-call | tf_op jit(solution)/shard_map/total/pallas_call | solution.py:101
  (15 shorter events, 0.0 us)
Async XLA Ops:
  0.0 20.7 %collective-permute-start.4 = (bf16[3,512,1024]{2,1,0:T(8,128)(2,1)}, bf16[3,512,1024]{2,1,0:T(8,128)(2,1)S(1)}, u32[]{:S(2)}, u32[]{:S(2)}) collective-permute-start(bf16[3,512,1024]{2,1,0:T(8,128)(2,1)} %bitcast.15), channel_id=1, source_target_pairs={{0,1},{1,0},{2,3},{3,2},{4,5},{5,4},{6,7},{7,6},{8,9},{9,8},{10,11... | collective-permute-start | bytes 9437192 | tf_op jit(solution)/shard_map/ppermute | solution.py:521
  0.7 1.4 %copy-start.2 = (bf16[192,4096]{1,0:T(8,128)(2,1)S(1)}, bf16[192,4096]{1,0:T(8,128)(2,1)}, u32[]{:S(2)}) copy-start(bf16[192,4096]{1,0:T(8,128)(2,1)} %tokens_ref.1) | copy-start | bytes 4718596
  2.8 9.3 %collective-permute-start.2 = (bf16[96,1024]{1,0:T(8,128)(2,1)S(1)}, bf16[96,1024]{1,0:T(8,128)(2,1)S(1)}, u32[]{:S(2)}, u32[]{:S(2)}) collective-permute-start(bf16[96,1024]{1,0:T(8,128)(2,1)S(1)} %get-tuple-element.67), channel_id=1, source_target_pairs={{0,6},{1,7},{2,4},{3,5},{4,2},{5,3},{6,0},{7,1},{8,14},{9,15},{10,... | collective-permute-start | bytes 589832 | tf_op jit(solution)/shard_map/ppermute | solution.py:525
  6.3 14.4 %collective-permute-start = (bf16[192,1024]{1,0:T(8,128)(2,1)S(1)}, bf16[192,1024]{1,0:T(8,128)(2,1)S(1)}, u32[]{:S(2)}, u32[]{:S(2)}) collective-permute-start(bf16[192,1024]{1,0:T(8,128)(2,1)S(1)} %get-tuple-element.65), channel_id=1, source_target_pairs={{0,4},{1,3},{2,6},{3,1},{4,0},{5,7},{6,2},{7,5},{8,12},{9,11},{10,... | collective-permute-start | bytes 1179656 | tf_op jit(solution)/shard_map/ppermute | solution.py:527
  6.8 13.9 %collective-permute-start.1 = (bf16[192,1024]{1,0:T(8,128)(2,1)S(1)}, bf16[192,1024]{1,0:T(8,128)(2,1)S(1)}, u32[]{:S(2)}, u32[]{:S(2)}) collective-permute-start(bf16[192,1024]{1,0:T(8,128)(2,1)S(1)} %get-tuple-element.66), channel_id=1, source_target_pairs={{0,2},{1,5},{2,0},{3,7},{4,6},{5,1},{6,4},{7,3},{8,10},{9,13},{10,... | collective-permute-start | bytes 1179656 | tf_op jit(solution)/shard_map/ppermute | solution.py:527
  12.1 8.0 %collective-permute-start.3 = (bf16[96,1024]{1,0:T(8,128)(2,1)S(1)}, bf16[96,1024]{1,0:T(8,128)(2,1)S(1)}, u32[]{:S(2)}, u32[]{:S(2)}) collective-permute-start(bf16[96,1024]{1,0:T(8,128)(2,1)S(1)} %collective-permute-done.2.mine_ref), channel_id=1, source_target_pairs={{0,8},{8,0},{16,24},{24,16},{1,9},{9,1},{17,25},{25,17},{2,10},{10... | collective-permute-start | bytes 589832 | tf_op jit(solution)/shard_map/ppermute | solution.py:526
  14.1 3.4 %copy-start = (bf16[1024,4096]{1,0:T(8,128)(2,1)S(1)}, bf16[1024,4096]{1,0:T(8,128)(2,1)}, u32[]{:S(2)}) copy-start(bf16[1024,4096]{1,0:T(8,128)(2,1)} %refs_1_) | copy-start | bytes 25165828
  17.4 1.9 %copy-start.1 = (bf16[512,3,1024]{2,0,1:T(8,128)(2,1)S(1)}, bf16[512,3,1024]{2,0,1:T(8,128)(2,1)}, u32[]{:S(2)}) copy-start(bf16[512,3,1024]{2,0,1:T(8,128)(2,1)} %param.7) | copy-start | bytes 9437188
  22.5 12.1 %collective-permute-start.5 = (bf16[1,2,768,256]{3,2,1,0:T(8,128)(2,1)S(1)}, bf16[1,2,768,256]{3,2,1,0:T(8,128)(2,1)S(1)}, u32[]{:S(2)}, u32[]{:S(2)}) collective-permute-start(bf16[1,2,768,256]{3,2,1,0:T(8,128)(2,1)S(1)} %project_mix.3), channel_id=1, source_target_pairs={{0,2},{1,5},{2,0},{3,7},{4,6},{5,1},{6,4},{7,3},{8,10},{9,13},{10,... | collective-permute-start | bytes 2359304 | tf_op jit(solution)/shard_map/ppermute | solution.py:531
  25.7 21.1 %collective-permute-start.7 = (bf16[1,2,768,256]{3,2,1,0:T(8,128)(2,1)S(1)}, bf16[1,2,768,256]{3,2,1,0:T(8,128)(2,1)S(1)}, u32[]{:S(2)}, u32[]{:S(2)}) collective-permute-start(bf16[1,2,768,256]{3,2,1,0:T(8,128)(2,1)S(1)} %project_mix.4), channel_id=1, source_target_pairs={{0,2},{1,5},{2,0},{3,7},{4,6},{5,1},{6,4},{7,3},{8,10},{9,13},{10,... | collective-permute-start | bytes 2359304 | tf_op jit(solution)/shard_map/ppermute | solution.py:534
  28.9 9.8 %copy-start.3 = (f32[3,3,1024]{2,1,0:T(4,128)S(1)}, f32[3,3,1024]{2,1,0:T(4,128)}, u32[]{:S(2)}) copy-start(f32[3,3,1024]{2,1,0:T(4,128)} %filt_ref.1) | copy-start | bytes 110596
  35.8 2.9 %collective-permute-start.6 = (bf16[4,16,1024]{2,1,0:T(8,128)(2,1)S(1)}, bf16[4,16,1024]{2,1,0:T(8,128)(2,1)S(1)}, u32[]{:S(2)}, u32[]{:S(2)}) collective-permute-start(bf16[4,16,1024]{2,1,0:T(8,128)(2,1)S(1)} %last_rows.1), channel_id=1, source_target_pairs={{0,1},{1,0},{2,3},{3,2},{4,5},{5,4},{6,7},{7,6},{8,9},{9,8},{10,11... | collective-permute-start | bytes 393224 | tf_op jit(solution)/shard_map/ppermute | solution.py:542
  35.9 15.5 %collective-permute-start.10 = (bf16[768,256]{1,0:T(8,128)(2,1)S(1)}, bf16[768,256]{1,0:T(8,128)(2,1)S(1)}, u32[]{:S(2)}, u32[]{:S(2)}) collective-permute-start(bf16[768,256]{1,0:T(8,128)(2,1)S(1)} %get-tuple-element.79), channel_id=1, source_target_pairs={{0,4},{1,3},{2,6},{3,1},{4,0},{5,7},{6,2},{7,5},{8,12},{9,11},{10,... | collective-permute-start | bytes 1179656 | tf_op jit(solution)/shard_map/ppermute | solution.py:538
  37.4 13.9 %collective-permute-start.11 = (bf16[768,256]{1,0:T(8,128)(2,1)S(1)}, bf16[768,256]{1,0:T(8,128)(2,1)S(1)}, u32[]{:S(2)}, u32[]{:S(2)}) collective-permute-start(bf16[768,256]{1,0:T(8,128)(2,1)S(1)} %get-tuple-element.94), channel_id=1, source_target_pairs={{0,5},{1,2},{2,7},{3,0},{4,1},{5,6},{6,3},{7,4},{8,13},{9,10},{10,... | collective-permute-start | bytes 1179656 | tf_op jit(solution)/shard_map/ppermute | solution.py:539
  41.6 9.7 %copy-start.4 = (f32[8,1024]{1,0:T(8,128)S(1)}, f32[8,1024]{1,0:T(8,128)}, u32[]{:S(2)}) copy-start(f32[8,1024]{1,0:T(8,128)} %decay_ref.1) | copy-start | bytes 98308
  41.7 9.7 %copy-start.5 = (f32[8,1024]{1,0:T(8,128)S(1)}, f32[8,1024]{1,0:T(8,128)}, u32[]{:S(2)}) copy-start(f32[8,1024]{1,0:T(8,128)} %residue_ref.1) | copy-start | bytes 98308
  47.6 3.8 %collective-permute-start.9 = (bf16[768,256]{1,0:T(8,128)(2,1)S(1)}, bf16[768,256]{1,0:T(8,128)(2,1)S(1)}, u32[]{:S(2)}, u32[]{:S(2)}) collective-permute-start(bf16[768,256]{1,0:T(8,128)(2,1)S(1)} %get-tuple-element.93), channel_id=1, source_target_pairs={{0,1},{1,0},{2,3},{3,2},{4,5},{5,4},{6,7},{7,6},{8,9},{9,8},{10,11... | collective-permute-start | bytes 1179656 | tf_op jit(solution)/shard_map/ppermute | solution.py:547
  47.7 9.0 %collective-permute-start.8 = (bf16[192,1280]{1,0:T(8,128)(2,1)S(1)}, bf16[192,1280]{1,0:T(8,128)(2,1)S(1)}, u32[]{:S(2)}, u32[]{:S(2)}) collective-permute-start(bf16[192,1280]{1,0:T(8,128)(2,1)S(1)} %get-tuple-element.91), channel_id=1, source_target_pairs={{0,2},{1,5},{2,0},{3,7},{4,6},{5,1},{6,4},{7,3},{8,10},{9,13},{10,... | collective-permute-start | bytes 1474568 | tf_op jit(solution)/shard_map/ppermute | solution.py:549
  54.3 2.3 %collective-permute-start.12 = (bf16[4,192,128]{2,1,0:T(8,128)(2,1)S(1)}, bf16[4,192,128]{2,1,0:T(8,128)(2,1)S(1)}, u32[]{:S(2)}, u32[]{:S(2)}) collective-permute-start(bf16[4,192,128]{2,1,0:T(8,128)(2,1)S(1)} %get-tuple-element.96), channel_id=1, source_target_pairs={{0,1},{1,0},{2,3},{3,2},{4,5},{5,4},{6,7},{7,6},{8,9},{9,8},{10,11... | collective-permute-start | bytes 589832 | tf_op jit(solution)/shard_map/ppermute | solution.py:553
  57.3 15.0 %collective-permute-start.13 = (bf16[192,1024]{1,0:T(8,128)(2,1)S(1)}, bf16[192,1024]{1,0:T(8,128)(2,1)S(1)}, u32[]{:S(2)}, u32[]{:S(2)}) collective-permute-start(bf16[192,1024]{1,0:T(8,128)(2,1)S(1)} %get-tuple-element.97), channel_id=1, source_target_pairs={{0,4},{1,3},{2,6},{3,1},{4,0},{5,7},{6,2},{7,5},{8,12},{9,11},{10,... | collective-permute-start | bytes 1179656 | tf_op jit(solution)/shard_map/ppermute | solution.py:555
  58.9 9.9 %collective-permute-start.14 = (bf16[192,768]{1,0:T(8,128)(2,1)S(1)}, bf16[192,768]{1,0:T(8,128)(2,1)S(1)}, u32[]{:S(2)}, u32[]{:S(2)}) collective-permute-start(bf16[192,768]{1,0:T(8,128)(2,1)S(1)} %get-tuple-element.98), channel_id=1, source_target_pairs={{0,2},{1,5},{2,0},{3,7},{4,6},{5,1},{6,4},{7,3},{8,10},{9,13},{10,... | collective-permute-start | bytes 884744 | tf_op jit(solution)/shard_map/ppermute | solution.py:550
  60.3 11.9 %collective-permute-start.15 = (bf16[2,192,128]{2,1,0:T(8,128)(2,1)S(1)}, bf16[2,192,128]{2,1,0:T(8,128)(2,1)S(1)}, u32[]{:S(2)}, u32[]{:S(2)}) collective-permute-start(bf16[2,192,128]{2,1,0:T(8,128)(2,1)S(1)} %get-tuple-element.100), channel_id=1, source_target_pairs={{0,4},{1,3},{2,6},{3,1},{4,0},{5,7},{6,2},{7,5},{8,12},{9,11},{10,... | collective-permute-start | bytes 294920 | tf_op jit(solution)/shard_map/ppermute | solution.py:556
  60.9 11.4 %collective-permute-start.16 = (bf16[2,192,128]{2,1,0:T(8,128)(2,1)S(1)}, bf16[2,192,128]{2,1,0:T(8,128)(2,1)S(1)}, u32[]{:S(2)}, u32[]{:S(2)}) collective-permute-start(bf16[2,192,128]{2,1,0:T(8,128)(2,1)S(1)} %get-tuple-element.101), channel_id=1, source_target_pairs={{0,2},{1,5},{2,0},{3,7},{4,6},{5,1},{6,4},{7,3},{8,10},{9,13},{10,... | collective-permute-start | bytes 294920 | tf_op jit(solution)/shard_map/ppermute | solution.py:556
  61.4 10.9 %collective-permute-start.17 = (bf16[2,192,128]{2,1,0:T(8,128)(2,1)S(1)}, bf16[2,192,128]{2,1,0:T(8,128)(2,1)S(1)}, u32[]{:S(2)}, u32[]{:S(2)}) collective-permute-start(bf16[2,192,128]{2,1,0:T(8,128)(2,1)S(1)} %get-tuple-element.102), channel_id=1, source_target_pairs={{0,6},{1,7},{2,4},{3,5},{4,2},{5,3},{6,0},{7,1},{8,14},{9,15},{10,... | collective-permute-start | bytes 294920 | tf_op jit(solution)/shard_map/ppermute | solution.py:556
  74.1 10.9 %collective-permute-start.18 = (bf16[192,1024]{1,0:T(8,128)(2,1)S(1)}, bf16[192,1024]{1,0:T(8,128)(2,1)S(1)}, u32[]{:S(2)}, u32[]{:S(2)}) collective-permute-start(bf16[192,1024]{1,0:T(8,128)(2,1)S(1)} %get-tuple-element.105), channel_id=1, source_target_pairs={{0,8},{8,0},{16,24},{24,16},{1,9},{9,1},{17,25},{25,17},{2,10},{10... | collective-permute-start | bytes 1179656 | tf_op jit(solution)/shard_map/ppermute | solution.py:464
  75.6 23.8 %collective-permute-start.19 = (bf16[192,1024]{1,0:T(8,128)(2,1)S(1)}, bf16[192,1024]{1,0:T(8,128)(2,1)S(1)}, u32[]{:S(2)}, u32[]{:S(2)}) collective-permute-start(bf16[192,1024]{1,0:T(8,128)(2,1)S(1)} %get-tuple-element.108), channel_id=1, source_target_pairs={{8,16},{16,8},{9,17},{17,9},{10,18},{18,10},{11,19},{19,11},{12,20... | collective-permute-start | bytes 1179656 | tf_op jit(solution)/shard_map/ppermute | solution.py:466
  77.4 15.8 %collective-permute-start.21 = (bf16[192,1024]{1,0:T(8,128)(2,1)S(1)}, bf16[192,1024]{1,0:T(8,128)(2,1)S(1)}, u32[]{:S(2)}, u32[]{:S(2)}) collective-permute-start(bf16[192,1024]{1,0:T(8,128)(2,1)S(1)} %get-tuple-element.108), channel_id=1, source_target_pairs={{0,8},{24,16},{1,9},{25,17},{2,10},{26,18},{3,11},{27,19},{4,12},{... | collective-permute-start | bytes 1179656 | tf_op jit(solution)/shard_map/ppermute | solution.py:469
  83.7 15.7 %collective-permute-start.20 = (bf16[192,1024]{1,0:T(8,128)(2,1)S(1)}, bf16[192,1024]{1,0:T(8,128)(2,1)S(1)}, u32[]{:S(2)}, u32[]{:S(2)}) collective-permute-start(bf16[192,1024]{1,0:T(8,128)(2,1)S(1)} %out_columns.3.far_ref), channel_id=1, source_target_pairs={{0,16},{24,8},{1,17},{25,9},{2,18},{26,10},{3,19},{27,11},{4,20},{... | collective-permute-start | bytes 1179656 | tf_op jit(solution)/shard_map/ppermute | solution.py:468
  85.7 19.8 %collective-permute-start.22 = (bf16[192,1024]{1,0:T(8,128)(2,1)S(1)}, bf16[192,1024]{1,0:T(8,128)(2,1)S(1)}, u32[]{:S(2)}, u32[]{:S(2)}) collective-permute-start(bf16[192,1024]{1,0:T(8,128)(2,1)S(1)} %both.1), channel_id=1, source_target_pairs={{8,24},{16,0},{9,25},{17,1},{10,26},{18,2},{11,27},{19,3},{12,28},... | collective-permute-start | bytes 1179656 | tf_op jit(solution)/shard_map/ppermute | solution.py:476

commit v5 on v4

--- a/solution.py
+++ b/solution.py
@@ -137,28 +137,21 @@
     return local(kernel, "join_rows", [((2 * half, wide), mine.dtype)], order, [mine, other])
 
 
-def stage(*arrays):
-    count = len(arrays)
-
-    def kernel(*refs):
-        sems = refs[2 * count]
-        copies = [
-            pltpu.make_async_copy(refs[i], refs[count + i], sems.at[i]) for i in range(count)
-        ]
-        for copy in copies:
-            copy.start()
-        for copy in copies:
-            copy.wait()
+def stage(array):
+    def kernel(array_ref, out_ref, sem):
+        copy = pltpu.make_async_copy(array_ref, out_ref, sem)
+        copy.start()
+        copy.wait()
 
     return pl.pallas_call(
         kernel,
-        out_shape=[jax.ShapeDtypeStruct(x.shape, x.dtype) for x in arrays],
-        in_specs=[pl.BlockSpec(memory_space=pl.ANY)] * count,
-        out_specs=[pl.BlockSpec(memory_space=pltpu.VMEM)] * count,
-        scratch_shapes=[pltpu.SemaphoreType.DMA((count,))],
+        out_shape=jax.ShapeDtypeStruct(array.shape, array.dtype),
+        in_specs=[pl.BlockSpec(memory_space=pl.ANY)],
+        out_specs=pl.BlockSpec(memory_space=pltpu.VMEM),
+        scratch_shapes=[pltpu.SemaphoreType.DMA],
         compiler_params=pltpu.CompilerParams(vmem_limit_bytes=VMEM_LIMIT),
         name="stage",
-    )(*arrays)
+    )(array)
 
 
 def gather_rows(core, x_refs, rows):
@@ -168,7 +161,7 @@
             rows[core ^ h, i * high : (i + 1) * high, :] = x_ref[:, h * depth : (h + 1) * depth]
 
 
-def project_mix(order, xs, own, other, slots, kind):
+def project_mix(order, xs, own, other, slots, kind, ends=0):
     chips = len(xs)
     streams, depth, chans = own.shape
     high = xs[0].shape[0]
@@ -176,9 +169,12 @@
     half = wide // 2
 
     def kernel(order, *refs):
-        x_refs, (own_ref, other_ref, out_ref, rows) = refs[:chips], refs[chips:]
+        x_refs, (own_ref, other_ref, out_ref, *end_refs, rows) = refs[:chips], refs[chips:]
         core = order[2 * chips]
         gather_rows(core, x_refs, rows)
+        for end_ref in end_refs:
+            for s in range(chips):
+                end_ref[s] = x_refs[s][high - ends :, :]
         for i, slot in enumerate(slots):
             at = columns(order[slot], wide)
             for g in range(1, streams):
@@ -191,17 +187,8 @@
 
     shape = (len(slots), 2, chips * high, (streams - 1) * half)
     scratch = [pltpu.VMEM((2, chips * high, depth), BF16)]
-    return local(kernel, "project_mix", [(shape, kind)], order, [*xs, own, other], scratch)
-
-
-def last_rows(order, xs, count):
-    high, wide = xs[0].shape
-
-    def kernel(order, *refs):
-        for s in range(len(xs)):
-            refs[-1][s] = refs[s][high - count :, :]
-
-    return local(kernel, "last_rows", [((len(xs), count, wide), BF16)], order, xs)
+    shapes = [(shape, kind)] + ([((chips, ends, 2 * depth), BF16)] if ends else [])
+    return local(kernel, "project_mix", shapes, order, [*xs, own, other], scratch)
 
 
 def project_query(order, xs, before, own, other, short_filter):
@@ -212,7 +199,6 @@
     step = some + high
     taps = short_filter.shape[0]
     tile = min(chans, 256)
-    extra = tile if chans > tile else 0
 
     def kernel(order, *refs):
         x_refs = refs[:chips]
@@ -236,17 +222,9 @@
                 value = filt_ref[0, 0:1, at] * total[first : first + high, :]
                 for j in range(1, taps):
                     value = value + filt_ref[j, 0:1, at] * total[first - j : first - j + high, :]
-                if i < 2:
-                    out_refs[i][:, at] = value
-                elif i == 3:
-                    out_refs[3][:, at] = value.astype(BF16)
-                elif at.start < extra:
-                    out_refs[3][:, chans + at.start : chans + at.stop] = value.astype(BF16)
-                else:
-                    out_refs[2][:, at.start - extra : at.stop - extra] = value.astype(BF16)
-
-    shapes = [((high, chans), F32)] * 2
-    shapes += [((high, chans - extra), BF16), ((high, chans + extra), BF16)]
+                out_refs[i][:, at] = value.astype(out_refs[i].dtype)
+
+    shapes = [((high, chans), F32 if i < 2 else BF16) for i in range(chips)]
     scratch = [
         pltpu.VMEM((2, chips * step, depth), BF16),
         pltpu.VMEM((chips + 1, some, 2 * depth), BF16),
@@ -419,11 +397,8 @@
         query_refs, long_refs = refs[: len(queries)], refs[len(queries) : len(queries) + chips]
         w_ref, gated_ref, pair_ref, side_ref, query = refs[len(queries) + chips :]
         core = scalars[2 * chips]
-        own_ref, second_ref, both_ref, first_ref = query_refs
-        extra = both_ref.shape[1] - chans
-        query[...] = own_ref[...] + second_ref[...].astype(F32)
-        query[:, :extra] += both_ref[:, chans:].astype(F32)
-        query[:, extra:] += first_ref[...].astype(F32)
+        own_ref, second_ref, first_ref = query_refs
+        query[...] = own_ref[...] + second_ref[...].astype(F32) + first_ref[...].astype(F32)
         for s, ref in enumerate(long_refs):
             for h in range(2):
                 at = columns(2 * scalars[s] + (core ^ h), part)
@@ -466,14 +441,15 @@
     middle_in = lax.ppermute(side, "dp", [(1, 2), (2, 1)])
     side, far = lax.optimization_barrier((side, far))
     end_in = lax.ppermute(far, "dp", [(0, 2), (3, 1)])
-    side_in = lax.ppermute(side, "dp", [(0, 1), (3, 2)])
+
+    def add(picks, far_ref, pair_ref, side_ref, out_ref):
+        value = far_ref[...].astype(F32) + pair_ref[...].astype(F32)
+        out_ref[...] = jnp.where(picks[4] == 1, value.astype(BF16), side_ref[...])
+
+    last = local(add, "last_step", [(far.shape, BF16)], picks, [far, pair_in, side])
+    gated, last = lax.optimization_barrier((gated, last))
+    last_in = lax.ppermute(last, "dp", [(0, 1), (1, 3), (2, 0), (3, 2)])
     own = out_columns(picks, 3, gated, w_out, groups, F32)
-
-    def add(picks, far_ref, pair_ref, out_ref):
-        out_ref[...] = (far_ref[...].astype(F32) + pair_ref[...].astype(F32)).astype(BF16)
-
-    both = local(add, "both", [(far.shape, BF16)], picks, [far, pair_in])
-    far_in = lax.ppermute(both, "dp", [(1, 3), (2, 0)])
 
     def early(picks, own_ref, pair_ref, *refs):
         inner = picks[4] == 1
@@ -482,12 +458,11 @@
             value = value + ref[...].astype(F32)
         refs[-1][...] = value
 
-    def total(picks, early_ref, far_ref, out_ref):
-        out_ref[...] = (early_ref[...] + far_ref[...].astype(F32)).astype(BF16)
-
-    arrays = [own, pair_in, middle_in, end_in, side_in]
-    own = local(early, "early", [(own.shape, F32)], picks, arrays)
-    return local(total, "total", [(own.shape, BF16)], picks, [own, far_in])
+    def total(picks, early_ref, last_ref, out_ref):
+        out_ref[...] = (early_ref[...] + last_ref[...].astype(F32)).astype(BF16)
+
+    own = local(early, "early", [(own.shape, F32)], picks, [own, pair_in, middle_in, end_in])
+    return local(total, "total", [(own.shape, BF16)], picks, [own, last_in])
 
 
 def on_device_chips(tokens, w_in, short_filter, mode_decay, residue, w_out):
@@ -520,8 +495,8 @@
 
     other_w = lax.ppermute(own_w, "ctx", swap)
     xs = cut(order, tokens, chips)
-    own_w, w_out, xs = lax.optimization_barrier((own_w, w_out, xs))
-    own_w, w_out = stage(own_w, w_out)
+    own_w, xs = lax.optimization_barrier((own_w, xs))
+    own_w = stage(own_w)
     half = lax.ppermute(xs[3], "ctx", route(3))
     other = lax.ppermute(half, "dp", [(i, i ^ 1) for i in range(groups)])
     xs = [xs[0]] + [lax.ppermute(xs[s], "ctx", route(s)) for s in (1, 2)]
@@ -533,15 +508,17 @@
     first = project_mix(order, xs, own_w, other_w, [2], BF16)
     first_in = lax.ppermute(first, "ctx", route(2))
     xs, first = lax.optimization_barrier((xs, first))
-    rest = project_mix(order, xs, own_w, other_w, [1, 0], F32)
+    rest, ends = project_mix(order, xs, own_w, other_w, [1, 0], F32, 16)
     second, swap_second = second_share(order, rest, both_in, chips)
     second_in = lax.ppermute(second, "ctx", route(1))
     swap_second = lax.ppermute(swap_second, "ctx", [(i, j ^ 1) for i, j in route(1)])
 
-    xs, second = lax.optimization_barrier((xs, second))
-    before = lax.ppermute(last_rows(order, xs, 16), "ctx", swap)
+    xs, ends, second = lax.optimization_barrier((xs, ends, second))
+    before = lax.ppermute(ends, "ctx", swap)
     q_own, q_next, q_first, q_both = project_query(order, xs, before, own_w, other_w, short_filter)
-    q_own, rest = lax.optimization_barrier((q_own, rest))
+    q_own, w_out = lax.optimization_barrier((q_own, w_out))
+    w_out = stage(w_out)
+    q_own, w_out, rest = lax.optimization_barrier((q_own, w_out, rest))
 
     own, other_half = first_share(order, rest, first_in, chips)
     other_half = lax.ppermute(other_half, "ctx", swap)
@@ -554,7 +531,7 @@
     q_second, *long_parts = payloads(order, q_next, q_both, keep, other_long)
     q_second = lax.ppermute(q_second, "ctx", route(1))
     long_parts = [long_parts[0]] + [lax.ppermute(long_parts[s], "ctx", route(s)) for s in (1, 2, 3)]
-    queries = [q_own, q_second, q_both, q_first]
+    queries = [q_own, q_second, q_first]
     gated, pair, side = gate(both_scalars, queries, long_parts, w_out, groups)
     return output_over_line(picks, gated, pair, side, w_out, groups)
 

time: 107 us -> 106 us (level)
  waiting for transfers between devices: 45.3 us -> 50.8 us
  local copies, waits for them, and re-layouts: 6.97 us -> 3.59 us
  starting transfers between devices: 30.9 us -> 28.7 us
    ppermute x3 -> x2, starting transfers between devices: 7.67 us -> 1.7 us  [the longest x1 1.63 us: output_over_line(): last_in = lax.ppermute(last, 'dp', [(0, 1), (1, 3), (2, 0), (3, 2)])]
    ppermute x1, starting transfers between devices: 1.31 us -> 5.75 us  [output_over_line(): end_in = lax.ppermute(far, 'dp', [(0, 2), (3, 1)])]
    unnamed x12 -> x14, local copies, waits for them, and re-layouts: 6.7 us -> 3.33 us
    ppermute x1, waiting for transfers between devices: 0.01 us -> 2.72 us  [output_over_line(): pair_in = lax.ppermute(pair, 'dp', [(0, 1), (1, 0), (2, 3), (3, 2)])]
    ppermute x1, waiting for transfers between devices: 0.01 us -> 2.46 us  [on_device_chips(): other = lax.ppermute(half, 'dp', [(i, i ^ 1) for i in range(groups)])]
    ppermute x3 -> x2, waiting for transfers between devices: 10.4 us -> 12.6 us  [the longest x1 12.6 us: output_over_line(): last_in = lax.ppermute(last, 'dp', [(0, 1), (1, 3), (2, 0), (3, 2)])]
    ppermute x1, waiting for transfers between devices: 2.23 us -> 0.08 us  [on_device_chips(): q_both = lax.ppermute(q_both, 'ctx', route(2))]
    ppermute x1, waiting for transfers between devices: 6.16 us -> 4.11 us  [output_over_line(): end_in = lax.ppermute(far, 'dp', [(0, 2), (3, 1)])]
  transfers between devices with their start and end apart: 23 -> 22, of which waited for: 10 -> 14; matrix products, arithmetic and copies ran while one was open for 0% -> 0% of each run, Pallas kernels for 17% -> 17%
where the time goes in v5:
time: 106 us
  waiting for transfers between devices  50.8 us (48%)
  starting transfers between devices  28.7 us (27%)
  Pallas kernels  22.7 us (21%)
  local copies, waits for them, and re-layouts  3.59 us (3%)
    pallas_call x16, Pallas kernels, local(): pl.pallas_call(kernel, out_shape=out if len(out) > 1 else out[0], in_spec...  21.9 us
    ppermute x1, waiting for transfers between devices, output_over_line(): last_in = lax.ppermute(last, 'dp', [(0, 1), (1, 3), (2, 0), (3, 2)])  12.6 us
    ppermute x1, waiting for transfers between devices, on_device_chips(): first_in = lax.ppermute(first, 'ctx', route(2))  6.61 us
    ppermute x1, starting transfers between devices, output_over_line(): end_in = lax.ppermute(far, 'dp', [(0, 2), (3, 1)])  5.75 us
    ppermute x1, waiting for transfers between devices, on_device_chips(): both_in = lax.ppermute(both, 'ctx', route(2))  5.55 us
    ppermute x3, waiting for transfers between devices, on_device_chips(): lax.ppermute(long_parts[s], 'ctx', route(s))  5.16 us
    ppermute x1, waiting for transfers between devices, on_device_chips(): half = lax.ppermute(xs[3], 'ctx', route(3))  5.15 us
    ppermute x1, waiting for transfers between devices, output_over_line(): end_in = lax.ppermute(far, 'dp', [(0, 2), (3, 1)])  4.11 us
  transfers between devices with their start and end apart: 22, of which 14 were waited for; matrix products, arithmetic and copies ran while one was open for 0% of the time, Pallas kernels for 17%

profile of v5, /device:TPU:0, one launch (start us, length us, event | category | flops | bytes accessed | tf_op | source)
XLA Modules:
  0.0 106.1 jit_solution(14815171703794681288)
XLA Ops:
  0.0 0.5 collective-permute-start.4
  0.5 0.1 stack.59.order
  0.5 0.1 concatenate.4.scalars
  0.6 0.1 stack.65.picks
  0.7 1.4 %copy-done.1 = bf16[192,4096]{1,0:T(8,128)(2,1)S(1)} copy-done((bf16[192,4096]{1,0:T(8,128)(2,1)S(1)}, bf16[192,4096]{1,0:T(8,128)(2,1)}, u32[]{:S(2)}) %copy-start.1) | copy-done | bytes 1572888
  2.1 0.6 cut.1
  2.8 3.5 %collective-permute-start.2 = (bf16[96,1024]{1,0:T(8,128)(2,1)S(1)}, bf16[96,1024]{1,0:T(8,128)(2,1)S(1)}, u32[]{:S(2)}, u32[]{:S(2)}) collective-permute-start(bf16[96,1024]{1,0:T(8,128)(2,1)S(1)} %get-tuple-element.72), channel_id=1, source_target_pairs={{0,6},{1,7},{2,4},{3,5},{4,2},{5,3},{6,0},{7,1},{8,14},{9,15},{10,... | collective-permute-start | bytes 589832 | tf_op jit(solution)/shard_map/ppermute | solution.py:500
  6.3 0.5 collective-permute-start
  6.8 0.1 collective-permute-start.1
  6.9 5.2 %collective-permute-done.2.mine_ref = bf16[96,1024]{1,0:T(8,128)(2,1)S(1)} collective-permute-done((bf16[96,1024]{1,0:T(8,128)(2,1)S(1)}, bf16[96,1024]{1,0:T(8,128)(2,1)S(1)}, u32[]{:S(2)}, u32[]{:S(2)}) %collective-permute-start.2) | collective-permute-done | bytes 196640 | tf_op jit(solution)/shard_map/ppermute | solution.py:500
  12.1 2.0 %collective-permute-start.3 = (bf16[96,1024]{1,0:T(8,128)(2,1)S(1)}, bf16[96,1024]{1,0:T(8,128)(2,1)S(1)}, u32[]{:S(2)}, u32[]{:S(2)}) collective-permute-start(bf16[96,1024]{1,0:T(8,128)(2,1)S(1)} %collective-permute-done.2.mine_ref), channel_id=1, source_target_pairs={{0,8},{8,0},{16,24},{24,16},{1,9},{9,1},{17,25},{25,17},{2,10},{10... | collective-permute-start | bytes 589832 | tf_op jit(solution)/shard_map/ppermute | solution.py:501
  14.1 1.9 %copy-done = bf16[512,3,1024]{2,0,1:T(8,128)(2,1)S(1)} copy-done((bf16[512,3,1024]{2,0,1:T(8,128)(2,1)S(1)}, bf16[512,3,1024]{2,0,1:T(8,128)(2,1)}, u32[]{:S(2)}) %copy-start) | copy-done | bytes 3145752
  15.9 0.2 stage.2.refs_4_.refs_5_
  16.2 2.5 %collective-permute-done.3.other_ref = bf16[96,1024]{1,0:T(8,128)(2,1)S(1)} collective-permute-done((bf16[96,1024]{1,0:T(8,128)(2,1)S(1)}, bf16[96,1024]{1,0:T(8,128)(2,1)S(1)}, u32[]{:S(2)}, u32[]{:S(2)}) %collective-permute-start.3) | collective-permute-done | bytes 196640 | tf_op jit(solution)/shard_map/ppermute | solution.py:501
  18.6 0.6 join_rows.1.refs_3_
  19.2 1.1 %collective-permute-done.refs_1_ = bf16[192,1024]{1,0:T(8,128)(2,1)S(1)} collective-permute-done((bf16[192,1024]{1,0:T(8,128)(2,1)S(1)}, bf16[192,1024]{1,0:T(8,128)(2,1)S(1)}, u32[]{:S(2)}, u32[]{:S(2)}) %collective-permute-start) | collective-permute-done | bytes 393248 | tf_op jit(solution)/shard_map/ppermute | solution.py:502
  20.3 0.3 collective-permute-done.1.refs_2_
  20.6 0.0 collective-permute-done.4.refs_5_.refs_6_
  20.6 1.7 %project_mix.3 = bf16[1,2,768,256]{3,2,1,0:T(8,128)(2,1)S(1)} custom-call(s32[11]{0:T(128)S(1)} %stack.59.order, bf16[192,1024]{1,0:T(8,128)(2,1)S(1)} %get-tuple-element.85.refs_0_, bf16[192,1024]{1,0:T(8,128)(2,1)S(1)} %collective-permute-done.refs_1_, bf16[192,1024]{1,0:T(8,128)(2,1)S(1)} %collective-permute-done.1.refs_2_, ...), custom_call_target="tpu_custom_call" | custom-call | tf_op jit(solution)/shard_map/project_mix/pallas_call | solution.py:101
  22.3 1.6 %collective-permute-start.5 = (bf16[1,2,768,256]{3,2,1,0:T(8,128)(2,1)S(1)}, bf16[1,2,768,256]{3,2,1,0:T(8,128)(2,1)S(1)}, u32[]{:S(2)}, u32[]{:S(2)}) collective-permute-start(bf16[1,2,768,256]{3,2,1,0:T(8,128)(2,1)S(1)} %project_mix.3), channel_id=1, source_target_pairs={{0,2},{1,5},{2,0},{3,7},{4,6},{5,1},{6,4},{7,3},{8,10},{9,13},{10,... | collective-permute-start | bytes 2359304 | tf_op jit(solution)/shard_map/ppermute | solution.py:506
  23.9 1.7 %project_mix.4 = bf16[1,2,768,256]{3,2,1,0:T(8,128)(2,1)S(1)} custom-call(s32[11]{0:T(128)S(1)} %stack.59.order, bf16[192,1024]{1,0:T(8,128)(2,1)S(1)} %get-tuple-element.85.refs_0_, bf16[192,1024]{1,0:T(8,128)(2,1)S(1)} %collective-permute-done.refs_1_, bf16[192,1024]{1,0:T(8,128)(2,1)S(1)} %collective-permute-done.1.refs_2_, ...), custom_call_target="tpu_custom_call" | custom-call | tf_op jit(solution)/shard_map/project_mix/pallas_call | solution.py:101
  25.6 0.6 collective-permute-start.7
  26.2 2.6 %project_mix.5 = (f32[2,2,768,256]{3,2,1,0:T(8,128)S(1)}, bf16[4,16,1024]{2,1,0:T(8,128)(2,1)S(1)}) custom-call(s32[11]{0:T(128)S(1)} %stack.59.order, bf16[192,1024]{1,0:T(8,128)(2,1)S(1)} %get-tuple-element.85.refs_0_, bf16[192,1024]{1,0:T(8,128)(2,1)S(1)} %collective-permute-done.refs_1_, bf16[192,1024]{1,0:T(8,128)(2,1)S(1)} %collective-permute-done.1.refs_2_, ...), custom_call_target="tpu_custom_call" | custom-call | tf_op jit(solution)/shard_map/project_mix/pallas_call | solution.py:101
  28.8 0.0 copy-start.2
  28.8 5.5 %collective-permute-done.5.both_ref = bf16[1,2,768,256]{3,2,1,0:T(8,128)(2,1)S(1)} collective-permute-done((bf16[1,2,768,256]{3,2,1,0:T(8,128)(2,1)S(1)}, bf16[1,2,768,256]{3,2,1,0:T(8,128)(2,1)S(1)}, u32[]{:S(2)}, u32[]{:S(2)}) %collective-permute-start.5) | collective-permute-done | bytes 786464 | tf_op jit(solution)/shard_map/ppermute | solution.py:506
  34.3 0.7 second_share.1
  35.0 0.1 collective-permute-start.6
  35.1 1.5 %collective-permute-start.10 = (bf16[768,256]{1,0:T(8,128)(2,1)S(1)}, bf16[768,256]{1,0:T(8,128)(2,1)S(1)}, u32[]{:S(2)}, u32[]{:S(2)}) collective-permute-start(bf16[768,256]{1,0:T(8,128)(2,1)S(1)} %get-tuple-element.84), channel_id=1, source_target_pairs={{0,4},{1,3},{2,6},{3,1},{4,0},{5,7},{6,2},{7,5},{8,12},{9,11},{10,... | collective-permute-start | bytes 1179656 | tf_op jit(solution)/shard_map/ppermute | solution.py:513
  36.6 0.5 collective-permute-start.11
  37.1 3.0 %project_query.1 = (f32[192,1024]{1,0:T(8,128)S(1)}, f32[192,1024]{1,0:T(8,128)S(1)}, bf16[192,1024]{1,0:T(8,128)(2,1)S(1)}, bf16[192,1024]{1,0:T(8,128)(2,1)S(1)}) custom-call(s32[11]{0:T(128)S(1)} %stack.59.order, bf16[192,1024]{1,0:T(8,128)(2,1)S(1)} %get-tuple-element.85.refs_0_, bf16[192,1024]{1,0:T(8,128)(2,1)S(1)} %collective-permute-done.refs_1_, ...), custom_call_target="tpu_custom_call" | custom-call | tf_op jit(solution)/shard_map/project_query/pallas_call | solution.py:101
  40.1 0.6 stage.3.refs_7_.w_ref
  40.6 0.0 copy-start.3
  40.7 0.0 copy-start.4
  40.7 6.6 %collective-permute-done.7.first_ref = bf16[1,2,768,256]{3,2,1,0:T(8,128)(2,1)S(1)} collective-permute-done((bf16[1,2,768,256]{3,2,1,0:T(8,128)(2,1)S(1)}, bf16[1,2,768,256]{3,2,1,0:T(8,128)(2,1)S(1)}, u32[]{:S(2)}, u32[]{:S(2)}) %collective-permute-start.7) | collective-permute-done | bytes 786464 | tf_op jit(solution)/shard_map/ppermute | solution.py:509
  47.3 0.7 first_share.1
  48.0 0.1 collective-permute-start.9
  48.0 1.6 %collective-permute-start.8 = (bf16[192,1024]{1,0:T(8,128)(2,1)S(1)}, bf16[192,1024]{1,0:T(8,128)(2,1)S(1)}, u32[]{:S(2)}, u32[]{:S(2)}) collective-permute-start(bf16[192,1024]{1,0:T(8,128)(2,1)S(1)} %get-tuple-element.99), channel_id=1, source_target_pairs={{0,2},{1,5},{2,0},{3,7},{4,6},{5,1},{6,4},{7,3},{8,10},{9,13},{10,... | collective-permute-start | bytes 1179656 | tf_op jit(solution)/shard_map/ppermute | solution.py:526
  49.6 1.6 %collective-permute-done.11.swap_second_ref = bf16[768,256]{1,0:T(8,128)(2,1)S(1)} collective-permute-done((bf16[768,256]{1,0:T(8,128)(2,1)S(1)}, bf16[768,256]{1,0:T(8,128)(2,1)S(1)}, u32[]{:S(2)}, u32[]{:S(2)}) %collective-permute-start.11) | collective-permute-done | bytes 393248 | tf_op jit(solution)/shard_map/ppermute | solution.py:514
  51.2 2.9 %hyena.1 = (bf16[4,192,128]{2,1,0:T(8,128)(2,1)S(1)}, bf16[4,192,128]{2,1,0:T(8,128)(2,1)S(1)}) custom-call(s32[11]{0:T(128)S(1)} %stack.59.order, f32[768,256]{1,0:T(8,128)S(1)} %get-tuple-element.100.own_ref, bf16[768,256]{1,0:T(8,128)(2,1)S(1)} %collective-permute-done.9.swap_ref, bf16[768,256]{1,0:T(8,128)(2,1)S(1)} %collective-permute-done.10.second_ref, ...), custom_call_target="tpu_custom_call" | custom-call | tf_op jit(solution)/shard_map/hyena/pallas_call | solution.py:101
  54.2 0.1 collective-permute-start.12
  54.2 1.6 %collective-permute-start.14 = (bf16[192,1024]{1,0:T(8,128)(2,1)S(1)}, bf16[192,1024]{1,0:T(8,128)(2,1)S(1)}, u32[]{:S(2)}, u32[]{:S(2)}) collective-permute-start(bf16[192,1024]{1,0:T(8,128)(2,1)S(1)} %get-tuple-element.106), channel_id=1, source_target_pairs={{0,2},{1,5},{2,0},{3,7},{4,6},{5,1},{6,4},{7,3},{8,10},{9,13},{10,... | collective-permute-start | bytes 1179656 | tf_op jit(solution)/shard_map/ppermute | solution.py:527
  55.8 0.1 collective-permute-done.8.in_ref
  55.9 0.0 collective-permute-done.12.other_ref
  55.9 0.6 payloads.1
  56.5 1.5 %collective-permute-start.13 = (bf16[192,1024]{1,0:T(8,128)(2,1)S(1)}, bf16[192,1024]{1,0:T(8,128)(2,1)S(1)}, u32[]{:S(2)}, u32[]{:S(2)}) collective-permute-start(bf16[192,1024]{1,0:T(8,128)(2,1)S(1)} %get-tuple-element.105), channel_id=1, source_target_pairs={{0,4},{1,3},{2,6},{3,1},{4,0},{5,7},{6,2},{7,5},{8,12},{9,11},{10,... | collective-permute-start | bytes 1179656 | tf_op jit(solution)/shard_map/ppermute | solution.py:532
  58.0 0.6 collective-permute-start.15
  58.6 1.5 %collective-permute-start.16 = (bf16[2,192,128]{2,1,0:T(8,128)(2,1)S(1)}, bf16[2,192,128]{2,1,0:T(8,128)(2,1)S(1)}, u32[]{:S(2)}, u32[]{:S(2)}) collective-permute-start(bf16[2,192,128]{2,1,0:T(8,128)(2,1)S(1)} %get-tuple-element.109), channel_id=1, source_target_pairs={{0,2},{1,5},{2,0},{3,7},{4,6},{5,1},{6,4},{7,3},{8,10},{9,13},{10,... | collective-permute-start | bytes 294920 | tf_op jit(solution)/shard_map/ppermute | solution.py:533
  60.1 1.4 %collective-permute-start.17 = (bf16[2,192,128]{2,1,0:T(8,128)(2,1)S(1)}, bf16[2,192,128]{2,1,0:T(8,128)(2,1)S(1)}, u32[]{:S(2)}, u32[]{:S(2)}) collective-permute-start(bf16[2,192,128]{2,1,0:T(8,128)(2,1)S(1)} %get-tuple-element.110), channel_id=1, source_target_pairs={{0,6},{1,7},{2,4},{3,5},{4,2},{5,3},{6,0},{7,1},{8,14},{9,15},{10,... | collective-permute-start | bytes 294920 | tf_op jit(solution)/shard_map/ppermute | solution.py:533
  61.5 3.4 %collective-permute-done.14.refs_2_ = bf16[192,1024]{1,0:T(8,128)(2,1)S(1)} collective-permute-done((bf16[192,1024]{1,0:T(8,128)(2,1)S(1)}, bf16[192,1024]{1,0:T(8,128)(2,1)S(1)}, u32[]{:S(2)}, u32[]{:S(2)}) %collective-permute-start.14) | collective-permute-done | bytes 393248 | tf_op jit(solution)/shard_map/ppermute | solution.py:527
  64.9 2.9 %collective-permute-done.15.refs_4_ = bf16[2,192,128]{2,1,0:T(8,128)(2,1)S(1)} collective-permute-done((bf16[2,192,128]{2,1,0:T(8,128)(2,1)S(1)}, bf16[2,192,128]{2,1,0:T(8,128)(2,1)S(1)}, u32[]{:S(2)}, u32[]{:S(2)}) %collective-permute-start.15) | collective-permute-done | bytes 98336 | tf_op jit(solution)/shard_map/ppermute | solution.py:533
  67.9 2.2 %collective-permute-done.17.refs_6_ = bf16[2,192,128]{2,1,0:T(8,128)(2,1)S(1)} collective-permute-done((bf16[2,192,128]{2,1,0:T(8,128)(2,1)S(1)}, bf16[2,192,128]{2,1,0:T(8,128)(2,1)S(1)}, u32[]{:S(2)}, u32[]{:S(2)}) %collective-permute-start.17) | collective-permute-done | bytes 98336 | tf_op jit(solution)/shard_map/ppermute | solution.py:533
  70.1 1.8 %gate.1 = (bf16[192,1024]{1,0:T(8,128)(2,1)S(1)}, bf16[192,1024]{1,0:T(8,128)(2,1)S(1)}, bf16[192,1024]{1,0:T(8,128)(2,1)S(1)}) custom-call(s32[16]{0:T(128)S(1)} %concatenate.4.scalars, f32[192,1024]{1,0:T(8,128)S(1)} %get-tuple-element.93.refs_0_, bf16[192,1024]{1,0:T(8,128)(2,1)S(1)} %collective-permute-done.13.refs_1_, ...), custom_call_target="tpu_custom_call" | custom-call | tf_op jit(solution)/shard_map/gate/pallas_call | solution.py:101
  71.9 1.6 %collective-permute-start.18 = (bf16[192,1024]{1,0:T(8,128)(2,1)S(1)}, bf16[192,1024]{1,0:T(8,128)(2,1)S(1)}, u32[]{:S(2)}, u32[]{:S(2)}) collective-permute-start(bf16[192,1024]{1,0:T(8,128)(2,1)S(1)} %get-tuple-element.115), channel_id=1, source_target_pairs={{0,8},{8,0},{16,24},{24,16},{1,9},{9,1},{17,25},{25,17},{2,10},{10... | collective-permute-start | bytes 1179656 | tf_op jit(solution)/shard_map/ppermute | solution.py:439
  73.6 0.7 collective-permute-start.19
  74.3 1.1 %out_columns.2.far_ref = bf16[192,1024]{1,0:T(8,128)(2,1)S(1)} custom-call(s32[5]{0:T(128)S(1)} %stack.65.picks, bf16[192,1024]{1,0:T(8,128)(2,1)S(1)} %get-tuple-element.117.x_ref, bf16[1024,4096]{1,0:T(8,128)(2,1)S(1)} %stage.3.refs_7_.w_ref), custom_call_target="tpu_custom_call" | custom-call | tf_op jit(solution)/shard_map/out_columns/pallas_call | solution.py:101
  75.4 5.8 %collective-permute-start.20 = (bf16[192,1024]{1,0:T(8,128)(2,1)S(1)}, bf16[192,1024]{1,0:T(8,128)(2,1)S(1)}, u32[]{:S(2)}, u32[]{:S(2)}) collective-permute-start(bf16[192,1024]{1,0:T(8,128)(2,1)S(1)} %out_columns.2.far_ref), channel_id=1, source_target_pairs={{0,16},{24,8},{1,17},{25,9},{2,18},{26,10},{3,19},{27,11},{4,20},{... | collective-permute-start | bytes 1179656 | tf_op jit(solution)/shard_map/ppermute | solution.py:443
  81.2 2.7 %collective-permute-done.18.pair_ref = bf16[192,1024]{1,0:T(8,128)(2,1)S(1)} collective-permute-done((bf16[192,1024]{1,0:T(8,128)(2,1)S(1)}, bf16[192,1024]{1,0:T(8,128)(2,1)S(1)}, u32[]{:S(2)}, u32[]{:S(2)}) %collective-permute-start.18) | collective-permute-done | bytes 393248 | tf_op jit(solution)/shard_map/ppermute | solution.py:439
  83.9 0.7 last_step.1
  84.5 1.6 %collective-permute-start.21 = (bf16[192,1024]{1,0:T(8,128)(2,1)S(1)}, bf16[192,1024]{1,0:T(8,128)(2,1)S(1)}, u32[]{:S(2)}, u32[]{:S(2)}) collective-permute-start(bf16[192,1024]{1,0:T(8,128)(2,1)S(1)} %last_step.1), channel_id=1, source_target_pairs={{0,8},{8,24},{16,0},{24,16},{1,9},{9,25},{17,1},{25,17},{2,10},{10... | collective-permute-start | bytes 1179656 | tf_op jit(solution)/shard_map/ppermute | solution.py:451
  86.2 1.1 %out_columns.3.own_ref = f32[192,1024]{1,0:T(8,128)S(1)} custom-call(s32[5]{0:T(128)S(1)} %stack.65.picks, bf16[192,1024]{1,0:T(8,128)(2,1)S(1)} %get-tuple-element.117.x_ref, bf16[1024,4096]{1,0:T(8,128)(2,1)S(1)} %stage.3.refs_7_.w_ref), custom_call_target="tpu_custom_call" | custom-call | tf_op jit(solution)/shard_map/out_columns/pallas_call | solution.py:101
  87.3 4.1 %collective-permute-done.20.refs_1_ = bf16[192,1024]{1,0:T(8,128)(2,1)S(1)} collective-permute-done((bf16[192,1024]{1,0:T(8,128)(2,1)S(1)}, bf16[192,1024]{1,0:T(8,128)(2,1)S(1)}, u32[]{:S(2)}, u32[]{:S(2)}) %collective-permute-start.20) | collective-permute-done | bytes 393248 | tf_op jit(solution)/shard_map/ppermute | solution.py:443
  91.4 0.7 early.1.early_ref
  92.2 12.6 %collective-permute-done.21.last_ref = bf16[192,1024]{1,0:T(8,128)(2,1)S(1)} collective-permute-done((bf16[192,1024]{1,0:T(8,128)(2,1)S(1)}, bf16[192,1024]{1,0:T(8,128)(2,1)S(1)}, u32[]{:S(2)}, u32[]{:S(2)}) %collective-permute-start.21) | collective-permute-done | bytes 393248 | tf_op jit(solution)/shard_map/ppermute | solution.py:451
  104.8 1.4 %total.1 = bf16[192,1024]{1,0:T(8,128)(2,1)} custom-call(s32[5]{0:T(128)S(1)} %stack.65.picks, f32[192,1024]{1,0:T(8,128)S(1)} %early.1.early_ref, bf16[192,1024]{1,0:T(8,128)(2,1)S(1)} %collective-permute-done.21.last_ref), custom_call_target="tpu_custom_call" | custom-call | tf_op jit(solution)/shard_map/total/pallas_call | solution.py:101
  (16 shorter events, 0.0 us)
Async XLA Ops:
  0.0 20.6 %collective-permute-start.4 = (bf16[3,512,1024]{2,1,0:T(8,128)(2,1)}, bf16[3,512,1024]{2,1,0:T(8,128)(2,1)S(1)}, u32[]{:S(2)}, u32[]{:S(2)}) collective-permute-start(bf16[3,512,1024]{2,1,0:T(8,128)(2,1)} %bitcast.17), channel_id=1, source_target_pairs={{0,1},{1,0},{2,3},{3,2},{4,5},{5,4},{6,7},{7,6},{8,9},{9,8},{10,11... | collective-permute-start | bytes 9437192 | tf_op jit(solution)/shard_map/ppermute | solution.py:496
  0.7 1.4 %copy-start.1 = (bf16[192,4096]{1,0:T(8,128)(2,1)S(1)}, bf16[192,4096]{1,0:T(8,128)(2,1)}, u32[]{:S(2)}) copy-start(bf16[192,4096]{1,0:T(8,128)(2,1)} %tokens_ref.1) | copy-start | bytes 4718596
  2.8 9.3 %collective-permute-start.2 = (bf16[96,1024]{1,0:T(8,128)(2,1)S(1)}, bf16[96,1024]{1,0:T(8,128)(2,1)S(1)}, u32[]{:S(2)}, u32[]{:S(2)}) collective-permute-start(bf16[96,1024]{1,0:T(8,128)(2,1)S(1)} %get-tuple-element.72), channel_id=1, source_target_pairs={{0,6},{1,7},{2,4},{3,5},{4,2},{5,3},{6,0},{7,1},{8,14},{9,15},{10,... | collective-permute-start | bytes 589832 | tf_op jit(solution)/shard_map/ppermute | solution.py:500
  6.3 14.0 %collective-permute-start = (bf16[192,1024]{1,0:T(8,128)(2,1)S(1)}, bf16[192,1024]{1,0:T(8,128)(2,1)S(1)}, u32[]{:S(2)}, u32[]{:S(2)}) collective-permute-start(bf16[192,1024]{1,0:T(8,128)(2,1)S(1)} %get-tuple-element.70), channel_id=1, source_target_pairs={{0,4},{1,3},{2,6},{3,1},{4,0},{5,7},{6,2},{7,5},{8,12},{9,11},{10,... | collective-permute-start | bytes 1179656 | tf_op jit(solution)/shard_map/ppermute | solution.py:502
  6.8 13.8 %collective-permute-start.1 = (bf16[192,1024]{1,0:T(8,128)(2,1)S(1)}, bf16[192,1024]{1,0:T(8,128)(2,1)S(1)}, u32[]{:S(2)}, u32[]{:S(2)}) collective-permute-start(bf16[192,1024]{1,0:T(8,128)(2,1)S(1)} %get-tuple-element.71), channel_id=1, source_target_pairs={{0,2},{1,5},{2,0},{3,7},{4,6},{5,1},{6,4},{7,3},{8,10},{9,13},{10,... | collective-permute-start | bytes 1179656 | tf_op jit(solution)/shard_map/ppermute | solution.py:502
  12.1 6.6 %collective-permute-start.3 = (bf16[96,1024]{1,0:T(8,128)(2,1)S(1)}, bf16[96,1024]{1,0:T(8,128)(2,1)S(1)}, u32[]{:S(2)}, u32[]{:S(2)}) collective-permute-start(bf16[96,1024]{1,0:T(8,128)(2,1)S(1)} %collective-permute-done.2.mine_ref), channel_id=1, source_target_pairs={{0,8},{8,0},{16,24},{24,16},{1,9},{9,1},{17,25},{25,17},{2,10},{10... | collective-permute-start | bytes 589832 | tf_op jit(solution)/shard_map/ppermute | solution.py:501
  14.1 1.9 %copy-start = (bf16[512,3,1024]{2,0,1:T(8,128)(2,1)S(1)}, bf16[512,3,1024]{2,0,1:T(8,128)(2,1)}, u32[]{:S(2)}) copy-start(bf16[512,3,1024]{2,0,1:T(8,128)(2,1)} %param.7) | copy-start | bytes 9437188
  22.3 12.1 %collective-permute-start.5 = (bf16[1,2,768,256]{3,2,1,0:T(8,128)(2,1)S(1)}, bf16[1,2,768,256]{3,2,1,0:T(8,128)(2,1)S(1)}, u32[]{:S(2)}, u32[]{:S(2)}) collective-permute-start(bf16[1,2,768,256]{3,2,1,0:T(8,128)(2,1)S(1)} %project_mix.3), channel_id=1, source_target_pairs={{0,2},{1,5},{2,0},{3,7},{4,6},{5,1},{6,4},{7,3},{8,10},{9,13},{10,... | collective-permute-start | bytes 2359304 | tf_op jit(solution)/shard_map/ppermute | solution.py:506
  25.6 21.7 %collective-permute-start.7 = (bf16[1,2,768,256]{3,2,1,0:T(8,128)(2,1)S(1)}, bf16[1,2,768,256]{3,2,1,0:T(8,128)(2,1)S(1)}, u32[]{:S(2)}, u32[]{:S(2)}) collective-permute-start(bf16[1,2,768,256]{3,2,1,0:T(8,128)(2,1)S(1)} %project_mix.4), channel_id=1, source_target_pairs={{0,2},{1,5},{2,0},{3,7},{4,6},{5,1},{6,4},{7,3},{8,10},{9,13},{10,... | collective-permute-start | bytes 2359304 | tf_op jit(solution)/shard_map/ppermute | solution.py:509
  26.2 13.9 %slice-start = ((s8[8388608]{0:T(1024)(128)(4,1)}), s8[4194304]{0:T(1024)(128)(4,1)S(1)}, s32[]{:S(2)}) async-start(s8[8388608]{0:T(1024)(128)(4,1)} %bitcast.15), calls=%async_computation | async-start | bytes 8388608
  28.8 8.3 %copy-start.2 = (f32[3,3,1024]{2,1,0:T(4,128)S(1)}, f32[3,3,1024]{2,1,0:T(4,128)}, u32[]{:S(2)}) copy-start(f32[3,3,1024]{2,1,0:T(4,128)} %filt_ref.1) | copy-start | bytes 110596
  34.3 5.7 %slice-start.1 = ((s8[8388608]{0:T(1024)(128)(4,1)}), s8[4194304]{0:T(1024)(128)(4,1)S(1)}, s32[]{:S(2)}) async-start(s8[8388608]{0:T(1024)(128)(4,1)} %bitcast.15), calls=%async_computation.1 | async-start | bytes 8388608
  35.0 2.0 %collective-permute-start.6 = (bf16[4,16,1024]{2,1,0:T(8,128)(2,1)S(1)}, bf16[4,16,1024]{2,1,0:T(8,128)(2,1)S(1)}, u32[]{:S(2)}, u32[]{:S(2)}) collective-permute-start(bf16[4,16,1024]{2,1,0:T(8,128)(2,1)S(1)} %get-tuple-element.89), channel_id=1, source_target_pairs={{0,1},{1,0},{2,3},{3,2},{4,5},{5,4},{6,7},{7,6},{8,9},{9,8},{10,11... | collective-permute-start | bytes 393224 | tf_op jit(solution)/shard_map/ppermute | solution.py:517
  35.1 16.1 %collective-permute-start.10 = (bf16[768,256]{1,0:T(8,128)(2,1)S(1)}, bf16[768,256]{1,0:T(8,128)(2,1)S(1)}, u32[]{:S(2)}, u32[]{:S(2)}) collective-permute-start(bf16[768,256]{1,0:T(8,128)(2,1)S(1)} %get-tuple-element.84), channel_id=1, source_target_pairs={{0,4},{1,3},{2,6},{3,1},{4,0},{5,7},{6,2},{7,5},{8,12},{9,11},{10,... | collective-permute-start | bytes 1179656 | tf_op jit(solution)/shard_map/ppermute | solution.py:513
  36.6 14.6 %collective-permute-start.11 = (bf16[768,256]{1,0:T(8,128)(2,1)S(1)}, bf16[768,256]{1,0:T(8,128)(2,1)S(1)}, u32[]{:S(2)}, u32[]{:S(2)}) collective-permute-start(bf16[768,256]{1,0:T(8,128)(2,1)S(1)} %get-tuple-element.102), channel_id=1, source_target_pairs={{0,5},{1,2},{2,7},{3,0},{4,1},{5,6},{6,3},{7,4},{8,13},{9,10},{10,... | collective-permute-start | bytes 1179656 | tf_op jit(solution)/shard_map/ppermute | solution.py:514
  40.6 10.6 %copy-start.3 = (f32[8,1024]{1,0:T(8,128)S(1)}, f32[8,1024]{1,0:T(8,128)}, u32[]{:S(2)}) copy-start(f32[8,1024]{1,0:T(8,128)} %decay_ref.1) | copy-start | bytes 98308
  40.7 10.6 %copy-start.4 = (f32[8,1024]{1,0:T(8,128)S(1)}, f32[8,1024]{1,0:T(8,128)}, u32[]{:S(2)}) copy-start(f32[8,1024]{1,0:T(8,128)} %residue_ref.1) | copy-start | bytes 98308
  48.0 3.2 %collective-permute-start.9 = (bf16[768,256]{1,0:T(8,128)(2,1)S(1)}, bf16[768,256]{1,0:T(8,128)(2,1)S(1)}, u32[]{:S(2)}, u32[]{:S(2)}) collective-permute-start(bf16[768,256]{1,0:T(8,128)(2,1)S(1)} %get-tuple-element.101), channel_id=1, source_target_pairs={{0,1},{1,0},{2,3},{3,2},{4,5},{5,4},{6,7},{7,6},{8,9},{9,8},{10,11... | collective-permute-start | bytes 1179656 | tf_op jit(solution)/shard_map/ppermute | solution.py:524
  48.0 7.8 %collective-permute-start.8 = (bf16[192,1024]{1,0:T(8,128)(2,1)S(1)}, bf16[192,1024]{1,0:T(8,128)(2,1)S(1)}, u32[]{:S(2)}, u32[]{:S(2)}) collective-permute-start(bf16[192,1024]{1,0:T(8,128)(2,1)S(1)} %get-tuple-element.99), channel_id=1, source_target_pairs={{0,2},{1,5},{2,0},{3,7},{4,6},{5,1},{6,4},{7,3},{8,10},{9,13},{10,... | collective-permute-start | bytes 1179656 | tf_op jit(solution)/shard_map/ppermute | solution.py:526
  54.2 1.7 %collective-permute-start.12 = (bf16[4,192,128]{2,1,0:T(8,128)(2,1)S(1)}, bf16[4,192,128]{2,1,0:T(8,128)(2,1)S(1)}, u32[]{:S(2)}, u32[]{:S(2)}) collective-permute-start(bf16[4,192,128]{2,1,0:T(8,128)(2,1)S(1)} %get-tuple-element.104), channel_id=1, source_target_pairs={{0,1},{1,0},{2,3},{3,2},{4,5},{5,4},{6,7},{7,6},{8,9},{9,8},{10,11... | collective-permute-start | bytes 589832 | tf_op jit(solution)/shard_map/ppermute | solution.py:530
  54.2 10.7 %collective-permute-start.14 = (bf16[192,1024]{1,0:T(8,128)(2,1)S(1)}, bf16[192,1024]{1,0:T(8,128)(2,1)S(1)}, u32[]{:S(2)}, u32[]{:S(2)}) collective-permute-start(bf16[192,1024]{1,0:T(8,128)(2,1)S(1)} %get-tuple-element.106), channel_id=1, source_target_pairs={{0,2},{1,5},{2,0},{3,7},{4,6},{5,1},{6,4},{7,3},{8,10},{9,13},{10,... | collective-permute-start | bytes 1179656 | tf_op jit(solution)/shard_map/ppermute | solution.py:527
  56.5 13.6 %collective-permute-start.13 = (bf16[192,1024]{1,0:T(8,128)(2,1)S(1)}, bf16[192,1024]{1,0:T(8,128)(2,1)S(1)}, u32[]{:S(2)}, u32[]{:S(2)}) collective-permute-start(bf16[192,1024]{1,0:T(8,128)(2,1)S(1)} %get-tuple-element.105), channel_id=1, source_target_pairs={{0,4},{1,3},{2,6},{3,1},{4,0},{5,7},{6,2},{7,5},{8,12},{9,11},{10,... | collective-permute-start | bytes 1179656 | tf_op jit(solution)/shard_map/ppermute | solution.py:532
  58.0 9.9 %collective-permute-start.15 = (bf16[2,192,128]{2,1,0:T(8,128)(2,1)S(1)}, bf16[2,192,128]{2,1,0:T(8,128)(2,1)S(1)}, u32[]{:S(2)}, u32[]{:S(2)}) collective-permute-start(bf16[2,192,128]{2,1,0:T(8,128)(2,1)S(1)} %get-tuple-element.108), channel_id=1, source_target_pairs={{0,4},{1,3},{2,6},{3,1},{4,0},{5,7},{6,2},{7,5},{8,12},{9,11},{10,... | collective-permute-start | bytes 294920 | tf_op jit(solution)/shard_map/ppermute | solution.py:533
  58.6 9.3 %collective-permute-start.16 = (bf16[2,192,128]{2,1,0:T(8,128)(2,1)S(1)}, bf16[2,192,128]{2,1,0:T(8,128)(2,1)S(1)}, u32[]{:S(2)}, u32[]{:S(2)}) collective-permute-start(bf16[2,192,128]{2,1,0:T(8,128)(2,1)S(1)} %get-tuple-element.109), channel_id=1, source_target_pairs={{0,2},{1,5},{2,0},{3,7},{4,6},{5,1},{6,4},{7,3},{8,10},{9,13},{10,... | collective-permute-start | bytes 294920 | tf_op jit(solution)/shard_map/ppermute | solution.py:533
  60.1 10.0 %collective-permute-start.17 = (bf16[2,192,128]{2,1,0:T(8,128)(2,1)S(1)}, bf16[2,192,128]{2,1,0:T(8,128)(2,1)S(1)}, u32[]{:S(2)}, u32[]{:S(2)}) collective-permute-start(bf16[2,192,128]{2,1,0:T(8,128)(2,1)S(1)} %get-tuple-element.110), channel_id=1, source_target_pairs={{0,6},{1,7},{2,4},{3,5},{4,2},{5,3},{6,0},{7,1},{8,14},{9,15},{10,... | collective-permute-start | bytes 294920 | tf_op jit(solution)/shard_map/ppermute | solution.py:533
  71.9 11.9 %collective-permute-start.18 = (bf16[192,1024]{1,0:T(8,128)(2,1)S(1)}, bf16[192,1024]{1,0:T(8,128)(2,1)S(1)}, u32[]{:S(2)}, u32[]{:S(2)}) collective-permute-start(bf16[192,1024]{1,0:T(8,128)(2,1)S(1)} %get-tuple-element.115), channel_id=1, source_target_pairs={{0,8},{8,0},{16,24},{24,16},{1,9},{9,1},{17,25},{25,17},{2,10},{10... | collective-permute-start | bytes 1179656 | tf_op jit(solution)/shard_map/ppermute | solution.py:439
  73.6 17.9 %collective-permute-start.19 = (bf16[192,1024]{1,0:T(8,128)(2,1)S(1)}, bf16[192,1024]{1,0:T(8,128)(2,1)S(1)}, u32[]{:S(2)}, u32[]{:S(2)}) collective-permute-start(bf16[192,1024]{1,0:T(8,128)(2,1)S(1)} %get-tuple-element.116.side_ref), channel_id=1, source_target_pairs={{8,16},{16,8},{9,17},{17,9},{10,18},{18,10},{11,19},{19,11},{12,20... | collective-permute-start | bytes 1179656 | tf_op jit(solution)/shard_map/ppermute | solution.py:441
  75.4 16.0 %collective-permute-start.20 = (bf16[192,1024]{1,0:T(8,128)(2,1)S(1)}, bf16[192,1024]{1,0:T(8,128)(2,1)S(1)}, u32[]{:S(2)}, u32[]{:S(2)}) collective-permute-start(bf16[192,1024]{1,0:T(8,128)(2,1)S(1)} %out_columns.2.far_ref), channel_id=1, source_target_pairs={{0,16},{24,8},{1,17},{25,9},{2,18},{26,10},{3,19},{27,11},{4,20},{... | collective-permute-start | bytes 1179656 | tf_op jit(solution)/shard_map/ppermute | solution.py:443
  84.5 20.2 %collective-permute-start.21 = (bf16[192,1024]{1,0:T(8,128)(2,1)S(1)}, bf16[192,1024]{1,0:T(8,128)(2,1)S(1)}, u32[]{:S(2)}, u32[]{:S(2)}) collective-permute-start(bf16[192,1024]{1,0:T(8,128)(2,1)S(1)} %last_step.1), channel_id=1, source_target_pairs={{0,8},{8,24},{16,0},{24,16},{1,9},{9,25},{17,1},{25,17},{2,10},{10... | collective-permute-start | bytes 1179656 | tf_op jit(solution)/shard_map/ppermute | solution.py:451

commit v6 on v5

--- a/solution.py
+++ b/solution.py
@@ -126,17 +126,6 @@
     return local(kernel, "cut", shapes, order, [tokens])
 
 
-def join_rows(order, mine, other):
-    half, wide = mine.shape
-    at = order.shape[0] - 1
-
-    def kernel(order, mine_ref, other_ref, out_ref):
-        out_ref[columns(order[at], half), :] = mine_ref[...]
-        out_ref[columns(1 - order[at], half), :] = other_ref[...]
-
-    return local(kernel, "join_rows", [((2 * half, wide), mine.dtype)], order, [mine, other])
-
-
 def stage(array):
     def kernel(array_ref, out_ref, sem):
         copy = pltpu.make_async_copy(array_ref, out_ref, sem)
@@ -189,6 +178,60 @@
     scratch = [pltpu.VMEM((2, chips * high, depth), BF16)]
     shapes = [(shape, kind)] + ([((chips, ends, 2 * depth), BF16)] if ends else [])
     return local(kernel, "project_mix", shapes, order, [*xs, own, other], scratch)
+
+
+def early_share(order, own_rows, mine, other_rows, own, other, slot, chips):
+    half, wide_x = mine.shape
+    high = 2 * half
+    streams, depth, chans = own.shape
+    wide = chans // chips
+    lanes = wide // 2
+    place = order.shape[0] - 1
+
+    def kernel(order, own_rows_ref, mine_ref, there_ref, own_ref, other_ref, joined_ref, out_ref, rows):
+        core = order[2 * chips]
+        joined_ref[columns(order[place], half), :] = mine_ref[...]
+        joined_ref[columns(1 - order[place], half), :] = there_ref[...]
+        gather_rows(core, (own_rows_ref, joined_ref), rows)
+        at = columns(order[slot], wide)
+        for g in range(1, streams):
+            total = jnp.dot(rows[0], own_ref[g, :, at], preferred_element_type=F32)
+            total += jnp.dot(rows[1], other_ref[g, :, at], preferred_element_type=F32)
+            for h in range(2):
+                to = slice((g - 1) * lanes, g * lanes)
+                out_ref[core ^ h, :, to] = total[:, h * lanes : (h + 1) * lanes].astype(BF16)
+
+    shapes = [((high, wide_x), BF16), ((2, 2 * high, (streams - 1) * lanes), BF16)]
+    scratch = [pltpu.VMEM((2, 2 * high, depth), BF16)]
+    arrays = [own_rows, mine, other_rows, own, other]
+    return local(kernel, "early_share", shapes, order, arrays, scratch)
+
+
+def rest_share(order, xs, early, own, other, slot, chips):
+    high = xs[0].shape[0]
+    streams, depth, chans = own.shape
+    wide = chans // chips
+    lanes = wide // 2
+
+    def kernel(order, first_ref, second_ref, early_ref, own_ref, other_ref, out_ref, rows):
+        core = order[2 * chips]
+        gather_rows(core, (first_ref, second_ref), rows)
+        at = columns(order[slot], wide)
+        for h in range(2):
+            out_ref[0, h, :high, :] = early_ref[h, :high, :]
+            out_ref[0, h, 3 * high :, :] = early_ref[h, high:, :]
+        for g in range(1, streams):
+            total = jnp.dot(rows[0], own_ref[g, :, at], preferred_element_type=F32)
+            total += jnp.dot(rows[1], other_ref[g, :, at], preferred_element_type=F32)
+            for h in range(2):
+                to = slice((g - 1) * lanes, g * lanes)
+                out_ref[0, core ^ h, high : 3 * high, to] = total[
+                    :, h * lanes : (h + 1) * lanes
+                ].astype(BF16)
+
+    shapes = [((1, 2, chips * high, (streams - 1) * lanes), BF16)]
+    scratch = [pltpu.VMEM((2, 2 * high, depth), BF16)]
+    return local(kernel, "rest_share", shapes, order, [*xs, early, own, other], scratch)
 
 
 def project_query(order, xs, before, own, other, short_filter):
@@ -500,9 +543,10 @@
     half = lax.ppermute(xs[3], "ctx", route(3))
     other = lax.ppermute(half, "dp", [(i, i ^ 1) for i in range(groups)])
     xs = [xs[0]] + [lax.ppermute(xs[s], "ctx", route(s)) for s in (1, 2)]
-    xs.append(join_rows(order, half, other))
-
-    both = project_mix(order, xs, own_w, other_w, [3], BF16)
+    joined, early = early_share(order, xs[0], half, other, own_w, other_w, 3, chips)
+    xs.append(joined)
+
+    both = rest_share(order, xs[1:3], early, own_w, other_w, 3, chips)
     both_in = lax.ppermute(both, "ctx", route(2))
     xs, both = lax.optimization_barrier((xs, both))
     first = project_mix(order, xs, own_w, other_w, [2], BF16)

time: 106 us -> 106 us (level)
  transfers between devices with their start and end apart: 22 -> 22, of which waited for: 14 -> 14; matrix products, arithmetic and copies ran while one was open for 0% -> 0% of each run, Pallas kernels for 17% -> 18%
where the time goes in v6:
time: 106 us
  waiting for transfers between devices  50 us (47%)
  starting transfers between devices  28.9 us (27%)
  Pallas kernels  22.9 us (22%)
  local copies, waits for them, and re-layouts  3.59 us (3%)
    pallas_call x16, Pallas kernels, local(): pl.pallas_call(kernel, out_shape=out if len(out) > 1 else out[0], in_spec...  22.1 us
    ppermute x1, waiting for transfers between devices, output_over_line(): last_in = lax.ppermute(last, 'dp', [(0, 1), (1, 3), (2, 0), (3, 2)])  12.6 us
    ppermute x1, waiting for transfers between devices, on_device_chips(): first_in = lax.ppermute(first, 'ctx', route(2))  6.4 us
    ppermute x1, starting transfers between devices, output_over_line(): end_in = lax.ppermute(far, 'dp', [(0, 2), (3, 1)])  5.75 us
    ppermute x1, waiting for transfers between devices, on_device_chips(): both_in = lax.ppermute(both, 'ctx', route(2))  5.54 us
    ppermute x1, waiting for transfers between devices, on_device_chips(): half = lax.ppermute(xs[3], 'ctx', route(3))  5.15 us
    ppermute x3, waiting for transfers between devices, on_device_chips(): lax.ppermute(long_parts[s], 'ctx', route(s))  5.14 us
    ppermute x1, waiting for transfers between devices, output_over_line(): end_in = lax.ppermute(far, 'dp', [(0, 2), (3, 1)])  4.11 us
  transfers between devices with their start and end apart: 22, of which 14 were waited for; matrix products, arithmetic and copies ran while one was open for 0% of the time, Pallas kernels for 18%

profile of v6, /device:TPU:0, one launch (start us, length us, event | category | flops | bytes accessed | tf_op | source)
XLA Modules:
  0.0 105.6 jit_solution(18087393216068229635)
XLA Ops:
  0.0 0.5 collective-permute-start.4
  0.5 0.1 stack.59.order
  0.5 0.1 concatenate.4.scalars
  0.6 0.1 stack.65.picks
  0.7 1.4 %copy-done.1 = bf16[192,4096]{1,0:T(8,128)(2,1)S(1)} copy-done((bf16[192,4096]{1,0:T(8,128)(2,1)S(1)}, bf16[192,4096]{1,0:T(8,128)(2,1)}, u32[]{:S(2)}) %copy-start.1) | copy-done | bytes 1572888
  2.1 0.6 cut.1
  2.8 3.5 %collective-permute-start.2 = (bf16[96,1024]{1,0:T(8,128)(2,1)S(1)}, bf16[96,1024]{1,0:T(8,128)(2,1)S(1)}, u32[]{:S(2)}, u32[]{:S(2)}) collective-permute-start(bf16[96,1024]{1,0:T(8,128)(2,1)S(1)} %get-tuple-element.74), channel_id=1, source_target_pairs={{0,6},{1,7},{2,4},{3,5},{4,2},{5,3},{6,0},{7,1},{8,14},{9,15},{10,... | collective-permute-start | bytes 589832 | tf_op jit(solution)/shard_map/ppermute | solution.py:543
  6.3 0.5 collective-permute-start
  6.8 0.1 collective-permute-start.1
  6.9 5.2 %collective-permute-done.2.mine_ref = bf16[96,1024]{1,0:T(8,128)(2,1)S(1)} collective-permute-done((bf16[96,1024]{1,0:T(8,128)(2,1)S(1)}, bf16[96,1024]{1,0:T(8,128)(2,1)S(1)}, u32[]{:S(2)}, u32[]{:S(2)}) %collective-permute-start.2) | collective-permute-done | bytes 196640 | tf_op jit(solution)/shard_map/ppermute | solution.py:543
  12.1 2.0 %collective-permute-start.3 = (bf16[96,1024]{1,0:T(8,128)(2,1)S(1)}, bf16[96,1024]{1,0:T(8,128)(2,1)S(1)}, u32[]{:S(2)}, u32[]{:S(2)}) collective-permute-start(bf16[96,1024]{1,0:T(8,128)(2,1)S(1)} %collective-permute-done.2.mine_ref), channel_id=1, source_target_pairs={{0,8},{8,0},{16,24},{24,16},{1,9},{9,1},{17,25},{25,17},{2,10},{10... | collective-permute-start | bytes 589832 | tf_op jit(solution)/shard_map/ppermute | solution.py:544
  14.1 1.9 %copy-done = bf16[512,3,1024]{2,0,1:T(8,128)(2,1)S(1)} copy-done((bf16[512,3,1024]{2,0,1:T(8,128)(2,1)S(1)}, bf16[512,3,1024]{2,0,1:T(8,128)(2,1)}, u32[]{:S(2)}) %copy-start) | copy-done | bytes 3145752
  15.9 0.2 stage.2.own_ref.refs_4_.refs_5_
  16.2 2.5 %collective-permute-done.3.there_ref = bf16[96,1024]{1,0:T(8,128)(2,1)S(1)} collective-permute-done((bf16[96,1024]{1,0:T(8,128)(2,1)S(1)}, bf16[96,1024]{1,0:T(8,128)(2,1)S(1)}, u32[]{:S(2)}, u32[]{:S(2)}) %collective-permute-start.3) | collective-permute-done | bytes 196640 | tf_op jit(solution)/shard_map/ppermute | solution.py:544
  18.6 0.0 collective-permute-done.4.other_ref.refs_5_.refs_6_
  18.6 1.2 %early_share.1 = (bf16[192,1024]{1,0:T(8,128)(2,1)S(1)}, bf16[2,384,256]{2,1,0:T(8,128)(2,1)S(1)}) custom-call(s32[11]{0:T(128)S(1)} %stack.59.order, bf16[192,1024]{1,0:T(8,128)(2,1)S(1)} %get-tuple-element.89.own_rows_ref.refs_0_, bf16[96,1024]{1,0:T(8,128)(2,1)S(1)} %collective-permute-done.2.mine_ref, ...), custom_call_target="tpu_custom_call" | custom-call | tf_op jit(solution)/shard_map/early_share/pallas_call | solution.py:101
  19.9 0.4 collective-permute-done.first_ref.refs_1_
  20.3 0.3 collective-permute-done.1.second_ref.refs_2_
  20.6 1.2 %rest_share.1 = bf16[1,2,768,256]{3,2,1,0:T(8,128)(2,1)S(1)} custom-call(s32[11]{0:T(128)S(1)} %stack.59.order, bf16[192,1024]{1,0:T(8,128)(2,1)S(1)} %collective-permute-done.first_ref.refs_1_, bf16[192,1024]{1,0:T(8,128)(2,1)S(1)} %collective-permute-done.1.second_ref.refs_2_, bf16[2,384,256]{2,1,0:T(8,128)(2,1)S(1)} %get-tuple-element.77.early_ref, ...), custom_call_target="tpu_custom_call" | custom-call | tf_op jit(solution)/shard_map/rest_share/pallas_call | solution.py:101
  21.8 1.6 %collective-permute-start.5 = (bf16[1,2,768,256]{3,2,1,0:T(8,128)(2,1)S(1)}, bf16[1,2,768,256]{3,2,1,0:T(8,128)(2,1)S(1)}, u32[]{:S(2)}, u32[]{:S(2)}) collective-permute-start(bf16[1,2,768,256]{3,2,1,0:T(8,128)(2,1)S(1)} %rest_share.1), channel_id=1, source_target_pairs={{0,2},{1,5},{2,0},{3,7},{4,6},{5,1},{6,4},{7,3},{8,10},{9,13},{10,... | collective-permute-start | bytes 2359304 | tf_op jit(solution)/shard_map/ppermute | solution.py:550
  23.4 1.7 %project_mix.2 = bf16[1,2,768,256]{3,2,1,0:T(8,128)(2,1)S(1)} custom-call(s32[11]{0:T(128)S(1)} %stack.59.order, bf16[192,1024]{1,0:T(8,128)(2,1)S(1)} %get-tuple-element.89.own_rows_ref.refs_0_, bf16[192,1024]{1,0:T(8,128)(2,1)S(1)} %collective-permute-done.first_ref.refs_1_, bf16[192,1024]{1,0:T(8,128)(2,1)S(1)} %collective-permute-done.1.second_ref.refs_2_, ...), custom_call_target="tpu_custom_call" | custom-call | tf_op jit(solution)/shard_map/project_mix/pallas_call | solution.py:101
  25.1 0.6 collective-permute-start.7
  25.7 2.6 %project_mix.3 = (f32[2,2,768,256]{3,2,1,0:T(8,128)S(1)}, bf16[4,16,1024]{2,1,0:T(8,128)(2,1)S(1)}) custom-call(s32[11]{0:T(128)S(1)} %stack.59.order, bf16[192,1024]{1,0:T(8,128)(2,1)S(1)} %get-tuple-element.89.own_rows_ref.refs_0_, bf16[192,1024]{1,0:T(8,128)(2,1)S(1)} %collective-permute-done.first_ref.refs_1_, ...), custom_call_target="tpu_custom_call" | custom-call | tf_op jit(solution)/shard_map/project_mix/pallas_call | solution.py:101
  28.3 0.0 copy-start.2
  28.3 5.5 %collective-permute-done.5.both_ref = bf16[1,2,768,256]{3,2,1,0:T(8,128)(2,1)S(1)} collective-permute-done((bf16[1,2,768,256]{3,2,1,0:T(8,128)(2,1)S(1)}, bf16[1,2,768,256]{3,2,1,0:T(8,128)(2,1)S(1)}, u32[]{:S(2)}, u32[]{:S(2)}) %collective-permute-start.5) | collective-permute-done | bytes 786464 | tf_op jit(solution)/shard_map/ppermute | solution.py:550
  33.8 0.7 second_share.1
  34.5 0.1 collective-permute-start.6
  34.6 1.5 %collective-permute-start.10 = (bf16[768,256]{1,0:T(8,128)(2,1)S(1)}, bf16[768,256]{1,0:T(8,128)(2,1)S(1)}, u32[]{:S(2)}, u32[]{:S(2)}) collective-permute-start(bf16[768,256]{1,0:T(8,128)(2,1)S(1)} %get-tuple-element.88), channel_id=1, source_target_pairs={{0,4},{1,3},{2,6},{3,1},{4,0},{5,7},{6,2},{7,5},{8,12},{9,11},{10,... | collective-permute-start | bytes 1179656 | tf_op jit(solution)/shard_map/ppermute | solution.py:557
  36.1 0.7 collective-permute-start.11
  36.8 0.0 collective-permute-done.6.refs_4_
  36.8 3.0 %project_query.1 = (f32[192,1024]{1,0:T(8,128)S(1)}, f32[192,1024]{1,0:T(8,128)S(1)}, bf16[192,1024]{1,0:T(8,128)(2,1)S(1)}, bf16[192,1024]{1,0:T(8,128)(2,1)S(1)}) custom-call(s32[11]{0:T(128)S(1)} %stack.59.order, bf16[192,1024]{1,0:T(8,128)(2,1)S(1)} %get-tuple-element.89.own_rows_ref.refs_0_, ...), custom_call_target="tpu_custom_call" | custom-call | tf_op jit(solution)/shard_map/project_query/pallas_call | solution.py:101
  39.8 0.6 stage.3.refs_7_.w_ref
  40.4 0.0 copy-start.3
  40.4 0.0 copy-start.4
  40.4 6.4 %collective-permute-done.7.first_ref = bf16[1,2,768,256]{3,2,1,0:T(8,128)(2,1)S(1)} collective-permute-done((bf16[1,2,768,256]{3,2,1,0:T(8,128)(2,1)S(1)}, bf16[1,2,768,256]{3,2,1,0:T(8,128)(2,1)S(1)}, u32[]{:S(2)}, u32[]{:S(2)}) %collective-permute-start.7) | collective-permute-done | bytes 786464 | tf_op jit(solution)/shard_map/ppermute | solution.py:553
  46.8 0.7 first_share.1
  47.5 0.1 collective-permute-start.9
  47.5 1.6 %collective-permute-start.8 = (bf16[192,1024]{1,0:T(8,128)(2,1)S(1)}, bf16[192,1024]{1,0:T(8,128)(2,1)S(1)}, u32[]{:S(2)}, u32[]{:S(2)}) collective-permute-start(bf16[192,1024]{1,0:T(8,128)(2,1)S(1)} %get-tuple-element.103), channel_id=1, source_target_pairs={{0,2},{1,5},{2,0},{3,7},{4,6},{5,1},{6,4},{7,3},{8,10},{9,13},{10,... | collective-permute-start | bytes 1179656 | tf_op jit(solution)/shard_map/ppermute | solution.py:570
  49.1 1.6 %collective-permute-done.11.swap_second_ref = bf16[768,256]{1,0:T(8,128)(2,1)S(1)} collective-permute-done((bf16[768,256]{1,0:T(8,128)(2,1)S(1)}, bf16[768,256]{1,0:T(8,128)(2,1)S(1)}, u32[]{:S(2)}, u32[]{:S(2)}) %collective-permute-start.11) | collective-permute-done | bytes 393248 | tf_op jit(solution)/shard_map/ppermute | solution.py:558
  50.7 2.9 %hyena.1 = (bf16[4,192,128]{2,1,0:T(8,128)(2,1)S(1)}, bf16[4,192,128]{2,1,0:T(8,128)(2,1)S(1)}) custom-call(s32[11]{0:T(128)S(1)} %stack.59.order, f32[768,256]{1,0:T(8,128)S(1)} %get-tuple-element.104.own_ref, bf16[768,256]{1,0:T(8,128)(2,1)S(1)} %collective-permute-done.9.swap_ref, bf16[768,256]{1,0:T(8,128)(2,1)S(1)} %collective-permute-done.10.second_ref, ...), custom_call_target="tpu_custom_call" | custom-call | tf_op jit(solution)/shard_map/hyena/pallas_call | solution.py:101
  53.6 0.1 collective-permute-start.12
  53.7 1.6 %collective-permute-start.14 = (bf16[192,1024]{1,0:T(8,128)(2,1)S(1)}, bf16[192,1024]{1,0:T(8,128)(2,1)S(1)}, u32[]{:S(2)}, u32[]{:S(2)}) collective-permute-start(bf16[192,1024]{1,0:T(8,128)(2,1)S(1)} %get-tuple-element.110), channel_id=1, source_target_pairs={{0,2},{1,5},{2,0},{3,7},{4,6},{5,1},{6,4},{7,3},{8,10},{9,13},{10,... | collective-permute-start | bytes 1179656 | tf_op jit(solution)/shard_map/ppermute | solution.py:571
  55.3 0.1 collective-permute-done.8.in_ref
  55.4 0.6 payloads.1
  56.0 1.5 %collective-permute-start.13 = (bf16[192,1024]{1,0:T(8,128)(2,1)S(1)}, bf16[192,1024]{1,0:T(8,128)(2,1)S(1)}, u32[]{:S(2)}, u32[]{:S(2)}) collective-permute-start(bf16[192,1024]{1,0:T(8,128)(2,1)S(1)} %get-tuple-element.109), channel_id=1, source_target_pairs={{0,4},{1,3},{2,6},{3,1},{4,0},{5,7},{6,2},{7,5},{8,12},{9,11},{10,... | collective-permute-start | bytes 1179656 | tf_op jit(solution)/shard_map/ppermute | solution.py:576
  57.5 0.6 collective-permute-start.15
  58.1 1.5 %collective-permute-start.16 = (bf16[2,192,128]{2,1,0:T(8,128)(2,1)S(1)}, bf16[2,192,128]{2,1,0:T(8,128)(2,1)S(1)}, u32[]{:S(2)}, u32[]{:S(2)}) collective-permute-start(bf16[2,192,128]{2,1,0:T(8,128)(2,1)S(1)} %get-tuple-element.113), channel_id=1, source_target_pairs={{0,2},{1,5},{2,0},{3,7},{4,6},{5,1},{6,4},{7,3},{8,10},{9,13},{10,... | collective-permute-start | bytes 294920 | tf_op jit(solution)/shard_map/ppermute | solution.py:577
  59.6 1.4 %collective-permute-start.17 = (bf16[2,192,128]{2,1,0:T(8,128)(2,1)S(1)}, bf16[2,192,128]{2,1,0:T(8,128)(2,1)S(1)}, u32[]{:S(2)}, u32[]{:S(2)}) collective-permute-start(bf16[2,192,128]{2,1,0:T(8,128)(2,1)S(1)} %get-tuple-element.114), channel_id=1, source_target_pairs={{0,6},{1,7},{2,4},{3,5},{4,2},{5,3},{6,0},{7,1},{8,14},{9,15},{10,... | collective-permute-start | bytes 294920 | tf_op jit(solution)/shard_map/ppermute | solution.py:577
  61.0 3.5 %collective-permute-done.14.refs_2_ = bf16[192,1024]{1,0:T(8,128)(2,1)S(1)} collective-permute-done((bf16[192,1024]{1,0:T(8,128)(2,1)S(1)}, bf16[192,1024]{1,0:T(8,128)(2,1)S(1)}, u32[]{:S(2)}, u32[]{:S(2)}) %collective-permute-start.14) | collective-permute-done | bytes 393248 | tf_op jit(solution)/shard_map/ppermute | solution.py:571
  64.4 2.9 %collective-permute-done.15.refs_4_ = bf16[2,192,128]{2,1,0:T(8,128)(2,1)S(1)} collective-permute-done((bf16[2,192,128]{2,1,0:T(8,128)(2,1)S(1)}, bf16[2,192,128]{2,1,0:T(8,128)(2,1)S(1)}, u32[]{:S(2)}, u32[]{:S(2)}) %collective-permute-start.15) | collective-permute-done | bytes 98336 | tf_op jit(solution)/shard_map/ppermute | solution.py:577
  67.4 2.2 %collective-permute-done.17.refs_6_ = bf16[2,192,128]{2,1,0:T(8,128)(2,1)S(1)} collective-permute-done((bf16[2,192,128]{2,1,0:T(8,128)(2,1)S(1)}, bf16[2,192,128]{2,1,0:T(8,128)(2,1)S(1)}, u32[]{:S(2)}, u32[]{:S(2)}) %collective-permute-start.17) | collective-permute-done | bytes 98336 | tf_op jit(solution)/shard_map/ppermute | solution.py:577
  69.6 1.8 %gate.1 = (bf16[192,1024]{1,0:T(8,128)(2,1)S(1)}, bf16[192,1024]{1,0:T(8,128)(2,1)S(1)}, bf16[192,1024]{1,0:T(8,128)(2,1)S(1)}) custom-call(s32[16]{0:T(128)S(1)} %concatenate.4.scalars, f32[192,1024]{1,0:T(8,128)S(1)} %get-tuple-element.97.refs_0_, bf16[192,1024]{1,0:T(8,128)(2,1)S(1)} %collective-permute-done.13.refs_1_, ...), custom_call_target="tpu_custom_call" | custom-call | tf_op jit(solution)/shard_map/gate/pallas_call | solution.py:101
  71.4 1.6 %collective-permute-start.18 = (bf16[192,1024]{1,0:T(8,128)(2,1)S(1)}, bf16[192,1024]{1,0:T(8,128)(2,1)S(1)}, u32[]{:S(2)}, u32[]{:S(2)}) collective-permute-start(bf16[192,1024]{1,0:T(8,128)(2,1)S(1)} %get-tuple-element.119), channel_id=1, source_target_pairs={{0,8},{8,0},{16,24},{24,16},{1,9},{9,1},{17,25},{25,17},{2,10},{10... | collective-permute-start | bytes 1179656 | tf_op jit(solution)/shard_map/ppermute | solution.py:482
  73.1 0.7 collective-permute-start.19
  73.7 1.1 %out_columns.2.far_ref = bf16[192,1024]{1,0:T(8,128)(2,1)S(1)} custom-call(s32[5]{0:T(128)S(1)} %stack.65.picks, bf16[192,1024]{1,0:T(8,128)(2,1)S(1)} %get-tuple-element.121.x_ref, bf16[1024,4096]{1,0:T(8,128)(2,1)S(1)} %stage.3.refs_7_.w_ref), custom_call_target="tpu_custom_call" | custom-call | tf_op jit(solution)/shard_map/out_columns/pallas_call | solution.py:101
  74.9 5.8 %collective-permute-start.20 = (bf16[192,1024]{1,0:T(8,128)(2,1)S(1)}, bf16[192,1024]{1,0:T(8,128)(2,1)S(1)}, u32[]{:S(2)}, u32[]{:S(2)}) collective-permute-start(bf16[192,1024]{1,0:T(8,128)(2,1)S(1)} %out_columns.2.far_ref), channel_id=1, source_target_pairs={{0,16},{24,8},{1,17},{25,9},{2,18},{26,10},{3,19},{27,11},{4,20},{... | collective-permute-start | bytes 1179656 | tf_op jit(solution)/shard_map/ppermute | solution.py:486
  80.7 2.7 %collective-permute-done.18.pair_ref = bf16[192,1024]{1,0:T(8,128)(2,1)S(1)} collective-permute-done((bf16[192,1024]{1,0:T(8,128)(2,1)S(1)}, bf16[192,1024]{1,0:T(8,128)(2,1)S(1)}, u32[]{:S(2)}, u32[]{:S(2)}) %collective-permute-start.18) | collective-permute-done | bytes 393248 | tf_op jit(solution)/shard_map/ppermute | solution.py:482
  83.4 0.7 last_step.1
  84.0 1.6 %collective-permute-start.21 = (bf16[192,1024]{1,0:T(8,128)(2,1)S(1)}, bf16[192,1024]{1,0:T(8,128)(2,1)S(1)}, u32[]{:S(2)}, u32[]{:S(2)}) collective-permute-start(bf16[192,1024]{1,0:T(8,128)(2,1)S(1)} %last_step.1), channel_id=1, source_target_pairs={{0,8},{8,24},{16,0},{24,16},{1,9},{9,25},{17,1},{25,17},{2,10},{10... | collective-permute-start | bytes 1179656 | tf_op jit(solution)/shard_map/ppermute | solution.py:494
  85.7 1.1 %out_columns.3.own_ref = f32[192,1024]{1,0:T(8,128)S(1)} custom-call(s32[5]{0:T(128)S(1)} %stack.65.picks, bf16[192,1024]{1,0:T(8,128)(2,1)S(1)} %get-tuple-element.121.x_ref, bf16[1024,4096]{1,0:T(8,128)(2,1)S(1)} %stage.3.refs_7_.w_ref), custom_call_target="tpu_custom_call" | custom-call | tf_op jit(solution)/shard_map/out_columns/pallas_call | solution.py:101
  86.8 4.1 %collective-permute-done.20.refs_1_ = bf16[192,1024]{1,0:T(8,128)(2,1)S(1)} collective-permute-done((bf16[192,1024]{1,0:T(8,128)(2,1)S(1)}, bf16[192,1024]{1,0:T(8,128)(2,1)S(1)}, u32[]{:S(2)}, u32[]{:S(2)}) %collective-permute-start.20) | collective-permute-done | bytes 393248 | tf_op jit(solution)/shard_map/ppermute | solution.py:486
  90.9 0.7 early.1.early_ref
  91.7 12.6 %collective-permute-done.21.last_ref = bf16[192,1024]{1,0:T(8,128)(2,1)S(1)} collective-permute-done((bf16[192,1024]{1,0:T(8,128)(2,1)S(1)}, bf16[192,1024]{1,0:T(8,128)(2,1)S(1)}, u32[]{:S(2)}, u32[]{:S(2)}) %collective-permute-start.21) | collective-permute-done | bytes 393248 | tf_op jit(solution)/shard_map/ppermute | solution.py:494
  104.2 1.4 %total.1 = bf16[192,1024]{1,0:T(8,128)(2,1)} custom-call(s32[5]{0:T(128)S(1)} %stack.65.picks, f32[192,1024]{1,0:T(8,128)S(1)} %early.1.early_ref, bf16[192,1024]{1,0:T(8,128)(2,1)S(1)} %collective-permute-done.21.last_ref), custom_call_target="tpu_custom_call" | custom-call | tf_op jit(solution)/shard_map/total/pallas_call | solution.py:101
  (16 shorter events, 0.0 us)
Async XLA Ops:
  0.0 18.6 %collective-permute-start.4 = (bf16[3,512,1024]{2,1,0:T(8,128)(2,1)}, bf16[3,512,1024]{2,1,0:T(8,128)(2,1)S(1)}, u32[]{:S(2)}, u32[]{:S(2)}) collective-permute-start(bf16[3,512,1024]{2,1,0:T(8,128)(2,1)} %bitcast.17), channel_id=1, source_target_pairs={{0,1},{1,0},{2,3},{3,2},{4,5},{5,4},{6,7},{7,6},{8,9},{9,8},{10,11... | collective-permute-start | bytes 9437192 | tf_op jit(solution)/shard_map/ppermute | solution.py:539
  0.7 1.4 %copy-start.1 = (bf16[192,4096]{1,0:T(8,128)(2,1)S(1)}, bf16[192,4096]{1,0:T(8,128)(2,1)}, u32[]{:S(2)}) copy-start(bf16[192,4096]{1,0:T(8,128)(2,1)} %tokens_ref.1) | copy-start | bytes 4718596
  2.8 9.3 %collective-permute-start.2 = (bf16[96,1024]{1,0:T(8,128)(2,1)S(1)}, bf16[96,1024]{1,0:T(8,128)(2,1)S(1)}, u32[]{:S(2)}, u32[]{:S(2)}) collective-permute-start(bf16[96,1024]{1,0:T(8,128)(2,1)S(1)} %get-tuple-element.74), channel_id=1, source_target_pairs={{0,6},{1,7},{2,4},{3,5},{4,2},{5,3},{6,0},{7,1},{8,14},{9,15},{10,... | collective-permute-start | bytes 589832 | tf_op jit(solution)/shard_map/ppermute | solution.py:543
  6.3 14.0 %collective-permute-start = (bf16[192,1024]{1,0:T(8,128)(2,1)S(1)}, bf16[192,1024]{1,0:T(8,128)(2,1)S(1)}, u32[]{:S(2)}, u32[]{:S(2)}) collective-permute-start(bf16[192,1024]{1,0:T(8,128)(2,1)S(1)} %get-tuple-element.72), channel_id=1, source_target_pairs={{0,4},{1,3},{2,6},{3,1},{4,0},{5,7},{6,2},{7,5},{8,12},{9,11},{10,... | collective-permute-start | bytes 1179656 | tf_op jit(solution)/shard_map/ppermute | solution.py:545
  6.8 13.8 %collective-permute-start.1 = (bf16[192,1024]{1,0:T(8,128)(2,1)S(1)}, bf16[192,1024]{1,0:T(8,128)(2,1)S(1)}, u32[]{:S(2)}, u32[]{:S(2)}) collective-permute-start(bf16[192,1024]{1,0:T(8,128)(2,1)S(1)} %get-tuple-element.73), channel_id=1, source_target_pairs={{0,2},{1,5},{2,0},{3,7},{4,6},{5,1},{6,4},{7,3},{8,10},{9,13},{10,... | collective-permute-start | bytes 1179656 | tf_op jit(solution)/shard_map/ppermute | solution.py:545
  12.1 6.6 %collective-permute-start.3 = (bf16[96,1024]{1,0:T(8,128)(2,1)S(1)}, bf16[96,1024]{1,0:T(8,128)(2,1)S(1)}, u32[]{:S(2)}, u32[]{:S(2)}) collective-permute-start(bf16[96,1024]{1,0:T(8,128)(2,1)S(1)} %collective-permute-done.2.mine_ref), channel_id=1, source_target_pairs={{0,8},{8,0},{16,24},{24,16},{1,9},{9,1},{17,25},{25,17},{2,10},{10... | collective-permute-start | bytes 589832 | tf_op jit(solution)/shard_map/ppermute | solution.py:544
  14.1 1.9 %copy-start = (bf16[512,3,1024]{2,0,1:T(8,128)(2,1)S(1)}, bf16[512,3,1024]{2,0,1:T(8,128)(2,1)}, u32[]{:S(2)}) copy-start(bf16[512,3,1024]{2,0,1:T(8,128)(2,1)} %param.7) | copy-start | bytes 9437188
  21.8 12.1 %collective-permute-start.5 = (bf16[1,2,768,256]{3,2,1,0:T(8,128)(2,1)S(1)}, bf16[1,2,768,256]{3,2,1,0:T(8,128)(2,1)S(1)}, u32[]{:S(2)}, u32[]{:S(2)}) collective-permute-start(bf16[1,2,768,256]{3,2,1,0:T(8,128)(2,1)S(1)} %rest_share.1), channel_id=1, source_target_pairs={{0,2},{1,5},{2,0},{3,7},{4,6},{5,1},{6,4},{7,3},{8,10},{9,13},{10,... | collective-permute-start | bytes 2359304 | tf_op jit(solution)/shard_map/ppermute | solution.py:550
  25.1 21.7 %collective-permute-start.7 = (bf16[1,2,768,256]{3,2,1,0:T(8,128)(2,1)S(1)}, bf16[1,2,768,256]{3,2,1,0:T(8,128)(2,1)S(1)}, u32[]{:S(2)}, u32[]{:S(2)}) collective-permute-start(bf16[1,2,768,256]{3,2,1,0:T(8,128)(2,1)S(1)} %project_mix.2), channel_id=1, source_target_pairs={{0,2},{1,5},{2,0},{3,7},{4,6},{5,1},{6,4},{7,3},{8,10},{9,13},{10,... | collective-permute-start | bytes 2359304 | tf_op jit(solution)/shard_map/ppermute | solution.py:553
  25.7 14.1 %slice-start = ((s8[8388608]{0:T(1024)(128)(4,1)}), s8[4194304]{0:T(1024)(128)(4,1)S(1)}, s32[]{:S(2)}) async-start(s8[8388608]{0:T(1024)(128)(4,1)} %bitcast.15), calls=%async_computation | async-start | bytes 8388608
  28.3 8.5 %copy-start.2 = (f32[3,3,1024]{2,1,0:T(4,128)S(1)}, f32[3,3,1024]{2,1,0:T(4,128)}, u32[]{:S(2)}) copy-start(f32[3,3,1024]{2,1,0:T(4,128)} %filt_ref.1) | copy-start | bytes 110596
  33.8 5.9 %slice-start.1 = ((s8[8388608]{0:T(1024)(128)(4,1)}), s8[4194304]{0:T(1024)(128)(4,1)S(1)}, s32[]{:S(2)}) async-start(s8[8388608]{0:T(1024)(128)(4,1)} %bitcast.15), calls=%async_computation.1 | async-start | bytes 8388608
  34.5 2.2 %collective-permute-start.6 = (bf16[4,16,1024]{2,1,0:T(8,128)(2,1)S(1)}, bf16[4,16,1024]{2,1,0:T(8,128)(2,1)S(1)}, u32[]{:S(2)}, u32[]{:S(2)}) collective-permute-start(bf16[4,16,1024]{2,1,0:T(8,128)(2,1)S(1)} %get-tuple-element.93), channel_id=1, source_target_pairs={{0,1},{1,0},{2,3},{3,2},{4,5},{5,4},{6,7},{7,6},{8,9},{9,8},{10,11... | collective-permute-start | bytes 393224 | tf_op jit(solution)/shard_map/ppermute | solution.py:561
  34.6 16.1 %collective-permute-start.10 = (bf16[768,256]{1,0:T(8,128)(2,1)S(1)}, bf16[768,256]{1,0:T(8,128)(2,1)S(1)}, u32[]{:S(2)}, u32[]{:S(2)}) collective-permute-start(bf16[768,256]{1,0:T(8,128)(2,1)S(1)} %get-tuple-element.88), channel_id=1, source_target_pairs={{0,4},{1,3},{2,6},{3,1},{4,0},{5,7},{6,2},{7,5},{8,12},{9,11},{10,... | collective-permute-start | bytes 1179656 | tf_op jit(solution)/shard_map/ppermute | solution.py:557
  36.1 14.6 %collective-permute-start.11 = (bf16[768,256]{1,0:T(8,128)(2,1)S(1)}, bf16[768,256]{1,0:T(8,128)(2,1)S(1)}, u32[]{:S(2)}, u32[]{:S(2)}) collective-permute-start(bf16[768,256]{1,0:T(8,128)(2,1)S(1)} %get-tuple-element.106), channel_id=1, source_target_pairs={{0,5},{1,2},{2,7},{3,0},{4,1},{5,6},{6,3},{7,4},{8,13},{9,10},{10,... | collective-permute-start | bytes 1179656 | tf_op jit(solution)/shard_map/ppermute | solution.py:558
  40.4 10.4 %copy-start.3 = (f32[8,1024]{1,0:T(8,128)S(1)}, f32[8,1024]{1,0:T(8,128)}, u32[]{:S(2)}) copy-start(f32[8,1024]{1,0:T(8,128)} %decay_ref.1) | copy-start | bytes 98308
  40.4 10.3 %copy-start.4 = (f32[8,1024]{1,0:T(8,128)S(1)}, f32[8,1024]{1,0:T(8,128)}, u32[]{:S(2)}) copy-start(f32[8,1024]{1,0:T(8,128)} %residue_ref.1) | copy-start | bytes 98308
  47.5 3.2 %collective-permute-start.9 = (bf16[768,256]{1,0:T(8,128)(2,1)S(1)}, bf16[768,256]{1,0:T(8,128)(2,1)S(1)}, u32[]{:S(2)}, u32[]{:S(2)}) collective-permute-start(bf16[768,256]{1,0:T(8,128)(2,1)S(1)} %get-tuple-element.105), channel_id=1, source_target_pairs={{0,1},{1,0},{2,3},{3,2},{4,5},{5,4},{6,7},{7,6},{8,9},{9,8},{10,11... | collective-permute-start | bytes 1179656 | tf_op jit(solution)/shard_map/ppermute | solution.py:568
  47.5 7.8 %collective-permute-start.8 = (bf16[192,1024]{1,0:T(8,128)(2,1)S(1)}, bf16[192,1024]{1,0:T(8,128)(2,1)S(1)}, u32[]{:S(2)}, u32[]{:S(2)}) collective-permute-start(bf16[192,1024]{1,0:T(8,128)(2,1)S(1)} %get-tuple-element.103), channel_id=1, source_target_pairs={{0,2},{1,5},{2,0},{3,7},{4,6},{5,1},{6,4},{7,3},{8,10},{9,13},{10,... | collective-permute-start | bytes 1179656 | tf_op jit(solution)/shard_map/ppermute | solution.py:570
  53.6 1.7 %collective-permute-start.12 = (bf16[4,192,128]{2,1,0:T(8,128)(2,1)S(1)}, bf16[4,192,128]{2,1,0:T(8,128)(2,1)S(1)}, u32[]{:S(2)}, u32[]{:S(2)}) collective-permute-start(bf16[4,192,128]{2,1,0:T(8,128)(2,1)S(1)} %get-tuple-element.108), channel_id=1, source_target_pairs={{0,1},{1,0},{2,3},{3,2},{4,5},{5,4},{6,7},{7,6},{8,9},{9,8},{10,11... | collective-permute-start | bytes 589832 | tf_op jit(solution)/shard_map/ppermute | solution.py:574
  53.7 10.7 %collective-permute-start.14 = (bf16[192,1024]{1,0:T(8,128)(2,1)S(1)}, bf16[192,1024]{1,0:T(8,128)(2,1)S(1)}, u32[]{:S(2)}, u32[]{:S(2)}) collective-permute-start(bf16[192,1024]{1,0:T(8,128)(2,1)S(1)} %get-tuple-element.110), channel_id=1, source_target_pairs={{0,2},{1,5},{2,0},{3,7},{4,6},{5,1},{6,4},{7,3},{8,10},{9,13},{10,... | collective-permute-start | bytes 1179656 | tf_op jit(solution)/shard_map/ppermute | solution.py:571
  56.0 13.6 %collective-permute-start.13 = (bf16[192,1024]{1,0:T(8,128)(2,1)S(1)}, bf16[192,1024]{1,0:T(8,128)(2,1)S(1)}, u32[]{:S(2)}, u32[]{:S(2)}) collective-permute-start(bf16[192,1024]{1,0:T(8,128)(2,1)S(1)} %get-tuple-element.109), channel_id=1, source_target_pairs={{0,4},{1,3},{2,6},{3,1},{4,0},{5,7},{6,2},{7,5},{8,12},{9,11},{10,... | collective-permute-start | bytes 1179656 | tf_op jit(solution)/shard_map/ppermute | solution.py:576
  57.5 9.9 %collective-permute-start.15 = (bf16[2,192,128]{2,1,0:T(8,128)(2,1)S(1)}, bf16[2,192,128]{2,1,0:T(8,128)(2,1)S(1)}, u32[]{:S(2)}, u32[]{:S(2)}) collective-permute-start(bf16[2,192,128]{2,1,0:T(8,128)(2,1)S(1)} %get-tuple-element.112), channel_id=1, source_target_pairs={{0,4},{1,3},{2,6},{3,1},{4,0},{5,7},{6,2},{7,5},{8,12},{9,11},{10,... | collective-permute-start | bytes 294920 | tf_op jit(solution)/shard_map/ppermute | solution.py:577
  58.1 9.2 %collective-permute-start.16 = (bf16[2,192,128]{2,1,0:T(8,128)(2,1)S(1)}, bf16[2,192,128]{2,1,0:T(8,128)(2,1)S(1)}, u32[]{:S(2)}, u32[]{:S(2)}) collective-permute-start(bf16[2,192,128]{2,1,0:T(8,128)(2,1)S(1)} %get-tuple-element.113), channel_id=1, source_target_pairs={{0,2},{1,5},{2,0},{3,7},{4,6},{5,1},{6,4},{7,3},{8,10},{9,13},{10,... | collective-permute-start | bytes 294920 | tf_op jit(solution)/shard_map/ppermute | solution.py:577
  59.6 10.0 %collective-permute-start.17 = (bf16[2,192,128]{2,1,0:T(8,128)(2,1)S(1)}, bf16[2,192,128]{2,1,0:T(8,128)(2,1)S(1)}, u32[]{:S(2)}, u32[]{:S(2)}) collective-permute-start(bf16[2,192,128]{2,1,0:T(8,128)(2,1)S(1)} %get-tuple-element.114), channel_id=1, source_target_pairs={{0,6},{1,7},{2,4},{3,5},{4,2},{5,3},{6,0},{7,1},{8,14},{9,15},{10,... | collective-permute-start | bytes 294920 | tf_op jit(solution)/shard_map/ppermute | solution.py:577
  71.4 11.9 %collective-permute-start.18 = (bf16[192,1024]{1,0:T(8,128)(2,1)S(1)}, bf16[192,1024]{1,0:T(8,128)(2,1)S(1)}, u32[]{:S(2)}, u32[]{:S(2)}) collective-permute-start(bf16[192,1024]{1,0:T(8,128)(2,1)S(1)} %get-tuple-element.119), channel_id=1, source_target_pairs={{0,8},{8,0},{16,24},{24,16},{1,9},{9,1},{17,25},{25,17},{2,10},{10... | collective-permute-start | bytes 1179656 | tf_op jit(solution)/shard_map/ppermute | solution.py:482
  73.1 17.9 %collective-permute-start.19 = (bf16[192,1024]{1,0:T(8,128)(2,1)S(1)}, bf16[192,1024]{1,0:T(8,128)(2,1)S(1)}, u32[]{:S(2)}, u32[]{:S(2)}) collective-permute-start(bf16[192,1024]{1,0:T(8,128)(2,1)S(1)} %get-tuple-element.120.side_ref), channel_id=1, source_target_pairs={{8,16},{16,8},{9,17},{17,9},{10,18},{18,10},{11,19},{19,11},{12,20... | collective-permute-start | bytes 1179656 | tf_op jit(solution)/shard_map/ppermute | solution.py:484
  74.9 16.0 %collective-permute-start.20 = (bf16[192,1024]{1,0:T(8,128)(2,1)S(1)}, bf16[192,1024]{1,0:T(8,128)(2,1)S(1)}, u32[]{:S(2)}, u32[]{:S(2)}) collective-permute-start(bf16[192,1024]{1,0:T(8,128)(2,1)S(1)} %out_columns.2.far_ref), channel_id=1, source_target_pairs={{0,16},{24,8},{1,17},{25,9},{2,18},{26,10},{3,19},{27,11},{4,20},{... | collective-permute-start | bytes 1179656 | tf_op jit(solution)/shard_map/ppermute | solution.py:486
  84.0 20.2 %collective-permute-start.21 = (bf16[192,1024]{1,0:T(8,128)(2,1)S(1)}, bf16[192,1024]{1,0:T(8,128)(2,1)S(1)}, u32[]{:S(2)}, u32[]{:S(2)}) collective-permute-start(bf16[192,1024]{1,0:T(8,128)(2,1)S(1)} %last_step.1), channel_id=1, source_target_pairs={{0,8},{8,24},{16,0},{24,16},{1,9},{9,25},{17,1},{25,17},{2,10},{10... | collective-permute-start | bytes 1179656 | tf_op jit(solution)/shard_map/ppermute | solution.py:494

commit v7 on v6

--- a/solution.py
+++ b/solution.py
@@ -501,11 +501,8 @@
             value = value + ref[...].astype(F32)
         refs[-1][...] = value
 
-    def total(picks, early_ref, last_ref, out_ref):
-        out_ref[...] = (early_ref[...] + last_ref[...].astype(F32)).astype(BF16)
-
     own = local(early, "early", [(own.shape, F32)], picks, [own, pair_in, middle_in, end_in])
-    return local(total, "total", [(own.shape, BF16)], picks, [own, last_in])
+    return (own + last_in.astype(F32)).astype(BF16)
 
 
 def on_device_chips(tokens, w_in, short_filter, mode_decay, residue, w_out):

time: 106 us -> 105 us (level)
  Pallas kernels: 22.9 us -> 21.5 us
    pallas_call x16 -> x15, Pallas kernels: 22.1 us -> 20.7 us  [local(): pl.pallas_call(kernel, out_shape=out if len(out) > 1 else out[0], in_spec...]
where the time goes in v7:
time: 105 us
  waiting for transfers between devices  50 us (48%)
  starting transfers between devices  28.9 us (28%)
  Pallas kernels  21.5 us (20%)
  local copies, waits for them, and re-layouts  3.59 us (3%)
    pallas_call x15, Pallas kernels, local(): pl.pallas_call(kernel, out_shape=out if len(out) > 1 else out[0], in_spec...  20.7 us
    ppermute x1, waiting for transfers between devices, output_over_line(): last_in = lax.ppermute(last, 'dp', [(0, 1), (1, 3), (2, 0), (3, 2)])  12.6 us
    ppermute x1, waiting for transfers between devices, on_device_chips(): first_in = lax.ppermute(first, 'ctx', route(2))  6.4 us
    ppermute x1, starting transfers between devices, output_over_line(): end_in = lax.ppermute(far, 'dp', [(0, 2), (3, 1)])  5.75 us
    ppermute x1, waiting for transfers between devices, on_device_chips(): both_in = lax.ppermute(both, 'ctx', route(2))  5.54 us
    ppermute x1, waiting for transfers between devices, on_device_chips(): half = lax.ppermute(xs[3], 'ctx', route(3))  5.15 us
    ppermute x3, waiting for transfers between devices, on_device_chips(): lax.ppermute(long_parts[s], 'ctx', route(s))  5.14 us
    ppermute x1, waiting for transfers between devices, output_over_line(): end_in = lax.ppermute(far, 'dp', [(0, 2), (3, 1)])  4.11 us
  transfers between devices with their start and end apart: 22, of which 14 were waited for; matrix products, arithmetic and copies ran while one was open for 0% of the time, Pallas kernels for 18%

profile of v7, /device:TPU:0, one launch (start us, length us, event | category | flops | bytes accessed | tf_op | source)
XLA Modules:
  0.0 105.1 jit_solution(574436920631627113)
XLA Ops:
  0.0 0.5 collective-permute-start.4
  0.5 0.1 stack.59.order
  0.5 0.1 concatenate.4.scalars
  0.6 0.1 stack.65.picks
  0.7 1.4 %copy-done.1 = bf16[192,4096]{1,0:T(8,128)(2,1)S(1)} copy-done((bf16[192,4096]{1,0:T(8,128)(2,1)S(1)}, bf16[192,4096]{1,0:T(8,128)(2,1)}, u32[]{:S(2)}) %copy-start.1) | copy-done | bytes 1572888
  2.1 0.6 cut.1
  2.8 3.5 %collective-permute-start.2 = (bf16[96,1024]{1,0:T(8,128)(2,1)S(1)}, bf16[96,1024]{1,0:T(8,128)(2,1)S(1)}, u32[]{:S(2)}, u32[]{:S(2)}) collective-permute-start(bf16[96,1024]{1,0:T(8,128)(2,1)S(1)} %get-tuple-element.74), channel_id=1, source_target_pairs={{0,6},{1,7},{2,4},{3,5},{4,2},{5,3},{6,0},{7,1},{8,14},{9,15},{10,... | collective-permute-start | bytes 589832 | tf_op jit(solution)/shard_map/ppermute | solution.py:540
  6.3 0.5 collective-permute-start
  6.8 0.1 collective-permute-start.1
  6.9 5.2 %collective-permute-done.2.mine_ref = bf16[96,1024]{1,0:T(8,128)(2,1)S(1)} collective-permute-done((bf16[96,1024]{1,0:T(8,128)(2,1)S(1)}, bf16[96,1024]{1,0:T(8,128)(2,1)S(1)}, u32[]{:S(2)}, u32[]{:S(2)}) %collective-permute-start.2) | collective-permute-done | bytes 196640 | tf_op jit(solution)/shard_map/ppermute | solution.py:540
  12.1 2.0 %collective-permute-start.3 = (bf16[96,1024]{1,0:T(8,128)(2,1)S(1)}, bf16[96,1024]{1,0:T(8,128)(2,1)S(1)}, u32[]{:S(2)}, u32[]{:S(2)}) collective-permute-start(bf16[96,1024]{1,0:T(8,128)(2,1)S(1)} %collective-permute-done.2.mine_ref), channel_id=1, source_target_pairs={{0,8},{8,0},{16,24},{24,16},{1,9},{9,1},{17,25},{25,17},{2,10},{10... | collective-permute-start | bytes 589832 | tf_op jit(solution)/shard_map/ppermute | solution.py:541
  14.1 1.9 %copy-done = bf16[512,3,1024]{2,0,1:T(8,128)(2,1)S(1)} copy-done((bf16[512,3,1024]{2,0,1:T(8,128)(2,1)S(1)}, bf16[512,3,1024]{2,0,1:T(8,128)(2,1)}, u32[]{:S(2)}) %copy-start) | copy-done | bytes 3145752
  15.9 0.2 stage.2.own_ref.refs_4_.refs_5_
  16.2 2.5 %collective-permute-done.3.there_ref = bf16[96,1024]{1,0:T(8,128)(2,1)S(1)} collective-permute-done((bf16[96,1024]{1,0:T(8,128)(2,1)S(1)}, bf16[96,1024]{1,0:T(8,128)(2,1)S(1)}, u32[]{:S(2)}, u32[]{:S(2)}) %collective-permute-start.3) | collective-permute-done | bytes 196640 | tf_op jit(solution)/shard_map/ppermute | solution.py:541
  18.6 0.0 collective-permute-done.4.other_ref.refs_5_.refs_6_
  18.6 1.2 %early_share.1 = (bf16[192,1024]{1,0:T(8,128)(2,1)S(1)}, bf16[2,384,256]{2,1,0:T(8,128)(2,1)S(1)}) custom-call(s32[11]{0:T(128)S(1)} %stack.59.order, bf16[192,1024]{1,0:T(8,128)(2,1)S(1)} %get-tuple-element.89.own_rows_ref.refs_0_, bf16[96,1024]{1,0:T(8,128)(2,1)S(1)} %collective-permute-done.2.mine_ref, ...), custom_call_target="tpu_custom_call" | custom-call | tf_op jit(solution)/shard_map/early_share/pallas_call | solution.py:101
  19.9 0.4 collective-permute-done.first_ref.refs_1_
  20.3 0.3 collective-permute-done.1.second_ref.refs_2_
  20.6 1.2 %rest_share.1 = bf16[1,2,768,256]{3,2,1,0:T(8,128)(2,1)S(1)} custom-call(s32[11]{0:T(128)S(1)} %stack.59.order, bf16[192,1024]{1,0:T(8,128)(2,1)S(1)} %collective-permute-done.first_ref.refs_1_, bf16[192,1024]{1,0:T(8,128)(2,1)S(1)} %collective-permute-done.1.second_ref.refs_2_, bf16[2,384,256]{2,1,0:T(8,128)(2,1)S(1)} %get-tuple-element.77.early_ref, ...), custom_call_target="tpu_custom_call" | custom-call | tf_op jit(solution)/shard_map/rest_share/pallas_call | solution.py:101
  21.8 1.6 %collective-permute-start.5 = (bf16[1,2,768,256]{3,2,1,0:T(8,128)(2,1)S(1)}, bf16[1,2,768,256]{3,2,1,0:T(8,128)(2,1)S(1)}, u32[]{:S(2)}, u32[]{:S(2)}) collective-permute-start(bf16[1,2,768,256]{3,2,1,0:T(8,128)(2,1)S(1)} %rest_share.1), channel_id=1, source_target_pairs={{0,2},{1,5},{2,0},{3,7},{4,6},{5,1},{6,4},{7,3},{8,10},{9,13},{10,... | collective-permute-start | bytes 2359304 | tf_op jit(solution)/shard_map/ppermute | solution.py:547
  23.4 1.7 %project_mix.2 = bf16[1,2,768,256]{3,2,1,0:T(8,128)(2,1)S(1)} custom-call(s32[11]{0:T(128)S(1)} %stack.59.order, bf16[192,1024]{1,0:T(8,128)(2,1)S(1)} %get-tuple-element.89.own_rows_ref.refs_0_, bf16[192,1024]{1,0:T(8,128)(2,1)S(1)} %collective-permute-done.first_ref.refs_1_, bf16[192,1024]{1,0:T(8,128)(2,1)S(1)} %collective-permute-done.1.second_ref.refs_2_, ...), custom_call_target="tpu_custom_call" | custom-call | tf_op jit(solution)/shard_map/project_mix/pallas_call | solution.py:101
  25.1 0.6 collective-permute-start.7
  25.7 2.6 %project_mix.3 = (f32[2,2,768,256]{3,2,1,0:T(8,128)S(1)}, bf16[4,16,1024]{2,1,0:T(8,128)(2,1)S(1)}) custom-call(s32[11]{0:T(128)S(1)} %stack.59.order, bf16[192,1024]{1,0:T(8,128)(2,1)S(1)} %get-tuple-element.89.own_rows_ref.refs_0_, bf16[192,1024]{1,0:T(8,128)(2,1)S(1)} %collective-permute-done.first_ref.refs_1_, ...), custom_call_target="tpu_custom_call" | custom-call | tf_op jit(solution)/shard_map/project_mix/pallas_call | solution.py:101
  28.3 0.0 copy-start.2
  28.3 5.5 %collective-permute-done.5.both_ref = bf16[1,2,768,256]{3,2,1,0:T(8,128)(2,1)S(1)} collective-permute-done((bf16[1,2,768,256]{3,2,1,0:T(8,128)(2,1)S(1)}, bf16[1,2,768,256]{3,2,1,0:T(8,128)(2,1)S(1)}, u32[]{:S(2)}, u32[]{:S(2)}) %collective-permute-start.5) | collective-permute-done | bytes 786464 | tf_op jit(solution)/shard_map/ppermute | solution.py:547
  33.8 0.7 second_share.1
  34.5 0.1 collective-permute-start.6
  34.6 1.5 %collective-permute-start.10 = (bf16[768,256]{1,0:T(8,128)(2,1)S(1)}, bf16[768,256]{1,0:T(8,128)(2,1)S(1)}, u32[]{:S(2)}, u32[]{:S(2)}) collective-permute-start(bf16[768,256]{1,0:T(8,128)(2,1)S(1)} %get-tuple-element.88), channel_id=1, source_target_pairs={{0,4},{1,3},{2,6},{3,1},{4,0},{5,7},{6,2},{7,5},{8,12},{9,11},{10,... | collective-permute-start | bytes 1179656 | tf_op jit(solution)/shard_map/ppermute | solution.py:554
  36.1 0.7 collective-permute-start.11
  36.8 0.0 collective-permute-done.6.refs_4_
  36.8 3.0 %project_query.1 = (f32[192,1024]{1,0:T(8,128)S(1)}, f32[192,1024]{1,0:T(8,128)S(1)}, bf16[192,1024]{1,0:T(8,128)(2,1)S(1)}, bf16[192,1024]{1,0:T(8,128)(2,1)S(1)}) custom-call(s32[11]{0:T(128)S(1)} %stack.59.order, bf16[192,1024]{1,0:T(8,128)(2,1)S(1)} %get-tuple-element.89.own_rows_ref.refs_0_, ...), custom_call_target="tpu_custom_call" | custom-call | tf_op jit(solution)/shard_map/project_query/pallas_call | solution.py:101
  39.8 0.6 stage.3.refs_7_.w_ref
  40.4 0.0 copy-start.3
  40.4 0.0 copy-start.4
  40.4 6.4 %collective-permute-done.7.first_ref = bf16[1,2,768,256]{3,2,1,0:T(8,128)(2,1)S(1)} collective-permute-done((bf16[1,2,768,256]{3,2,1,0:T(8,128)(2,1)S(1)}, bf16[1,2,768,256]{3,2,1,0:T(8,128)(2,1)S(1)}, u32[]{:S(2)}, u32[]{:S(2)}) %collective-permute-start.7) | collective-permute-done | bytes 786464 | tf_op jit(solution)/shard_map/ppermute | solution.py:550
  46.8 0.7 first_share.1
  47.5 0.1 collective-permute-start.9
  47.5 1.6 %collective-permute-start.8 = (bf16[192,1024]{1,0:T(8,128)(2,1)S(1)}, bf16[192,1024]{1,0:T(8,128)(2,1)S(1)}, u32[]{:S(2)}, u32[]{:S(2)}) collective-permute-start(bf16[192,1024]{1,0:T(8,128)(2,1)S(1)} %get-tuple-element.103), channel_id=1, source_target_pairs={{0,2},{1,5},{2,0},{3,7},{4,6},{5,1},{6,4},{7,3},{8,10},{9,13},{10,... | collective-permute-start | bytes 1179656 | tf_op jit(solution)/shard_map/ppermute | solution.py:567
  49.1 1.6 %collective-permute-done.11.swap_second_ref = bf16[768,256]{1,0:T(8,128)(2,1)S(1)} collective-permute-done((bf16[768,256]{1,0:T(8,128)(2,1)S(1)}, bf16[768,256]{1,0:T(8,128)(2,1)S(1)}, u32[]{:S(2)}, u32[]{:S(2)}) %collective-permute-start.11) | collective-permute-done | bytes 393248 | tf_op jit(solution)/shard_map/ppermute | solution.py:555
  50.7 2.9 %hyena.1 = (bf16[4,192,128]{2,1,0:T(8,128)(2,1)S(1)}, bf16[4,192,128]{2,1,0:T(8,128)(2,1)S(1)}) custom-call(s32[11]{0:T(128)S(1)} %stack.59.order, f32[768,256]{1,0:T(8,128)S(1)} %get-tuple-element.104.own_ref, bf16[768,256]{1,0:T(8,128)(2,1)S(1)} %collective-permute-done.9.swap_ref, bf16[768,256]{1,0:T(8,128)(2,1)S(1)} %collective-permute-done.10.second_ref, ...), custom_call_target="tpu_custom_call" | custom-call | tf_op jit(solution)/shard_map/hyena/pallas_call | solution.py:101
  53.6 0.1 collective-permute-start.12
  53.7 1.6 %collective-permute-start.14 = (bf16[192,1024]{1,0:T(8,128)(2,1)S(1)}, bf16[192,1024]{1,0:T(8,128)(2,1)S(1)}, u32[]{:S(2)}, u32[]{:S(2)}) collective-permute-start(bf16[192,1024]{1,0:T(8,128)(2,1)S(1)} %get-tuple-element.110), channel_id=1, source_target_pairs={{0,2},{1,5},{2,0},{3,7},{4,6},{5,1},{6,4},{7,3},{8,10},{9,13},{10,... | collective-permute-start | bytes 1179656 | tf_op jit(solution)/shard_map/ppermute | solution.py:568
  55.3 0.1 collective-permute-done.8.in_ref
  55.4 0.6 payloads.1
  56.0 1.5 %collective-permute-start.13 = (bf16[192,1024]{1,0:T(8,128)(2,1)S(1)}, bf16[192,1024]{1,0:T(8,128)(2,1)S(1)}, u32[]{:S(2)}, u32[]{:S(2)}) collective-permute-start(bf16[192,1024]{1,0:T(8,128)(2,1)S(1)} %get-tuple-element.109), channel_id=1, source_target_pairs={{0,4},{1,3},{2,6},{3,1},{4,0},{5,7},{6,2},{7,5},{8,12},{9,11},{10,... | collective-permute-start | bytes 1179656 | tf_op jit(solution)/shard_map/ppermute | solution.py:573
  57.5 0.6 collective-permute-start.15
  58.1 1.5 %collective-permute-start.16 = (bf16[2,192,128]{2,1,0:T(8,128)(2,1)S(1)}, bf16[2,192,128]{2,1,0:T(8,128)(2,1)S(1)}, u32[]{:S(2)}, u32[]{:S(2)}) collective-permute-start(bf16[2,192,128]{2,1,0:T(8,128)(2,1)S(1)} %get-tuple-element.113), channel_id=1, source_target_pairs={{0,2},{1,5},{2,0},{3,7},{4,6},{5,1},{6,4},{7,3},{8,10},{9,13},{10,... | collective-permute-start | bytes 294920 | tf_op jit(solution)/shard_map/ppermute | solution.py:574
  59.6 1.4 %collective-permute-start.17 = (bf16[2,192,128]{2,1,0:T(8,128)(2,1)S(1)}, bf16[2,192,128]{2,1,0:T(8,128)(2,1)S(1)}, u32[]{:S(2)}, u32[]{:S(2)}) collective-permute-start(bf16[2,192,128]{2,1,0:T(8,128)(2,1)S(1)} %get-tuple-element.114), channel_id=1, source_target_pairs={{0,6},{1,7},{2,4},{3,5},{4,2},{5,3},{6,0},{7,1},{8,14},{9,15},{10,... | collective-permute-start | bytes 294920 | tf_op jit(solution)/shard_map/ppermute | solution.py:574
  61.0 3.5 %collective-permute-done.14.refs_2_ = bf16[192,1024]{1,0:T(8,128)(2,1)S(1)} collective-permute-done((bf16[192,1024]{1,0:T(8,128)(2,1)S(1)}, bf16[192,1024]{1,0:T(8,128)(2,1)S(1)}, u32[]{:S(2)}, u32[]{:S(2)}) %collective-permute-start.14) | collective-permute-done | bytes 393248 | tf_op jit(solution)/shard_map/ppermute | solution.py:568
  64.4 2.9 %collective-permute-done.15.refs_4_ = bf16[2,192,128]{2,1,0:T(8,128)(2,1)S(1)} collective-permute-done((bf16[2,192,128]{2,1,0:T(8,128)(2,1)S(1)}, bf16[2,192,128]{2,1,0:T(8,128)(2,1)S(1)}, u32[]{:S(2)}, u32[]{:S(2)}) %collective-permute-start.15) | collective-permute-done | bytes 98336 | tf_op jit(solution)/shard_map/ppermute | solution.py:574
  67.4 2.2 %collective-permute-done.17.refs_6_ = bf16[2,192,128]{2,1,0:T(8,128)(2,1)S(1)} collective-permute-done((bf16[2,192,128]{2,1,0:T(8,128)(2,1)S(1)}, bf16[2,192,128]{2,1,0:T(8,128)(2,1)S(1)}, u32[]{:S(2)}, u32[]{:S(2)}) %collective-permute-start.17) | collective-permute-done | bytes 98336 | tf_op jit(solution)/shard_map/ppermute | solution.py:574
  69.6 1.8 %gate.1 = (bf16[192,1024]{1,0:T(8,128)(2,1)S(1)}, bf16[192,1024]{1,0:T(8,128)(2,1)S(1)}, bf16[192,1024]{1,0:T(8,128)(2,1)S(1)}) custom-call(s32[16]{0:T(128)S(1)} %concatenate.4.scalars, f32[192,1024]{1,0:T(8,128)S(1)} %get-tuple-element.97.refs_0_, bf16[192,1024]{1,0:T(8,128)(2,1)S(1)} %collective-permute-done.13.refs_1_, ...), custom_call_target="tpu_custom_call" | custom-call | tf_op jit(solution)/shard_map/gate/pallas_call | solution.py:101
  71.4 1.6 %collective-permute-start.18 = (bf16[192,1024]{1,0:T(8,128)(2,1)S(1)}, bf16[192,1024]{1,0:T(8,128)(2,1)S(1)}, u32[]{:S(2)}, u32[]{:S(2)}) collective-permute-start(bf16[192,1024]{1,0:T(8,128)(2,1)S(1)} %get-tuple-element.119), channel_id=1, source_target_pairs={{0,8},{8,0},{16,24},{24,16},{1,9},{9,1},{17,25},{25,17},{2,10},{10... | collective-permute-start | bytes 1179656 | tf_op jit(solution)/shard_map/ppermute | solution.py:482
  73.1 0.7 collective-permute-start.19
  73.7 1.1 %out_columns.2.far_ref = bf16[192,1024]{1,0:T(8,128)(2,1)S(1)} custom-call(s32[5]{0:T(128)S(1)} %stack.65.picks, bf16[192,1024]{1,0:T(8,128)(2,1)S(1)} %get-tuple-element.121.x_ref, bf16[1024,4096]{1,0:T(8,128)(2,1)S(1)} %stage.3.refs_7_.w_ref), custom_call_target="tpu_custom_call" | custom-call | tf_op jit(solution)/shard_map/out_columns/pallas_call | solution.py:101
  74.9 5.8 %collective-permute-start.20 = (bf16[192,1024]{1,0:T(8,128)(2,1)S(1)}, bf16[192,1024]{1,0:T(8,128)(2,1)S(1)}, u32[]{:S(2)}, u32[]{:S(2)}) collective-permute-start(bf16[192,1024]{1,0:T(8,128)(2,1)S(1)} %out_columns.2.far_ref), channel_id=1, source_target_pairs={{0,16},{24,8},{1,17},{25,9},{2,18},{26,10},{3,19},{27,11},{4,20},{... | collective-permute-start | bytes 1179656 | tf_op jit(solution)/shard_map/ppermute | solution.py:486
  80.7 2.7 %collective-permute-done.18.pair_ref = bf16[192,1024]{1,0:T(8,128)(2,1)S(1)} collective-permute-done((bf16[192,1024]{1,0:T(8,128)(2,1)S(1)}, bf16[192,1024]{1,0:T(8,128)(2,1)S(1)}, u32[]{:S(2)}, u32[]{:S(2)}) %collective-permute-start.18) | collective-permute-done | bytes 393248 | tf_op jit(solution)/shard_map/ppermute | solution.py:482
  83.4 0.7 last_step.1
  84.0 1.6 %collective-permute-start.21 = (bf16[192,1024]{1,0:T(8,128)(2,1)S(1)}, bf16[192,1024]{1,0:T(8,128)(2,1)S(1)}, u32[]{:S(2)}, u32[]{:S(2)}) collective-permute-start(bf16[192,1024]{1,0:T(8,128)(2,1)S(1)} %last_step.1), channel_id=1, source_target_pairs={{0,8},{8,24},{16,0},{24,16},{1,9},{9,25},{17,1},{25,17},{2,10},{10... | collective-permute-start | bytes 1179656 | tf_op jit(solution)/shard_map/ppermute | solution.py:494
  85.7 1.1 %out_columns.3.own_ref = f32[192,1024]{1,0:T(8,128)S(1)} custom-call(s32[5]{0:T(128)S(1)} %stack.65.picks, bf16[192,1024]{1,0:T(8,128)(2,1)S(1)} %get-tuple-element.121.x_ref, bf16[1024,4096]{1,0:T(8,128)(2,1)S(1)} %stage.3.refs_7_.w_ref), custom_call_target="tpu_custom_call" | custom-call | tf_op jit(solution)/shard_map/out_columns/pallas_call | solution.py:101
  86.8 4.1 %collective-permute-done.20.refs_1_ = bf16[192,1024]{1,0:T(8,128)(2,1)S(1)} collective-permute-done((bf16[192,1024]{1,0:T(8,128)(2,1)S(1)}, bf16[192,1024]{1,0:T(8,128)(2,1)S(1)}, u32[]{:S(2)}, u32[]{:S(2)}) %collective-permute-start.20) | collective-permute-done | bytes 393248 | tf_op jit(solution)/shard_map/ppermute | solution.py:486
  90.9 0.7 early.1
  91.7 12.6 %collective-permute-done.21 = bf16[192,1024]{1,0:T(8,128)(2,1)S(1)} collective-permute-done((bf16[192,1024]{1,0:T(8,128)(2,1)S(1)}, bf16[192,1024]{1,0:T(8,128)(2,1)S(1)}, u32[]{:S(2)}, u32[]{:S(2)}) %collective-permute-start.21) | collective-permute-done | bytes 393248 | tf_op jit(solution)/shard_map/ppermute | solution.py:494
  104.2 0.8 add_convert_fusion
  (16 shorter events, 0.0 us)
Async XLA Ops:
  0.0 18.6 %collective-permute-start.4 = (bf16[3,512,1024]{2,1,0:T(8,128)(2,1)}, bf16[3,512,1024]{2,1,0:T(8,128)(2,1)S(1)}, u32[]{:S(2)}, u32[]{:S(2)}) collective-permute-start(bf16[3,512,1024]{2,1,0:T(8,128)(2,1)} %bitcast.17), channel_id=1, source_target_pairs={{0,1},{1,0},{2,3},{3,2},{4,5},{5,4},{6,7},{7,6},{8,9},{9,8},{10,11... | collective-permute-start | bytes 9437192 | tf_op jit(solution)/shard_map/ppermute | solution.py:536
  0.7 1.4 %copy-start.1 = (bf16[192,4096]{1,0:T(8,128)(2,1)S(1)}, bf16[192,4096]{1,0:T(8,128)(2,1)}, u32[]{:S(2)}) copy-start(bf16[192,4096]{1,0:T(8,128)(2,1)} %tokens_ref.1) | copy-start | bytes 4718596
  2.8 9.3 %collective-permute-start.2 = (bf16[96,1024]{1,0:T(8,128)(2,1)S(1)}, bf16[96,1024]{1,0:T(8,128)(2,1)S(1)}, u32[]{:S(2)}, u32[]{:S(2)}) collective-permute-start(bf16[96,1024]{1,0:T(8,128)(2,1)S(1)} %get-tuple-element.74), channel_id=1, source_target_pairs={{0,6},{1,7},{2,4},{3,5},{4,2},{5,3},{6,0},{7,1},{8,14},{9,15},{10,... | collective-permute-start | bytes 589832 | tf_op jit(solution)/shard_map/ppermute | solution.py:540
  6.3 14.0 %collective-permute-start = (bf16[192,1024]{1,0:T(8,128)(2,1)S(1)}, bf16[192,1024]{1,0:T(8,128)(2,1)S(1)}, u32[]{:S(2)}, u32[]{:S(2)}) collective-permute-start(bf16[192,1024]{1,0:T(8,128)(2,1)S(1)} %get-tuple-element.72), channel_id=1, source_target_pairs={{0,4},{1,3},{2,6},{3,1},{4,0},{5,7},{6,2},{7,5},{8,12},{9,11},{10,... | collective-permute-start | bytes 1179656 | tf_op jit(solution)/shard_map/ppermute | solution.py:542
  6.8 13.8 %collective-permute-start.1 = (bf16[192,1024]{1,0:T(8,128)(2,1)S(1)}, bf16[192,1024]{1,0:T(8,128)(2,1)S(1)}, u32[]{:S(2)}, u32[]{:S(2)}) collective-permute-start(bf16[192,1024]{1,0:T(8,128)(2,1)S(1)} %get-tuple-element.73), channel_id=1, source_target_pairs={{0,2},{1,5},{2,0},{3,7},{4,6},{5,1},{6,4},{7,3},{8,10},{9,13},{10,... | collective-permute-start | bytes 1179656 | tf_op jit(solution)/shard_map/ppermute | solution.py:542
  12.1 6.6 %collective-permute-start.3 = (bf16[96,1024]{1,0:T(8,128)(2,1)S(1)}, bf16[96,1024]{1,0:T(8,128)(2,1)S(1)}, u32[]{:S(2)}, u32[]{:S(2)}) collective-permute-start(bf16[96,1024]{1,0:T(8,128)(2,1)S(1)} %collective-permute-done.2.mine_ref), channel_id=1, source_target_pairs={{0,8},{8,0},{16,24},{24,16},{1,9},{9,1},{17,25},{25,17},{2,10},{10... | collective-permute-start | bytes 589832 | tf_op jit(solution)/shard_map/ppermute | solution.py:541
  14.1 1.9 %copy-start = (bf16[512,3,1024]{2,0,1:T(8,128)(2,1)S(1)}, bf16[512,3,1024]{2,0,1:T(8,128)(2,1)}, u32[]{:S(2)}) copy-start(bf16[512,3,1024]{2,0,1:T(8,128)(2,1)} %param.7) | copy-start | bytes 9437188
  21.8 12.1 %collective-permute-start.5 = (bf16[1,2,768,256]{3,2,1,0:T(8,128)(2,1)S(1)}, bf16[1,2,768,256]{3,2,1,0:T(8,128)(2,1)S(1)}, u32[]{:S(2)}, u32[]{:S(2)}) collective-permute-start(bf16[1,2,768,256]{3,2,1,0:T(8,128)(2,1)S(1)} %rest_share.1), channel_id=1, source_target_pairs={{0,2},{1,5},{2,0},{3,7},{4,6},{5,1},{6,4},{7,3},{8,10},{9,13},{10,... | collective-permute-start | bytes 2359304 | tf_op jit(solution)/shard_map/ppermute | solution.py:547
  25.1 21.7 %collective-permute-start.7 = (bf16[1,2,768,256]{3,2,1,0:T(8,128)(2,1)S(1)}, bf16[1,2,768,256]{3,2,1,0:T(8,128)(2,1)S(1)}, u32[]{:S(2)}, u32[]{:S(2)}) collective-permute-start(bf16[1,2,768,256]{3,2,1,0:T(8,128)(2,1)S(1)} %project_mix.2), channel_id=1, source_target_pairs={{0,2},{1,5},{2,0},{3,7},{4,6},{5,1},{6,4},{7,3},{8,10},{9,13},{10,... | collective-permute-start | bytes 2359304 | tf_op jit(solution)/shard_map/ppermute | solution.py:550
  25.7 14.1 %slice-start = ((s8[8388608]{0:T(1024)(128)(4,1)}), s8[4194304]{0:T(1024)(128)(4,1)S(1)}, s32[]{:S(2)}) async-start(s8[8388608]{0:T(1024)(128)(4,1)} %bitcast.15), calls=%async_computation | async-start | bytes 8388608
  28.3 8.5 %copy-start.2 = (f32[3,3,1024]{2,1,0:T(4,128)S(1)}, f32[3,3,1024]{2,1,0:T(4,128)}, u32[]{:S(2)}) copy-start(f32[3,3,1024]{2,1,0:T(4,128)} %filt_ref.1) | copy-start | bytes 110596
  33.8 5.9 %slice-start.1 = ((s8[8388608]{0:T(1024)(128)(4,1)}), s8[4194304]{0:T(1024)(128)(4,1)S(1)}, s32[]{:S(2)}) async-start(s8[8388608]{0:T(1024)(128)(4,1)} %bitcast.15), calls=%async_computation.1 | async-start | bytes 8388608
  34.5 2.2 %collective-permute-start.6 = (bf16[4,16,1024]{2,1,0:T(8,128)(2,1)S(1)}, bf16[4,16,1024]{2,1,0:T(8,128)(2,1)S(1)}, u32[]{:S(2)}, u32[]{:S(2)}) collective-permute-start(bf16[4,16,1024]{2,1,0:T(8,128)(2,1)S(1)} %get-tuple-element.93), channel_id=1, source_target_pairs={{0,1},{1,0},{2,3},{3,2},{4,5},{5,4},{6,7},{7,6},{8,9},{9,8},{10,11... | collective-permute-start | bytes 393224 | tf_op jit(solution)/shard_map/ppermute | solution.py:558
  34.6 16.1 %collective-permute-start.10 = (bf16[768,256]{1,0:T(8,128)(2,1)S(1)}, bf16[768,256]{1,0:T(8,128)(2,1)S(1)}, u32[]{:S(2)}, u32[]{:S(2)}) collective-permute-start(bf16[768,256]{1,0:T(8,128)(2,1)S(1)} %get-tuple-element.88), channel_id=1, source_target_pairs={{0,4},{1,3},{2,6},{3,1},{4,0},{5,7},{6,2},{7,5},{8,12},{9,11},{10,... | collective-permute-start | bytes 1179656 | tf_op jit(solution)/shard_map/ppermute | solution.py:554
  36.1 14.6 %collective-permute-start.11 = (bf16[768,256]{1,0:T(8,128)(2,1)S(1)}, bf16[768,256]{1,0:T(8,128)(2,1)S(1)}, u32[]{:S(2)}, u32[]{:S(2)}) collective-permute-start(bf16[768,256]{1,0:T(8,128)(2,1)S(1)} %get-tuple-element.106), channel_id=1, source_target_pairs={{0,5},{1,2},{2,7},{3,0},{4,1},{5,6},{6,3},{7,4},{8,13},{9,10},{10,... | collective-permute-start | bytes 1179656 | tf_op jit(solution)/shard_map/ppermute | solution.py:555
  40.4 10.4 %copy-start.3 = (f32[8,1024]{1,0:T(8,128)S(1)}, f32[8,1024]{1,0:T(8,128)}, u32[]{:S(2)}) copy-start(f32[8,1024]{1,0:T(8,128)} %decay_ref.1) | copy-start | bytes 98308
  40.4 10.3 %copy-start.4 = (f32[8,1024]{1,0:T(8,128)S(1)}, f32[8,1024]{1,0:T(8,128)}, u32[]{:S(2)}) copy-start(f32[8,1024]{1,0:T(8,128)} %residue_ref.1) | copy-start | bytes 98308
  47.5 3.2 %collective-permute-start.9 = (bf16[768,256]{1,0:T(8,128)(2,1)S(1)}, bf16[768,256]{1,0:T(8,128)(2,1)S(1)}, u32[]{:S(2)}, u32[]{:S(2)}) collective-permute-start(bf16[768,256]{1,0:T(8,128)(2,1)S(1)} %get-tuple-element.105), channel_id=1, source_target_pairs={{0,1},{1,0},{2,3},{3,2},{4,5},{5,4},{6,7},{7,6},{8,9},{9,8},{10,11... | collective-permute-start | bytes 1179656 | tf_op jit(solution)/shard_map/ppermute | solution.py:565
  47.5 7.8 %collective-permute-start.8 = (bf16[192,1024]{1,0:T(8,128)(2,1)S(1)}, bf16[192,1024]{1,0:T(8,128)(2,1)S(1)}, u32[]{:S(2)}, u32[]{:S(2)}) collective-permute-start(bf16[192,1024]{1,0:T(8,128)(2,1)S(1)} %get-tuple-element.103), channel_id=1, source_target_pairs={{0,2},{1,5},{2,0},{3,7},{4,6},{5,1},{6,4},{7,3},{8,10},{9,13},{10,... | collective-permute-start | bytes 1179656 | tf_op jit(solution)/shard_map/ppermute | solution.py:567
  53.6 1.7 %collective-permute-start.12 = (bf16[4,192,128]{2,1,0:T(8,128)(2,1)S(1)}, bf16[4,192,128]{2,1,0:T(8,128)(2,1)S(1)}, u32[]{:S(2)}, u32[]{:S(2)}) collective-permute-start(bf16[4,192,128]{2,1,0:T(8,128)(2,1)S(1)} %get-tuple-element.108), channel_id=1, source_target_pairs={{0,1},{1,0},{2,3},{3,2},{4,5},{5,4},{6,7},{7,6},{8,9},{9,8},{10,11... | collective-permute-start | bytes 589832 | tf_op jit(solution)/shard_map/ppermute | solution.py:571
  53.7 10.7 %collective-permute-start.14 = (bf16[192,1024]{1,0:T(8,128)(2,1)S(1)}, bf16[192,1024]{1,0:T(8,128)(2,1)S(1)}, u32[]{:S(2)}, u32[]{:S(2)}) collective-permute-start(bf16[192,1024]{1,0:T(8,128)(2,1)S(1)} %get-tuple-element.110), channel_id=1, source_target_pairs={{0,2},{1,5},{2,0},{3,7},{4,6},{5,1},{6,4},{7,3},{8,10},{9,13},{10,... | collective-permute-start | bytes 1179656 | tf_op jit(solution)/shard_map/ppermute | solution.py:568
  56.0 13.6 %collective-permute-start.13 = (bf16[192,1024]{1,0:T(8,128)(2,1)S(1)}, bf16[192,1024]{1,0:T(8,128)(2,1)S(1)}, u32[]{:S(2)}, u32[]{:S(2)}) collective-permute-start(bf16[192,1024]{1,0:T(8,128)(2,1)S(1)} %get-tuple-element.109), channel_id=1, source_target_pairs={{0,4},{1,3},{2,6},{3,1},{4,0},{5,7},{6,2},{7,5},{8,12},{9,11},{10,... | collective-permute-start | bytes 1179656 | tf_op jit(solution)/shard_map/ppermute | solution.py:573
  57.5 9.9 %collective-permute-start.15 = (bf16[2,192,128]{2,1,0:T(8,128)(2,1)S(1)}, bf16[2,192,128]{2,1,0:T(8,128)(2,1)S(1)}, u32[]{:S(2)}, u32[]{:S(2)}) collective-permute-start(bf16[2,192,128]{2,1,0:T(8,128)(2,1)S(1)} %get-tuple-element.112), channel_id=1, source_target_pairs={{0,4},{1,3},{2,6},{3,1},{4,0},{5,7},{6,2},{7,5},{8,12},{9,11},{10,... | collective-permute-start | bytes 294920 | tf_op jit(solution)/shard_map/ppermute | solution.py:574
  58.1 9.2 %collective-permute-start.16 = (bf16[2,192,128]{2,1,0:T(8,128)(2,1)S(1)}, bf16[2,192,128]{2,1,0:T(8,128)(2,1)S(1)}, u32[]{:S(2)}, u32[]{:S(2)}) collective-permute-start(bf16[2,192,128]{2,1,0:T(8,128)(2,1)S(1)} %get-tuple-element.113), channel_id=1, source_target_pairs={{0,2},{1,5},{2,0},{3,7},{4,6},{5,1},{6,4},{7,3},{8,10},{9,13},{10,... | collective-permute-start | bytes 294920 | tf_op jit(solution)/shard_map/ppermute | solution.py:574
  59.6 10.0 %collective-permute-start.17 = (bf16[2,192,128]{2,1,0:T(8,128)(2,1)S(1)}, bf16[2,192,128]{2,1,0:T(8,128)(2,1)S(1)}, u32[]{:S(2)}, u32[]{:S(2)}) collective-permute-start(bf16[2,192,128]{2,1,0:T(8,128)(2,1)S(1)} %get-tuple-element.114), channel_id=1, source_target_pairs={{0,6},{1,7},{2,4},{3,5},{4,2},{5,3},{6,0},{7,1},{8,14},{9,15},{10,... | collective-permute-start | bytes 294920 | tf_op jit(solution)/shard_map/ppermute | solution.py:574
  71.4 11.9 %collective-permute-start.18 = (bf16[192,1024]{1,0:T(8,128)(2,1)S(1)}, bf16[192,1024]{1,0:T(8,128)(2,1)S(1)}, u32[]{:S(2)}, u32[]{:S(2)}) collective-permute-start(bf16[192,1024]{1,0:T(8,128)(2,1)S(1)} %get-tuple-element.119), channel_id=1, source_target_pairs={{0,8},{8,0},{16,24},{24,16},{1,9},{9,1},{17,25},{25,17},{2,10},{10... | collective-permute-start | bytes 1179656 | tf_op jit(solution)/shard_map/ppermute | solution.py:482
  73.1 17.9 %collective-permute-start.19 = (bf16[192,1024]{1,0:T(8,128)(2,1)S(1)}, bf16[192,1024]{1,0:T(8,128)(2,1)S(1)}, u32[]{:S(2)}, u32[]{:S(2)}) collective-permute-start(bf16[192,1024]{1,0:T(8,128)(2,1)S(1)} %get-tuple-element.120.side_ref), channel_id=1, source_target_pairs={{8,16},{16,8},{9,17},{17,9},{10,18},{18,10},{11,19},{19,11},{12,20... | collective-permute-start | bytes 1179656 | tf_op jit(solution)/shard_map/ppermute | solution.py:484
  74.9 16.0 %collective-permute-start.20 = (bf16[192,1024]{1,0:T(8,128)(2,1)S(1)}, bf16[192,1024]{1,0:T(8,128)(2,1)S(1)}, u32[]{:S(2)}, u32[]{:S(2)}) collective-permute-start(bf16[192,1024]{1,0:T(8,128)(2,1)S(1)} %out_columns.2.far_ref), channel_id=1, source_target_pairs={{0,16},{24,8},{1,17},{25,9},{2,18},{26,10},{3,19},{27,11},{4,20},{... | collective-permute-start | bytes 1179656 | tf_op jit(solution)/shard_map/ppermute | solution.py:486
  84.0 20.2 %collective-permute-start.21 = (bf16[192,1024]{1,0:T(8,128)(2,1)S(1)}, bf16[192,1024]{1,0:T(8,128)(2,1)S(1)}, u32[]{:S(2)}, u32[]{:S(2)}) collective-permute-start(bf16[192,1024]{1,0:T(8,128)(2,1)S(1)} %last_step.1), channel_id=1, source_target_pairs={{0,8},{8,24},{16,0},{24,16},{1,9},{9,25},{17,1},{25,17},{2,10},{10... | collective-permute-start | bytes 1179656 | tf_op jit(solution)/shard_map/ppermute | solution.py:494

commit v8 on v7

--- a/solution.py
+++ b/solution.py
@@ -98,15 +98,33 @@
 def local(kernel, name, shapes, scalars, arrays, scratch=()):
     whole = pl.BlockSpec(memory_space=pltpu.VMEM)
     out = [jax.ShapeDtypeStruct(*shape) for shape in shapes]
+
+    def placed(*refs):
+        kernel(scalars() if scalars else None, *refs)
+
     return pl.pallas_call(
-        kernel,
+        placed,
         out_shape=out if len(out) > 1 else out[0],
-        in_specs=[pl.BlockSpec(memory_space=pltpu.SMEM)] + [whole] * len(arrays),
+        in_specs=[whole] * len(arrays),
         out_specs=[whole] * len(out) if len(out) > 1 else whole,
         scratch_shapes=list(scratch),
         compiler_params=pltpu.CompilerParams(vmem_limit_bytes=VMEM_LIMIT),
         name=name,
-    )(scalars, *arrays)
+    )(*arrays)
+
+
+def slot_order(chips):
+    me, line = lax.axis_index("ctx"), lax.axis_index("dp")
+    core, chip = lax.rem(me, 2), lax.div(me, 2)
+
+    def chip_of(slot, core):
+        high_bit, low_bit = slot >> 1, slot & 1
+        one, two = high_bit + 2 * low_bit, 2 * high_bit + low_bit
+        return chip ^ (one + (two - one) * core)
+
+    mine = [chip_of(s, core) for s in range(chips)]
+    other = [chip_of(s, 1 - core) for s in range(chips)]
+    return mine + other + [core, me, lax.rem(line, 2)]
 
 
 def columns(index, wide):
@@ -186,7 +204,7 @@
     streams, depth, chans = own.shape
     wide = chans // chips
     lanes = wide // 2
-    place = order.shape[0] - 1
+    place = 2 * chips + 2
 
     def kernel(order, own_rows_ref, mine_ref, there_ref, own_ref, other_ref, joined_ref, out_ref, rows):
         core = order[2 * chips]
@@ -289,7 +307,7 @@
                 out_ref[here, :] = (rest_ref[0, h, here, :] + term).astype(BF16)
 
     shapes = [((rows, lanes), BF16)] * 2
-    return local(kernel, "second_share", shapes, order, [rest, both_in])
+    return local(kernel, "second_share", shapes, None, [rest, both_in])
 
 
 def first_share(order, rest, first_in, chips):
@@ -304,7 +322,7 @@
                 out_ref[here, :] = total.astype(out_ref.dtype)
 
     shapes = [((rows, lanes), F32), ((rows, lanes), BF16)]
-    return local(kernel, "first_share", shapes, order, [rest, first_in])
+    return local(kernel, "first_share", shapes, None, [rest, first_in])
 
 
 def hyena_kernel(
@@ -426,7 +444,7 @@
             out_ref[1] = other_ref[s]
 
     shapes = [(q_next.shape, BF16)] + [((2, high, keep.shape[2]), BF16)] * chips
-    return local(kernel, "payloads", shapes, order, [q_next, q_in, keep, other])
+    return local(kernel, "payloads", shapes, None, [q_next, q_in, keep, other])
 
 
 def gate(scalars, queries, long_parts, w_out, groups):
@@ -475,7 +493,7 @@
 def line_picks():
     z = lax.axis_index("dp")
     table = [[3, 0, 3, 0], [1, 2, 1, 2], [2, 3, 0, 1], [0, 1, 2, 3], [0, 1, 1, 0]]
-    return jnp.stack([sum(jnp.where(z == i, v, 0) for i, v in enumerate(row)) for row in table])
+    return [sum(jnp.where(z == i, v, 0) for i, v in enumerate(row)) for row in table]
 
 
 def output_over_line(picks, gated, pair, side, w_out, groups):
@@ -508,8 +526,6 @@
 def on_device_chips(tokens, w_in, short_filter, mode_decay, residue, w_out):
     count, groups = lax.axis_size("ctx"), lax.axis_size("dp")
     chips = count // 2
-    me = lax.axis_index("ctx")
-    core, chip = me % 2, me // 2
 
     def across(i, slot):
         high_bit, low_bit = slot >> 1, slot & 1
@@ -519,16 +535,10 @@
     def route(slot):
         return [(i, across(i, slot)) for i in range(count)]
 
-    def relative(slot, core):
-        high_bit, low_bit = slot >> 1, slot & 1
-        return jnp.where(core == 0, high_bit + 2 * low_bit, 2 * high_bit + low_bit)
-
-    slot_chip = [chip ^ relative(s, core) for s in range(chips)]
-    slot_other = [chip ^ relative(s, 1 - core) for s in range(chips)]
-    order = jnp.stack(slot_chip + slot_other + [core, me, lax.axis_index("dp") % 2]).astype(jnp.int32)
-    picks = line_picks().astype(jnp.int32)
-    both_scalars = jnp.concatenate([order, picks])
-    order, picks, both_scalars = lax.optimization_barrier((order, picks, both_scalars))
+    order, picks = functools.partial(slot_order, chips), line_picks
+
+    def both_scalars():
+        return order() + picks()
 
     own_w = jnp.transpose(w_in, (1, 0, 2))
     swap = [(i, i ^ 1) for i in range(count)]

time: 105 us -> 104 us (level)
  Pallas kernels: 21.5 us -> 13.3 us
  waiting for transfers between devices: 50 us -> 56.8 us
    pallas_call x15, Pallas kernels: 20.7 us -> 12.6 us  [local(): pl.pallas_call(placed, out_shape=out if len(out) > 1 else out[0], in_spec...]
    ppermute x1, waiting for transfers between devices: 6.4 us -> 8.3 us  [on_device_chips(): first_in = lax.ppermute(first, 'ctx', route(2))]
    ppermute x1, waiting for transfers between devices: 5.54 us -> 6.66 us  [on_device_chips(): both_in = lax.ppermute(both, 'ctx', route(2))]
    ppermute x1, waiting for transfers between devices: 4.11 us -> 5.21 us  [output_over_line(): end_in = lax.ppermute(far, 'dp', [(0, 2), (3, 1)])]
  transfers between devices with their start and end apart: 22 -> 22, of which waited for: 14 -> 14; matrix products, arithmetic and copies ran while one was open for 0% -> 0% of each run, Pallas kernels for 18% -> 11%
where the time goes in v8:
time: 104 us
  waiting for transfers between devices  56.8 us (55%)
  starting transfers between devices  29 us (28%)
  Pallas kernels  13.3 us (13%)
  local copies, waits for them, and re-layouts  3.32 us (3%)
    ppermute x1, waiting for transfers between devices, output_over_line(): last_in = lax.ppermute(last, 'dp', [(0, 1), (1, 3), (2, 0), (3, 2)])  13.5 us
    pallas_call x15, Pallas kernels, local(): pl.pallas_call(placed, out_shape=out if len(out) > 1 else out[0], in_spec...  12.6 us
    ppermute x1, waiting for transfers between devices, on_device_chips(): first_in = lax.ppermute(first, 'ctx', route(2))  8.3 us
    ppermute x1, waiting for transfers between devices, on_device_chips(): both_in = lax.ppermute(both, 'ctx', route(2))  6.66 us
    ppermute x1, starting transfers between devices, output_over_line(): end_in = lax.ppermute(far, 'dp', [(0, 2), (3, 1)])  5.75 us
    ppermute x1, waiting for transfers between devices, output_over_line(): end_in = lax.ppermute(far, 'dp', [(0, 2), (3, 1)])  5.21 us
    ppermute x1, waiting for transfers between devices, on_device_chips(): half = lax.ppermute(xs[3], 'ctx', route(3))  5.15 us
    ppermute x3, waiting for transfers between devices, on_device_chips(): lax.ppermute(long_parts[s], 'ctx', route(s))  5.08 us
  transfers between devices with their start and end apart: 22, of which 14 were waited for; matrix products, arithmetic and copies ran while one was open for 0% of the time, Pallas kernels for 11%

profile of v8, /device:TPU:0, one launch (start us, length us, event | category | flops | bytes accessed | tf_op | source)
XLA Modules:
  0.0 103.5 jit_solution(7151555097704059)
XLA Ops:
  0.0 0.5 collective-permute-start.4
  0.5 1.4 %copy-done.1 = bf16[192,4096]{1,0:T(8,128)(2,1)S(1)} copy-done((bf16[192,4096]{1,0:T(8,128)(2,1)S(1)}, bf16[192,4096]{1,0:T(8,128)(2,1)}, u32[]{:S(2)}) %copy-start.1) | copy-done | bytes 1572888
  1.9 0.1 cut.1
  2.0 3.5 %collective-permute-start.2 = (bf16[96,1024]{1,0:T(8,128)(2,1)S(1)}, bf16[96,1024]{1,0:T(8,128)(2,1)S(1)}, u32[]{:S(2)}, u32[]{:S(2)}) collective-permute-start(bf16[96,1024]{1,0:T(8,128)(2,1)S(1)} %get-tuple-element.68), channel_id=1, source_target_pairs={{0,6},{1,7},{2,4},{3,5},{4,2},{5,3},{6,0},{7,1},{8,14},{9,15},{10,... | collective-permute-start | bytes 589832 | tf_op jit(solution)/shard_map/ppermute | solution.py:550
  5.5 0.5 collective-permute-start
  6.0 0.1 collective-permute-start.1
  6.1 5.2 %collective-permute-done.2.refs_1_ = bf16[96,1024]{1,0:T(8,128)(2,1)S(1)} collective-permute-done((bf16[96,1024]{1,0:T(8,128)(2,1)S(1)}, bf16[96,1024]{1,0:T(8,128)(2,1)S(1)}, u32[]{:S(2)}, u32[]{:S(2)}) %collective-permute-start.2) | collective-permute-done | bytes 196640 | tf_op jit(solution)/shard_map/ppermute | solution.py:550
  11.3 2.0 %collective-permute-start.3 = (bf16[96,1024]{1,0:T(8,128)(2,1)S(1)}, bf16[96,1024]{1,0:T(8,128)(2,1)S(1)}, u32[]{:S(2)}, u32[]{:S(2)}) collective-permute-start(bf16[96,1024]{1,0:T(8,128)(2,1)S(1)} %collective-permute-done.2.refs_1_), channel_id=1, source_target_pairs={{0,8},{8,0},{16,24},{24,16},{1,9},{9,1},{17,25},{25,17},{2,10},{10... | collective-permute-start | bytes 589832 | tf_op jit(solution)/shard_map/ppermute | solution.py:551
  13.2 1.9 %copy-done = bf16[512,3,1024]{2,0,1:T(8,128)(2,1)S(1)} copy-done((bf16[512,3,1024]{2,0,1:T(8,128)(2,1)S(1)}, bf16[512,3,1024]{2,0,1:T(8,128)(2,1)}, u32[]{:S(2)}) %copy-start) | copy-done | bytes 3145752
  15.1 0.2 stage.2.refs_3_.refs_4_.refs_5_
  15.4 2.5 %collective-permute-done.3.refs_2_ = bf16[96,1024]{1,0:T(8,128)(2,1)S(1)} collective-permute-done((bf16[96,1024]{1,0:T(8,128)(2,1)S(1)}, bf16[96,1024]{1,0:T(8,128)(2,1)S(1)}, u32[]{:S(2)}, u32[]{:S(2)}) %collective-permute-start.3) | collective-permute-done | bytes 196640 | tf_op jit(solution)/shard_map/ppermute | solution.py:551
  17.8 0.0 collective-permute-done.4.refs_4_.refs_5_.refs_6_
  17.8 0.7 early_share.1
  18.5 0.9 collective-permute-done.refs_0_.refs_1_
  19.5 0.3 collective-permute-done.1.refs_1_.refs_2_
  19.8 0.7 rest_share.1
  20.4 1.6 %collective-permute-start.5 = (bf16[1,2,768,256]{3,2,1,0:T(8,128)(2,1)S(1)}, bf16[1,2,768,256]{3,2,1,0:T(8,128)(2,1)S(1)}, u32[]{:S(2)}, u32[]{:S(2)}) collective-permute-start(bf16[1,2,768,256]{3,2,1,0:T(8,128)(2,1)S(1)} %rest_share.1), channel_id=1, source_target_pairs={{0,2},{1,5},{2,0},{3,7},{4,6},{5,1},{6,4},{7,3},{8,10},{9,13},{10,... | collective-permute-start | bytes 2359304 | tf_op jit(solution)/shard_map/ppermute | solution.py:557
  22.0 1.2 %project_mix.2 = bf16[1,2,768,256]{3,2,1,0:T(8,128)(2,1)S(1)} custom-call(bf16[192,1024]{1,0:T(8,128)(2,1)S(1)} %get-tuple-element.83.refs_0_, bf16[192,1024]{1,0:T(8,128)(2,1)S(1)} %collective-permute-done.refs_0_.refs_1_, bf16[192,1024]{1,0:T(8,128)(2,1)S(1)} %collective-permute-done.1.refs_1_.refs_2_, bf16[192,1024]{1,0:T(8,128)(2,1)S(1)} %get-tuple-element.86.refs_3_, ...), custom_call_target="tpu_custom_call" | custom-call | tf_op jit(solution)/shard_map/project_mix/pallas_call | solution.py:105
  23.2 0.6 collective-permute-start.7
  23.8 2.1 %project_mix.3 = (f32[2,2,768,256]{3,2,1,0:T(8,128)S(1)}, bf16[4,16,1024]{2,1,0:T(8,128)(2,1)S(1)}) custom-call(bf16[192,1024]{1,0:T(8,128)(2,1)S(1)} %get-tuple-element.83.refs_0_, bf16[192,1024]{1,0:T(8,128)(2,1)S(1)} %collective-permute-done.refs_0_.refs_1_, bf16[192,1024]{1,0:T(8,128)(2,1)S(1)} %collective-permute-done.1.refs_1_.refs_2_, ...), custom_call_target="tpu_custom_call" | custom-call | tf_op jit(solution)/shard_map/project_mix/pallas_call | solution.py:105
  25.8 0.0 copy-start.2
  25.8 6.7 %collective-permute-done.5.refs_1_ = bf16[1,2,768,256]{3,2,1,0:T(8,128)(2,1)S(1)} collective-permute-done((bf16[1,2,768,256]{3,2,1,0:T(8,128)(2,1)S(1)}, bf16[1,2,768,256]{3,2,1,0:T(8,128)(2,1)S(1)}, u32[]{:S(2)}, u32[]{:S(2)}) %collective-permute-start.5) | collective-permute-done | bytes 786464 | tf_op jit(solution)/shard_map/ppermute | solution.py:557
  32.5 0.1 second_share.1
  32.6 0.1 collective-permute-start.6
  32.7 1.5 %collective-permute-start.10 = (bf16[768,256]{1,0:T(8,128)(2,1)S(1)}, bf16[768,256]{1,0:T(8,128)(2,1)S(1)}, u32[]{:S(2)}, u32[]{:S(2)}) collective-permute-start(bf16[768,256]{1,0:T(8,128)(2,1)S(1)} %get-tuple-element.82), channel_id=1, source_target_pairs={{0,4},{1,3},{2,6},{3,1},{4,0},{5,7},{6,2},{7,5},{8,12},{9,11},{10,... | collective-permute-start | bytes 1179656 | tf_op jit(solution)/shard_map/ppermute | solution.py:564
  34.2 0.4 collective-permute-start.11
  34.7 0.0 collective-permute-done.6.refs_4_
  34.7 2.4 %project_query.1 = (f32[192,1024]{1,0:T(8,128)S(1)}, f32[192,1024]{1,0:T(8,128)S(1)}, bf16[192,1024]{1,0:T(8,128)(2,1)S(1)}, bf16[192,1024]{1,0:T(8,128)(2,1)S(1)}) custom-call(bf16[192,1024]{1,0:T(8,128)(2,1)S(1)} %get-tuple-element.83.refs_0_, bf16[192,1024]{1,0:T(8,128)(2,1)S(1)} %collective-permute-done.refs_0_.refs_1_, ...), custom_call_target="tpu_custom_call" | custom-call | tf_op jit(solution)/shard_map/project_query/pallas_call | solution.py:105
  37.1 0.6 stage.3.refs_7_.refs_1_
  37.7 0.0 copy-start.3
  37.7 0.0 copy-start.4
  37.7 8.3 %collective-permute-done.7.refs_1_ = bf16[1,2,768,256]{3,2,1,0:T(8,128)(2,1)S(1)} collective-permute-done((bf16[1,2,768,256]{3,2,1,0:T(8,128)(2,1)S(1)}, bf16[1,2,768,256]{3,2,1,0:T(8,128)(2,1)S(1)}, u32[]{:S(2)}, u32[]{:S(2)}) %collective-permute-start.7) | collective-permute-done | bytes 786464 | tf_op jit(solution)/shard_map/ppermute | solution.py:560
  46.0 0.1 first_share.1
  46.1 0.1 collective-permute-start.9
  46.2 1.6 %collective-permute-start.8 = (bf16[192,1024]{1,0:T(8,128)(2,1)S(1)}, bf16[192,1024]{1,0:T(8,128)(2,1)S(1)}, u32[]{:S(2)}, u32[]{:S(2)}) collective-permute-start(bf16[192,1024]{1,0:T(8,128)(2,1)S(1)} %get-tuple-element.97), channel_id=1, source_target_pairs={{0,2},{1,5},{2,0},{3,7},{4,6},{5,1},{6,4},{7,3},{8,10},{9,13},{10,... | collective-permute-start | bytes 1179656 | tf_op jit(solution)/shard_map/ppermute | solution.py:577
  47.8 1.6 %collective-permute-done.11.refs_3_ = bf16[768,256]{1,0:T(8,128)(2,1)S(1)} collective-permute-done((bf16[768,256]{1,0:T(8,128)(2,1)S(1)}, bf16[768,256]{1,0:T(8,128)(2,1)S(1)}, u32[]{:S(2)}, u32[]{:S(2)}) %collective-permute-start.11) | collective-permute-done | bytes 393248 | tf_op jit(solution)/shard_map/ppermute | solution.py:565
  49.4 0.0 collective-permute-done.10.refs_2_
  49.4 2.4 %hyena.1 = (bf16[4,192,128]{2,1,0:T(8,128)(2,1)S(1)}, bf16[4,192,128]{2,1,0:T(8,128)(2,1)S(1)}) custom-call(f32[768,256]{1,0:T(8,128)S(1)} %get-tuple-element.98.refs_0_, bf16[768,256]{1,0:T(8,128)(2,1)S(1)} %collective-permute-done.9.refs_1_, bf16[768,256]{1,0:T(8,128)(2,1)S(1)} %collective-permute-done.10.refs_2_, ...), custom_call_target="tpu_custom_call" | custom-call | tf_op jit(solution)/shard_map/hyena/pallas_call | solution.py:105
  51.8 0.1 collective-permute-start.12
  51.8 1.6 %collective-permute-start.14 = (bf16[192,1024]{1,0:T(8,128)(2,1)S(1)}, bf16[192,1024]{1,0:T(8,128)(2,1)S(1)}, u32[]{:S(2)}, u32[]{:S(2)}) collective-permute-start(bf16[192,1024]{1,0:T(8,128)(2,1)S(1)} %get-tuple-element.104), channel_id=1, source_target_pairs={{0,2},{1,5},{2,0},{3,7},{4,6},{5,1},{6,4},{7,3},{8,10},{9,13},{10,... | collective-permute-start | bytes 1179656 | tf_op jit(solution)/shard_map/ppermute | solution.py:578
  53.4 0.6 collective-permute-done.8.refs_1_
  54.0 0.0 collective-permute-done.12.refs_3_
  54.0 0.1 payloads.1
  54.1 1.5 %collective-permute-start.13 = (bf16[192,1024]{1,0:T(8,128)(2,1)S(1)}, bf16[192,1024]{1,0:T(8,128)(2,1)S(1)}, u32[]{:S(2)}, u32[]{:S(2)}) collective-permute-start(bf16[192,1024]{1,0:T(8,128)(2,1)S(1)} %get-tuple-element.103), channel_id=1, source_target_pairs={{0,4},{1,3},{2,6},{3,1},{4,0},{5,7},{6,2},{7,5},{8,12},{9,11},{10,... | collective-permute-start | bytes 1179656 | tf_op jit(solution)/shard_map/ppermute | solution.py:583
  55.6 0.6 collective-permute-start.15
  56.2 1.5 %collective-permute-start.16 = (bf16[2,192,128]{2,1,0:T(8,128)(2,1)S(1)}, bf16[2,192,128]{2,1,0:T(8,128)(2,1)S(1)}, u32[]{:S(2)}, u32[]{:S(2)}) collective-permute-start(bf16[2,192,128]{2,1,0:T(8,128)(2,1)S(1)} %get-tuple-element.107), channel_id=1, source_target_pairs={{0,2},{1,5},{2,0},{3,7},{4,6},{5,1},{6,4},{7,3},{8,10},{9,13},{10,... | collective-permute-start | bytes 294920 | tf_op jit(solution)/shard_map/ppermute | solution.py:584
  57.7 1.4 %collective-permute-start.17 = (bf16[2,192,128]{2,1,0:T(8,128)(2,1)S(1)}, bf16[2,192,128]{2,1,0:T(8,128)(2,1)S(1)}, u32[]{:S(2)}, u32[]{:S(2)}) collective-permute-start(bf16[2,192,128]{2,1,0:T(8,128)(2,1)S(1)} %get-tuple-element.108), channel_id=1, source_target_pairs={{0,6},{1,7},{2,4},{3,5},{4,2},{5,3},{6,0},{7,1},{8,14},{9,15},{10,... | collective-permute-start | bytes 294920 | tf_op jit(solution)/shard_map/ppermute | solution.py:584
  59.1 3.9 %collective-permute-done.14.refs_2_ = bf16[192,1024]{1,0:T(8,128)(2,1)S(1)} collective-permute-done((bf16[192,1024]{1,0:T(8,128)(2,1)S(1)}, bf16[192,1024]{1,0:T(8,128)(2,1)S(1)}, u32[]{:S(2)}, u32[]{:S(2)}) %collective-permute-start.14) | collective-permute-done | bytes 393248 | tf_op jit(solution)/shard_map/ppermute | solution.py:578
  63.0 2.4 %collective-permute-done.15.refs_4_ = bf16[2,192,128]{2,1,0:T(8,128)(2,1)S(1)} collective-permute-done((bf16[2,192,128]{2,1,0:T(8,128)(2,1)S(1)}, bf16[2,192,128]{2,1,0:T(8,128)(2,1)S(1)}, u32[]{:S(2)}, u32[]{:S(2)}) %collective-permute-start.15) | collective-permute-done | bytes 98336 | tf_op jit(solution)/shard_map/ppermute | solution.py:584
  65.5 2.6 %collective-permute-done.17.refs_6_ = bf16[2,192,128]{2,1,0:T(8,128)(2,1)S(1)} collective-permute-done((bf16[2,192,128]{2,1,0:T(8,128)(2,1)S(1)}, bf16[2,192,128]{2,1,0:T(8,128)(2,1)S(1)}, u32[]{:S(2)}, u32[]{:S(2)}) %collective-permute-start.17) | collective-permute-done | bytes 98336 | tf_op jit(solution)/shard_map/ppermute | solution.py:584
  68.1 1.3 %gate.1 = (bf16[192,1024]{1,0:T(8,128)(2,1)S(1)}, bf16[192,1024]{1,0:T(8,128)(2,1)S(1)}, bf16[192,1024]{1,0:T(8,128)(2,1)S(1)}) custom-call(f32[192,1024]{1,0:T(8,128)S(1)} %get-tuple-element.91.refs_0_, bf16[192,1024]{1,0:T(8,128)(2,1)S(1)} %collective-permute-done.13.refs_1_, bf16[192,1024]{1,0:T(8,128)(2,1)S(1)} %collective-permute-done.14.refs_2_, ...), custom_call_target="tpu_custom_call" | custom-call | tf_op jit(solution)/shard_map/gate/pallas_call | solution.py:105
  69.4 1.6 %collective-permute-start.18 = (bf16[192,1024]{1,0:T(8,128)(2,1)S(1)}, bf16[192,1024]{1,0:T(8,128)(2,1)S(1)}, u32[]{:S(2)}, u32[]{:S(2)}) collective-permute-start(bf16[192,1024]{1,0:T(8,128)(2,1)S(1)} %get-tuple-element.113), channel_id=1, source_target_pairs={{0,8},{8,0},{16,24},{24,16},{1,9},{9,1},{17,25},{25,17},{2,10},{10... | collective-permute-start | bytes 1179656 | tf_op jit(solution)/shard_map/ppermute | solution.py:500
  71.0 0.6 out_columns.2.refs_0_
  71.6 0.7 collective-permute-start.19
  72.3 5.8 %collective-permute-start.20 = (bf16[192,1024]{1,0:T(8,128)(2,1)S(1)}, bf16[192,1024]{1,0:T(8,128)(2,1)S(1)}, u32[]{:S(2)}, u32[]{:S(2)}) collective-permute-start(bf16[192,1024]{1,0:T(8,128)(2,1)S(1)} %out_columns.2.refs_0_), channel_id=1, source_target_pairs={{0,16},{24,8},{1,17},{25,9},{2,18},{26,10},{3,19},{27,11},{4,20},{... | collective-permute-start | bytes 1179656 | tf_op jit(solution)/shard_map/ppermute | solution.py:504
  78.1 3.1 %collective-permute-done.18.refs_1_ = bf16[192,1024]{1,0:T(8,128)(2,1)S(1)} collective-permute-done((bf16[192,1024]{1,0:T(8,128)(2,1)S(1)}, bf16[192,1024]{1,0:T(8,128)(2,1)S(1)}, u32[]{:S(2)}, u32[]{:S(2)}) %collective-permute-start.18) | collective-permute-done | bytes 393248 | tf_op jit(solution)/shard_map/ppermute | solution.py:500
  81.2 0.1 last_step.1
  81.3 1.9 %collective-permute-start.21 = (bf16[192,1024]{1,0:T(8,128)(2,1)S(1)}, bf16[192,1024]{1,0:T(8,128)(2,1)S(1)}, u32[]{:S(2)}, u32[]{:S(2)}) collective-permute-start(bf16[192,1024]{1,0:T(8,128)(2,1)S(1)} %last_step.1), channel_id=1, source_target_pairs={{0,8},{8,24},{16,0},{24,16},{1,9},{9,25},{17,1},{25,17},{2,10},{10... | collective-permute-start | bytes 1179656 | tf_op jit(solution)/shard_map/ppermute | solution.py:512
  83.2 0.6 out_columns.3.refs_0_
  83.8 5.2 %collective-permute-done.20.refs_3_ = bf16[192,1024]{1,0:T(8,128)(2,1)S(1)} collective-permute-done((bf16[192,1024]{1,0:T(8,128)(2,1)S(1)}, bf16[192,1024]{1,0:T(8,128)(2,1)S(1)}, u32[]{:S(2)}, u32[]{:S(2)}) %collective-permute-start.20) | collective-permute-done | bytes 393248 | tf_op jit(solution)/shard_map/ppermute | solution.py:504
  89.0 0.0 collective-permute-done.19.refs_2_
  89.0 0.2 early.1
  89.2 13.5 %collective-permute-done.21 = bf16[192,1024]{1,0:T(8,128)(2,1)S(1)} collective-permute-done((bf16[192,1024]{1,0:T(8,128)(2,1)S(1)}, bf16[192,1024]{1,0:T(8,128)(2,1)S(1)}, u32[]{:S(2)}, u32[]{:S(2)}) %collective-permute-start.21) | collective-permute-done | bytes 393248 | tf_op jit(solution)/shard_map/ppermute | solution.py:512
  102.7 0.8 add_convert_fusion
  (13 shorter events, 0.0 us)
Async XLA Ops:
  0.0 17.8 %collective-permute-start.4 = (bf16[3,512,1024]{2,1,0:T(8,128)(2,1)}, bf16[3,512,1024]{2,1,0:T(8,128)(2,1)S(1)}, u32[]{:S(2)}, u32[]{:S(2)}) collective-permute-start(bf16[3,512,1024]{2,1,0:T(8,128)(2,1)} %bitcast.3), channel_id=1, source_target_pairs={{0,1},{1,0},{2,3},{3,2},{4,5},{5,4},{6,7},{7,6},{8,9},{9,8},{10,11... | collective-permute-start | bytes 9437192 | tf_op jit(solution)/shard_map/ppermute | solution.py:546
  0.5 1.4 %copy-start.1 = (bf16[192,4096]{1,0:T(8,128)(2,1)S(1)}, bf16[192,4096]{1,0:T(8,128)(2,1)}, u32[]{:S(2)}) copy-start(bf16[192,4096]{1,0:T(8,128)(2,1)} %refs_0_.1) | copy-start | bytes 4718596
  2.0 9.3 %collective-permute-start.2 = (bf16[96,1024]{1,0:T(8,128)(2,1)S(1)}, bf16[96,1024]{1,0:T(8,128)(2,1)S(1)}, u32[]{:S(2)}, u32[]{:S(2)}) collective-permute-start(bf16[96,1024]{1,0:T(8,128)(2,1)S(1)} %get-tuple-element.68), channel_id=1, source_target_pairs={{0,6},{1,7},{2,4},{3,5},{4,2},{5,3},{6,0},{7,1},{8,14},{9,15},{10,... | collective-permute-start | bytes 589832 | tf_op jit(solution)/shard_map/ppermute | solution.py:550
  5.5 14.0 %collective-permute-start = (bf16[192,1024]{1,0:T(8,128)(2,1)S(1)}, bf16[192,1024]{1,0:T(8,128)(2,1)S(1)}, u32[]{:S(2)}, u32[]{:S(2)}) collective-permute-start(bf16[192,1024]{1,0:T(8,128)(2,1)S(1)} %get-tuple-element.66), channel_id=1, source_target_pairs={{0,4},{1,3},{2,6},{3,1},{4,0},{5,7},{6,2},{7,5},{8,12},{9,11},{10,... | collective-permute-start | bytes 1179656 | tf_op jit(solution)/shard_map/ppermute | solution.py:552
  6.0 13.8 %collective-permute-start.1 = (bf16[192,1024]{1,0:T(8,128)(2,1)S(1)}, bf16[192,1024]{1,0:T(8,128)(2,1)S(1)}, u32[]{:S(2)}, u32[]{:S(2)}) collective-permute-start(bf16[192,1024]{1,0:T(8,128)(2,1)S(1)} %get-tuple-element.67), channel_id=1, source_target_pairs={{0,2},{1,5},{2,0},{3,7},{4,6},{5,1},{6,4},{7,3},{8,10},{9,13},{10,... | collective-permute-start | bytes 1179656 | tf_op jit(solution)/shard_map/ppermute | solution.py:552
  11.3 6.6 %collective-permute-start.3 = (bf16[96,1024]{1,0:T(8,128)(2,1)S(1)}, bf16[96,1024]{1,0:T(8,128)(2,1)S(1)}, u32[]{:S(2)}, u32[]{:S(2)}) collective-permute-start(bf16[96,1024]{1,0:T(8,128)(2,1)S(1)} %collective-permute-done.2.refs_1_), channel_id=1, source_target_pairs={{0,8},{8,0},{16,24},{24,16},{1,9},{9,1},{17,25},{25,17},{2,10},{10... | collective-permute-start | bytes 589832 | tf_op jit(solution)/shard_map/ppermute | solution.py:551
  13.2 1.9 %copy-start = (bf16[512,3,1024]{2,0,1:T(8,128)(2,1)S(1)}, bf16[512,3,1024]{2,0,1:T(8,128)(2,1)}, u32[]{:S(2)}) copy-start(bf16[512,3,1024]{2,0,1:T(8,128)(2,1)} %param.7) | copy-start | bytes 9437188
  20.4 12.1 %collective-permute-start.5 = (bf16[1,2,768,256]{3,2,1,0:T(8,128)(2,1)S(1)}, bf16[1,2,768,256]{3,2,1,0:T(8,128)(2,1)S(1)}, u32[]{:S(2)}, u32[]{:S(2)}) collective-permute-start(bf16[1,2,768,256]{3,2,1,0:T(8,128)(2,1)S(1)} %rest_share.1), channel_id=1, source_target_pairs={{0,2},{1,5},{2,0},{3,7},{4,6},{5,1},{6,4},{7,3},{8,10},{9,13},{10,... | collective-permute-start | bytes 2359304 | tf_op jit(solution)/shard_map/ppermute | solution.py:557
  23.2 22.8 %collective-permute-start.7 = (bf16[1,2,768,256]{3,2,1,0:T(8,128)(2,1)S(1)}, bf16[1,2,768,256]{3,2,1,0:T(8,128)(2,1)S(1)}, u32[]{:S(2)}, u32[]{:S(2)}) collective-permute-start(bf16[1,2,768,256]{3,2,1,0:T(8,128)(2,1)S(1)} %project_mix.2), channel_id=1, source_target_pairs={{0,2},{1,5},{2,0},{3,7},{4,6},{5,1},{6,4},{7,3},{8,10},{9,13},{10,... | collective-permute-start | bytes 2359304 | tf_op jit(solution)/shard_map/ppermute | solution.py:560
  23.8 13.3 %slice-start = ((s8[8388608]{0:T(1024)(128)(4,1)}), s8[4194304]{0:T(1024)(128)(4,1)S(1)}, s32[]{:S(2)}) async-start(s8[8388608]{0:T(1024)(128)(4,1)} %bitcast.1), calls=%async_computation | async-start | bytes 8388608
  25.8 8.8 %copy-start.2 = (f32[3,3,1024]{2,1,0:T(4,128)S(1)}, f32[3,3,1024]{2,1,0:T(4,128)}, u32[]{:S(2)}) copy-start(f32[3,3,1024]{2,1,0:T(4,128)} %refs_4_.1) | copy-start | bytes 110596
  32.5 4.6 %slice-start.1 = ((s8[8388608]{0:T(1024)(128)(4,1)}), s8[4194304]{0:T(1024)(128)(4,1)S(1)}, s32[]{:S(2)}) async-start(s8[8388608]{0:T(1024)(128)(4,1)} %bitcast.1), calls=%async_computation.1 | async-start | bytes 8388608
  32.6 2.0 %collective-permute-start.6 = (bf16[4,16,1024]{2,1,0:T(8,128)(2,1)S(1)}, bf16[4,16,1024]{2,1,0:T(8,128)(2,1)S(1)}, u32[]{:S(2)}, u32[]{:S(2)}) collective-permute-start(bf16[4,16,1024]{2,1,0:T(8,128)(2,1)S(1)} %get-tuple-element.87), channel_id=1, source_target_pairs={{0,1},{1,0},{2,3},{3,2},{4,5},{5,4},{6,7},{7,6},{8,9},{9,8},{10,11... | collective-permute-start | bytes 393224 | tf_op jit(solution)/shard_map/ppermute | solution.py:568
  32.7 16.6 %collective-permute-start.10 = (bf16[768,256]{1,0:T(8,128)(2,1)S(1)}, bf16[768,256]{1,0:T(8,128)(2,1)S(1)}, u32[]{:S(2)}, u32[]{:S(2)}) collective-permute-start(bf16[768,256]{1,0:T(8,128)(2,1)S(1)} %get-tuple-element.82), channel_id=1, source_target_pairs={{0,4},{1,3},{2,6},{3,1},{4,0},{5,7},{6,2},{7,5},{8,12},{9,11},{10,... | collective-permute-start | bytes 1179656 | tf_op jit(solution)/shard_map/ppermute | solution.py:564
  34.2 15.1 %collective-permute-start.11 = (bf16[768,256]{1,0:T(8,128)(2,1)S(1)}, bf16[768,256]{1,0:T(8,128)(2,1)S(1)}, u32[]{:S(2)}, u32[]{:S(2)}) collective-permute-start(bf16[768,256]{1,0:T(8,128)(2,1)S(1)} %get-tuple-element.100), channel_id=1, source_target_pairs={{0,5},{1,2},{2,7},{3,0},{4,1},{5,6},{6,3},{7,4},{8,13},{9,10},{10,... | collective-permute-start | bytes 1179656 | tf_op jit(solution)/shard_map/ppermute | solution.py:565
  37.7 11.7 %copy-start.3 = (f32[8,1024]{1,0:T(8,128)S(1)}, f32[8,1024]{1,0:T(8,128)}, u32[]{:S(2)}) copy-start(f32[8,1024]{1,0:T(8,128)} %refs_5_.1) | copy-start | bytes 98308
  37.7 11.7 %copy-start.4 = (f32[8,1024]{1,0:T(8,128)S(1)}, f32[8,1024]{1,0:T(8,128)}, u32[]{:S(2)}) copy-start(f32[8,1024]{1,0:T(8,128)} %refs_6_.1) | copy-start | bytes 98308
  46.1 3.2 %collective-permute-start.9 = (bf16[768,256]{1,0:T(8,128)(2,1)S(1)}, bf16[768,256]{1,0:T(8,128)(2,1)S(1)}, u32[]{:S(2)}, u32[]{:S(2)}) collective-permute-start(bf16[768,256]{1,0:T(8,128)(2,1)S(1)} %get-tuple-element.99), channel_id=1, source_target_pairs={{0,1},{1,0},{2,3},{3,2},{4,5},{5,4},{6,7},{7,6},{8,9},{9,8},{10,11... | collective-permute-start | bytes 1179656 | tf_op jit(solution)/shard_map/ppermute | solution.py:575
  46.2 7.8 %collective-permute-start.8 = (bf16[192,1024]{1,0:T(8,128)(2,1)S(1)}, bf16[192,1024]{1,0:T(8,128)(2,1)S(1)}, u32[]{:S(2)}, u32[]{:S(2)}) collective-permute-start(bf16[192,1024]{1,0:T(8,128)(2,1)S(1)} %get-tuple-element.97), channel_id=1, source_target_pairs={{0,2},{1,5},{2,0},{3,7},{4,6},{5,1},{6,4},{7,3},{8,10},{9,13},{10,... | collective-permute-start | bytes 1179656 | tf_op jit(solution)/shard_map/ppermute | solution.py:577
  51.8 2.3 %collective-permute-start.12 = (bf16[4,192,128]{2,1,0:T(8,128)(2,1)S(1)}, bf16[4,192,128]{2,1,0:T(8,128)(2,1)S(1)}, u32[]{:S(2)}, u32[]{:S(2)}) collective-permute-start(bf16[4,192,128]{2,1,0:T(8,128)(2,1)S(1)} %get-tuple-element.102), channel_id=1, source_target_pairs={{0,1},{1,0},{2,3},{3,2},{4,5},{5,4},{6,7},{7,6},{8,9},{9,8},{10,11... | collective-permute-start | bytes 589832 | tf_op jit(solution)/shard_map/ppermute | solution.py:581
  51.8 11.2 %collective-permute-start.14 = (bf16[192,1024]{1,0:T(8,128)(2,1)S(1)}, bf16[192,1024]{1,0:T(8,128)(2,1)S(1)}, u32[]{:S(2)}, u32[]{:S(2)}) collective-permute-start(bf16[192,1024]{1,0:T(8,128)(2,1)S(1)} %get-tuple-element.104), channel_id=1, source_target_pairs={{0,2},{1,5},{2,0},{3,7},{4,6},{5,1},{6,4},{7,3},{8,10},{9,13},{10,... | collective-permute-start | bytes 1179656 | tf_op jit(solution)/shard_map/ppermute | solution.py:578
  54.1 14.0 %collective-permute-start.13 = (bf16[192,1024]{1,0:T(8,128)(2,1)S(1)}, bf16[192,1024]{1,0:T(8,128)(2,1)S(1)}, u32[]{:S(2)}, u32[]{:S(2)}) collective-permute-start(bf16[192,1024]{1,0:T(8,128)(2,1)S(1)} %get-tuple-element.103), channel_id=1, source_target_pairs={{0,4},{1,3},{2,6},{3,1},{4,0},{5,7},{6,2},{7,5},{8,12},{9,11},{10,... | collective-permute-start | bytes 1179656 | tf_op jit(solution)/shard_map/ppermute | solution.py:583
  55.6 9.8 %collective-permute-start.15 = (bf16[2,192,128]{2,1,0:T(8,128)(2,1)S(1)}, bf16[2,192,128]{2,1,0:T(8,128)(2,1)S(1)}, u32[]{:S(2)}, u32[]{:S(2)}) collective-permute-start(bf16[2,192,128]{2,1,0:T(8,128)(2,1)S(1)} %get-tuple-element.106), channel_id=1, source_target_pairs={{0,4},{1,3},{2,6},{3,1},{4,0},{5,7},{6,2},{7,5},{8,12},{9,11},{10,... | collective-permute-start | bytes 294920 | tf_op jit(solution)/shard_map/ppermute | solution.py:584
  56.2 9.2 %collective-permute-start.16 = (bf16[2,192,128]{2,1,0:T(8,128)(2,1)S(1)}, bf16[2,192,128]{2,1,0:T(8,128)(2,1)S(1)}, u32[]{:S(2)}, u32[]{:S(2)}) collective-permute-start(bf16[2,192,128]{2,1,0:T(8,128)(2,1)S(1)} %get-tuple-element.107), channel_id=1, source_target_pairs={{0,2},{1,5},{2,0},{3,7},{4,6},{5,1},{6,4},{7,3},{8,10},{9,13},{10,... | collective-permute-start | bytes 294920 | tf_op jit(solution)/shard_map/ppermute | solution.py:584
  57.7 10.4 %collective-permute-start.17 = (bf16[2,192,128]{2,1,0:T(8,128)(2,1)S(1)}, bf16[2,192,128]{2,1,0:T(8,128)(2,1)S(1)}, u32[]{:S(2)}, u32[]{:S(2)}) collective-permute-start(bf16[2,192,128]{2,1,0:T(8,128)(2,1)S(1)} %get-tuple-element.108), channel_id=1, source_target_pairs={{0,6},{1,7},{2,4},{3,5},{4,2},{5,3},{6,0},{7,1},{8,14},{9,15},{10,... | collective-permute-start | bytes 294920 | tf_op jit(solution)/shard_map/ppermute | solution.py:584
  69.4 11.8 %collective-permute-start.18 = (bf16[192,1024]{1,0:T(8,128)(2,1)S(1)}, bf16[192,1024]{1,0:T(8,128)(2,1)S(1)}, u32[]{:S(2)}, u32[]{:S(2)}) collective-permute-start(bf16[192,1024]{1,0:T(8,128)(2,1)S(1)} %get-tuple-element.113), channel_id=1, source_target_pairs={{0,8},{8,0},{16,24},{24,16},{1,9},{9,1},{17,25},{25,17},{2,10},{10... | collective-permute-start | bytes 1179656 | tf_op jit(solution)/shard_map/ppermute | solution.py:500
  71.6 17.4 %collective-permute-start.19 = (bf16[192,1024]{1,0:T(8,128)(2,1)S(1)}, bf16[192,1024]{1,0:T(8,128)(2,1)S(1)}, u32[]{:S(2)}, u32[]{:S(2)}) collective-permute-start(bf16[192,1024]{1,0:T(8,128)(2,1)S(1)} %get-tuple-element.114.refs_2_), channel_id=1, source_target_pairs={{8,16},{16,8},{9,17},{17,9},{10,18},{18,10},{11,19},{19,11},{12,20... | collective-permute-start | bytes 1179656 | tf_op jit(solution)/shard_map/ppermute | solution.py:502
  72.3 16.7 %collective-permute-start.20 = (bf16[192,1024]{1,0:T(8,128)(2,1)S(1)}, bf16[192,1024]{1,0:T(8,128)(2,1)S(1)}, u32[]{:S(2)}, u32[]{:S(2)}) collective-permute-start(bf16[192,1024]{1,0:T(8,128)(2,1)S(1)} %out_columns.2.refs_0_), channel_id=1, source_target_pairs={{0,16},{24,8},{1,17},{25,9},{2,18},{26,10},{3,19},{27,11},{4,20},{... | collective-permute-start | bytes 1179656 | tf_op jit(solution)/shard_map/ppermute | solution.py:504
  81.3 21.4 %collective-permute-start.21 = (bf16[192,1024]{1,0:T(8,128)(2,1)S(1)}, bf16[192,1024]{1,0:T(8,128)(2,1)S(1)}, u32[]{:S(2)}, u32[]{:S(2)}) collective-permute-start(bf16[192,1024]{1,0:T(8,128)(2,1)S(1)} %last_step.1), channel_id=1, source_target_pairs={{0,8},{8,24},{16,0},{24,16},{1,9},{9,25},{17,1},{25,17},{2,10},{10... | collective-permute-start | bytes 1179656 | tf_op jit(solution)/shard_map/ppermute | solution.py:512

commit v9 on v8

--- a/solution.py
+++ b/solution.py
@@ -456,7 +456,7 @@
 
     def kernel(scalars, *refs):
         query_refs, long_refs = refs[: len(queries)], refs[len(queries) : len(queries) + chips]
-        w_ref, gated_ref, pair_ref, side_ref, query = refs[len(queries) + chips :]
+        w_ref, gated_ref, pair_ref, query = refs[len(queries) + chips :]
         core = scalars[2 * chips]
         own_ref, second_ref, first_ref = query_refs
         query[...] = own_ref[...] + second_ref[...].astype(F32) + first_ref[...].astype(F32)
@@ -464,15 +464,12 @@
             for h in range(2):
                 at = columns(2 * scalars[s] + (core ^ h), part)
                 gated_ref[:, at] = (query[:, at] * ref[h].astype(F32)).astype(BF16)
-        for pick, out_ref in enumerate((pair_ref, side_ref)):
-            total = jnp.dot(
-                gated_ref[...],
-                w_ref[:, columns(scalars[first_pick + pick], wide)],
-                preferred_element_type=F32,
-            )
-            out_ref[...] = total.astype(BF16)
-
-    shapes = [((rows, chans), BF16), ((rows, wide), BF16), ((rows, wide), BF16)]
+        total = jnp.dot(
+            gated_ref[...], w_ref[:, columns(scalars[first_pick], wide)], preferred_element_type=F32
+        )
+        pair_ref[...] = total.astype(BF16)
+
+    shapes = [((rows, chans), BF16), ((rows, wide), BF16)]
     arrays = [*queries, *long_parts, w_out]
     scratch = [pltpu.VMEM((rows, chans), F32)]
     return local(kernel, "gate", shapes, scalars, arrays, scratch)
@@ -496,11 +493,12 @@
     return [sum(jnp.where(z == i, v, 0) for i, v in enumerate(row)) for row in table]
 
 
-def output_over_line(picks, gated, pair, side, w_out, groups):
+def output_over_line(picks, gated, pair, w_out, groups):
     pair_in = lax.ppermute(pair, "dp", [(0, 1), (1, 0), (2, 3), (3, 2)])
+    side = out_columns(picks, 1, gated, w_out, groups, BF16)
+    middle_in = lax.ppermute(side, "dp", [(1, 2), (2, 1)])
+    gated, side = lax.optimization_barrier((gated, side))
     far = out_columns(picks, 2, gated, w_out, groups, BF16)
-    middle_in = lax.ppermute(side, "dp", [(1, 2), (2, 1)])
-    side, far = lax.optimization_barrier((side, far))
     end_in = lax.ppermute(far, "dp", [(0, 2), (3, 1)])
 
     def add(picks, far_ref, pair_ref, side_ref, out_ref):
@@ -583,8 +581,8 @@
     q_second = lax.ppermute(q_second, "ctx", route(1))
     long_parts = [long_parts[0]] + [lax.ppermute(long_parts[s], "ctx", route(s)) for s in (1, 2, 3)]
     queries = [q_own, q_second, q_first]
-    gated, pair, side = gate(both_scalars, queries, long_parts, w_out, groups)
-    return output_over_line(picks, gated, pair, side, w_out, groups)
+    gated, pair = gate(both_scalars, queries, long_parts, w_out, groups)
+    return output_over_line(picks, gated, pair, w_out, groups)
 
 
 def solution(mesh):

time: 104 us -> 103 us (level)
    pallas_call x15 -> x16, Pallas kernels: 12.6 us -> 12.8 us  [local(): pl.pallas_call(placed, out_shape=out if len(out) > 1 else out[0], in_spec...]
  transfers between devices with their start and end apart: 22 -> 22, of which waited for: 14 -> 14; matrix products, arithmetic and copies ran while one was open for 0% -> 0% of each run, Pallas kernels for 11% -> 12%
where the time goes in v9:
time: 103 us
  waiting for transfers between devices  56.2 us (55%)
  starting transfers between devices  29 us (28%)
  Pallas kernels  13.5 us (13%)
  local copies, waits for them, and re-layouts  3.32 us (3%)
    ppermute x1, waiting for transfers between devices, output_over_line(): last_in = lax.ppermute(last, 'dp', [(0, 1), (1, 3), (2, 0), (3, 2)])  13.5 us
    pallas_call x16, Pallas kernels, local(): pl.pallas_call(placed, out_shape=out if len(out) > 1 else out[0], in_spec...  12.8 us
    ppermute x1, waiting for transfers between devices, on_device_chips(): first_in = lax.ppermute(first, 'ctx', route(2))  8.3 us
    ppermute x1, waiting for transfers between devices, on_device_chips(): both_in = lax.ppermute(both, 'ctx', route(2))  6.66 us
    ppermute x1, starting transfers between devices, output_over_line(): end_in = lax.ppermute(far, 'dp', [(0, 2), (3, 1)])  5.77 us
    ppermute x1, waiting for transfers between devices, output_over_line(): end_in = lax.ppermute(far, 'dp', [(0, 2), (3, 1)])  5.21 us
    ppermute x1, waiting for transfers between devices, on_device_chips(): half = lax.ppermute(xs[3], 'ctx', route(3))  5.15 us
    ppermute x3, waiting for transfers between devices, on_device_chips(): lax.ppermute(long_parts[s], 'ctx', route(s))  5.08 us
  transfers between devices with their start and end apart: 22, of which 14 were waited for; matrix products, arithmetic and copies ran while one was open for 0% of the time, Pallas kernels for 12%

profile of v9, /device:TPU:0, one launch (start us, length us, event | category | flops | bytes accessed | tf_op | source)
XLA Modules:
  0.0 103.1 jit_solution(5626142721517821090)
XLA Ops:
  0.0 0.5 collective-permute-start.4
  0.5 1.4 %copy-done.1 = bf16[192,4096]{1,0:T(8,128)(2,1)S(1)} copy-done((bf16[192,4096]{1,0:T(8,128)(2,1)S(1)}, bf16[192,4096]{1,0:T(8,128)(2,1)}, u32[]{:S(2)}) %copy-start.1) | copy-done | bytes 1572888
  1.9 0.1 cut.1
  2.0 3.5 %collective-permute-start.2 = (bf16[96,1024]{1,0:T(8,128)(2,1)S(1)}, bf16[96,1024]{1,0:T(8,128)(2,1)S(1)}, u32[]{:S(2)}, u32[]{:S(2)}) collective-permute-start(bf16[96,1024]{1,0:T(8,128)(2,1)S(1)} %get-tuple-element.67), channel_id=1, source_target_pairs={{0,6},{1,7},{2,4},{3,5},{4,2},{5,3},{6,0},{7,1},{8,14},{9,15},{10,... | collective-permute-start | bytes 589832 | tf_op jit(solution)/shard_map/ppermute | solution.py:548
  5.5 0.5 collective-permute-start
  6.0 0.1 collective-permute-start.1
  6.1 5.2 %collective-permute-done.2.refs_1_ = bf16[96,1024]{1,0:T(8,128)(2,1)S(1)} collective-permute-done((bf16[96,1024]{1,0:T(8,128)(2,1)S(1)}, bf16[96,1024]{1,0:T(8,128)(2,1)S(1)}, u32[]{:S(2)}, u32[]{:S(2)}) %collective-permute-start.2) | collective-permute-done | bytes 196640 | tf_op jit(solution)/shard_map/ppermute | solution.py:548
  11.3 2.0 %collective-permute-start.3 = (bf16[96,1024]{1,0:T(8,128)(2,1)S(1)}, bf16[96,1024]{1,0:T(8,128)(2,1)S(1)}, u32[]{:S(2)}, u32[]{:S(2)}) collective-permute-start(bf16[96,1024]{1,0:T(8,128)(2,1)S(1)} %collective-permute-done.2.refs_1_), channel_id=1, source_target_pairs={{0,8},{8,0},{16,24},{24,16},{1,9},{9,1},{17,25},{25,17},{2,10},{10... | collective-permute-start | bytes 589832 | tf_op jit(solution)/shard_map/ppermute | solution.py:549
  13.2 1.9 %copy-done = bf16[512,3,1024]{2,0,1:T(8,128)(2,1)S(1)} copy-done((bf16[512,3,1024]{2,0,1:T(8,128)(2,1)S(1)}, bf16[512,3,1024]{2,0,1:T(8,128)(2,1)}, u32[]{:S(2)}) %copy-start) | copy-done | bytes 3145752
  15.1 0.2 stage.2.refs_3_.refs_4_.refs_5_
  15.4 2.5 %collective-permute-done.3.refs_2_ = bf16[96,1024]{1,0:T(8,128)(2,1)S(1)} collective-permute-done((bf16[96,1024]{1,0:T(8,128)(2,1)S(1)}, bf16[96,1024]{1,0:T(8,128)(2,1)S(1)}, u32[]{:S(2)}, u32[]{:S(2)}) %collective-permute-start.3) | collective-permute-done | bytes 196640 | tf_op jit(solution)/shard_map/ppermute | solution.py:549
  17.8 0.0 collective-permute-done.4.refs_4_.refs_5_.refs_6_
  17.8 0.7 early_share.1
  18.5 0.9 collective-permute-done.refs_0_.refs_1_
  19.5 0.3 collective-permute-done.1.refs_1_.refs_2_
  19.8 0.7 rest_share.1
  20.4 1.6 %collective-permute-start.5 = (bf16[1,2,768,256]{3,2,1,0:T(8,128)(2,1)S(1)}, bf16[1,2,768,256]{3,2,1,0:T(8,128)(2,1)S(1)}, u32[]{:S(2)}, u32[]{:S(2)}) collective-permute-start(bf16[1,2,768,256]{3,2,1,0:T(8,128)(2,1)S(1)} %rest_share.1), channel_id=1, source_target_pairs={{0,2},{1,5},{2,0},{3,7},{4,6},{5,1},{6,4},{7,3},{8,10},{9,13},{10,... | collective-permute-start | bytes 2359304 | tf_op jit(solution)/shard_map/ppermute | solution.py:555
  22.0 1.2 %project_mix.2 = bf16[1,2,768,256]{3,2,1,0:T(8,128)(2,1)S(1)} custom-call(bf16[192,1024]{1,0:T(8,128)(2,1)S(1)} %get-tuple-element.82.refs_0_, bf16[192,1024]{1,0:T(8,128)(2,1)S(1)} %collective-permute-done.refs_0_.refs_1_, bf16[192,1024]{1,0:T(8,128)(2,1)S(1)} %collective-permute-done.1.refs_1_.refs_2_, bf16[192,1024]{1,0:T(8,128)(2,1)S(1)} %get-tuple-element.85.refs_3_, ...), custom_call_target="tpu_custom_call" | custom-call | tf_op jit(solution)/shard_map/project_mix/pallas_call | solution.py:105
  23.2 0.6 collective-permute-start.7
  23.8 2.1 %project_mix.3 = (f32[2,2,768,256]{3,2,1,0:T(8,128)S(1)}, bf16[4,16,1024]{2,1,0:T(8,128)(2,1)S(1)}) custom-call(bf16[192,1024]{1,0:T(8,128)(2,1)S(1)} %get-tuple-element.82.refs_0_, bf16[192,1024]{1,0:T(8,128)(2,1)S(1)} %collective-permute-done.refs_0_.refs_1_, bf16[192,1024]{1,0:T(8,128)(2,1)S(1)} %collective-permute-done.1.refs_1_.refs_2_, ...), custom_call_target="tpu_custom_call" | custom-call | tf_op jit(solution)/shard_map/project_mix/pallas_call | solution.py:105
  25.8 0.0 copy-start.2
  25.8 6.7 %collective-permute-done.5.refs_1_ = bf16[1,2,768,256]{3,2,1,0:T(8,128)(2,1)S(1)} collective-permute-done((bf16[1,2,768,256]{3,2,1,0:T(8,128)(2,1)S(1)}, bf16[1,2,768,256]{3,2,1,0:T(8,128)(2,1)S(1)}, u32[]{:S(2)}, u32[]{:S(2)}) %collective-permute-start.5) | collective-permute-done | bytes 786464 | tf_op jit(solution)/shard_map/ppermute | solution.py:555
  32.5 0.1 second_share.1
  32.6 0.1 collective-permute-start.6
  32.7 1.5 %collective-permute-start.10 = (bf16[768,256]{1,0:T(8,128)(2,1)S(1)}, bf16[768,256]{1,0:T(8,128)(2,1)S(1)}, u32[]{:S(2)}, u32[]{:S(2)}) collective-permute-start(bf16[768,256]{1,0:T(8,128)(2,1)S(1)} %get-tuple-element.81), channel_id=1, source_target_pairs={{0,4},{1,3},{2,6},{3,1},{4,0},{5,7},{6,2},{7,5},{8,12},{9,11},{10,... | collective-permute-start | bytes 1179656 | tf_op jit(solution)/shard_map/ppermute | solution.py:562
  34.2 0.4 collective-permute-start.11
  34.7 0.0 collective-permute-done.6.refs_4_
  34.7 2.4 %project_query.1 = (f32[192,1024]{1,0:T(8,128)S(1)}, f32[192,1024]{1,0:T(8,128)S(1)}, bf16[192,1024]{1,0:T(8,128)(2,1)S(1)}, bf16[192,1024]{1,0:T(8,128)(2,1)S(1)}) custom-call(bf16[192,1024]{1,0:T(8,128)(2,1)S(1)} %get-tuple-element.82.refs_0_, bf16[192,1024]{1,0:T(8,128)(2,1)S(1)} %collective-permute-done.refs_0_.refs_1_, ...), custom_call_target="tpu_custom_call" | custom-call | tf_op jit(solution)/shard_map/project_query/pallas_call | solution.py:105
  37.1 0.6 stage.3.refs_7_.refs_1_
  37.7 0.0 copy-start.3
  37.7 0.0 copy-start.4
  37.7 8.3 %collective-permute-done.7.refs_1_ = bf16[1,2,768,256]{3,2,1,0:T(8,128)(2,1)S(1)} collective-permute-done((bf16[1,2,768,256]{3,2,1,0:T(8,128)(2,1)S(1)}, bf16[1,2,768,256]{3,2,1,0:T(8,128)(2,1)S(1)}, u32[]{:S(2)}, u32[]{:S(2)}) %collective-permute-start.7) | collective-permute-done | bytes 786464 | tf_op jit(solution)/shard_map/ppermute | solution.py:558
  46.0 0.1 first_share.1
  46.1 0.1 collective-permute-start.9
  46.2 1.6 %collective-permute-start.8 = (bf16[192,1024]{1,0:T(8,128)(2,1)S(1)}, bf16[192,1024]{1,0:T(8,128)(2,1)S(1)}, u32[]{:S(2)}, u32[]{:S(2)}) collective-permute-start(bf16[192,1024]{1,0:T(8,128)(2,1)S(1)} %get-tuple-element.96), channel_id=1, source_target_pairs={{0,2},{1,5},{2,0},{3,7},{4,6},{5,1},{6,4},{7,3},{8,10},{9,13},{10,... | collective-permute-start | bytes 1179656 | tf_op jit(solution)/shard_map/ppermute | solution.py:575
  47.8 1.6 %collective-permute-done.11.refs_3_ = bf16[768,256]{1,0:T(8,128)(2,1)S(1)} collective-permute-done((bf16[768,256]{1,0:T(8,128)(2,1)S(1)}, bf16[768,256]{1,0:T(8,128)(2,1)S(1)}, u32[]{:S(2)}, u32[]{:S(2)}) %collective-permute-start.11) | collective-permute-done | bytes 393248 | tf_op jit(solution)/shard_map/ppermute | solution.py:563
  49.4 2.4 %hyena.1 = (bf16[4,192,128]{2,1,0:T(8,128)(2,1)S(1)}, bf16[4,192,128]{2,1,0:T(8,128)(2,1)S(1)}) custom-call(f32[768,256]{1,0:T(8,128)S(1)} %get-tuple-element.97.refs_0_, bf16[768,256]{1,0:T(8,128)(2,1)S(1)} %collective-permute-done.9.refs_1_, bf16[768,256]{1,0:T(8,128)(2,1)S(1)} %collective-permute-done.10.refs_2_, ...), custom_call_target="tpu_custom_call" | custom-call | tf_op jit(solution)/shard_map/hyena/pallas_call | solution.py:105
  51.8 0.1 collective-permute-start.12
  51.8 1.6 %collective-permute-start.14 = (bf16[192,1024]{1,0:T(8,128)(2,1)S(1)}, bf16[192,1024]{1,0:T(8,128)(2,1)S(1)}, u32[]{:S(2)}, u32[]{:S(2)}) collective-permute-start(bf16[192,1024]{1,0:T(8,128)(2,1)S(1)} %get-tuple-element.103), channel_id=1, source_target_pairs={{0,2},{1,5},{2,0},{3,7},{4,6},{5,1},{6,4},{7,3},{8,10},{9,13},{10,... | collective-permute-start | bytes 1179656 | tf_op jit(solution)/shard_map/ppermute | solution.py:576
  53.4 0.6 collective-permute-done.8.refs_1_
  54.0 0.0 collective-permute-done.12.refs_3_
  54.0 0.1 payloads.1
  54.1 1.5 %collective-permute-start.13 = (bf16[192,1024]{1,0:T(8,128)(2,1)S(1)}, bf16[192,1024]{1,0:T(8,128)(2,1)S(1)}, u32[]{:S(2)}, u32[]{:S(2)}) collective-permute-start(bf16[192,1024]{1,0:T(8,128)(2,1)S(1)} %get-tuple-element.102), channel_id=1, source_target_pairs={{0,4},{1,3},{2,6},{3,1},{4,0},{5,7},{6,2},{7,5},{8,12},{9,11},{10,... | collective-permute-start | bytes 1179656 | tf_op jit(solution)/shard_map/ppermute | solution.py:581
  55.6 0.6 collective-permute-start.15
  56.2 1.5 %collective-permute-start.16 = (bf16[2,192,128]{2,1,0:T(8,128)(2,1)S(1)}, bf16[2,192,128]{2,1,0:T(8,128)(2,1)S(1)}, u32[]{:S(2)}, u32[]{:S(2)}) collective-permute-start(bf16[2,192,128]{2,1,0:T(8,128)(2,1)S(1)} %get-tuple-element.106), channel_id=1, source_target_pairs={{0,2},{1,5},{2,0},{3,7},{4,6},{5,1},{6,4},{7,3},{8,10},{9,13},{10,... | collective-permute-start | bytes 294920 | tf_op jit(solution)/shard_map/ppermute | solution.py:582
  57.7 1.4 %collective-permute-start.17 = (bf16[2,192,128]{2,1,0:T(8,128)(2,1)S(1)}, bf16[2,192,128]{2,1,0:T(8,128)(2,1)S(1)}, u32[]{:S(2)}, u32[]{:S(2)}) collective-permute-start(bf16[2,192,128]{2,1,0:T(8,128)(2,1)S(1)} %get-tuple-element.107), channel_id=1, source_target_pairs={{0,6},{1,7},{2,4},{3,5},{4,2},{5,3},{6,0},{7,1},{8,14},{9,15},{10,... | collective-permute-start | bytes 294920 | tf_op jit(solution)/shard_map/ppermute | solution.py:582
  59.1 3.9 %collective-permute-done.14.refs_2_ = bf16[192,1024]{1,0:T(8,128)(2,1)S(1)} collective-permute-done((bf16[192,1024]{1,0:T(8,128)(2,1)S(1)}, bf16[192,1024]{1,0:T(8,128)(2,1)S(1)}, u32[]{:S(2)}, u32[]{:S(2)}) %collective-permute-start.14) | collective-permute-done | bytes 393248 | tf_op jit(solution)/shard_map/ppermute | solution.py:576
  63.0 2.4 %collective-permute-done.15.refs_4_ = bf16[2,192,128]{2,1,0:T(8,128)(2,1)S(1)} collective-permute-done((bf16[2,192,128]{2,1,0:T(8,128)(2,1)S(1)}, bf16[2,192,128]{2,1,0:T(8,128)(2,1)S(1)}, u32[]{:S(2)}, u32[]{:S(2)}) %collective-permute-start.15) | collective-permute-done | bytes 98336 | tf_op jit(solution)/shard_map/ppermute | solution.py:582
  65.5 0.0 collective-permute-done.16.refs_5_
  65.5 2.6 %collective-permute-done.17.refs_6_ = bf16[2,192,128]{2,1,0:T(8,128)(2,1)S(1)} collective-permute-done((bf16[2,192,128]{2,1,0:T(8,128)(2,1)S(1)}, bf16[2,192,128]{2,1,0:T(8,128)(2,1)S(1)}, u32[]{:S(2)}, u32[]{:S(2)}) %collective-permute-start.17) | collective-permute-done | bytes 98336 | tf_op jit(solution)/shard_map/ppermute | solution.py:582
  68.1 0.9 gate.1
  69.0 1.6 %collective-permute-start.18 = (bf16[192,1024]{1,0:T(8,128)(2,1)S(1)}, bf16[192,1024]{1,0:T(8,128)(2,1)S(1)}, u32[]{:S(2)}, u32[]{:S(2)}) collective-permute-start(bf16[192,1024]{1,0:T(8,128)(2,1)S(1)} %get-tuple-element.111), channel_id=1, source_target_pairs={{0,8},{8,0},{16,24},{24,16},{1,9},{9,1},{17,25},{25,17},{2,10},{10... | collective-permute-start | bytes 1179656 | tf_op jit(solution)/shard_map/ppermute | solution.py:497
  70.6 0.6 out_columns.3.refs_2_
  71.2 0.7 collective-permute-start.19
  71.9 0.6 out_columns.4.refs_0_
  72.5 5.8 %collective-permute-start.20 = (bf16[192,1024]{1,0:T(8,128)(2,1)S(1)}, bf16[192,1024]{1,0:T(8,128)(2,1)S(1)}, u32[]{:S(2)}, u32[]{:S(2)}) collective-permute-start(bf16[192,1024]{1,0:T(8,128)(2,1)S(1)} %out_columns.4.refs_0_), channel_id=1, source_target_pairs={{0,16},{24,8},{1,17},{25,9},{2,18},{26,10},{3,19},{27,11},{4,20},{... | collective-permute-start | bytes 1179656 | tf_op jit(solution)/shard_map/ppermute | solution.py:502
  78.3 2.5 %collective-permute-done.18.refs_1_ = bf16[192,1024]{1,0:T(8,128)(2,1)S(1)} collective-permute-done((bf16[192,1024]{1,0:T(8,128)(2,1)S(1)}, bf16[192,1024]{1,0:T(8,128)(2,1)S(1)}, u32[]{:S(2)}, u32[]{:S(2)}) %collective-permute-start.18) | collective-permute-done | bytes 393248 | tf_op jit(solution)/shard_map/ppermute | solution.py:497
  80.8 0.1 last_step.1
  80.9 1.9 %collective-permute-start.21 = (bf16[192,1024]{1,0:T(8,128)(2,1)S(1)}, bf16[192,1024]{1,0:T(8,128)(2,1)S(1)}, u32[]{:S(2)}, u32[]{:S(2)}) collective-permute-start(bf16[192,1024]{1,0:T(8,128)(2,1)S(1)} %last_step.1), channel_id=1, source_target_pairs={{0,8},{8,24},{16,0},{24,16},{1,9},{9,25},{17,1},{25,17},{2,10},{10... | collective-permute-start | bytes 1179656 | tf_op jit(solution)/shard_map/ppermute | solution.py:510
  82.8 0.6 out_columns.5.refs_0_
  83.4 5.2 %collective-permute-done.20.refs_3_ = bf16[192,1024]{1,0:T(8,128)(2,1)S(1)} collective-permute-done((bf16[192,1024]{1,0:T(8,128)(2,1)S(1)}, bf16[192,1024]{1,0:T(8,128)(2,1)S(1)}, u32[]{:S(2)}, u32[]{:S(2)}) %collective-permute-start.20) | collective-permute-done | bytes 393248 | tf_op jit(solution)/shard_map/ppermute | solution.py:502
  88.6 0.2 early.1
  88.8 13.5 %collective-permute-done.21 = bf16[192,1024]{1,0:T(8,128)(2,1)S(1)} collective-permute-done((bf16[192,1024]{1,0:T(8,128)(2,1)S(1)}, bf16[192,1024]{1,0:T(8,128)(2,1)S(1)}, u32[]{:S(2)}, u32[]{:S(2)}) %collective-permute-start.21) | collective-permute-done | bytes 393248 | tf_op jit(solution)/shard_map/ppermute | solution.py:510
  102.3 0.8 add_convert_fusion
  (14 shorter events, 0.0 us)
Async XLA Ops:
  0.0 17.8 %collective-permute-start.4 = (bf16[3,512,1024]{2,1,0:T(8,128)(2,1)}, bf16[3,512,1024]{2,1,0:T(8,128)(2,1)S(1)}, u32[]{:S(2)}, u32[]{:S(2)}) collective-permute-start(bf16[3,512,1024]{2,1,0:T(8,128)(2,1)} %bitcast.3), channel_id=1, source_target_pairs={{0,1},{1,0},{2,3},{3,2},{4,5},{5,4},{6,7},{7,6},{8,9},{9,8},{10,11... | collective-permute-start | bytes 9437192 | tf_op jit(solution)/shard_map/ppermute | solution.py:544
  0.5 1.4 %copy-start.1 = (bf16[192,4096]{1,0:T(8,128)(2,1)S(1)}, bf16[192,4096]{1,0:T(8,128)(2,1)}, u32[]{:S(2)}) copy-start(bf16[192,4096]{1,0:T(8,128)(2,1)} %refs_0_.1) | copy-start | bytes 4718596
  2.0 9.3 %collective-permute-start.2 = (bf16[96,1024]{1,0:T(8,128)(2,1)S(1)}, bf16[96,1024]{1,0:T(8,128)(2,1)S(1)}, u32[]{:S(2)}, u32[]{:S(2)}) collective-permute-start(bf16[96,1024]{1,0:T(8,128)(2,1)S(1)} %get-tuple-element.67), channel_id=1, source_target_pairs={{0,6},{1,7},{2,4},{3,5},{4,2},{5,3},{6,0},{7,1},{8,14},{9,15},{10,... | collective-permute-start | bytes 589832 | tf_op jit(solution)/shard_map/ppermute | solution.py:548
  5.5 14.0 %collective-permute-start = (bf16[192,1024]{1,0:T(8,128)(2,1)S(1)}, bf16[192,1024]{1,0:T(8,128)(2,1)S(1)}, u32[]{:S(2)}, u32[]{:S(2)}) collective-permute-start(bf16[192,1024]{1,0:T(8,128)(2,1)S(1)} %get-tuple-element.65), channel_id=1, source_target_pairs={{0,4},{1,3},{2,6},{3,1},{4,0},{5,7},{6,2},{7,5},{8,12},{9,11},{10,... | collective-permute-start | bytes 1179656 | tf_op jit(solution)/shard_map/ppermute | solution.py:550
  6.0 13.8 %collective-permute-start.1 = (bf16[192,1024]{1,0:T(8,128)(2,1)S(1)}, bf16[192,1024]{1,0:T(8,128)(2,1)S(1)}, u32[]{:S(2)}, u32[]{:S(2)}) collective-permute-start(bf16[192,1024]{1,0:T(8,128)(2,1)S(1)} %get-tuple-element.66), channel_id=1, source_target_pairs={{0,2},{1,5},{2,0},{3,7},{4,6},{5,1},{6,4},{7,3},{8,10},{9,13},{10,... | collective-permute-start | bytes 1179656 | tf_op jit(solution)/shard_map/ppermute | solution.py:550
  11.3 6.6 %collective-permute-start.3 = (bf16[96,1024]{1,0:T(8,128)(2,1)S(1)}, bf16[96,1024]{1,0:T(8,128)(2,1)S(1)}, u32[]{:S(2)}, u32[]{:S(2)}) collective-permute-start(bf16[96,1024]{1,0:T(8,128)(2,1)S(1)} %collective-permute-done.2.refs_1_), channel_id=1, source_target_pairs={{0,8},{8,0},{16,24},{24,16},{1,9},{9,1},{17,25},{25,17},{2,10},{10... | collective-permute-start | bytes 589832 | tf_op jit(solution)/shard_map/ppermute | solution.py:549
  13.2 1.9 %copy-start = (bf16[512,3,1024]{2,0,1:T(8,128)(2,1)S(1)}, bf16[512,3,1024]{2,0,1:T(8,128)(2,1)}, u32[]{:S(2)}) copy-start(bf16[512,3,1024]{2,0,1:T(8,128)(2,1)} %param.7) | copy-start | bytes 9437188
  20.4 12.1 %collective-permute-start.5 = (bf16[1,2,768,256]{3,2,1,0:T(8,128)(2,1)S(1)}, bf16[1,2,768,256]{3,2,1,0:T(8,128)(2,1)S(1)}, u32[]{:S(2)}, u32[]{:S(2)}) collective-permute-start(bf16[1,2,768,256]{3,2,1,0:T(8,128)(2,1)S(1)} %rest_share.1), channel_id=1, source_target_pairs={{0,2},{1,5},{2,0},{3,7},{4,6},{5,1},{6,4},{7,3},{8,10},{9,13},{10,... | collective-permute-start | bytes 2359304 | tf_op jit(solution)/shard_map/ppermute | solution.py:555
  23.2 22.8 %collective-permute-start.7 = (bf16[1,2,768,256]{3,2,1,0:T(8,128)(2,1)S(1)}, bf16[1,2,768,256]{3,2,1,0:T(8,128)(2,1)S(1)}, u32[]{:S(2)}, u32[]{:S(2)}) collective-permute-start(bf16[1,2,768,256]{3,2,1,0:T(8,128)(2,1)S(1)} %project_mix.2), channel_id=1, source_target_pairs={{0,2},{1,5},{2,0},{3,7},{4,6},{5,1},{6,4},{7,3},{8,10},{9,13},{10,... | collective-permute-start | bytes 2359304 | tf_op jit(solution)/shard_map/ppermute | solution.py:558
  23.8 13.3 %slice-start = ((s8[8388608]{0:T(1024)(128)(4,1)}), s8[4194304]{0:T(1024)(128)(4,1)S(1)}, s32[]{:S(2)}) async-start(s8[8388608]{0:T(1024)(128)(4,1)} %bitcast.1), calls=%async_computation | async-start | bytes 8388608
  25.8 8.8 %copy-start.2 = (f32[3,3,1024]{2,1,0:T(4,128)S(1)}, f32[3,3,1024]{2,1,0:T(4,128)}, u32[]{:S(2)}) copy-start(f32[3,3,1024]{2,1,0:T(4,128)} %refs_4_.1) | copy-start | bytes 110596
  32.5 4.6 %slice-start.1 = ((s8[8388608]{0:T(1024)(128)(4,1)}), s8[4194304]{0:T(1024)(128)(4,1)S(1)}, s32[]{:S(2)}) async-start(s8[8388608]{0:T(1024)(128)(4,1)} %bitcast.1), calls=%async_computation.1 | async-start | bytes 8388608
  32.6 2.0 %collective-permute-start.6 = (bf16[4,16,1024]{2,1,0:T(8,128)(2,1)S(1)}, bf16[4,16,1024]{2,1,0:T(8,128)(2,1)S(1)}, u32[]{:S(2)}, u32[]{:S(2)}) collective-permute-start(bf16[4,16,1024]{2,1,0:T(8,128)(2,1)S(1)} %get-tuple-element.86), channel_id=1, source_target_pairs={{0,1},{1,0},{2,3},{3,2},{4,5},{5,4},{6,7},{7,6},{8,9},{9,8},{10,11... | collective-permute-start | bytes 393224 | tf_op jit(solution)/shard_map/ppermute | solution.py:566
  32.7 16.6 %collective-permute-start.10 = (bf16[768,256]{1,0:T(8,128)(2,1)S(1)}, bf16[768,256]{1,0:T(8,128)(2,1)S(1)}, u32[]{:S(2)}, u32[]{:S(2)}) collective-permute-start(bf16[768,256]{1,0:T(8,128)(2,1)S(1)} %get-tuple-element.81), channel_id=1, source_target_pairs={{0,4},{1,3},{2,6},{3,1},{4,0},{5,7},{6,2},{7,5},{8,12},{9,11},{10,... | collective-permute-start | bytes 1179656 | tf_op jit(solution)/shard_map/ppermute | solution.py:562
  34.2 15.1 %collective-permute-start.11 = (bf16[768,256]{1,0:T(8,128)(2,1)S(1)}, bf16[768,256]{1,0:T(8,128)(2,1)S(1)}, u32[]{:S(2)}, u32[]{:S(2)}) collective-permute-start(bf16[768,256]{1,0:T(8,128)(2,1)S(1)} %get-tuple-element.99), channel_id=1, source_target_pairs={{0,5},{1,2},{2,7},{3,0},{4,1},{5,6},{6,3},{7,4},{8,13},{9,10},{10,... | collective-permute-start | bytes 1179656 | tf_op jit(solution)/shard_map/ppermute | solution.py:563
  37.7 11.7 %copy-start.3 = (f32[8,1024]{1,0:T(8,128)S(1)}, f32[8,1024]{1,0:T(8,128)}, u32[]{:S(2)}) copy-start(f32[8,1024]{1,0:T(8,128)} %refs_5_.1) | copy-start | bytes 98308
  37.7 11.7 %copy-start.4 = (f32[8,1024]{1,0:T(8,128)S(1)}, f32[8,1024]{1,0:T(8,128)}, u32[]{:S(2)}) copy-start(f32[8,1024]{1,0:T(8,128)} %refs_6_.1) | copy-start | bytes 98308
  46.1 3.2 %collective-permute-start.9 = (bf16[768,256]{1,0:T(8,128)(2,1)S(1)}, bf16[768,256]{1,0:T(8,128)(2,1)S(1)}, u32[]{:S(2)}, u32[]{:S(2)}) collective-permute-start(bf16[768,256]{1,0:T(8,128)(2,1)S(1)} %get-tuple-element.98), channel_id=1, source_target_pairs={{0,1},{1,0},{2,3},{3,2},{4,5},{5,4},{6,7},{7,6},{8,9},{9,8},{10,11... | collective-permute-start | bytes 1179656 | tf_op jit(solution)/shard_map/ppermute | solution.py:573
  46.2 7.8 %collective-permute-start.8 = (bf16[192,1024]{1,0:T(8,128)(2,1)S(1)}, bf16[192,1024]{1,0:T(8,128)(2,1)S(1)}, u32[]{:S(2)}, u32[]{:S(2)}) collective-permute-start(bf16[192,1024]{1,0:T(8,128)(2,1)S(1)} %get-tuple-element.96), channel_id=1, source_target_pairs={{0,2},{1,5},{2,0},{3,7},{4,6},{5,1},{6,4},{7,3},{8,10},{9,13},{10,... | collective-permute-start | bytes 1179656 | tf_op jit(solution)/shard_map/ppermute | solution.py:575
  51.8 2.3 %collective-permute-start.12 = (bf16[4,192,128]{2,1,0:T(8,128)(2,1)S(1)}, bf16[4,192,128]{2,1,0:T(8,128)(2,1)S(1)}, u32[]{:S(2)}, u32[]{:S(2)}) collective-permute-start(bf16[4,192,128]{2,1,0:T(8,128)(2,1)S(1)} %get-tuple-element.101), channel_id=1, source_target_pairs={{0,1},{1,0},{2,3},{3,2},{4,5},{5,4},{6,7},{7,6},{8,9},{9,8},{10,11... | collective-permute-start | bytes 589832 | tf_op jit(solution)/shard_map/ppermute | solution.py:579
  51.8 11.2 %collective-permute-start.14 = (bf16[192,1024]{1,0:T(8,128)(2,1)S(1)}, bf16[192,1024]{1,0:T(8,128)(2,1)S(1)}, u32[]{:S(2)}, u32[]{:S(2)}) collective-permute-start(bf16[192,1024]{1,0:T(8,128)(2,1)S(1)} %get-tuple-element.103), channel_id=1, source_target_pairs={{0,2},{1,5},{2,0},{3,7},{4,6},{5,1},{6,4},{7,3},{8,10},{9,13},{10,... | collective-permute-start | bytes 1179656 | tf_op jit(solution)/shard_map/ppermute | solution.py:576
  54.1 14.0 %collective-permute-start.13 = (bf16[192,1024]{1,0:T(8,128)(2,1)S(1)}, bf16[192,1024]{1,0:T(8,128)(2,1)S(1)}, u32[]{:S(2)}, u32[]{:S(2)}) collective-permute-start(bf16[192,1024]{1,0:T(8,128)(2,1)S(1)} %get-tuple-element.102), channel_id=1, source_target_pairs={{0,4},{1,3},{2,6},{3,1},{4,0},{5,7},{6,2},{7,5},{8,12},{9,11},{10,... | collective-permute-start | bytes 1179656 | tf_op jit(solution)/shard_map/ppermute | solution.py:581
  55.6 9.8 %collective-permute-start.15 = (bf16[2,192,128]{2,1,0:T(8,128)(2,1)S(1)}, bf16[2,192,128]{2,1,0:T(8,128)(2,1)S(1)}, u32[]{:S(2)}, u32[]{:S(2)}) collective-permute-start(bf16[2,192,128]{2,1,0:T(8,128)(2,1)S(1)} %get-tuple-element.105), channel_id=1, source_target_pairs={{0,4},{1,3},{2,6},{3,1},{4,0},{5,7},{6,2},{7,5},{8,12},{9,11},{10,... | collective-permute-start | bytes 294920 | tf_op jit(solution)/shard_map/ppermute | solution.py:582
  56.2 9.2 %collective-permute-start.16 = (bf16[2,192,128]{2,1,0:T(8,128)(2,1)S(1)}, bf16[2,192,128]{2,1,0:T(8,128)(2,1)S(1)}, u32[]{:S(2)}, u32[]{:S(2)}) collective-permute-start(bf16[2,192,128]{2,1,0:T(8,128)(2,1)S(1)} %get-tuple-element.106), channel_id=1, source_target_pairs={{0,2},{1,5},{2,0},{3,7},{4,6},{5,1},{6,4},{7,3},{8,10},{9,13},{10,... | collective-permute-start | bytes 294920 | tf_op jit(solution)/shard_map/ppermute | solution.py:582
  57.7 10.4 %collective-permute-start.17 = (bf16[2,192,128]{2,1,0:T(8,128)(2,1)S(1)}, bf16[2,192,128]{2,1,0:T(8,128)(2,1)S(1)}, u32[]{:S(2)}, u32[]{:S(2)}) collective-permute-start(bf16[2,192,128]{2,1,0:T(8,128)(2,1)S(1)} %get-tuple-element.107), channel_id=1, source_target_pairs={{0,6},{1,7},{2,4},{3,5},{4,2},{5,3},{6,0},{7,1},{8,14},{9,15},{10,... | collective-permute-start | bytes 294920 | tf_op jit(solution)/shard_map/ppermute | solution.py:582
  69.0 11.8 %collective-permute-start.18 = (bf16[192,1024]{1,0:T(8,128)(2,1)S(1)}, bf16[192,1024]{1,0:T(8,128)(2,1)S(1)}, u32[]{:S(2)}, u32[]{:S(2)}) collective-permute-start(bf16[192,1024]{1,0:T(8,128)(2,1)S(1)} %get-tuple-element.111), channel_id=1, source_target_pairs={{0,8},{8,0},{16,24},{24,16},{1,9},{9,1},{17,25},{25,17},{2,10},{10... | collective-permute-start | bytes 1179656 | tf_op jit(solution)/shard_map/ppermute | solution.py:497
  71.2 17.4 %collective-permute-start.19 = (bf16[192,1024]{1,0:T(8,128)(2,1)S(1)}, bf16[192,1024]{1,0:T(8,128)(2,1)S(1)}, u32[]{:S(2)}, u32[]{:S(2)}) collective-permute-start(bf16[192,1024]{1,0:T(8,128)(2,1)S(1)} %out_columns.3.refs_2_), channel_id=1, source_target_pairs={{8,16},{16,8},{9,17},{17,9},{10,18},{18,10},{11,19},{19,11},{12,20... | collective-permute-start | bytes 1179656 | tf_op jit(solution)/shard_map/ppermute | solution.py:499
  72.5 16.1 %collective-permute-start.20 = (bf16[192,1024]{1,0:T(8,128)(2,1)S(1)}, bf16[192,1024]{1,0:T(8,128)(2,1)S(1)}, u32[]{:S(2)}, u32[]{:S(2)}) collective-permute-start(bf16[192,1024]{1,0:T(8,128)(2,1)S(1)} %out_columns.4.refs_0_), channel_id=1, source_target_pairs={{0,16},{24,8},{1,17},{25,9},{2,18},{26,10},{3,19},{27,11},{4,20},{... | collective-permute-start | bytes 1179656 | tf_op jit(solution)/shard_map/ppermute | solution.py:502
  80.9 21.4 %collective-permute-start.21 = (bf16[192,1024]{1,0:T(8,128)(2,1)S(1)}, bf16[192,1024]{1,0:T(8,128)(2,1)S(1)}, u32[]{:S(2)}, u32[]{:S(2)}) collective-permute-start(bf16[192,1024]{1,0:T(8,128)(2,1)S(1)} %last_step.1), channel_id=1, source_target_pairs={{0,8},{8,24},{16,0},{24,16},{1,9},{9,25},{17,1},{25,17},{2,10},{10... | collective-permute-start | bytes 1179656 | tf_op jit(solution)/shard_map/ppermute | solution.py:510

commit v10 on v9

--- a/solution.py
+++ b/solution.py
@@ -569,9 +569,10 @@
     w_out = stage(w_out)
     q_own, w_out, rest = lax.optimization_barrier((q_own, w_out, rest))
 
+    q_both, first_in = lax.optimization_barrier((q_both, first_in))
     own, other_half = first_share(order, rest, first_in, chips)
     other_half = lax.ppermute(other_half, "ctx", swap)
-    q_both, q_first, own = lax.optimization_barrier((q_both, q_first, own))
+    q_first, own = lax.optimization_barrier((q_first, own))
     q_both = lax.ppermute(q_both, "ctx", route(2))
     q_first = lax.ppermute(q_first, "ctx", route(2))
     parts = [own, other_half, second_in, swap_second]

time: 103 us -> 103 us (level)
    ppermute x1, waiting for transfers between devices: 3.9 us -> 2.59 us  [on_device_chips(): q_first = lax.ppermute(q_first, 'ctx', route(2))]
where the time goes in v10:
time: 103 us; the launch traced here: 102 us
  waiting for transfers between devices  55.7 us (54%)
  starting transfers between devices  28.7 us (28%)
  Pallas kernels  13.5 us (13%)
  local copies, waits for them, and re-layouts  3.32 us (3%)
    ppermute x1, waiting for transfers between devices, output_over_line(): last_in = lax.ppermute(last, 'dp', [(0, 1), (1, 3), (2, 0), (3, 2)])  13.7 us
    pallas_call x16, Pallas kernels, local(): pl.pallas_call(placed, out_shape=out if len(out) > 1 else out[0], in_spec...  12.8 us
    ppermute x1, waiting for transfers between devices, on_device_chips(): first_in = lax.ppermute(first, 'ctx', route(2))  8.93 us
    ppermute x1, waiting for transfers between devices, on_device_chips(): both_in = lax.ppermute(both, 'ctx', route(2))  6.66 us
    ppermute x1, starting transfers between devices, output_over_line(): end_in = lax.ppermute(far, 'dp', [(0, 2), (3, 1)])  5.76 us
    ppermute x1, waiting for transfers between devices, output_over_line(): end_in = lax.ppermute(far, 'dp', [(0, 2), (3, 1)])  5.21 us
    ppermute x1, waiting for transfers between devices, on_device_chips(): half = lax.ppermute(xs[3], 'ctx', route(3))  5.15 us
    ppermute x3, waiting for transfers between devices, on_device_chips(): lax.ppermute(long_parts[s], 'ctx', route(s))  5.09 us
  transfers between devices with their start and end apart: 22, of which 14 were waited for; matrix products, arithmetic and copies ran while one was open for 0% of the time, Pallas kernels for 12%

profile of v10, /device:TPU:0, one launch (start us, length us, event | category | flops | bytes accessed | tf_op | source)
XLA Modules:
  0.0 102.3 jit_solution(1986535718436348665)
XLA Ops:
  0.0 0.5 collective-permute-start.4
  0.5 1.4 %copy-done.1 = bf16[192,4096]{1,0:T(8,128)(2,1)S(1)} copy-done((bf16[192,4096]{1,0:T(8,128)(2,1)S(1)}, bf16[192,4096]{1,0:T(8,128)(2,1)}, u32[]{:S(2)}) %copy-start.1) | copy-done | bytes 1572888
  1.9 0.1 cut.1
  2.0 3.5 %collective-permute-start.2 = (bf16[96,1024]{1,0:T(8,128)(2,1)S(1)}, bf16[96,1024]{1,0:T(8,128)(2,1)S(1)}, u32[]{:S(2)}, u32[]{:S(2)}) collective-permute-start(bf16[96,1024]{1,0:T(8,128)(2,1)S(1)} %get-tuple-element.68), channel_id=1, source_target_pairs={{0,6},{1,7},{2,4},{3,5},{4,2},{5,3},{6,0},{7,1},{8,14},{9,15},{10,... | collective-permute-start | bytes 589832 | tf_op jit(solution)/shard_map/ppermute | solution.py:548
  5.5 0.5 collective-permute-start
  6.0 0.1 collective-permute-start.1
  6.1 5.2 %collective-permute-done.2.refs_1_ = bf16[96,1024]{1,0:T(8,128)(2,1)S(1)} collective-permute-done((bf16[96,1024]{1,0:T(8,128)(2,1)S(1)}, bf16[96,1024]{1,0:T(8,128)(2,1)S(1)}, u32[]{:S(2)}, u32[]{:S(2)}) %collective-permute-start.2) | collective-permute-done | bytes 196640 | tf_op jit(solution)/shard_map/ppermute | solution.py:548
  11.3 2.0 %collective-permute-start.3 = (bf16[96,1024]{1,0:T(8,128)(2,1)S(1)}, bf16[96,1024]{1,0:T(8,128)(2,1)S(1)}, u32[]{:S(2)}, u32[]{:S(2)}) collective-permute-start(bf16[96,1024]{1,0:T(8,128)(2,1)S(1)} %collective-permute-done.2.refs_1_), channel_id=1, source_target_pairs={{0,8},{8,0},{16,24},{24,16},{1,9},{9,1},{17,25},{25,17},{2,10},{10... | collective-permute-start | bytes 589832 | tf_op jit(solution)/shard_map/ppermute | solution.py:549
  13.2 1.9 %copy-done = bf16[512,3,1024]{2,0,1:T(8,128)(2,1)S(1)} copy-done((bf16[512,3,1024]{2,0,1:T(8,128)(2,1)S(1)}, bf16[512,3,1024]{2,0,1:T(8,128)(2,1)}, u32[]{:S(2)}) %copy-start) | copy-done | bytes 3145752
  15.1 0.2 stage.2.refs_3_.refs_4_.refs_5_
  15.4 2.5 %collective-permute-done.3.refs_2_ = bf16[96,1024]{1,0:T(8,128)(2,1)S(1)} collective-permute-done((bf16[96,1024]{1,0:T(8,128)(2,1)S(1)}, bf16[96,1024]{1,0:T(8,128)(2,1)S(1)}, u32[]{:S(2)}, u32[]{:S(2)}) %collective-permute-start.3) | collective-permute-done | bytes 196640 | tf_op jit(solution)/shard_map/ppermute | solution.py:549
  17.8 0.0 collective-permute-done.4.refs_4_.refs_5_.refs_6_
  17.8 0.7 early_share.1
  18.5 0.9 collective-permute-done.refs_0_.refs_1_
  19.5 0.3 collective-permute-done.1.refs_1_.refs_2_
  19.8 0.7 rest_share.1
  20.4 1.6 %collective-permute-start.5 = (bf16[1,2,768,256]{3,2,1,0:T(8,128)(2,1)S(1)}, bf16[1,2,768,256]{3,2,1,0:T(8,128)(2,1)S(1)}, u32[]{:S(2)}, u32[]{:S(2)}) collective-permute-start(bf16[1,2,768,256]{3,2,1,0:T(8,128)(2,1)S(1)} %rest_share.1), channel_id=1, source_target_pairs={{0,2},{1,5},{2,0},{3,7},{4,6},{5,1},{6,4},{7,3},{8,10},{9,13},{10,... | collective-permute-start | bytes 2359304 | tf_op jit(solution)/shard_map/ppermute | solution.py:555
  22.0 1.2 %project_mix.2 = bf16[1,2,768,256]{3,2,1,0:T(8,128)(2,1)S(1)} custom-call(bf16[192,1024]{1,0:T(8,128)(2,1)S(1)} %get-tuple-element.83.refs_0_, bf16[192,1024]{1,0:T(8,128)(2,1)S(1)} %collective-permute-done.refs_0_.refs_1_, bf16[192,1024]{1,0:T(8,128)(2,1)S(1)} %collective-permute-done.1.refs_1_.refs_2_, bf16[192,1024]{1,0:T(8,128)(2,1)S(1)} %get-tuple-element.86.refs_3_, ...), custom_call_target="tpu_custom_call" | custom-call | tf_op jit(solution)/shard_map/project_mix/pallas_call | solution.py:105
  23.2 0.6 collective-permute-start.7
  23.8 2.1 %project_mix.3 = (f32[2,2,768,256]{3,2,1,0:T(8,128)S(1)}, bf16[4,16,1024]{2,1,0:T(8,128)(2,1)S(1)}) custom-call(bf16[192,1024]{1,0:T(8,128)(2,1)S(1)} %get-tuple-element.83.refs_0_, bf16[192,1024]{1,0:T(8,128)(2,1)S(1)} %collective-permute-done.refs_0_.refs_1_, bf16[192,1024]{1,0:T(8,128)(2,1)S(1)} %collective-permute-done.1.refs_1_.refs_2_, ...), custom_call_target="tpu_custom_call" | custom-call | tf_op jit(solution)/shard_map/project_mix/pallas_call | solution.py:105
  25.8 0.0 copy-start.2
  25.8 6.7 %collective-permute-done.5.refs_1_ = bf16[1,2,768,256]{3,2,1,0:T(8,128)(2,1)S(1)} collective-permute-done((bf16[1,2,768,256]{3,2,1,0:T(8,128)(2,1)S(1)}, bf16[1,2,768,256]{3,2,1,0:T(8,128)(2,1)S(1)}, u32[]{:S(2)}, u32[]{:S(2)}) %collective-permute-start.5) | collective-permute-done | bytes 786464 | tf_op jit(solution)/shard_map/ppermute | solution.py:555
  32.5 0.1 second_share.1
  32.6 0.1 collective-permute-start.6
  32.7 1.5 %collective-permute-start.10 = (bf16[768,256]{1,0:T(8,128)(2,1)S(1)}, bf16[768,256]{1,0:T(8,128)(2,1)S(1)}, u32[]{:S(2)}, u32[]{:S(2)}) collective-permute-start(bf16[768,256]{1,0:T(8,128)(2,1)S(1)} %get-tuple-element.82), channel_id=1, source_target_pairs={{0,4},{1,3},{2,6},{3,1},{4,0},{5,7},{6,2},{7,5},{8,12},{9,11},{10,... | collective-permute-start | bytes 1179656 | tf_op jit(solution)/shard_map/ppermute | solution.py:562
  34.2 0.4 collective-permute-start.11
  34.7 2.4 %project_query.1 = (f32[192,1024]{1,0:T(8,128)S(1)}, f32[192,1024]{1,0:T(8,128)S(1)}, bf16[192,1024]{1,0:T(8,128)(2,1)S(1)}, bf16[192,1024]{1,0:T(8,128)(2,1)S(1)}) custom-call(bf16[192,1024]{1,0:T(8,128)(2,1)S(1)} %get-tuple-element.83.refs_0_, bf16[192,1024]{1,0:T(8,128)(2,1)S(1)} %collective-permute-done.refs_0_.refs_1_, ...), custom_call_target="tpu_custom_call" | custom-call | tf_op jit(solution)/shard_map/project_query/pallas_call | solution.py:105
  37.1 8.9 %collective-permute-done.7.refs_1_ = bf16[1,2,768,256]{3,2,1,0:T(8,128)(2,1)S(1)} collective-permute-done((bf16[1,2,768,256]{3,2,1,0:T(8,128)(2,1)S(1)}, bf16[1,2,768,256]{3,2,1,0:T(8,128)(2,1)S(1)}, u32[]{:S(2)}, u32[]{:S(2)}) %collective-permute-start.7) | collective-permute-done | bytes 786464 | tf_op jit(solution)/shard_map/ppermute | solution.py:558
  46.0 0.6 stage.3.refs_7_.refs_1_
  46.6 0.0 copy-start.3
  46.6 0.0 copy-start.4
  46.6 0.1 first_share.1
  46.7 0.1 collective-permute-start.9
  46.8 1.6 %collective-permute-start.8 = (bf16[192,1024]{1,0:T(8,128)(2,1)S(1)}, bf16[192,1024]{1,0:T(8,128)(2,1)S(1)}, u32[]{:S(2)}, u32[]{:S(2)}) collective-permute-start(bf16[192,1024]{1,0:T(8,128)(2,1)S(1)} %get-tuple-element.94), channel_id=1, source_target_pairs={{0,2},{1,5},{2,0},{3,7},{4,6},{5,1},{6,4},{7,3},{8,10},{9,13},{10,... | collective-permute-start | bytes 1179656 | tf_op jit(solution)/shard_map/ppermute | solution.py:576
  48.4 1.0 collective-permute-done.11.refs_3_
  49.4 0.0 collective-permute-done.10.refs_2_
  49.4 0.0 collective-permute-done.9.refs_1_
  49.4 2.4 %hyena.1 = (bf16[4,192,128]{2,1,0:T(8,128)(2,1)S(1)}, bf16[4,192,128]{2,1,0:T(8,128)(2,1)S(1)}) custom-call(f32[768,256]{1,0:T(8,128)S(1)} %get-tuple-element.99.refs_0_, bf16[768,256]{1,0:T(8,128)(2,1)S(1)} %collective-permute-done.9.refs_1_, bf16[768,256]{1,0:T(8,128)(2,1)S(1)} %collective-permute-done.10.refs_2_, ...), custom_call_target="tpu_custom_call" | custom-call | tf_op jit(solution)/shard_map/hyena/pallas_call | solution.py:105
  51.8 0.1 collective-permute-start.12
  51.8 1.6 %collective-permute-start.14 = (bf16[192,1024]{1,0:T(8,128)(2,1)S(1)}, bf16[192,1024]{1,0:T(8,128)(2,1)S(1)}, u32[]{:S(2)}, u32[]{:S(2)}) collective-permute-start(bf16[192,1024]{1,0:T(8,128)(2,1)S(1)} %get-tuple-element.105), channel_id=1, source_target_pairs={{0,2},{1,5},{2,0},{3,7},{4,6},{5,1},{6,4},{7,3},{8,10},{9,13},{10,... | collective-permute-start | bytes 1179656 | tf_op jit(solution)/shard_map/ppermute | solution.py:577
  53.4 1.2 %collective-permute-done.8.refs_1_ = bf16[192,1024]{1,0:T(8,128)(2,1)S(1)} collective-permute-done((bf16[192,1024]{1,0:T(8,128)(2,1)S(1)}, bf16[192,1024]{1,0:T(8,128)(2,1)S(1)}, u32[]{:S(2)}, u32[]{:S(2)}) %collective-permute-start.8) | collective-permute-done | bytes 393248 | tf_op jit(solution)/shard_map/ppermute | solution.py:576
  54.6 0.0 collective-permute-done.12.refs_3_
  54.7 0.1 payloads.1
  54.7 1.5 %collective-permute-start.13 = (bf16[192,1024]{1,0:T(8,128)(2,1)S(1)}, bf16[192,1024]{1,0:T(8,128)(2,1)S(1)}, u32[]{:S(2)}, u32[]{:S(2)}) collective-permute-start(bf16[192,1024]{1,0:T(8,128)(2,1)S(1)} %get-tuple-element.104), channel_id=1, source_target_pairs={{0,4},{1,3},{2,6},{3,1},{4,0},{5,7},{6,2},{7,5},{8,12},{9,11},{10,... | collective-permute-start | bytes 1179656 | tf_op jit(solution)/shard_map/ppermute | solution.py:582
  56.2 0.6 collective-permute-start.15
  56.8 1.5 %collective-permute-start.16 = (bf16[2,192,128]{2,1,0:T(8,128)(2,1)S(1)}, bf16[2,192,128]{2,1,0:T(8,128)(2,1)S(1)}, u32[]{:S(2)}, u32[]{:S(2)}) collective-permute-start(bf16[2,192,128]{2,1,0:T(8,128)(2,1)S(1)} %get-tuple-element.108), channel_id=1, source_target_pairs={{0,2},{1,5},{2,0},{3,7},{4,6},{5,1},{6,4},{7,3},{8,10},{9,13},{10,... | collective-permute-start | bytes 294920 | tf_op jit(solution)/shard_map/ppermute | solution.py:583
  58.3 1.4 %collective-permute-start.17 = (bf16[2,192,128]{2,1,0:T(8,128)(2,1)S(1)}, bf16[2,192,128]{2,1,0:T(8,128)(2,1)S(1)}, u32[]{:S(2)}, u32[]{:S(2)}) collective-permute-start(bf16[2,192,128]{2,1,0:T(8,128)(2,1)S(1)} %get-tuple-element.109), channel_id=1, source_target_pairs={{0,6},{1,7},{2,4},{3,5},{4,2},{5,3},{6,0},{7,1},{8,14},{9,15},{10,... | collective-permute-start | bytes 294920 | tf_op jit(solution)/shard_map/ppermute | solution.py:583
  59.7 2.6 %collective-permute-done.14.refs_2_ = bf16[192,1024]{1,0:T(8,128)(2,1)S(1)} collective-permute-done((bf16[192,1024]{1,0:T(8,128)(2,1)S(1)}, bf16[192,1024]{1,0:T(8,128)(2,1)S(1)}, u32[]{:S(2)}, u32[]{:S(2)}) %collective-permute-start.14) | collective-permute-done | bytes 393248 | tf_op jit(solution)/shard_map/ppermute | solution.py:577
  62.3 3.3 %collective-permute-done.15.refs_4_ = bf16[2,192,128]{2,1,0:T(8,128)(2,1)S(1)} collective-permute-done((bf16[2,192,128]{2,1,0:T(8,128)(2,1)S(1)}, bf16[2,192,128]{2,1,0:T(8,128)(2,1)S(1)}, u32[]{:S(2)}, u32[]{:S(2)}) %collective-permute-start.15) | collective-permute-done | bytes 98336 | tf_op jit(solution)/shard_map/ppermute | solution.py:583
  65.6 1.8 %collective-permute-done.17.refs_6_ = bf16[2,192,128]{2,1,0:T(8,128)(2,1)S(1)} collective-permute-done((bf16[2,192,128]{2,1,0:T(8,128)(2,1)S(1)}, bf16[2,192,128]{2,1,0:T(8,128)(2,1)S(1)}, u32[]{:S(2)}, u32[]{:S(2)}) %collective-permute-start.17) | collective-permute-done | bytes 98336 | tf_op jit(solution)/shard_map/ppermute | solution.py:583
  67.4 0.9 gate.1
  68.3 1.6 %collective-permute-start.18 = (bf16[192,1024]{1,0:T(8,128)(2,1)S(1)}, bf16[192,1024]{1,0:T(8,128)(2,1)S(1)}, u32[]{:S(2)}, u32[]{:S(2)}) collective-permute-start(bf16[192,1024]{1,0:T(8,128)(2,1)S(1)} %get-tuple-element.113), channel_id=1, source_target_pairs={{0,8},{8,0},{16,24},{24,16},{1,9},{9,1},{17,25},{25,17},{2,10},{10... | collective-permute-start | bytes 1179656 | tf_op jit(solution)/shard_map/ppermute | solution.py:497
  69.9 0.6 out_columns.3.refs_2_
  70.5 0.7 collective-permute-start.19
  71.2 0.6 out_columns.4.refs_0_
  71.8 5.8 %collective-permute-start.20 = (bf16[192,1024]{1,0:T(8,128)(2,1)S(1)}, bf16[192,1024]{1,0:T(8,128)(2,1)S(1)}, u32[]{:S(2)}, u32[]{:S(2)}) collective-permute-start(bf16[192,1024]{1,0:T(8,128)(2,1)S(1)} %out_columns.4.refs_0_), channel_id=1, source_target_pairs={{0,16},{24,8},{1,17},{25,9},{2,18},{26,10},{3,19},{27,11},{4,20},{... | collective-permute-start | bytes 1179656 | tf_op jit(solution)/shard_map/ppermute | solution.py:502
  77.6 2.4 %collective-permute-done.18.refs_1_ = bf16[192,1024]{1,0:T(8,128)(2,1)S(1)} collective-permute-done((bf16[192,1024]{1,0:T(8,128)(2,1)S(1)}, bf16[192,1024]{1,0:T(8,128)(2,1)S(1)}, u32[]{:S(2)}, u32[]{:S(2)}) %collective-permute-start.18) | collective-permute-done | bytes 393248 | tf_op jit(solution)/shard_map/ppermute | solution.py:497
  80.0 0.1 last_step.1
  80.1 1.6 %collective-permute-start.21 = (bf16[192,1024]{1,0:T(8,128)(2,1)S(1)}, bf16[192,1024]{1,0:T(8,128)(2,1)S(1)}, u32[]{:S(2)}, u32[]{:S(2)}) collective-permute-start(bf16[192,1024]{1,0:T(8,128)(2,1)S(1)} %last_step.1), channel_id=1, source_target_pairs={{0,8},{8,24},{16,0},{24,16},{1,9},{9,25},{17,1},{25,17},{2,10},{10... | collective-permute-start | bytes 1179656 | tf_op jit(solution)/shard_map/ppermute | solution.py:510
  81.8 0.6 out_columns.5.refs_0_
  82.3 5.2 %collective-permute-done.20.refs_3_ = bf16[192,1024]{1,0:T(8,128)(2,1)S(1)} collective-permute-done((bf16[192,1024]{1,0:T(8,128)(2,1)S(1)}, bf16[192,1024]{1,0:T(8,128)(2,1)S(1)}, u32[]{:S(2)}, u32[]{:S(2)}) %collective-permute-start.20) | collective-permute-done | bytes 393248 | tf_op jit(solution)/shard_map/ppermute | solution.py:502
  87.6 0.2 early.1
  87.8 13.7 %collective-permute-done.21 = bf16[192,1024]{1,0:T(8,128)(2,1)S(1)} collective-permute-done((bf16[192,1024]{1,0:T(8,128)(2,1)S(1)}, bf16[192,1024]{1,0:T(8,128)(2,1)S(1)}, u32[]{:S(2)}, u32[]{:S(2)}) %collective-permute-start.21) | collective-permute-done | bytes 393248 | tf_op jit(solution)/shard_map/ppermute | solution.py:510
  101.5 0.8 add_convert_fusion
  (14 shorter events, 0.0 us)
Async XLA Ops:
  0.0 17.8 %collective-permute-start.4 = (bf16[3,512,1024]{2,1,0:T(8,128)(2,1)}, bf16[3,512,1024]{2,1,0:T(8,128)(2,1)S(1)}, u32[]{:S(2)}, u32[]{:S(2)}) collective-permute-start(bf16[3,512,1024]{2,1,0:T(8,128)(2,1)} %bitcast.3), channel_id=1, source_target_pairs={{0,1},{1,0},{2,3},{3,2},{4,5},{5,4},{6,7},{7,6},{8,9},{9,8},{10,11... | collective-permute-start | bytes 9437192 | tf_op jit(solution)/shard_map/ppermute | solution.py:544
  0.5 1.4 %copy-start.1 = (bf16[192,4096]{1,0:T(8,128)(2,1)S(1)}, bf16[192,4096]{1,0:T(8,128)(2,1)}, u32[]{:S(2)}) copy-start(bf16[192,4096]{1,0:T(8,128)(2,1)} %refs_0_.1) | copy-start | bytes 4718596
  2.0 9.3 %collective-permute-start.2 = (bf16[96,1024]{1,0:T(8,128)(2,1)S(1)}, bf16[96,1024]{1,0:T(8,128)(2,1)S(1)}, u32[]{:S(2)}, u32[]{:S(2)}) collective-permute-start(bf16[96,1024]{1,0:T(8,128)(2,1)S(1)} %get-tuple-element.68), channel_id=1, source_target_pairs={{0,6},{1,7},{2,4},{3,5},{4,2},{5,3},{6,0},{7,1},{8,14},{9,15},{10,... | collective-permute-start | bytes 589832 | tf_op jit(solution)/shard_map/ppermute | solution.py:548
  5.5 14.0 %collective-permute-start = (bf16[192,1024]{1,0:T(8,128)(2,1)S(1)}, bf16[192,1024]{1,0:T(8,128)(2,1)S(1)}, u32[]{:S(2)}, u32[]{:S(2)}) collective-permute-start(bf16[192,1024]{1,0:T(8,128)(2,1)S(1)} %get-tuple-element.66), channel_id=1, source_target_pairs={{0,4},{1,3},{2,6},{3,1},{4,0},{5,7},{6,2},{7,5},{8,12},{9,11},{10,... | collective-permute-start | bytes 1179656 | tf_op jit(solution)/shard_map/ppermute | solution.py:550
  6.0 13.8 %collective-permute-start.1 = (bf16[192,1024]{1,0:T(8,128)(2,1)S(1)}, bf16[192,1024]{1,0:T(8,128)(2,1)S(1)}, u32[]{:S(2)}, u32[]{:S(2)}) collective-permute-start(bf16[192,1024]{1,0:T(8,128)(2,1)S(1)} %get-tuple-element.67), channel_id=1, source_target_pairs={{0,2},{1,5},{2,0},{3,7},{4,6},{5,1},{6,4},{7,3},{8,10},{9,13},{10,... | collective-permute-start | bytes 1179656 | tf_op jit(solution)/shard_map/ppermute | solution.py:550
  11.3 6.6 %collective-permute-start.3 = (bf16[96,1024]{1,0:T(8,128)(2,1)S(1)}, bf16[96,1024]{1,0:T(8,128)(2,1)S(1)}, u32[]{:S(2)}, u32[]{:S(2)}) collective-permute-start(bf16[96,1024]{1,0:T(8,128)(2,1)S(1)} %collective-permute-done.2.refs_1_), channel_id=1, source_target_pairs={{0,8},{8,0},{16,24},{24,16},{1,9},{9,1},{17,25},{25,17},{2,10},{10... | collective-permute-start | bytes 589832 | tf_op jit(solution)/shard_map/ppermute | solution.py:549
  13.2 1.9 %copy-start = (bf16[512,3,1024]{2,0,1:T(8,128)(2,1)S(1)}, bf16[512,3,1024]{2,0,1:T(8,128)(2,1)}, u32[]{:S(2)}) copy-start(bf16[512,3,1024]{2,0,1:T(8,128)(2,1)} %param.7) | copy-start | bytes 9437188
  20.4 12.1 %collective-permute-start.5 = (bf16[1,2,768,256]{3,2,1,0:T(8,128)(2,1)S(1)}, bf16[1,2,768,256]{3,2,1,0:T(8,128)(2,1)S(1)}, u32[]{:S(2)}, u32[]{:S(2)}) collective-permute-start(bf16[1,2,768,256]{3,2,1,0:T(8,128)(2,1)S(1)} %rest_share.1), channel_id=1, source_target_pairs={{0,2},{1,5},{2,0},{3,7},{4,6},{5,1},{6,4},{7,3},{8,10},{9,13},{10,... | collective-permute-start | bytes 2359304 | tf_op jit(solution)/shard_map/ppermute | solution.py:555
  23.2 22.8 %collective-permute-start.7 = (bf16[1,2,768,256]{3,2,1,0:T(8,128)(2,1)S(1)}, bf16[1,2,768,256]{3,2,1,0:T(8,128)(2,1)S(1)}, u32[]{:S(2)}, u32[]{:S(2)}) collective-permute-start(bf16[1,2,768,256]{3,2,1,0:T(8,128)(2,1)S(1)} %project_mix.2), channel_id=1, source_target_pairs={{0,2},{1,5},{2,0},{3,7},{4,6},{5,1},{6,4},{7,3},{8,10},{9,13},{10,... | collective-permute-start | bytes 2359304 | tf_op jit(solution)/shard_map/ppermute | solution.py:558
  23.8 22.2 %slice-start = ((s8[8388608]{0:T(1024)(128)(4,1)}), s8[4194304]{0:T(1024)(128)(4,1)S(1)}, s32[]{:S(2)}) async-start(s8[8388608]{0:T(1024)(128)(4,1)} %bitcast.1), calls=%async_computation | async-start | bytes 8388608
  25.8 8.8 %copy-start.2 = (f32[3,3,1024]{2,1,0:T(4,128)S(1)}, f32[3,3,1024]{2,1,0:T(4,128)}, u32[]{:S(2)}) copy-start(f32[3,3,1024]{2,1,0:T(4,128)} %refs_4_.1) | copy-start | bytes 110596
  32.5 13.5 %slice-start.1 = ((s8[8388608]{0:T(1024)(128)(4,1)}), s8[4194304]{0:T(1024)(128)(4,1)S(1)}, s32[]{:S(2)}) async-start(s8[8388608]{0:T(1024)(128)(4,1)} %bitcast.1), calls=%async_computation.1 | async-start | bytes 8388608
  32.6 2.0 %collective-permute-start.6 = (bf16[4,16,1024]{2,1,0:T(8,128)(2,1)S(1)}, bf16[4,16,1024]{2,1,0:T(8,128)(2,1)S(1)}, u32[]{:S(2)}, u32[]{:S(2)}) collective-permute-start(bf16[4,16,1024]{2,1,0:T(8,128)(2,1)S(1)} %get-tuple-element.87), channel_id=1, source_target_pairs={{0,1},{1,0},{2,3},{3,2},{4,5},{5,4},{6,7},{7,6},{8,9},{9,8},{10,11... | collective-permute-start | bytes 393224 | tf_op jit(solution)/shard_map/ppermute | solution.py:566
  32.7 16.6 %collective-permute-start.10 = (bf16[768,256]{1,0:T(8,128)(2,1)S(1)}, bf16[768,256]{1,0:T(8,128)(2,1)S(1)}, u32[]{:S(2)}, u32[]{:S(2)}) collective-permute-start(bf16[768,256]{1,0:T(8,128)(2,1)S(1)} %get-tuple-element.82), channel_id=1, source_target_pairs={{0,4},{1,3},{2,6},{3,1},{4,0},{5,7},{6,2},{7,5},{8,12},{9,11},{10,... | collective-permute-start | bytes 1179656 | tf_op jit(solution)/shard_map/ppermute | solution.py:562
  34.2 15.1 %collective-permute-start.11 = (bf16[768,256]{1,0:T(8,128)(2,1)S(1)}, bf16[768,256]{1,0:T(8,128)(2,1)S(1)}, u32[]{:S(2)}, u32[]{:S(2)}) collective-permute-start(bf16[768,256]{1,0:T(8,128)(2,1)S(1)} %get-tuple-element.101), channel_id=1, source_target_pairs={{0,5},{1,2},{2,7},{3,0},{4,1},{5,6},{6,3},{7,4},{8,13},{9,10},{10,... | collective-permute-start | bytes 1179656 | tf_op jit(solution)/shard_map/ppermute | solution.py:563
  46.6 2.8 %copy-start.3 = (f32[8,1024]{1,0:T(8,128)S(1)}, f32[8,1024]{1,0:T(8,128)}, u32[]{:S(2)}) copy-start(f32[8,1024]{1,0:T(8,128)} %refs_5_.1) | copy-start | bytes 98308
  46.6 2.8 %copy-start.4 = (f32[8,1024]{1,0:T(8,128)S(1)}, f32[8,1024]{1,0:T(8,128)}, u32[]{:S(2)}) copy-start(f32[8,1024]{1,0:T(8,128)} %refs_6_.1) | copy-start | bytes 98308
  46.7 2.6 %collective-permute-start.9 = (bf16[768,256]{1,0:T(8,128)(2,1)S(1)}, bf16[768,256]{1,0:T(8,128)(2,1)S(1)}, u32[]{:S(2)}, u32[]{:S(2)}) collective-permute-start(bf16[768,256]{1,0:T(8,128)(2,1)S(1)} %get-tuple-element.100), channel_id=1, source_target_pairs={{0,1},{1,0},{2,3},{3,2},{4,5},{5,4},{6,7},{7,6},{8,9},{9,8},{10,11... | collective-permute-start | bytes 1179656 | tf_op jit(solution)/shard_map/ppermute | solution.py:574
  46.8 7.8 %collective-permute-start.8 = (bf16[192,1024]{1,0:T(8,128)(2,1)S(1)}, bf16[192,1024]{1,0:T(8,128)(2,1)S(1)}, u32[]{:S(2)}, u32[]{:S(2)}) collective-permute-start(bf16[192,1024]{1,0:T(8,128)(2,1)S(1)} %get-tuple-element.94), channel_id=1, source_target_pairs={{0,2},{1,5},{2,0},{3,7},{4,6},{5,1},{6,4},{7,3},{8,10},{9,13},{10,... | collective-permute-start | bytes 1179656 | tf_op jit(solution)/shard_map/ppermute | solution.py:576
  51.8 2.9 %collective-permute-start.12 = (bf16[4,192,128]{2,1,0:T(8,128)(2,1)S(1)}, bf16[4,192,128]{2,1,0:T(8,128)(2,1)S(1)}, u32[]{:S(2)}, u32[]{:S(2)}) collective-permute-start(bf16[4,192,128]{2,1,0:T(8,128)(2,1)S(1)} %get-tuple-element.103), channel_id=1, source_target_pairs={{0,1},{1,0},{2,3},{3,2},{4,5},{5,4},{6,7},{7,6},{8,9},{9,8},{10,11... | collective-permute-start | bytes 589832 | tf_op jit(solution)/shard_map/ppermute | solution.py:580
  51.8 10.5 %collective-permute-start.14 = (bf16[192,1024]{1,0:T(8,128)(2,1)S(1)}, bf16[192,1024]{1,0:T(8,128)(2,1)S(1)}, u32[]{:S(2)}, u32[]{:S(2)}) collective-permute-start(bf16[192,1024]{1,0:T(8,128)(2,1)S(1)} %get-tuple-element.105), channel_id=1, source_target_pairs={{0,2},{1,5},{2,0},{3,7},{4,6},{5,1},{6,4},{7,3},{8,10},{9,13},{10,... | collective-permute-start | bytes 1179656 | tf_op jit(solution)/shard_map/ppermute | solution.py:577
  54.7 12.7 %collective-permute-start.13 = (bf16[192,1024]{1,0:T(8,128)(2,1)S(1)}, bf16[192,1024]{1,0:T(8,128)(2,1)S(1)}, u32[]{:S(2)}, u32[]{:S(2)}) collective-permute-start(bf16[192,1024]{1,0:T(8,128)(2,1)S(1)} %get-tuple-element.104), channel_id=1, source_target_pairs={{0,4},{1,3},{2,6},{3,1},{4,0},{5,7},{6,2},{7,5},{8,12},{9,11},{10,... | collective-permute-start | bytes 1179656 | tf_op jit(solution)/shard_map/ppermute | solution.py:582
  56.2 9.4 %collective-permute-start.15 = (bf16[2,192,128]{2,1,0:T(8,128)(2,1)S(1)}, bf16[2,192,128]{2,1,0:T(8,128)(2,1)S(1)}, u32[]{:S(2)}, u32[]{:S(2)}) collective-permute-start(bf16[2,192,128]{2,1,0:T(8,128)(2,1)S(1)} %get-tuple-element.107), channel_id=1, source_target_pairs={{0,4},{1,3},{2,6},{3,1},{4,0},{5,7},{6,2},{7,5},{8,12},{9,11},{10,... | collective-permute-start | bytes 294920 | tf_op jit(solution)/shard_map/ppermute | solution.py:583
  56.8 8.8 %collective-permute-start.16 = (bf16[2,192,128]{2,1,0:T(8,128)(2,1)S(1)}, bf16[2,192,128]{2,1,0:T(8,128)(2,1)S(1)}, u32[]{:S(2)}, u32[]{:S(2)}) collective-permute-start(bf16[2,192,128]{2,1,0:T(8,128)(2,1)S(1)} %get-tuple-element.108), channel_id=1, source_target_pairs={{0,2},{1,5},{2,0},{3,7},{4,6},{5,1},{6,4},{7,3},{8,10},{9,13},{10,... | collective-permute-start | bytes 294920 | tf_op jit(solution)/shard_map/ppermute | solution.py:583
  58.3 9.1 %collective-permute-start.17 = (bf16[2,192,128]{2,1,0:T(8,128)(2,1)S(1)}, bf16[2,192,128]{2,1,0:T(8,128)(2,1)S(1)}, u32[]{:S(2)}, u32[]{:S(2)}) collective-permute-start(bf16[2,192,128]{2,1,0:T(8,128)(2,1)S(1)} %get-tuple-element.109), channel_id=1, source_target_pairs={{0,6},{1,7},{2,4},{3,5},{4,2},{5,3},{6,0},{7,1},{8,14},{9,15},{10,... | collective-permute-start | bytes 294920 | tf_op jit(solution)/shard_map/ppermute | solution.py:583
  68.3 11.7 %collective-permute-start.18 = (bf16[192,1024]{1,0:T(8,128)(2,1)S(1)}, bf16[192,1024]{1,0:T(8,128)(2,1)S(1)}, u32[]{:S(2)}, u32[]{:S(2)}) collective-permute-start(bf16[192,1024]{1,0:T(8,128)(2,1)S(1)} %get-tuple-element.113), channel_id=1, source_target_pairs={{0,8},{8,0},{16,24},{24,16},{1,9},{9,1},{17,25},{25,17},{2,10},{10... | collective-permute-start | bytes 1179656 | tf_op jit(solution)/shard_map/ppermute | solution.py:497
  70.5 17.0 %collective-permute-start.19 = (bf16[192,1024]{1,0:T(8,128)(2,1)S(1)}, bf16[192,1024]{1,0:T(8,128)(2,1)S(1)}, u32[]{:S(2)}, u32[]{:S(2)}) collective-permute-start(bf16[192,1024]{1,0:T(8,128)(2,1)S(1)} %out_columns.3.refs_2_), channel_id=1, source_target_pairs={{8,16},{16,8},{9,17},{17,9},{10,18},{18,10},{11,19},{19,11},{12,20... | collective-permute-start | bytes 1179656 | tf_op jit(solution)/shard_map/ppermute | solution.py:499
  71.8 15.7 %collective-permute-start.20 = (bf16[192,1024]{1,0:T(8,128)(2,1)S(1)}, bf16[192,1024]{1,0:T(8,128)(2,1)S(1)}, u32[]{:S(2)}, u32[]{:S(2)}) collective-permute-start(bf16[192,1024]{1,0:T(8,128)(2,1)S(1)} %out_columns.4.refs_0_), channel_id=1, source_target_pairs={{0,16},{24,8},{1,17},{25,9},{2,18},{26,10},{3,19},{27,11},{4,20},{... | collective-permute-start | bytes 1179656 | tf_op jit(solution)/shard_map/ppermute | solution.py:502
  80.1 21.4 %collective-permute-start.21 = (bf16[192,1024]{1,0:T(8,128)(2,1)S(1)}, bf16[192,1024]{1,0:T(8,128)(2,1)S(1)}, u32[]{:S(2)}, u32[]{:S(2)}) collective-permute-start(bf16[192,1024]{1,0:T(8,128)(2,1)S(1)} %last_step.1), channel_id=1, source_target_pairs={{0,8},{8,24},{16,0},{24,16},{1,9},{9,25},{17,1},{25,17},{2,10},{10... | collective-permute-start | bytes 1179656 | tf_op jit(solution)/shard_map/ppermute | solution.py:510

commit v11 on v9

--- a/solution.py
+++ b/solution.py
@@ -569,9 +569,9 @@
     w_out = stage(w_out)
     q_own, w_out, rest = lax.optimization_barrier((q_own, w_out, rest))
 
+    q_both, q_first, first_in = lax.optimization_barrier((q_both, q_first, first_in))
     own, other_half = first_share(order, rest, first_in, chips)
     other_half = lax.ppermute(other_half, "ctx", swap)
-    q_both, q_first, own = lax.optimization_barrier((q_both, q_first, own))
     q_both = lax.ppermute(q_both, "ctx", route(2))
     q_first = lax.ppermute(q_first, "ctx", route(2))
     parts = [own, other_half, second_in, swap_second]

time: 103 us -> 103 us (level)
    ppermute x1, waiting for transfers between devices: 3.9 us -> 2.59 us  [on_device_chips(): q_first = lax.ppermute(q_first, 'ctx', route(2))]
where the time goes in v11:
time: 103 us; the launch traced here: 102 us
  waiting for transfers between devices  55.7 us (54%)
  starting transfers between devices  28.7 us (28%)
  Pallas kernels  13.5 us (13%)
  local copies, waits for them, and re-layouts  3.32 us (3%)
    ppermute x1, waiting for transfers between devices, output_over_line(): last_in = lax.ppermute(last, 'dp', [(0, 1), (1, 3), (2, 0), (3, 2)])  13.7 us
    pallas_call x16, Pallas kernels, local(): pl.pallas_call(placed, out_shape=out if len(out) > 1 else out[0], in_spec...  12.8 us
    ppermute x1, waiting for transfers between devices, on_device_chips(): first_in = lax.ppermute(first, 'ctx', route(2))  8.93 us
    ppermute x1, waiting for transfers between devices, on_device_chips(): both_in = lax.ppermute(both, 'ctx', route(2))  6.66 us
    ppermute x1, starting transfers between devices, output_over_line(): end_in = lax.ppermute(far, 'dp', [(0, 2), (3, 1)])  5.76 us
    ppermute x1, waiting for transfers between devices, output_over_line(): end_in = lax.ppermute(far, 'dp', [(0, 2), (3, 1)])  5.21 us
    ppermute x1, waiting for transfers between devices, on_device_chips(): half = lax.ppermute(xs[3], 'ctx', route(3))  5.15 us
    ppermute x3, waiting for transfers between devices, on_device_chips(): lax.ppermute(long_parts[s], 'ctx', route(s))  5.09 us
  transfers between devices with their start and end apart: 22, of which 14 were waited for; matrix products, arithmetic and copies ran while one was open for 0% of the time, Pallas kernels for 12%

profile of v11, /device:TPU:0, one launch (start us, length us, event | category | flops | bytes accessed | tf_op | source)
XLA Modules:
  0.0 102.3 jit_solution(1986535718436348665)
XLA Ops:
  0.0 0.5 collective-permute-start.4
  0.5 1.4 %copy-done.1 = bf16[192,4096]{1,0:T(8,128)(2,1)S(1)} copy-done((bf16[192,4096]{1,0:T(8,128)(2,1)S(1)}, bf16[192,4096]{1,0:T(8,128)(2,1)}, u32[]{:S(2)}) %copy-start.1) | copy-done | bytes 1572888
  1.9 0.1 cut.1
  2.0 3.5 %collective-permute-start.2 = (bf16[96,1024]{1,0:T(8,128)(2,1)S(1)}, bf16[96,1024]{1,0:T(8,128)(2,1)S(1)}, u32[]{:S(2)}, u32[]{:S(2)}) collective-permute-start(bf16[96,1024]{1,0:T(8,128)(2,1)S(1)} %get-tuple-element.67), channel_id=1, source_target_pairs={{0,6},{1,7},{2,4},{3,5},{4,2},{5,3},{6,0},{7,1},{8,14},{9,15},{10,... | collective-permute-start | bytes 589832 | tf_op jit(solution)/shard_map/ppermute | solution.py:548
  5.5 0.5 collective-permute-start
  6.0 0.1 collective-permute-start.1
  6.1 5.2 %collective-permute-done.2.refs_1_ = bf16[96,1024]{1,0:T(8,128)(2,1)S(1)} collective-permute-done((bf16[96,1024]{1,0:T(8,128)(2,1)S(1)}, bf16[96,1024]{1,0:T(8,128)(2,1)S(1)}, u32[]{:S(2)}, u32[]{:S(2)}) %collective-permute-start.2) | collective-permute-done | bytes 196640 | tf_op jit(solution)/shard_map/ppermute | solution.py:548
  11.3 2.0 %collective-permute-start.3 = (bf16[96,1024]{1,0:T(8,128)(2,1)S(1)}, bf16[96,1024]{1,0:T(8,128)(2,1)S(1)}, u32[]{:S(2)}, u32[]{:S(2)}) collective-permute-start(bf16[96,1024]{1,0:T(8,128)(2,1)S(1)} %collective-permute-done.2.refs_1_), channel_id=1, source_target_pairs={{0,8},{8,0},{16,24},{24,16},{1,9},{9,1},{17,25},{25,17},{2,10},{10... | collective-permute-start | bytes 589832 | tf_op jit(solution)/shard_map/ppermute | solution.py:549
  13.2 1.9 %copy-done = bf16[512,3,1024]{2,0,1:T(8,128)(2,1)S(1)} copy-done((bf16[512,3,1024]{2,0,1:T(8,128)(2,1)S(1)}, bf16[512,3,1024]{2,0,1:T(8,128)(2,1)}, u32[]{:S(2)}) %copy-start) | copy-done | bytes 3145752
  15.1 0.2 stage.2.refs_3_.refs_4_.refs_5_
  15.4 2.5 %collective-permute-done.3.refs_2_ = bf16[96,1024]{1,0:T(8,128)(2,1)S(1)} collective-permute-done((bf16[96,1024]{1,0:T(8,128)(2,1)S(1)}, bf16[96,1024]{1,0:T(8,128)(2,1)S(1)}, u32[]{:S(2)}, u32[]{:S(2)}) %collective-permute-start.3) | collective-permute-done | bytes 196640 | tf_op jit(solution)/shard_map/ppermute | solution.py:549
  17.8 0.0 collective-permute-done.4.refs_4_.refs_5_.refs_6_
  17.8 0.7 early_share.1
  18.5 0.9 collective-permute-done.refs_0_.refs_1_
  19.5 0.3 collective-permute-done.1.refs_1_.refs_2_
  19.8 0.7 rest_share.1
  20.4 1.6 %collective-permute-start.5 = (bf16[1,2,768,256]{3,2,1,0:T(8,128)(2,1)S(1)}, bf16[1,2,768,256]{3,2,1,0:T(8,128)(2,1)S(1)}, u32[]{:S(2)}, u32[]{:S(2)}) collective-permute-start(bf16[1,2,768,256]{3,2,1,0:T(8,128)(2,1)S(1)} %rest_share.1), channel_id=1, source_target_pairs={{0,2},{1,5},{2,0},{3,7},{4,6},{5,1},{6,4},{7,3},{8,10},{9,13},{10,... | collective-permute-start | bytes 2359304 | tf_op jit(solution)/shard_map/ppermute | solution.py:555
  22.0 1.2 %project_mix.2 = bf16[1,2,768,256]{3,2,1,0:T(8,128)(2,1)S(1)} custom-call(bf16[192,1024]{1,0:T(8,128)(2,1)S(1)} %get-tuple-element.82.refs_0_, bf16[192,1024]{1,0:T(8,128)(2,1)S(1)} %collective-permute-done.refs_0_.refs_1_, bf16[192,1024]{1,0:T(8,128)(2,1)S(1)} %collective-permute-done.1.refs_1_.refs_2_, bf16[192,1024]{1,0:T(8,128)(2,1)S(1)} %get-tuple-element.85.refs_3_, ...), custom_call_target="tpu_custom_call" | custom-call | tf_op jit(solution)/shard_map/project_mix/pallas_call | solution.py:105
  23.2 0.6 collective-permute-start.7
  23.8 2.1 %project_mix.3 = (f32[2,2,768,256]{3,2,1,0:T(8,128)S(1)}, bf16[4,16,1024]{2,1,0:T(8,128)(2,1)S(1)}) custom-call(bf16[192,1024]{1,0:T(8,128)(2,1)S(1)} %get-tuple-element.82.refs_0_, bf16[192,1024]{1,0:T(8,128)(2,1)S(1)} %collective-permute-done.refs_0_.refs_1_, bf16[192,1024]{1,0:T(8,128)(2,1)S(1)} %collective-permute-done.1.refs_1_.refs_2_, ...), custom_call_target="tpu_custom_call" | custom-call | tf_op jit(solution)/shard_map/project_mix/pallas_call | solution.py:105
  25.8 0.0 copy-start.2
  25.8 6.7 %collective-permute-done.5.refs_1_ = bf16[1,2,768,256]{3,2,1,0:T(8,128)(2,1)S(1)} collective-permute-done((bf16[1,2,768,256]{3,2,1,0:T(8,128)(2,1)S(1)}, bf16[1,2,768,256]{3,2,1,0:T(8,128)(2,1)S(1)}, u32[]{:S(2)}, u32[]{:S(2)}) %collective-permute-start.5) | collective-permute-done | bytes 786464 | tf_op jit(solution)/shard_map/ppermute | solution.py:555
  32.5 0.1 second_share.1
  32.6 0.1 collective-permute-start.6
  32.7 1.5 %collective-permute-start.10 = (bf16[768,256]{1,0:T(8,128)(2,1)S(1)}, bf16[768,256]{1,0:T(8,128)(2,1)S(1)}, u32[]{:S(2)}, u32[]{:S(2)}) collective-permute-start(bf16[768,256]{1,0:T(8,128)(2,1)S(1)} %get-tuple-element.81), channel_id=1, source_target_pairs={{0,4},{1,3},{2,6},{3,1},{4,0},{5,7},{6,2},{7,5},{8,12},{9,11},{10,... | collective-permute-start | bytes 1179656 | tf_op jit(solution)/shard_map/ppermute | solution.py:562
  34.2 0.4 collective-permute-start.11
  34.7 2.4 %project_query.1 = (f32[192,1024]{1,0:T(8,128)S(1)}, f32[192,1024]{1,0:T(8,128)S(1)}, bf16[192,1024]{1,0:T(8,128)(2,1)S(1)}, bf16[192,1024]{1,0:T(8,128)(2,1)S(1)}) custom-call(bf16[192,1024]{1,0:T(8,128)(2,1)S(1)} %get-tuple-element.82.refs_0_, bf16[192,1024]{1,0:T(8,128)(2,1)S(1)} %collective-permute-done.refs_0_.refs_1_, ...), custom_call_target="tpu_custom_call" | custom-call | tf_op jit(solution)/shard_map/project_query/pallas_call | solution.py:105
  37.1 8.9 %collective-permute-done.7.refs_1_ = bf16[1,2,768,256]{3,2,1,0:T(8,128)(2,1)S(1)} collective-permute-done((bf16[1,2,768,256]{3,2,1,0:T(8,128)(2,1)S(1)}, bf16[1,2,768,256]{3,2,1,0:T(8,128)(2,1)S(1)}, u32[]{:S(2)}, u32[]{:S(2)}) %collective-permute-start.7) | collective-permute-done | bytes 786464 | tf_op jit(solution)/shard_map/ppermute | solution.py:558
  46.0 0.6 stage.3.refs_7_.refs_1_
  46.6 0.0 copy-start.3
  46.6 0.0 copy-start.4
  46.6 0.1 first_share.1
  46.7 0.1 collective-permute-start.9
  46.8 1.6 %collective-permute-start.8 = (bf16[192,1024]{1,0:T(8,128)(2,1)S(1)}, bf16[192,1024]{1,0:T(8,128)(2,1)S(1)}, u32[]{:S(2)}, u32[]{:S(2)}) collective-permute-start(bf16[192,1024]{1,0:T(8,128)(2,1)S(1)} %get-tuple-element.94), channel_id=1, source_target_pairs={{0,2},{1,5},{2,0},{3,7},{4,6},{5,1},{6,4},{7,3},{8,10},{9,13},{10,... | collective-permute-start | bytes 1179656 | tf_op jit(solution)/shard_map/ppermute | solution.py:575
  48.4 1.0 collective-permute-done.11.refs_3_
  49.4 0.0 collective-permute-done.10.refs_2_
  49.4 0.0 collective-permute-done.9.refs_1_
  49.4 2.4 %hyena.1 = (bf16[4,192,128]{2,1,0:T(8,128)(2,1)S(1)}, bf16[4,192,128]{2,1,0:T(8,128)(2,1)S(1)}) custom-call(f32[768,256]{1,0:T(8,128)S(1)} %get-tuple-element.97.refs_0_, bf16[768,256]{1,0:T(8,128)(2,1)S(1)} %collective-permute-done.9.refs_1_, bf16[768,256]{1,0:T(8,128)(2,1)S(1)} %collective-permute-done.10.refs_2_, ...), custom_call_target="tpu_custom_call" | custom-call | tf_op jit(solution)/shard_map/hyena/pallas_call | solution.py:105
  51.8 0.1 collective-permute-start.12
  51.8 1.6 %collective-permute-start.14 = (bf16[192,1024]{1,0:T(8,128)(2,1)S(1)}, bf16[192,1024]{1,0:T(8,128)(2,1)S(1)}, u32[]{:S(2)}, u32[]{:S(2)}) collective-permute-start(bf16[192,1024]{1,0:T(8,128)(2,1)S(1)} %get-tuple-element.103), channel_id=1, source_target_pairs={{0,2},{1,5},{2,0},{3,7},{4,6},{5,1},{6,4},{7,3},{8,10},{9,13},{10,... | collective-permute-start | bytes 1179656 | tf_op jit(solution)/shard_map/ppermute | solution.py:576
  53.4 1.2 %collective-permute-done.8.refs_1_ = bf16[192,1024]{1,0:T(8,128)(2,1)S(1)} collective-permute-done((bf16[192,1024]{1,0:T(8,128)(2,1)S(1)}, bf16[192,1024]{1,0:T(8,128)(2,1)S(1)}, u32[]{:S(2)}, u32[]{:S(2)}) %collective-permute-start.8) | collective-permute-done | bytes 393248 | tf_op jit(solution)/shard_map/ppermute | solution.py:575
  54.6 0.0 collective-permute-done.12.refs_3_
  54.7 0.1 payloads.1
  54.7 1.5 %collective-permute-start.13 = (bf16[192,1024]{1,0:T(8,128)(2,1)S(1)}, bf16[192,1024]{1,0:T(8,128)(2,1)S(1)}, u32[]{:S(2)}, u32[]{:S(2)}) collective-permute-start(bf16[192,1024]{1,0:T(8,128)(2,1)S(1)} %get-tuple-element.102), channel_id=1, source_target_pairs={{0,4},{1,3},{2,6},{3,1},{4,0},{5,7},{6,2},{7,5},{8,12},{9,11},{10,... | collective-permute-start | bytes 1179656 | tf_op jit(solution)/shard_map/ppermute | solution.py:581
  56.2 0.6 collective-permute-start.15
  56.8 1.5 %collective-permute-start.16 = (bf16[2,192,128]{2,1,0:T(8,128)(2,1)S(1)}, bf16[2,192,128]{2,1,0:T(8,128)(2,1)S(1)}, u32[]{:S(2)}, u32[]{:S(2)}) collective-permute-start(bf16[2,192,128]{2,1,0:T(8,128)(2,1)S(1)} %get-tuple-element.106), channel_id=1, source_target_pairs={{0,2},{1,5},{2,0},{3,7},{4,6},{5,1},{6,4},{7,3},{8,10},{9,13},{10,... | collective-permute-start | bytes 294920 | tf_op jit(solution)/shard_map/ppermute | solution.py:582
  58.3 1.4 %collective-permute-start.17 = (bf16[2,192,128]{2,1,0:T(8,128)(2,1)S(1)}, bf16[2,192,128]{2,1,0:T(8,128)(2,1)S(1)}, u32[]{:S(2)}, u32[]{:S(2)}) collective-permute-start(bf16[2,192,128]{2,1,0:T(8,128)(2,1)S(1)} %get-tuple-element.107), channel_id=1, source_target_pairs={{0,6},{1,7},{2,4},{3,5},{4,2},{5,3},{6,0},{7,1},{8,14},{9,15},{10,... | collective-permute-start | bytes 294920 | tf_op jit(solution)/shard_map/ppermute | solution.py:582
  59.7 2.6 %collective-permute-done.14.refs_2_ = bf16[192,1024]{1,0:T(8,128)(2,1)S(1)} collective-permute-done((bf16[192,1024]{1,0:T(8,128)(2,1)S(1)}, bf16[192,1024]{1,0:T(8,128)(2,1)S(1)}, u32[]{:S(2)}, u32[]{:S(2)}) %collective-permute-start.14) | collective-permute-done | bytes 393248 | tf_op jit(solution)/shard_map/ppermute | solution.py:576
  62.3 3.3 %collective-permute-done.15.refs_4_ = bf16[2,192,128]{2,1,0:T(8,128)(2,1)S(1)} collective-permute-done((bf16[2,192,128]{2,1,0:T(8,128)(2,1)S(1)}, bf16[2,192,128]{2,1,0:T(8,128)(2,1)S(1)}, u32[]{:S(2)}, u32[]{:S(2)}) %collective-permute-start.15) | collective-permute-done | bytes 98336 | tf_op jit(solution)/shard_map/ppermute | solution.py:582
  65.6 1.8 %collective-permute-done.17.refs_6_ = bf16[2,192,128]{2,1,0:T(8,128)(2,1)S(1)} collective-permute-done((bf16[2,192,128]{2,1,0:T(8,128)(2,1)S(1)}, bf16[2,192,128]{2,1,0:T(8,128)(2,1)S(1)}, u32[]{:S(2)}, u32[]{:S(2)}) %collective-permute-start.17) | collective-permute-done | bytes 98336 | tf_op jit(solution)/shard_map/ppermute | solution.py:582
  67.4 0.9 gate.1
  68.3 1.6 %collective-permute-start.18 = (bf16[192,1024]{1,0:T(8,128)(2,1)S(1)}, bf16[192,1024]{1,0:T(8,128)(2,1)S(1)}, u32[]{:S(2)}, u32[]{:S(2)}) collective-permute-start(bf16[192,1024]{1,0:T(8,128)(2,1)S(1)} %get-tuple-element.111), channel_id=1, source_target_pairs={{0,8},{8,0},{16,24},{24,16},{1,9},{9,1},{17,25},{25,17},{2,10},{10... | collective-permute-start | bytes 1179656 | tf_op jit(solution)/shard_map/ppermute | solution.py:497
  69.9 0.6 out_columns.3.refs_2_
  70.5 0.7 collective-permute-start.19
  71.2 0.6 out_columns.4.refs_0_
  71.8 5.8 %collective-permute-start.20 = (bf16[192,1024]{1,0:T(8,128)(2,1)S(1)}, bf16[192,1024]{1,0:T(8,128)(2,1)S(1)}, u32[]{:S(2)}, u32[]{:S(2)}) collective-permute-start(bf16[192,1024]{1,0:T(8,128)(2,1)S(1)} %out_columns.4.refs_0_), channel_id=1, source_target_pairs={{0,16},{24,8},{1,17},{25,9},{2,18},{26,10},{3,19},{27,11},{4,20},{... | collective-permute-start | bytes 1179656 | tf_op jit(solution)/shard_map/ppermute | solution.py:502
  77.6 2.4 %collective-permute-done.18.refs_1_ = bf16[192,1024]{1,0:T(8,128)(2,1)S(1)} collective-permute-done((bf16[192,1024]{1,0:T(8,128)(2,1)S(1)}, bf16[192,1024]{1,0:T(8,128)(2,1)S(1)}, u32[]{:S(2)}, u32[]{:S(2)}) %collective-permute-start.18) | collective-permute-done | bytes 393248 | tf_op jit(solution)/shard_map/ppermute | solution.py:497
  80.0 0.1 last_step.1
  80.1 1.6 %collective-permute-start.21 = (bf16[192,1024]{1,0:T(8,128)(2,1)S(1)}, bf16[192,1024]{1,0:T(8,128)(2,1)S(1)}, u32[]{:S(2)}, u32[]{:S(2)}) collective-permute-start(bf16[192,1024]{1,0:T(8,128)(2,1)S(1)} %last_step.1), channel_id=1, source_target_pairs={{0,8},{8,24},{16,0},{24,16},{1,9},{9,25},{17,1},{25,17},{2,10},{10... | collective-permute-start | bytes 1179656 | tf_op jit(solution)/shard_map/ppermute | solution.py:510
  81.8 0.6 out_columns.5.refs_0_
  82.3 5.2 %collective-permute-done.20.refs_3_ = bf16[192,1024]{1,0:T(8,128)(2,1)S(1)} collective-permute-done((bf16[192,1024]{1,0:T(8,128)(2,1)S(1)}, bf16[192,1024]{1,0:T(8,128)(2,1)S(1)}, u32[]{:S(2)}, u32[]{:S(2)}) %collective-permute-start.20) | collective-permute-done | bytes 393248 | tf_op jit(solution)/shard_map/ppermute | solution.py:502
  87.6 0.2 early.1
  87.8 13.7 %collective-permute-done.21 = bf16[192,1024]{1,0:T(8,128)(2,1)S(1)} collective-permute-done((bf16[192,1024]{1,0:T(8,128)(2,1)S(1)}, bf16[192,1024]{1,0:T(8,128)(2,1)S(1)}, u32[]{:S(2)}, u32[]{:S(2)}) %collective-permute-start.21) | collective-permute-done | bytes 393248 | tf_op jit(solution)/shard_map/ppermute | solution.py:510
  101.5 0.8 add_convert_fusion
  (14 shorter events, 0.0 us)
Async XLA Ops:
  0.0 17.8 %collective-permute-start.4 = (bf16[3,512,1024]{2,1,0:T(8,128)(2,1)}, bf16[3,512,1024]{2,1,0:T(8,128)(2,1)S(1)}, u32[]{:S(2)}, u32[]{:S(2)}) collective-permute-start(bf16[3,512,1024]{2,1,0:T(8,128)(2,1)} %bitcast.3), channel_id=1, source_target_pairs={{0,1},{1,0},{2,3},{3,2},{4,5},{5,4},{6,7},{7,6},{8,9},{9,8},{10,11... | collective-permute-start | bytes 9437192 | tf_op jit(solution)/shard_map/ppermute | solution.py:544
  0.5 1.4 %copy-start.1 = (bf16[192,4096]{1,0:T(8,128)(2,1)S(1)}, bf16[192,4096]{1,0:T(8,128)(2,1)}, u32[]{:S(2)}) copy-start(bf16[192,4096]{1,0:T(8,128)(2,1)} %refs_0_.1) | copy-start | bytes 4718596
  2.0 9.3 %collective-permute-start.2 = (bf16[96,1024]{1,0:T(8,128)(2,1)S(1)}, bf16[96,1024]{1,0:T(8,128)(2,1)S(1)}, u32[]{:S(2)}, u32[]{:S(2)}) collective-permute-start(bf16[96,1024]{1,0:T(8,128)(2,1)S(1)} %get-tuple-element.67), channel_id=1, source_target_pairs={{0,6},{1,7},{2,4},{3,5},{4,2},{5,3},{6,0},{7,1},{8,14},{9,15},{10,... | collective-permute-start | bytes 589832 | tf_op jit(solution)/shard_map/ppermute | solution.py:548
  5.5 14.0 %collective-permute-start = (bf16[192,1024]{1,0:T(8,128)(2,1)S(1)}, bf16[192,1024]{1,0:T(8,128)(2,1)S(1)}, u32[]{:S(2)}, u32[]{:S(2)}) collective-permute-start(bf16[192,1024]{1,0:T(8,128)(2,1)S(1)} %get-tuple-element.65), channel_id=1, source_target_pairs={{0,4},{1,3},{2,6},{3,1},{4,0},{5,7},{6,2},{7,5},{8,12},{9,11},{10,... | collective-permute-start | bytes 1179656 | tf_op jit(solution)/shard_map/ppermute | solution.py:550
  6.0 13.8 %collective-permute-start.1 = (bf16[192,1024]{1,0:T(8,128)(2,1)S(1)}, bf16[192,1024]{1,0:T(8,128)(2,1)S(1)}, u32[]{:S(2)}, u32[]{:S(2)}) collective-permute-start(bf16[192,1024]{1,0:T(8,128)(2,1)S(1)} %get-tuple-element.66), channel_id=1, source_target_pairs={{0,2},{1,5},{2,0},{3,7},{4,6},{5,1},{6,4},{7,3},{8,10},{9,13},{10,... | collective-permute-start | bytes 1179656 | tf_op jit(solution)/shard_map/ppermute | solution.py:550
  11.3 6.6 %collective-permute-start.3 = (bf16[96,1024]{1,0:T(8,128)(2,1)S(1)}, bf16[96,1024]{1,0:T(8,128)(2,1)S(1)}, u32[]{:S(2)}, u32[]{:S(2)}) collective-permute-start(bf16[96,1024]{1,0:T(8,128)(2,1)S(1)} %collective-permute-done.2.refs_1_), channel_id=1, source_target_pairs={{0,8},{8,0},{16,24},{24,16},{1,9},{9,1},{17,25},{25,17},{2,10},{10... | collective-permute-start | bytes 589832 | tf_op jit(solution)/shard_map/ppermute | solution.py:549
  13.2 1.9 %copy-start = (bf16[512,3,1024]{2,0,1:T(8,128)(2,1)S(1)}, bf16[512,3,1024]{2,0,1:T(8,128)(2,1)}, u32[]{:S(2)}) copy-start(bf16[512,3,1024]{2,0,1:T(8,128)(2,1)} %param.7) | copy-start | bytes 9437188
  20.4 12.1 %collective-permute-start.5 = (bf16[1,2,768,256]{3,2,1,0:T(8,128)(2,1)S(1)}, bf16[1,2,768,256]{3,2,1,0:T(8,128)(2,1)S(1)}, u32[]{:S(2)}, u32[]{:S(2)}) collective-permute-start(bf16[1,2,768,256]{3,2,1,0:T(8,128)(2,1)S(1)} %rest_share.1), channel_id=1, source_target_pairs={{0,2},{1,5},{2,0},{3,7},{4,6},{5,1},{6,4},{7,3},{8,10},{9,13},{10,... | collective-permute-start | bytes 2359304 | tf_op jit(solution)/shard_map/ppermute | solution.py:555
  23.2 22.8 %collective-permute-start.7 = (bf16[1,2,768,256]{3,2,1,0:T(8,128)(2,1)S(1)}, bf16[1,2,768,256]{3,2,1,0:T(8,128)(2,1)S(1)}, u32[]{:S(2)}, u32[]{:S(2)}) collective-permute-start(bf16[1,2,768,256]{3,2,1,0:T(8,128)(2,1)S(1)} %project_mix.2), channel_id=1, source_target_pairs={{0,2},{1,5},{2,0},{3,7},{4,6},{5,1},{6,4},{7,3},{8,10},{9,13},{10,... | collective-permute-start | bytes 2359304 | tf_op jit(solution)/shard_map/ppermute | solution.py:558
  23.8 22.2 %slice-start = ((s8[8388608]{0:T(1024)(128)(4,1)}), s8[4194304]{0:T(1024)(128)(4,1)S(1)}, s32[]{:S(2)}) async-start(s8[8388608]{0:T(1024)(128)(4,1)} %bitcast.1), calls=%async_computation | async-start | bytes 8388608
  25.8 8.8 %copy-start.2 = (f32[3,3,1024]{2,1,0:T(4,128)S(1)}, f32[3,3,1024]{2,1,0:T(4,128)}, u32[]{:S(2)}) copy-start(f32[3,3,1024]{2,1,0:T(4,128)} %refs_4_.1) | copy-start | bytes 110596
  32.5 13.5 %slice-start.1 = ((s8[8388608]{0:T(1024)(128)(4,1)}), s8[4194304]{0:T(1024)(128)(4,1)S(1)}, s32[]{:S(2)}) async-start(s8[8388608]{0:T(1024)(128)(4,1)} %bitcast.1), calls=%async_computation.1 | async-start | bytes 8388608
  32.6 2.0 %collective-permute-start.6 = (bf16[4,16,1024]{2,1,0:T(8,128)(2,1)S(1)}, bf16[4,16,1024]{2,1,0:T(8,128)(2,1)S(1)}, u32[]{:S(2)}, u32[]{:S(2)}) collective-permute-start(bf16[4,16,1024]{2,1,0:T(8,128)(2,1)S(1)} %get-tuple-element.86), channel_id=1, source_target_pairs={{0,1},{1,0},{2,3},{3,2},{4,5},{5,4},{6,7},{7,6},{8,9},{9,8},{10,11... | collective-permute-start | bytes 393224 | tf_op jit(solution)/shard_map/ppermute | solution.py:566
  32.7 16.6 %collective-permute-start.10 = (bf16[768,256]{1,0:T(8,128)(2,1)S(1)}, bf16[768,256]{1,0:T(8,128)(2,1)S(1)}, u32[]{:S(2)}, u32[]{:S(2)}) collective-permute-start(bf16[768,256]{1,0:T(8,128)(2,1)S(1)} %get-tuple-element.81), channel_id=1, source_target_pairs={{0,4},{1,3},{2,6},{3,1},{4,0},{5,7},{6,2},{7,5},{8,12},{9,11},{10,... | collective-permute-start | bytes 1179656 | tf_op jit(solution)/shard_map/ppermute | solution.py:562
  34.2 15.1 %collective-permute-start.11 = (bf16[768,256]{1,0:T(8,128)(2,1)S(1)}, bf16[768,256]{1,0:T(8,128)(2,1)S(1)}, u32[]{:S(2)}, u32[]{:S(2)}) collective-permute-start(bf16[768,256]{1,0:T(8,128)(2,1)S(1)} %get-tuple-element.99), channel_id=1, source_target_pairs={{0,5},{1,2},{2,7},{3,0},{4,1},{5,6},{6,3},{7,4},{8,13},{9,10},{10,... | collective-permute-start | bytes 1179656 | tf_op jit(solution)/shard_map/ppermute | solution.py:563
  46.6 2.8 %copy-start.3 = (f32[8,1024]{1,0:T(8,128)S(1)}, f32[8,1024]{1,0:T(8,128)}, u32[]{:S(2)}) copy-start(f32[8,1024]{1,0:T(8,128)} %refs_5_.1) | copy-start | bytes 98308
  46.6 2.8 %copy-start.4 = (f32[8,1024]{1,0:T(8,128)S(1)}, f32[8,1024]{1,0:T(8,128)}, u32[]{:S(2)}) copy-start(f32[8,1024]{1,0:T(8,128)} %refs_6_.1) | copy-start | bytes 98308
  46.7 2.6 %collective-permute-start.9 = (bf16[768,256]{1,0:T(8,128)(2,1)S(1)}, bf16[768,256]{1,0:T(8,128)(2,1)S(1)}, u32[]{:S(2)}, u32[]{:S(2)}) collective-permute-start(bf16[768,256]{1,0:T(8,128)(2,1)S(1)} %get-tuple-element.98), channel_id=1, source_target_pairs={{0,1},{1,0},{2,3},{3,2},{4,5},{5,4},{6,7},{7,6},{8,9},{9,8},{10,11... | collective-permute-start | bytes 1179656 | tf_op jit(solution)/shard_map/ppermute | solution.py:574
  46.8 7.8 %collective-permute-start.8 = (bf16[192,1024]{1,0:T(8,128)(2,1)S(1)}, bf16[192,1024]{1,0:T(8,128)(2,1)S(1)}, u32[]{:S(2)}, u32[]{:S(2)}) collective-permute-start(bf16[192,1024]{1,0:T(8,128)(2,1)S(1)} %get-tuple-element.94), channel_id=1, source_target_pairs={{0,2},{1,5},{2,0},{3,7},{4,6},{5,1},{6,4},{7,3},{8,10},{9,13},{10,... | collective-permute-start | bytes 1179656 | tf_op jit(solution)/shard_map/ppermute | solution.py:575
  51.8 2.9 %collective-permute-start.12 = (bf16[4,192,128]{2,1,0:T(8,128)(2,1)S(1)}, bf16[4,192,128]{2,1,0:T(8,128)(2,1)S(1)}, u32[]{:S(2)}, u32[]{:S(2)}) collective-permute-start(bf16[4,192,128]{2,1,0:T(8,128)(2,1)S(1)} %get-tuple-element.101), channel_id=1, source_target_pairs={{0,1},{1,0},{2,3},{3,2},{4,5},{5,4},{6,7},{7,6},{8,9},{9,8},{10,11... | collective-permute-start | bytes 589832 | tf_op jit(solution)/shard_map/ppermute | solution.py:579
  51.8 10.5 %collective-permute-start.14 = (bf16[192,1024]{1,0:T(8,128)(2,1)S(1)}, bf16[192,1024]{1,0:T(8,128)(2,1)S(1)}, u32[]{:S(2)}, u32[]{:S(2)}) collective-permute-start(bf16[192,1024]{1,0:T(8,128)(2,1)S(1)} %get-tuple-element.103), channel_id=1, source_target_pairs={{0,2},{1,5},{2,0},{3,7},{4,6},{5,1},{6,4},{7,3},{8,10},{9,13},{10,... | collective-permute-start | bytes 1179656 | tf_op jit(solution)/shard_map/ppermute | solution.py:576
  54.7 12.7 %collective-permute-start.13 = (bf16[192,1024]{1,0:T(8,128)(2,1)S(1)}, bf16[192,1024]{1,0:T(8,128)(2,1)S(1)}, u32[]{:S(2)}, u32[]{:S(2)}) collective-permute-start(bf16[192,1024]{1,0:T(8,128)(2,1)S(1)} %get-tuple-element.102), channel_id=1, source_target_pairs={{0,4},{1,3},{2,6},{3,1},{4,0},{5,7},{6,2},{7,5},{8,12},{9,11},{10,... | collective-permute-start | bytes 1179656 | tf_op jit(solution)/shard_map/ppermute | solution.py:581
  56.2 9.4 %collective-permute-start.15 = (bf16[2,192,128]{2,1,0:T(8,128)(2,1)S(1)}, bf16[2,192,128]{2,1,0:T(8,128)(2,1)S(1)}, u32[]{:S(2)}, u32[]{:S(2)}) collective-permute-start(bf16[2,192,128]{2,1,0:T(8,128)(2,1)S(1)} %get-tuple-element.105), channel_id=1, source_target_pairs={{0,4},{1,3},{2,6},{3,1},{4,0},{5,7},{6,2},{7,5},{8,12},{9,11},{10,... | collective-permute-start | bytes 294920 | tf_op jit(solution)/shard_map/ppermute | solution.py:582
  56.8 8.8 %collective-permute-start.16 = (bf16[2,192,128]{2,1,0:T(8,128)(2,1)S(1)}, bf16[2,192,128]{2,1,0:T(8,128)(2,1)S(1)}, u32[]{:S(2)}, u32[]{:S(2)}) collective-permute-start(bf16[2,192,128]{2,1,0:T(8,128)(2,1)S(1)} %get-tuple-element.106), channel_id=1, source_target_pairs={{0,2},{1,5},{2,0},{3,7},{4,6},{5,1},{6,4},{7,3},{8,10},{9,13},{10,... | collective-permute-start | bytes 294920 | tf_op jit(solution)/shard_map/ppermute | solution.py:582
  58.3 9.1 %collective-permute-start.17 = (bf16[2,192,128]{2,1,0:T(8,128)(2,1)S(1)}, bf16[2,192,128]{2,1,0:T(8,128)(2,1)S(1)}, u32[]{:S(2)}, u32[]{:S(2)}) collective-permute-start(bf16[2,192,128]{2,1,0:T(8,128)(2,1)S(1)} %get-tuple-element.107), channel_id=1, source_target_pairs={{0,6},{1,7},{2,4},{3,5},{4,2},{5,3},{6,0},{7,1},{8,14},{9,15},{10,... | collective-permute-start | bytes 294920 | tf_op jit(solution)/shard_map/ppermute | solution.py:582
  68.3 11.7 %collective-permute-start.18 = (bf16[192,1024]{1,0:T(8,128)(2,1)S(1)}, bf16[192,1024]{1,0:T(8,128)(2,1)S(1)}, u32[]{:S(2)}, u32[]{:S(2)}) collective-permute-start(bf16[192,1024]{1,0:T(8,128)(2,1)S(1)} %get-tuple-element.111), channel_id=1, source_target_pairs={{0,8},{8,0},{16,24},{24,16},{1,9},{9,1},{17,25},{25,17},{2,10},{10... | collective-permute-start | bytes 1179656 | tf_op jit(solution)/shard_map/ppermute | solution.py:497
  70.5 17.0 %collective-permute-start.19 = (bf16[192,1024]{1,0:T(8,128)(2,1)S(1)}, bf16[192,1024]{1,0:T(8,128)(2,1)S(1)}, u32[]{:S(2)}, u32[]{:S(2)}) collective-permute-start(bf16[192,1024]{1,0:T(8,128)(2,1)S(1)} %out_columns.3.refs_2_), channel_id=1, source_target_pairs={{8,16},{16,8},{9,17},{17,9},{10,18},{18,10},{11,19},{19,11},{12,20... | collective-permute-start | bytes 1179656 | tf_op jit(solution)/shard_map/ppermute | solution.py:499
  71.8 15.7 %collective-permute-start.20 = (bf16[192,1024]{1,0:T(8,128)(2,1)S(1)}, bf16[192,1024]{1,0:T(8,128)(2,1)S(1)}, u32[]{:S(2)}, u32[]{:S(2)}) collective-permute-start(bf16[192,1024]{1,0:T(8,128)(2,1)S(1)} %out_columns.4.refs_0_), channel_id=1, source_target_pairs={{0,16},{24,8},{1,17},{25,9},{2,18},{26,10},{3,19},{27,11},{4,20},{... | collective-permute-start | bytes 1179656 | tf_op jit(solution)/shard_map/ppermute | solution.py:502
  80.1 21.4 %collective-permute-start.21 = (bf16[192,1024]{1,0:T(8,128)(2,1)S(1)}, bf16[192,1024]{1,0:T(8,128)(2,1)S(1)}, u32[]{:S(2)}, u32[]{:S(2)}) collective-permute-start(bf16[192,1024]{1,0:T(8,128)(2,1)S(1)} %last_step.1), channel_id=1, source_target_pairs={{0,8},{8,24},{16,0},{24,16},{1,9},{9,25},{17,1},{25,17},{2,10},{10... | collective-permute-start | bytes 1179656 | tf_op jit(solution)/shard_map/ppermute | solution.py:510
